TPU v7x, 32 devices: a whole 2x2x4 slice. The times are simulated.
32 devices in a mesh: dom: 4 (over y, core), feat: 8 (over z, x).
Axes of the slice: x: 2, y: 2, z: 4, core: 2. Of those that a mesh axis runs over, the one named last changes fastest.
Arguments:
- node_feats: bfloat16 [1024, 16384], P('feat', 'dom'), may hold values from -6 to 6
- send_rows: int32 [2048], P('dom'), may hold values from 0 to 4095
- hub_rows: int32 [512], P('dom'), may hold values from 0 to 4095
- tile_dst: int32 [2048], P('dom'), may hold values from 0 to 7
- tile_src: int32 [2048], P('dom'), may hold values from 0 to 39
- tile_count: int32 [4], P('dom'), may hold values from 128 to 512, as said below
- tile_vals: bfloat16 [2048, 128, 128], P('dom'), may hold values from -0.0625 to 0.0625
- w_self: bfloat16 [1024, 1024], P('feat'), may hold values from -0.1875 to 0.1875
- w_neigh: bfloat16 [1024, 1024], P('feat'), may hold values from -0.1875 to 0.1875
- bias_vec: float32 [1024], P('feat'), may hold values from -3 to 3
- cotangent: bfloat16 [1024, 4096], P('feat', 'dom'), may hold values from -6 to 6
Outputs:
- activations: bfloat16 [1024, 4096], P('feat', 'dom')
- grad_feats: float32 [1024, 16384], P('feat', 'dom')
- grad_w_self: float32 [1024, 1024], P('feat')
- grad_w_neigh: float32 [1024, 1024], P('feat')
- grad_bias: float32 [1024], P('feat')
Inputs may be any that keep to these rules, and one draw needn't show every extreme that they name: `tile_count`: every partition has at least 128 live slots, and some partition has all 512 live; slots at or past the count are not edges: their tile_vals may hold any values and must be ignored.
All inputs are finite; a program needn't handle non-finite values.
Results may differ from a plain program's by a relative error of at most 0.0075.
Values may be sent and summed in bfloat16 or wider, within the bound.
No kernel may reach another device: no remote copies, remote signals or barrier semaphores. Data moves between devices by JAX's collectives and lax.ppermute only.
A program may use at most 128 MiB of HBM per device.

v0:
```python
import jax
import jax.numpy as jnp
from jax import lax
from jax.sharding import PartitionSpec as P


def contract_first(left, right):
    return lax.dot_general(
        left, right, (((0,), (0,)), ((), ())), preferred_element_type=jnp.float32
    )


def contract_last(left, right):
    return lax.dot_general(
        left, right, (((1,), (1,)), ((), ())), preferred_element_type=jnp.float32
    )


def body(
    node_feats,
    send_rows,
    hub_rows,
    tile_dst,
    tile_src,
    tile_count,
    tile_vals,
    w_self,
    w_neigh,
    bias_vec,
    cotangent,
):
    feat_cols = node_feats.shape[0]
    own_rows = node_feats.shape[1]
    dst_rows = cotangent.shape[1]
    sent_total = send_rows.shape[0]
    outgoing = jnp.take(node_feats, send_rows, axis=1)
    halo_cols = lax.all_to_all(outgoing, "dom", split_axis=1, concat_axis=1, tiled=True)
    hub_cols = lax.all_gather(jnp.take(node_feats, hub_rows, axis=1), "dom", axis=1, tiled=True)
    source_table = jnp.concatenate([node_feats, halo_cols, hub_cols], axis=1)
    tile_total = source_table.shape[1] // 128
    dst_tiles = dst_rows // 128
    live_mask = (jnp.arange(tile_dst.shape[0]) < tile_count[0]).astype(jnp.float32)
    dst_hot = (tile_dst[:, None] == jnp.arange(dst_tiles)[None, :]).astype(jnp.float32) * live_mask[
        :, None
    ]
    src_hot = (tile_src[:, None] == jnp.arange(tile_total)[None, :]).astype(
        jnp.float32
    ) * live_mask[:, None]
    picked = source_table.reshape(feat_cols, tile_total, 128)[:, tile_src, :]
    products = jnp.einsum("fkj,kij->fki", picked, tile_vals, preferred_element_type=jnp.float32)
    summed = jnp.einsum("fki,ku->fui", products, dst_hot, precision=lax.Precision.HIGHEST)
    aggregate = summed.reshape(feat_cols, dst_rows).astype(jnp.bfloat16)
    dst_feats = node_feats[:, :dst_rows]
    whole_self, whole_agg = (
        lax.all_gather(dst_feats, "feat", axis=0, tiled=True),
        lax.all_gather(aggregate, "feat", axis=0, tiled=True),
    )
    pre_act = (
        jnp.dot(w_self, whole_self, preferred_element_type=jnp.float32)
        + jnp.dot(w_neigh, whole_agg, preferred_element_type=jnp.float32)
        + bias_vec[:, None]
    )
    sig_val = jax.nn.sigmoid(pre_act)
    activations = (pre_act * sig_val).astype(jnp.bfloat16)
    grad_pre = (cotangent.astype(jnp.float32) * sig_val * (1.0 + pre_act * (1.0 - sig_val))).astype(
        jnp.bfloat16
    )
    local_self = contract_last(grad_pre, whole_self)
    local_neigh = contract_last(grad_pre, whole_agg)
    local_bias = jnp.sum(grad_pre.astype(jnp.float32), axis=1)
    grad_w_self, grad_w_neigh, grad_bias = lax.psum((local_self, local_neigh, local_bias), "dom")
    both_grads = lax.psum_scatter(
        jnp.concatenate(
            [contract_first(w_self, grad_pre), contract_first(w_neigh, grad_pre)], axis=1
        ),
        "feat",
        scatter_dimension=0,
        tiled=True,
    )
    grad_self_in = both_grads[:, :dst_rows]
    grad_agg = both_grads[:, dst_rows:].astype(jnp.bfloat16)
    upstream = grad_agg.reshape(feat_cols, dst_tiles, 128)[:, tile_dst, :]
    back_terms = jnp.einsum("fki,kij->fkj", upstream, tile_vals, preferred_element_type=jnp.float32)
    placed = jnp.einsum("fkj,kt->ftj", back_terms, src_hot, precision=lax.Precision.HIGHEST)
    grad_table = placed.reshape(feat_cols, tile_total * 128)
    halo_grad = grad_table[:, own_rows : own_rows + sent_total]
    hub_grad = grad_table[:, own_rows + sent_total :]
    returned = lax.all_to_all(
        halo_grad.astype(jnp.bfloat16), "dom", split_axis=1, concat_axis=1, tiled=True
    ).astype(halo_grad.dtype)
    hub_total = lax.psum_scatter(
        hub_grad.astype(jnp.bfloat16), "dom", scatter_dimension=1, tiled=True
    ).astype(jnp.float32)
    grad_feats = grad_table[:, :own_rows]
    grad_feats = grad_feats.at[:, send_rows].add(returned)
    grad_feats = grad_feats.at[:, hub_rows].add(hub_total)
    grad_feats = grad_feats.at[:, :dst_rows].add(grad_self_in)
    return (activations, grad_feats, grad_w_self, grad_w_neigh, grad_bias)


def solution(mesh):
    return jax.shard_map(
        body,
        mesh=mesh,
        in_specs=(
            P("feat", "dom"),
            P("dom"),
            P("dom"),
            P("dom"),
            P("dom"),
            P("dom"),
            P("dom", None, None),
            P("feat", None),
            P("feat", None),
            P("feat"),
            P("feat", "dom"),
        ),
        out_specs=(P("feat", "dom"), P("feat", "dom"), P("feat", None), P("feat", None), P("feat")),
        check_vma=False,
    )
```

profile of v0, /device:TPU:0, one launch (start us, length us, event | category | flops | bytes accessed | tf_op | source)
XLA Modules:
  0.0 480.8 jit_solution(5123513261814923447)
XLA Ops:
  7.2 1.7 slice.40
  9.0 0.7 and_bitcast_fusion
  9.7 0.7 compare_select_fusion.2
  10.4 1.6 copy.44
  12.0 1.3 gather_fusion
  13.3 0.8 broadcast_select_fusion
  14.1 4.2 all-to-all-start
  19.1 0.7 gather_fusion.1
  19.8 0.1 select_bitcast_fusion
  19.9 5.7 %all_gather.10 = bf16[128,512]{0,1:T(8,128)(2,1)S(1)} all-gather(bf16[128,128]{0,1:T(8,128)(2,1)S(1)} %select_bitcast_fusion), channel_id=1, replica_groups=mesh['dom'=4,'feat'=8] {'dom'}, dimensions={1}, use_global_device_ids=true | all-gather | bytes 163840 | tf_op jit(solution)/shard_map/all_gather | solution.py:38
  25.6 0.1 pad_maximum_fusion.1
  25.6 0.8 copy.45
  26.4 14.0 %gather_fusion.2 = bf16[512,128,128]{2,1,0:T(8,128)(2,1)} fusion(bf16[128,40,128]{2,0,1:T(8,128)(2,1)S(1)} %copy.45, s32[1024]{0:T(1024)S(1)} %pad_clamp_fusion.1), kind=kCustom, calls=%fused_computation.2 | custom fusion | bytes 33556480 | tf_op jit(solution)/shard_map/gather | solution.py:49
  40.4 28.3 %fusion.8 = f32[128,512,128]{2,0,1:T(8,128)} fusion(bf16[512,128,128]{2,1,0:T(8,128)(2,1)} %param.19, bf16[512,128,128]{2,1,0:T(8,128)(2,1)} %gather_fusion.2), kind=kOutput, calls=%fused_computation.14 | convolution fusion | flops 2147483648 | bytes 67108864 | tf_op jit(solution)/shard_map/fkj,kij->fki/dot_general | solution.py:50
  68.7 43.4 %fusion.19 = bf16[8,128,128]{2,0,1:T(8,128)(2,1)S(1)} fusion(f32[128,512,128]{2,0,1:T(8,128)} %fusion.8, f32[512]{0:T(512)S(1)} %fusion.37, s32[512]{0:T(512)S(1)} %copy-done.5), kind=kOutput, calls=%fused_computation.24 | convolution fusion | flops 805445632 | bytes 33820672 | tf_op jit(solution)/shard_map/fki,ku->fui/dot_general | solution.py:51
  112.1 0.8 copy.65
  112.9 0.3 reduce-scatter.3.cloned.1.call-start
  113.2 2.0 fusion.41
  115.2 49.2 %all-gather.5.cloned.1.call-done = bf16[1024,1024]{1,0:T(8,128)(2,1)} async-done(((bf16[128,1024]{1,0:T(8,128)(2,1)}), bf16[1024,1024]{1,0:T(8,128)(2,1)}) %all-gather.5.cloned.1.call-update) | async-done | bytes 2097168 | tf_op jit(solution)/shard_map/all_gather | solution.py:56
  164.4 2.8 convert_reduce_fusion
  167.3 0.7 convolution_bitcast_fusion
  168.0 0.7 convolution_bitcast_fusion.1
  168.8 4.1 pad_maximum_fusion
  172.9 0.0 reduce-scatter.5.cloned.1.call-start
  172.9 1.5 copy-done.2
  174.4 1.6 fusion.43
  176.0 144.9 %reduce-scatter.3.cloned.1.call-done = f32[128,2048]{0,1:T(8,128)} async-done(((f32[1024,2048]{0,1:T(8,128)}), f32[128,2048]{0,1:T(8,128)}) %reduce-scatter.3.cloned.1.call-update) | async-done | bytes 1048592 | tf_op jit(solution)/shard_map/reduce_scatter | solution.py:72
  320.9 1.1 slice.64
  322.0 0.2 copy.48
  322.2 13.8 %gather_fusion.3 = bf16[512,128,128]{2,1,0:T(8,128)(2,1)} fusion(bf16[128,8,128]{2,0,1:T(8,128)(2,1)S(1)} %copy.48, s32[1024]{0:T(1024)S(1)} %pad_clamp_fusion), kind=kCustom, calls=%fused_computation.3 | custom fusion | bytes 33556480 | tf_op jit(solution)/shard_map/gather | solution.py:82
  336.0 24.4 %fusion.11 = f32[128,512,128]{2,0,1:T(8,128)} fusion(bf16[512,128,128]{2,1,0:T(8,128)(2,1)} %param.19, bf16[512,128,128]{2,1,0:T(8,128)(2,1)} %gather_fusion.3), kind=kOutput, calls=%fused_computation.15 | convolution fusion | flops 2147483648 | bytes 67108864 | tf_op jit(solution)/shard_map/fki,kij->fkj/dot_general | solution.py:83
  360.3 48.5 %fusion.14 = f32[128,40,128]{2,1,0:T(8,128)} fusion(f32[128,512,128]{2,0,1:T(8,128)} %fusion.11, f32[512]{0:T(512)S(1)} %fusion.37, s32[512]{0:T(512)S(1)} %copy-done.6), kind=kOutput, calls=%fused_computation.19 | convolution fusion | flops 4026572800 | bytes 36179968 | tf_op jit(solution)/shard_map/fkj,kt->ftj/dot_general | solution.py:84
  408.9 2.6 copy.54
  411.5 0.1 bitcast_convert_fusion
  411.6 0.7 fusion.40
  412.3 0.0 all-reduce.3.cloned.1.call-start
  412.4 3.2 fusion.42
  415.6 3.3 all-to-all-start.1
  419.0 0.6 compare_reduce_fusion
  419.6 8.1 %psum.23 = f32[128]{0:T(128)} all-reduce(f32[128]{0:T(128)S(1)} %get-tuple-element.39), channel_id=1, replica_groups=mesh['dom'=4,'feat'=8] {'dom'}, use_global_device_ids=true, to_apply=%region_8.9 | all-reduce | flops 128 | bytes 1024 | tf_op jit(solution)/shard_map/psum | solution.py:71
  427.8 1.5 slice.56
  429.2 6.0 %scatter_custom_fusion = f32[128,4096]{0,1:T(8,128)} fusion(f32[128,4096]{0,1:T(8,128)} %slice.56, s32[512]{0:T(512)S(1)} %compare_select_fusion.2, bf16[128,512]{0,1:T(8,128)(2,1)S(1)} %bitcast.80), kind=kCustom, calls=%fused_computation.34 | custom fusion | flops 131072 | bytes 2228224 | tf_op jit(solution)/shard_map/scatter-add | solution.py:95
  435.3 4.3 scatter_custom_fusion.1
  439.6 2.5 fusion.22
  442.1 2.9 copy.52
  444.9 25.1 %all-reduce.3.cloned.1.call-done = (f32[128,1024]{1,0:T(8,128)}, f32[128,1024]{1,0:T(8,128)}) async-done(((f32[128,1024]{1,0:T(8,128)}, f32[128,1024]{1,0:T(8,128)}), (f32[128,1024]{1,0:T(8,128)}, f32[128,1024]{1,0:T(8,128)})) %all-reduce.3.cloned.1.call-update) | async-done | bytes 1048592 | tf_op jit(solution)/shard_map/psum | solution.py:71
  470.0 1.9 copy.72
  471.9 1.9 copy.73
  (39 shorter events, 0.2 us)
Async XLA Ops:
  7.2 157.3 %copy-start = (bf16[128,1024]{1,0:T(8,128)(2,1)S(1)}, bf16[128,1024]{1,0:T(8,128)(2,1)}, u32[]{:S(2)}) copy-start(bf16[128,1024]{1,0:T(8,128)(2,1)} %param.21) | copy-start | bytes 786436
  7.2 11.2 %copy-start.8 = (s32[128]{0:T(128)S(1)}, s32[128]{0:T(128)}, u32[]{:S(2)}) copy-start(s32[128]{0:T(128)} %param.15) | copy-start | bytes 1540
  7.2 11.8 %copy-start.6 = (s32[512]{0:T(512)S(1)}, s32[512]{0:T(512)}, u32[]{:S(2)}) copy-start(s32[512]{0:T(512)} %param.17) | copy-start | bytes 6148
  7.2 106.0 %all-gather.3.cloned.1.call-start = ((), (), s32[]{:S(2)}) async-start(), calls=%async_computation.4 | async-start | bytes 2359296 | tf_op jit(solution)/shard_map/all_gather | solution.py:55
  14.1 11.4 %all-to-all-start = ((bf16[128,4,128]{0,2,1:T(8,128)(2,1)}), bf16[128,4,128]{0,2,1:T(8,128)(2,1)S(1)}, u32[]{:S(2)}, u32[]{:S(2)}) async-start(bf16[128,4,128]{0,2,1:T(8,128)(2,1)} %broadcast_select_fusion), calls=%async_computation | async-start | bytes 262144 | tf_op jit(solution)/shard_map/all_to_all | solution.py:37
  18.4 146.1 %all-gather.5.cloned.1.call-start = ((), (), s32[]{:S(2)}) async-start(), calls=%async_computation.5 | async-start | bytes 2359296 | tf_op jit(solution)/shard_map/all_gather | solution.py:56
  40.4 28.3 %copy-start.5 = (s32[512]{0:T(512)S(1)}, s32[512]{0:T(512)}, u32[]{:S(2)}) copy-start(s32[512]{0:T(512)} %param.16) | copy-start | bytes 6148
  68.7 44.5 %copy-start.3 = (bf16[128,1024]{1,0:T(8,128)(2,1)S(1)}, bf16[128,1024]{1,0:T(8,128)(2,1)}, u32[]{:S(2)}) copy-start(bf16[128,1024]{1,0:T(8,128)(2,1)} %param.20) | copy-start | bytes 786436
  112.1 52.4 %copy-start.7 = (bf16[128,1024]{1,0:T(8,128)(2,1)S(1)}, bf16[128,1024]{1,0:T(8,128)(2,1)}, u32[]{:S(2)}) copy-start(bf16[128,1024]{1,0:T(8,128)(2,1)} %param.23) | copy-start | bytes 786436
  112.1 52.3 %copy-start.9 = (f32[128]{0:T(128)S(1)}, f32[128]{0:T(128)}, u32[]{:S(2)}) copy-start(f32[128]{0:T(128)} %param.22) | copy-start | bytes 1540
  112.9 208.1 %reduce-scatter.3.cloned.1.call-start = ((), (), s32[]{:S(2)}) async-start(), calls=%async_computation.6 | async-start | bytes 9437184 | tf_op jit(solution)/shard_map/reduce_scatter | solution.py:72
  172.8 1.6 copy-start.2
  172.9 262.4 %reduce-scatter.5.cloned.1.call-start = ((), (), s32[]{:S(2)}) async-start(), calls=%async_computation.7 | async-start | bytes 163840 | tf_op jit(solution)/shard_map/reduce_scatter | solution.py:91
  412.3 57.7 %all-reduce.3.cloned.1.call-start = ((), (), s32[]{:S(2)}) async-start(), calls=%async_computation.8 | async-start | bytes 2097152 | tf_op jit(solution)/shard_map/psum | solution.py:71
  415.6 13.6 %all-to-all-start.1 = ((bf16[128,4,128]{0,2,1:T(8,128)(2,1)}), bf16[128,4,128]{0,2,1:T(8,128)(2,1)S(1)}, u32[]{:S(2)}, u32[]{:S(2)}) async-start(bf16[128,4,128]{0,2,1:T(8,128)(2,1)} %bitcast.19), calls=%async_computation.2 | async-start | bytes 262144 | tf_op jit(solution)/shard_map/all_to_all | solution.py:88
  429.2 10.3 %copy-start.4 = (f32[128,2048]{0,1:T(8,128)S(1)}, f32[128,2048]{0,1:T(8,128)}, u32[]{:S(2)}) copy-start(f32[128,2048]{0,1:T(8,128)} %reduce-scatter.3.cloned.1.call-done) | copy-start | bytes 3145732
  439.6 34.2 %copy-start.1 = (bf16[128,1024]{1,0:T(8,128)(2,1)S(1)}, bf16[128,1024]{1,0:T(8,128)(2,1)}, u32[]{:S(2)}) copy-start(bf16[128,1024]{1,0:T(8,128)(2,1)} %param.21) | copy-start | bytes 786436
Sparse Core Ops, SparseCore 0:
  10.7 51.9 all-gather.2
  113.0 51.3 all-gather.4
  173.0 147.9 reduce-scatter.2
  412.5 18.4 reduce-scatter.4
  433.9 36.1 all-reduce.2
where the time goes:
time: 487 us; the launch traced here: 481 us
  waiting for transfers between devices  219 us (45%)
  matrix products  156 us (32%)
  local copies, waits for them, and re-layouts  48.8 us (10%)
  other arithmetic  20.1 us (4%)
  between operations  15.1 us (3%)
  blocking collectives  13.8 us (3%)
  starting transfers between devices  7.95 us (2%)
    reduce_scatter x1, waiting for transfers between devices, body(): lax.psum_scatter(jnp.concatenate([contract_first(w_self, grad_pre), contr...  145 us
    all_gather x1, waiting for transfers between devices, body(): lax.all_gather(aggregate, 'feat', axis=0, tiled=True)  49.2 us
    dot_general x1, matrix products, body(): jnp.einsum('fkj,kt->ftj', back_terms, src_hot, precision=lax.Precision.HI...  48.5 us
    dot_general x1, matrix products, body(): jnp.einsum('fki,ku->fui', products, dst_hot, precision=lax.Precision.HIGH...  43.4 us
    dot_general x1, matrix products, body(): jnp.einsum('fkj,kij->fki', picked, tile_vals, preferred_element_type=jnp....  28.3 us
    psum x1, waiting for transfers between devices, body(): lax.psum((local_self, local_neigh, local_bias), 'dom')  25.1 us
    dot_general x1, matrix products, body(): jnp.einsum('fki,kij->fkj', upstream, tile_vals, preferred_element_type=jn...  24.4 us
    gather x1, local copies, waits for them, and re-layouts, body(): picked = source_table.reshape(feat_cols, tile_total, 128)[:, tile_src, :]  14 us
  transfers between devices with their start and end apart: 7, of which 3 were waited for; matrix products, arithmetic and copies ran while one was open for 25% of the time, Pallas kernels for 0%

commit v1 on v0

v1 whole, which is shorter than its diff:
```python
import functools

import jax
import jax.numpy as jnp
from jax import lax
from jax.experimental import pallas as pl
from jax.experimental.pallas import tpu as pltpu
from jax.sharding import Mesh, PartitionSpec as P

T = 128
BF = jnp.bfloat16
F32 = jnp.float32
MIB = 1 << 20


def dot(left, right, dims):
    return lax.dot_general(left, right, (dims, ((), ())), preferred_element_type=F32)


def params(mib):
    return pltpu.CompilerParams(vmem_limit_bytes=mib * MIB)


def gather_kernel(x_ref, idx_ref, out_ref):
    readers = out_ref.shape[0]
    x = x_ref[...]
    rows = lax.broadcasted_iota(jnp.int32, (x.shape[1], T), 0)
    for q in range(readers + 1):
        hot = (rows == idx_ref[q : q + 1, :]).astype(F32).astype(BF)
        got = dot(x, hot, ((1,), (0,))).astype(BF)
        if q < readers:
            out_ref[q, :, :T] = got
        else:
            for r in range(readers):
                out_ref[r, :, T:] = got


def gather_cols(x, idx):
    readers = idx.shape[0] - 1
    return pl.pallas_call(
        gather_kernel,
        out_shape=jax.ShapeDtypeStruct((readers, x.shape[0], 2 * T), BF),
        in_specs=[pl.BlockSpec(memory_space=pltpu.VMEM)] * 2,
        out_specs=pl.BlockSpec(memory_space=pltpu.VMEM),
        compiler_params=params(40),
        name="gather_cols",
    )(x, idx)


def build_kernel(per, n_src, n_own, pos_ref, count_ref, vals_ref, own_ref, ext_ref, acc_ref):
    step = pl.program_id(0)
    blocks = pos_ref.shape[0] // per

    @pl.when(step == 0)
    def _():
        def clear(i, c):
            acc_ref[i] = jnp.zeros((T, T), F32)
            return c

        lax.fori_loop(0, acc_ref.shape[0], clear, 0, unroll=4)

    @pl.when(step < blocks)
    def _():
        live = jnp.clip(count_ref[0] - step * per, 0, per)

        def add(i, c):
            at = pos_ref[step * per + i]
            acc_ref[at] += vals_ref[i].astype(F32)
            return c

        lax.fori_loop(0, live, add, 0)

    @pl.when(step >= blocks)
    def _():
        u = step - blocks
        for s in range(n_src):
            tile = acc_ref[u * n_src + s].astype(BF)
            if s < n_own:
                own_ref[:, s * T : (s + 1) * T] = tile
            else:
                ext_ref[:, (s - n_own) * T : (s - n_own + 1) * T] = tile


def build_dense(vals, pos, count, n_dst, n_src, n_own):
    per = 32
    slots = vals.shape[0]
    blocks = slots // per

    def vals_map(i, pos, count):
        return (jnp.minimum(i, (count[0] - 1) // per), 0, 0)

    def out_map(i, pos, count):
        return (jnp.maximum(i - blocks, 0), 0)

    return pl.pallas_call(
        functools.partial(build_kernel, per, n_src, n_own),
        out_shape=(
            jax.ShapeDtypeStruct((n_dst * T, n_own * T), BF),
            jax.ShapeDtypeStruct((n_dst * T, (n_src - n_own) * T), BF),
        ),
        grid_spec=pltpu.PrefetchScalarGridSpec(
            num_scalar_prefetch=2,
            grid=(blocks + n_dst,),
            in_specs=[pl.BlockSpec((per, T, T), vals_map)],
            out_specs=[
                pl.BlockSpec((T, n_own * T), out_map),
                pl.BlockSpec((T, (n_src - n_own) * T), out_map),
            ],
            scratch_shapes=[pltpu.VMEM((n_dst * n_src, T, T), F32)],
        ),
        compiler_params=params(48),
        cost_estimate=pl.CostEstimate(flops=0, bytes_accessed=slots * T * T * 2 * 2, transcendentals=0),
        name="build_dense",
    )(pos, count, vals)


def middle_kernel(w_ref, xc_ref, agg_ref, bias_ref, act_ref, g_ref, gagg_ref, gself_ref):
    groups, sub = w_ref.shape[0], w_ref.shape[1] // 2
    width = w_ref.shape[2]
    rows = groups * sub
    w_self = w_ref[:, :sub, :].reshape(rows, width)
    w_neigh = w_ref[:, sub:, :].reshape(rows, width)
    bias = bias_ref[...]
    for p in range(agg_ref.shape[0]):
        pre = dot(w_self, xc_ref[p, :width, :], ((1,), (0,)))
        pre += dot(w_neigh, agg_ref[p], ((1,), (0,)))
        pre += bias
        sig = 1.0 / (1.0 + jnp.exp(-pre))
        act_ref[p] = (pre * sig).astype(BF)
        cot = xc_ref[p, width:, :].astype(F32)
        grad = (cot * sig * (1.0 + pre * (1.0 - sig))).astype(BF)
        g_ref[p] = grad
        gagg_ref[p] = dot(w_neigh, grad, ((0,), (0,))).astype(BF)
        gself_ref[p] = dot(w_self, grad, ((0,), (0,))).astype(BF)


def middle(w, xc, agg, bias):
    parts, width, n = agg.shape
    rows = w.shape[0] * w.shape[1] // 2
    small = jax.ShapeDtypeStruct((parts, rows, n), BF)
    large = jax.ShapeDtypeStruct((parts, width, n), BF)
    return pl.pallas_call(
        middle_kernel,
        out_shape=(small, small, large, large),
        in_specs=[pl.BlockSpec(memory_space=pltpu.VMEM)] * 4,
        out_specs=[pl.BlockSpec(memory_space=pltpu.VMEM)] * 4,
        compiler_params=params(48),
        name="middle",
    )(w, xc, agg, bias)


def wgrad_kernel(g_ref, xc_ref, agg_ref, out_ref):
    parts, rows, _ = g_ref.shape
    width = agg_ref.shape[1]
    groups, sub, _ = out_ref.shape
    own = jnp.zeros((rows, width), F32)
    neigh = jnp.zeros((rows, width), F32)
    total = jnp.zeros((rows, 1), F32)
    for p in range(parts):
        grad = g_ref[p]
        own += dot(grad, xc_ref[p, :width, :], ((1,), (1,)))
        neigh += dot(grad, agg_ref[p], ((1,), (1,)))
        total += jnp.sum(grad.astype(F32), axis=1, keepdims=True)
    out_ref[:, :, :width] = own.astype(BF).reshape(groups, sub, width)
    out_ref[:, :, width : 2 * width] = neigh.astype(BF).reshape(groups, sub, width)
    high = total.astype(BF).astype(F32)
    lane = lax.broadcasted_iota(jnp.int32, (rows, T), 1)
    both = jnp.where(lane == 0, high, jnp.where(lane == 1, total - high, 0.0))
    out_ref[:, :, 2 * width :] = both.astype(BF).reshape(groups, sub, T)


def wgrad(g, xc, agg, groups):
    rows, width = g.shape[1], agg.shape[1]
    return pl.pallas_call(
        wgrad_kernel,
        out_shape=jax.ShapeDtypeStruct((groups, rows // groups, 2 * width + T), BF),
        in_specs=[pl.BlockSpec(memory_space=pltpu.VMEM)] * 3,
        out_specs=pl.BlockSpec(memory_space=pltpu.VMEM),
        compiler_params=params(48),
        name="wgrad",
    )(g, xc, agg)


def finish_kernel(dst_blocks, base_ref, ret_ref, idx_ref, gself_ref, out_ref):
    step = pl.program_id(0)
    readers, _, k = ret_ref.shape
    width = out_ref.shape[1]
    cols = lax.broadcasted_iota(jnp.int32, (k, width), 1) + step * width
    total = base_ref[...]
    for q in range(readers):
        hot = (cols == idx_ref[q]).astype(F32).astype(BF)
        total += dot(ret_ref[q], hot, ((1,), (0,)))
    own = gself_ref[...].astype(F32)
    out_ref[...] = total + jnp.where(step < dst_blocks, own, 0.0)


def finish(base, ret, idx, gself):
    rows, n = base.shape
    width = 512
    dst_blocks = gself.shape[1] // width
    return pl.pallas_call(
        functools.partial(finish_kernel, dst_blocks),
        out_shape=jax.ShapeDtypeStruct((rows, n), F32),
        grid=(n // width,),
        in_specs=[
            pl.BlockSpec((rows, width), lambda i: (0, i)),
            pl.BlockSpec(ret.shape, lambda i: (0, 0, 0)),
            pl.BlockSpec(idx.shape, lambda i: (0, 0, 0)),
            pl.BlockSpec((rows, width), lambda i: (0, jnp.minimum(i, dst_blocks - 1))),
        ],
        out_specs=pl.BlockSpec((rows, width), lambda i: (0, i)),
        compiler_params=params(40),
        name="finish",
    )(base, ret, idx, gself)


def body(
    node_feats,
    send_rows,
    hub_rows,
    tile_dst,
    tile_src,
    tile_count,
    tile_vals,
    w_self,
    w_neigh,
    bias_vec,
    cotangent,
):
    dom = ("c", "y")
    n_dom = lax.axis_size("y") * lax.axis_size("c")
    n_feat = lax.axis_size("feat")
    rows = node_feats.shape[0]
    own_rows = node_feats.shape[1]
    dst_rows = cotangent.shape[1]
    width = w_self.shape[1]
    n_own, n_dst = own_rows // T, dst_rows // T
    n_src = n_own + 2 * n_dom
    piece = dst_rows // n_feat
    sub = w_self.shape[0] // n_dom
    d = lax.axis_index(dom)

    halo_tile = n_own + 2 * (tile_src - n_own)
    hub_tile = n_own + 2 * (tile_src - n_own - n_dom) + 1
    place = jnp.where(
        tile_src < n_own, tile_src, jnp.where(tile_src < n_own + n_dom, halo_tile, hub_tile)
    )
    pos = tile_dst * n_src + place
    idx = jnp.concatenate([send_rows.reshape(n_dom, T), hub_rows[None, :]], axis=0)
    outgoing = gather_cols(node_feats, idx)
    incoming = lax.all_to_all(outgoing, ("y", "c"), 0, 0, tiled=True)

    high = bias_vec.astype(BF)
    low = (bias_vec - high.astype(F32)).astype(BF)
    bias_rows = jnp.pad(jnp.stack([high, low]), ((0, 14), (0, 0)))

    def by_piece(x):
        return x.reshape(rows, n_feat, piece).transpose(1, 0, 2)

    xc = jnp.concatenate(
        [
            by_piece(node_feats[:, :dst_rows]),
            by_piece(cotangent),
            jnp.broadcast_to(bias_rows[None], (n_feat, 16, rows)),
        ],
        axis=1,
    )
    xc = lax.all_to_all(xc, "feat", 0, 0, tiled=True)

    mine = jnp.concatenate(
        [
            lax.dynamic_slice_in_dim(w_self, d * sub, sub, axis=0),
            lax.dynamic_slice_in_dim(w_neigh, d * sub, sub, axis=0),
        ],
        axis=0,
    )
    w_part = lax.all_to_all(
        jnp.broadcast_to(mine[None], (n_feat, 2 * sub, width)), "feat", 0, 0, tiled=True
    )

    a_own, a_ext = build_dense(tile_vals, pos, tile_count, n_dst, n_src, n_own)
    agg_own = dot(node_feats, a_own, ((1,), (1,)))

    x_all = xc[:, :rows, :].reshape(1, width, piece)
    cot = xc[:, rows : 2 * rows, :].reshape(n_feat, n_dom, sub, piece).transpose(1, 0, 2, 3)
    xc_dom = jnp.concatenate(
        [
            jnp.broadcast_to(x_all, (n_dom, width, piece)),
            cot.reshape(n_dom, n_feat * sub, piece),
        ],
        axis=1,
    )
    xc_dom = lax.all_to_all(xc_dom, dom, 0, 0, tiled=True)
    bias = xc[:, 2 * rows, :].astype(F32) + xc[:, 2 * rows + 1, :].astype(F32)
    bias = lax.dynamic_slice_in_dim(bias, d * sub, sub, axis=1).reshape(n_feat * sub, 1)

    halo = incoming.transpose(1, 0, 2).reshape(rows, 2 * n_dom * T)
    agg = (agg_own + dot(halo, a_ext, ((1,), (1,)))).astype(BF)
    agg = lax.all_to_all(by_piece(agg), "feat", 0, 0, tiled=True)
    agg = agg.reshape(1, width, piece)
    agg = lax.all_gather(agg, "y", axis=0, tiled=True)
    agg = lax.all_gather(agg, "c", axis=0, tiled=True)

    act, grad, gagg, gself = middle(w_part, xc_dom, agg, bias)

    gagg = lax.all_to_all(gagg, dom, 0, 0, tiled=True)
    gagg = jnp.sum(gagg.astype(F32), axis=0).astype(BF)
    gagg = lax.all_to_all(gagg.reshape(n_feat, rows, piece), "feat", 0, 0, tiled=True)
    gagg = gagg.transpose(1, 0, 2).reshape(rows, dst_rows)

    halo_grad = dot(gagg, a_ext, ((1,), (0,))).astype(BF)
    halo_grad = halo_grad.reshape(rows, n_dom, 2 * T).transpose(1, 0, 2)
    returned = lax.all_to_all(halo_grad, ("y", "c"), 0, 0, tiled=True)
    base = dot(gagg, a_own, ((1,), (0,)))

    parts = wgrad(grad, xc_dom, agg, n_feat)
    parts = lax.all_to_all(parts, "feat", 0, 0, tiled=True)
    parts = jnp.sum(parts.astype(F32), axis=0)

    back = lax.all_to_all(jnp.concatenate([gself, act], axis=1), dom, 0, 0, tiled=True)
    own = jnp.sum(back[:, :width, :].astype(F32), axis=0).astype(BF).reshape(n_feat, rows, piece)
    act = back[:, width:, :].reshape(n_dom, n_feat, sub, piece).transpose(1, 0, 2, 3)
    back = jnp.concatenate([own, act.reshape(n_feat, rows, piece)], axis=1)
    back = lax.all_to_all(back, "feat", 0, 0, tiled=True)
    gself = back[:, :rows, :].transpose(1, 0, 2).reshape(rows, dst_rows)
    activations = back[:, rows:, :].transpose(1, 0, 2).reshape(rows, dst_rows)

    ret_idx = jnp.concatenate(
        [send_rows.reshape(n_dom, T), jnp.broadcast_to(hub_rows[None], (n_dom, T))], axis=1
    )
    grad_feats = finish(base, returned, ret_idx[:, :, None], gself)

    bias_grad = parts[:, 2 * width] + parts[:, 2 * width + 1]
    bias_high = bias_grad.astype(BF).astype(F32)
    tail = jnp.stack([bias_high, bias_grad - bias_high], axis=1)
    parts = jnp.concatenate([parts[:, : 2 * width], jnp.pad(tail, ((0, 0), (0, T - 2)))], axis=1)
    whole = lax.all_gather(parts.astype(BF), "y", axis=0, tiled=True)
    whole = lax.all_gather(whole, "c", axis=0, tiled=True).astype(F32)
    grad_bias = whole[:, 2 * width] + whole[:, 2 * width + 1]
    return (activations, grad_feats, whole[:, :width], whole[:, width : 2 * width], grad_bias)


def solution(mesh):
    n_dom, n_feat = mesh.devices.shape
    fine = Mesh(mesh.devices.reshape(n_dom // 2, 2, n_feat), ("y", "c", "feat"))
    dom = ("y", "c")
    return jax.shard_map(
        body,
        mesh=fine,
        in_specs=(
            P("feat", dom),
            P(dom),
            P(dom),
            P(dom),
            P(dom),
            P(dom),
            P(dom, None, None),
            P("feat", None),
            P("feat", None),
            P("feat"),
            P("feat", dom),
        ),
        out_specs=(P("feat", dom), P("feat", dom), P("feat", None), P("feat", None), P("feat")),
        check_vma=False,
    )
```

time: 487 us -> 275 us (0.56); the launches traced: 481 us -> 274 us
  matrix products: 156 us -> 15.8 us
  waiting for transfers between devices: 219 us -> 95.8 us
  starting transfers between devices: 7.95 us -> 43.6 us
  Pallas kernels: 0 us -> 30.4 us
  local copies, waits for them, and re-layouts: 48.8 us -> 26.1 us
  blocking collectives: 13.8 us -> 34.3 us
  other arithmetic: 20.1 us -> 12.9 us
    reduce_scatter x2 -> x0, waiting for transfers between devices: 145 us -> none  [the longest x1 145 us: body(): lax.psum_scatter(jnp.concatenate([contract_first(w_self, grad_pre), contr...]
    dot_general x10 -> x4, matrix products: 156 us -> 15.8 us  [dot(): lax.dot_general(left, right, (dims, ((), ())), preferred_element_type=F32)]
    all_to_all x2 -> x10, waiting for transfers between devices: 0.01 us -> 95.7 us  [the longest x1 16.2 us: body(): xc_dom = lax.all_to_all(xc_dom, dom, 0, 0, tiled=True)]
    all_gather x2 -> x1, waiting for transfers between devices: 49.2 us -> 0.02 us  [body(): agg = lax.all_gather(agg, 'c', axis=0, tiled=True)]
    all_to_all x2 -> x10, starting transfers between devices: 7.57 us -> 43.5 us  [the longest x1 7.07 us: body(): agg = lax.all_to_all(by_piece(agg), 'feat', 0, 0, tiled=True)]
    pallas_call x0 -> x5, Pallas kernels: none -> 30.4 us  [the longest x1 17.9 us: build_dense(): pl.pallas_call(functools.partial(build_kernel, per, n_src, n_own), out_sh...]
    gather x4 -> x0, local copies, waits for them, and re-layouts: 29.8 us -> none  [the longest x1 14 us: body(): picked = source_table.reshape(feat_cols, tile_total, 128)[:, tile_src, :]]
    psum x1 -> x0, waiting for transfers between devices: 25.1 us -> none  [body(): lax.psum((local_self, local_neigh, local_bias), 'dom')]
  transfers between devices with their start and end apart: 7 -> 11, of which waited for: 3 -> 9; matrix products, arithmetic and copies ran while one was open for 25% -> 13% of each run, Pallas kernels for 0% -> 9%
where the time goes in v1:
time: 275 us; the launch traced here: 274 us
  waiting for transfers between devices  95.8 us (35%)
  starting transfers between devices  43.6 us (16%)
  blocking collectives  34.3 us (12%)
  Pallas kernels  30.4 us (11%)
  local copies, waits for them, and re-layouts  26.1 us (9%)
  matrix products  15.8 us (6%)
  between operations  15.1 us (5%)
  other arithmetic  12.9 us (5%)
    pallas_call x1, Pallas kernels, build_dense(): pl.pallas_call(functools.partial(build_kernel, per, n_src, n_own), out_sh...  17.9 us
    all_to_all x1, blocking collectives, body(): gagg = lax.all_to_all(gagg, dom, 0, 0, tiled=True)  17.6 us
    all_to_all x1, waiting for transfers between devices, body(): xc_dom = lax.all_to_all(xc_dom, dom, 0, 0, tiled=True)  16.2 us
    dot_general x4, matrix products, dot(): lax.dot_general(left, right, (dims, ((), ())), preferred_element_type=F32)  15.8 us
    all_to_all x1, waiting for transfers between devices, body(): xc = lax.all_to_all(xc, 'feat', 0, 0, tiled=True)  15.3 us
    all_to_all x1, waiting for transfers between devices, body(): lax.all_to_all(jnp.broadcast_to(mine[None], (n_feat, 2 * sub, width)), 'f...  13.6 us
    all_to_all x1, waiting for transfers between devices, body(): parts = lax.all_to_all(parts, 'feat', 0, 0, tiled=True)  13.3 us
    all_to_all x1, waiting for transfers between devices, body(): back = lax.all_to_all(back, 'feat', 0, 0, tiled=True)  12.3 us
  transfers between devices with their start and end apart: 11, of which 9 were waited for; matrix products, arithmetic and copies ran while one was open for 13% of the time, Pallas kernels for 9%

profile of v1, /device:TPU:0, one launch (start us, length us, event | category | flops | bytes accessed | tf_op | source)
XLA Modules:
  0.0 274.0 jit_solution(5696058421335129573)
XLA Ops:
  7.9 1.2 copy-done.4
  9.1 2.4 gather_cols.1
  11.5 4.2 %all-to-all-start.3 = ((bf16[4,128,256]{2,1,0:T(8,128)(2,1)}), bf16[4,128,256]{2,1,0:T(8,128)(2,1)}, u32[]{:S(2)}, u32[]{:S(2)}) async-start(bf16[4,128,256]{2,1,0:T(8,128)(2,1)} %gather_cols.1), calls=%async_computation.3 | async-start | bytes 524288 | tf_op jit(solution)/shard_map/all_to_all | solution.py:251
  17.1 17.9 %build_dense.1 = (bf16[1024,4096]{1,0:T(8,128)(2,1)}, bf16[1024,1024]{1,0:T(8,128)(2,1)S(1)}) custom-call(s32[512]{0:T(512)S(1)} %fusion.6.pos_ref, s32[1]{0:T(128)S(6)} %copy.134.count_ref, bf16[512,128,128]{2,1,0:T(8,128)(2,1)} %vals_ref.1), custom_call_target="tpu_custom_call" | custom-call | bytes 33554432 | tf_op jit(solution)/shard_map/build_dense/pallas_call | solution.py:95
  34.9 6.5 %convolution_bitcast_fusion = f32[128,1024]{0,1:T(8,128)} fusion(bf16[1024,4096]{1,0:T(8,128)(2,1)} %get-tuple-element.11, bf16[128,4096]{1,0:T(8,128)(2,1)S(1)} %copy-done.5), kind=kOutput, calls=%fused_computation.3 | convolution fusion | flops 1073741824 | bytes 9961472 | tf_op jit(solution)/shard_map/dot_general | solution.py:17
  41.5 1.2 copy.110
  42.6 2.5 fusion
  45.1 7.1 %all-to-all-start.4 = ((bf16[8,128,128]{1,2,0:T(8,128)(2,1)}), bf16[8,128,128]{1,2,0:T(8,128)(2,1)S(1)}, u32[]{:S(2)}, u32[]{:S(2)}) async-start(bf16[8,128,128]{1,2,0:T(8,128)(2,1)} %bitcast.16), calls=%async_computation.4 | async-start | bytes 524288 | tf_op jit(solution)/shard_map/all_to_all | solution.py:299
  55.6 4.8 %all-to-all-done.4 = bf16[8,128,128]{1,2,0:T(8,128)(2,1)S(1)} async-done(((bf16[8,128,128]{1,2,0:T(8,128)(2,1)}), bf16[8,128,128]{1,2,0:T(8,128)(2,1)S(1)}, u32[]{:S(2)}, u32[]{:S(2)}) %all-to-all-start.4) | async-done | bytes 262176 | tf_op jit(solution)/shard_map/all_to_all | solution.py:299
  60.5 4.2 %all-to-all-start.1 = ((bf16[8,272,128]{2,1,0:T(8,128)(2,1)}), bf16[8,272,128]{2,1,0:T(8,128)(2,1)S(1)}, u32[]{:S(2)}, u32[]{:S(2)}) async-start(bf16[8,272,128]{2,1,0:T(8,128)(2,1)} %copy.108), calls=%async_computation.1 | async-start | bytes 1114112 | tf_op jit(solution)/shard_map/all_to_all | solution.py:268
  65.6 15.3 %all-to-all-done.1 = bf16[8,272,128]{2,1,0:T(8,128)(2,1)S(1)} async-done(((bf16[8,272,128]{2,1,0:T(8,128)(2,1)}), bf16[8,272,128]{2,1,0:T(8,128)(2,1)S(1)}, u32[]{:S(2)}, u32[]{:S(2)}) %all-to-all-start.1) | async-done | bytes 557088 | tf_op jit(solution)/shard_map/all_to_all | solution.py:268
  80.9 1.2 broadcast_in_dim.14
  82.1 4.1 %all-to-all-start = ((bf16[8,64,1024]{2,1,0:T(8,128)(2,1)}), bf16[8,64,1024]{2,1,0:T(8,128)(2,1)S(1)}, u32[]{:S(2)}, u32[]{:S(2)}) async-start(bf16[8,64,1024]{2,1,0:T(8,128)(2,1)} %broadcast_in_dim.14), calls=%async_computation | async-start | bytes 2097152 | tf_op jit(solution)/shard_map/all_to_all | solution.py:277
  86.2 1.1 copy.112
  87.3 8.8 %all_gather.12 = bf16[2,1024,128]{2,1,0:T(8,128)(2,1)} all-gather(bf16[1,1024,128]{2,1,0:T(8,128)(2,1)S(1)} %bitcast.60), channel_id=1, replica_groups=mesh['y'=2,'c'=2,'feat'=8] {'y'}, dimensions={0}, use_global_device_ids=true | all-gather | bytes 786432 | tf_op jit(solution)/shard_map/all_gather | solution.py:301
  97.4 1.1 pad_maximum_fusion
  98.6 13.6 %all-to-all-done.w_ref = bf16[8,64,1024]{2,1,0:T(8,128)(2,1)S(1)} async-done(((bf16[8,64,1024]{2,1,0:T(8,128)(2,1)}), bf16[8,64,1024]{2,1,0:T(8,128)(2,1)S(1)}, u32[]{:S(2)}, u32[]{:S(2)}) %all-to-all-start) | async-done | bytes 1048608 | tf_op jit(solution)/shard_map/all_to_all | solution.py:277
  113.2 3.5 %all-to-all-start.2 = ((bf16[4,1280,128]{2,1,0:T(8,128)(2,1)}), bf16[4,1280,128]{2,1,0:T(8,128)(2,1)S(1)}, u32[]{:S(2)}, u32[]{:S(2)}) async-start(bf16[4,1280,128]{2,1,0:T(8,128)(2,1)} %pad_maximum_fusion), calls=%async_computation.2 | async-start | bytes 2621440 | tf_op jit(solution)/shard_map/all_to_all | solution.py:293
  117.8 16.2 %all-to-all-done.2.xc_ref = bf16[4,1280,128]{2,1,0:T(8,128)(2,1)S(1)} async-done(((bf16[4,1280,128]{2,1,0:T(8,128)(2,1)}), bf16[4,1280,128]{2,1,0:T(8,128)(2,1)S(1)}, u32[]{:S(2)}, u32[]{:S(2)}) %all-to-all-start.2) | async-done | bytes 1310752 | tf_op jit(solution)/shard_map/all_to_all | solution.py:293
  134.0 1.2 copy-done
  135.2 1.2 copy-done.3
  136.4 3.0 %middle.1 = (bf16[4,256,128]{2,1,0:T(8,128)(2,1)S(1)}, bf16[4,256,128]{2,1,0:T(8,128)(2,1)S(1)}, bf16[4,1024,128]{2,1,0:T(8,128)(2,1)S(1)}, bf16[4,1024,128]{2,1,0:T(8,128)(2,1)S(1)}) custom-call(bf16[8,64,1024]{2,1,0:T(8,128)(2,1)S(1)} %copy-done.3, bf16[4,1280,128]{2,1,0:T(8,128)(2,1)S(1)} %all-to-all-done.2.xc_ref, bf16[4,1024,128]{2,1,0:T(8,128)(2,1)S(1)} %copy-done, ...), custom_call_target="tpu_custom_call" | custom-call | tf_op jit(solution)/shard_map/middle/pallas_call | solution.py:142
  141.8 17.6 %all_to_all.55 = bf16[4,1024,128]{2,1,0:T(8,128)(2,1)} all-to-all(bf16[4,1024,128]{2,1,0:T(8,128)(2,1)S(1)} %get-tuple-element.15), channel_id=1, replica_groups=mesh['y'=2,'c'=2,'feat'=8] {'c','y'}, dimensions={0} | all-to-all | bytes 2097152 | tf_op jit(solution)/shard_map/all_to_all | solution.py:306
  159.4 2.1 reduce_sum.34
  161.6 4.0 %all-to-all-start.8 = ((bf16[8,128,128]{2,1,0:T(8,128)(2,1)}), bf16[8,128,128]{2,1,0:T(8,128)(2,1)}, u32[]{:S(2)}, u32[]{:S(2)}) async-start(bf16[8,128,128]{2,1,0:T(8,128)(2,1)} %bitcast.57), calls=%async_computation.8 | async-start | bytes 524288 | tf_op jit(solution)/shard_map/all_to_all | solution.py:308
  165.6 2.5 pad_maximum_fusion.1
  168.1 6.4 %all-to-all-done.8 = bf16[8,128,128]{2,1,0:T(8,128)(2,1)} async-done(((bf16[8,128,128]{2,1,0:T(8,128)(2,1)}), bf16[8,128,128]{2,1,0:T(8,128)(2,1)}, u32[]{:S(2)}, u32[]{:S(2)}) %all-to-all-start.8) | async-done | bytes 262176 | tf_op jit(solution)/shard_map/all_to_all | solution.py:308
  174.5 4.3 %all-to-all-start.5 = ((bf16[4,1280,128]{2,1,0:T(8,128)(2,1)}), bf16[4,1280,128]{2,1,0:T(8,128)(2,1)}, u32[]{:S(2)}, u32[]{:S(2)}) async-start(bf16[4,1280,128]{2,1,0:T(8,128)(2,1)} %pad_maximum_fusion.1), calls=%async_computation.5 | async-start | bytes 2621440 | tf_op jit(solution)/shard_map/all_to_all | solution.py:320
  178.8 1.8 copy.116
  180.6 2.1 convolution_convert_fusion
  182.7 1.1 copy.117
  184.7 11.4 %all-to-all-done.5 = bf16[4,1280,128]{2,1,0:T(8,128)(2,1)} async-done(((bf16[4,1280,128]{2,1,0:T(8,128)(2,1)}), bf16[4,1280,128]{2,1,0:T(8,128)(2,1)}, u32[]{:S(2)}, u32[]{:S(2)}) %all-to-all-start.5) | async-done | bytes 1310752 | tf_op jit(solution)/shard_map/all_to_all | solution.py:320
  196.1 3.6 %all-to-all-start.9 = ((bf16[4,128,256]{2,1,0:T(8,128)(2,1)}), bf16[4,128,256]{2,1,0:T(8,128)(2,1)S(1)}, u32[]{:S(2)}, u32[]{:S(2)}) async-start(bf16[4,128,256]{2,1,0:T(8,128)(2,1)} %bitcast.28), calls=%async_computation.9 | async-start | bytes 524288 | tf_op jit(solution)/shard_map/all_to_all | solution.py:313
  199.7 1.5 slice_reduce_fusion
  203.0 2.5 all-to-all-done.9.ret_ref
  205.5 4.1 %all-to-all-start.6 = ((bf16[8,256,128]{2,1,0:T(8,128)(2,1)}), bf16[8,256,128]{2,1,0:T(8,128)(2,1)}, u32[]{:S(2)}, u32[]{:S(2)}) async-start(bf16[8,256,128]{2,1,0:T(8,128)(2,1)} %pad_maximum_fusion.3), calls=%async_computation.6 | async-start | bytes 1048576 | tf_op jit(solution)/shard_map/all_to_all | solution.py:324
  209.7 2.2 wgrad.1
  212.0 12.3 %all-to-all-done.6 = bf16[8,256,128]{2,1,0:T(8,128)(2,1)} async-done(((bf16[8,256,128]{2,1,0:T(8,128)(2,1)}), bf16[8,256,128]{2,1,0:T(8,128)(2,1)}, u32[]{:S(2)}, u32[]{:S(2)}) %all-to-all-start.6) | async-done | bytes 524320 | tf_op jit(solution)/shard_map/all_to_all | solution.py:324
  224.3 4.3 %all-to-all-start.10 = ((bf16[8,32,2176]{2,1,0:T(8,128)(2,1)}), bf16[8,32,2176]{2,1,0:T(8,128)(2,1)}, u32[]{:S(2)}, u32[]{:S(2)}) async-start(bf16[8,32,2176]{2,1,0:T(8,128)(2,1)} %wgrad.1), calls=%async_computation.10 | async-start | bytes 2228224 | tf_op jit(solution)/shard_map/all_to_all | solution.py:317
  228.8 4.7 %fusion.11.base_ref = f32[128,4096]{1,0:T(8,128)S(1)} fusion(bf16[128,1024]{0,1:T(8,128)(2,1)S(1)} %bitcast.56, bf16[1024,4096]{1,0:T(8,128)(2,1)} %get-tuple-element.11), kind=kOutput, calls=%fused_computation.40 | convolution fusion | flops 1073741824 | bytes 10747904 | tf_op jit(solution)/shard_map/dot_general | solution.py:17
  233.5 1.8 slice_bitcast_fusion
  235.3 1.1 copy.115
  237.3 4.9 %finish.1 = f32[128,4096]{1,0:T(8,128)} custom-call(f32[128,4096]{1,0:T(8,128)S(1)} %fusion.11.base_ref, bf16[4,128,256]{2,1,0:T(8,128)(2,1)S(1)} %all-to-all-done.9.ret_ref, s32[4,256,1]{2,1,0:T(8,128)S(1)} %copy.120.idx_ref, bf16[128,1024]{1,0:T(8,128)(2,1)S(1)} %bitcast.54), custom_call_target="tpu_custom_call" | custom-call | tf_op jit(solution)/shard_map/finish/pallas_call | solution.py:201
  242.2 13.3 %all-to-all-done.10 = bf16[8,32,2176]{2,1,0:T(8,128)(2,1)} async-done(((bf16[8,32,2176]{2,1,0:T(8,128)(2,1)}), bf16[8,32,2176]{2,1,0:T(8,128)(2,1)}, u32[]{:S(2)}, u32[]{:S(2)}) %all-to-all-start.10) | async-done | bytes 1114144 | tf_op jit(solution)/shard_map/all_to_all | solution.py:317
  255.5 1.4 convert_reduce_fusion
  257.3 5.7 %all_gather.14 = bf16[64,2176]{1,0:T(8,128)(2,1)S(1)} all-gather(bf16[32,2176]{1,0:T(8,128)(2,1)S(1)} %fusion.2), channel_id=1, replica_groups=mesh['y'=2,'c'=2,'feat'=8] {'y'}, dimensions={0}, use_global_device_ids=true | all-gather | bytes 417792 | tf_op jit(solution)/shard_map/all_gather | solution.py:337
  263.1 2.2 all_gather.15
  265.3 1.1 fusion.7
  (75 shorter events, 16.5 us)
Async XLA Ops:
  7.9 1.2 copy-start.4
  11.5 30.0 %all-to-all-start.3 = ((bf16[4,128,256]{2,1,0:T(8,128)(2,1)}), bf16[4,128,256]{2,1,0:T(8,128)(2,1)}, u32[]{:S(2)}, u32[]{:S(2)}) async-start(bf16[4,128,256]{2,1,0:T(8,128)(2,1)} %gather_cols.1), calls=%async_computation.3 | async-start | bytes 524288 | tf_op jit(solution)/shard_map/all_to_all | solution.py:251
  17.1 17.9 %copy-start.5 = (bf16[128,4096]{1,0:T(8,128)(2,1)S(1)}, bf16[128,4096]{1,0:T(8,128)(2,1)}, u32[]{:S(2)}) copy-start(bf16[128,4096]{1,0:T(8,128)(2,1)} %x_ref.1) | copy-start | bytes 3145732
  41.5 10.8 %copy-start.16 = (f32[128]{0:T(128)S(1)}, f32[128]{0:T(128)}, u32[]{:S(2)}) copy-start(f32[128]{0:T(128)} %param.20) | copy-start | bytes 1540
  41.5 10.9 %slice-start = ((bf16[128,4096]{1,0:T(8,128)(2,1)}), bf16[128,1024]{1,0:T(8,128)(2,1)S(1)}, s32[]{:S(2)}) async-start(bf16[128,4096]{1,0:T(8,128)(2,1)} %x_ref.1), calls=%async_computation.12 | async-start | bytes 524288 | tf_op jit(solution)/shard_map/slice | solution.py:262
  42.6 9.9 %copy-start.13 = (bf16[128,1024]{1,0:T(8,128)(2,1)S(1)}, bf16[128,1024]{1,0:T(8,128)(2,1)}, u32[]{:S(2)}) copy-start(bf16[128,1024]{1,0:T(8,128)(2,1)} %param.21) | copy-start | bytes 786436
  45.1 15.3 %all-to-all-start.4 = ((bf16[8,128,128]{1,2,0:T(8,128)(2,1)}), bf16[8,128,128]{1,2,0:T(8,128)(2,1)S(1)}, u32[]{:S(2)}, u32[]{:S(2)}) async-start(bf16[8,128,128]{1,2,0:T(8,128)(2,1)} %bitcast.16), calls=%async_computation.4 | async-start | bytes 524288 | tf_op jit(solution)/shard_map/all_to_all | solution.py:299
  60.5 21.6 %copy-start.12 = (bf16[8,128,128]{1,2,0:T(8,128)(2,1)}, bf16[8,128,128]{1,2,0:T(8,128)(2,1)S(1)}, u32[]{:S(2)}) copy-start(bf16[8,128,128]{1,2,0:T(8,128)(2,1)S(1)} %all-to-all-done.4) | copy-start | bytes 786436
  60.5 20.4 %all-to-all-start.1 = ((bf16[8,272,128]{2,1,0:T(8,128)(2,1)}), bf16[8,272,128]{2,1,0:T(8,128)(2,1)S(1)}, u32[]{:S(2)}, u32[]{:S(2)}) async-start(bf16[8,272,128]{2,1,0:T(8,128)(2,1)} %copy.108), calls=%async_computation.1 | async-start | bytes 1114112 | tf_op jit(solution)/shard_map/all_to_all | solution.py:268
  80.9 1.2 copy-start.11
  82.1 30.1 %all-to-all-start = ((bf16[8,64,1024]{2,1,0:T(8,128)(2,1)}), bf16[8,64,1024]{2,1,0:T(8,128)(2,1)S(1)}, u32[]{:S(2)}, u32[]{:S(2)}) async-start(bf16[8,64,1024]{2,1,0:T(8,128)(2,1)} %broadcast_in_dim.14), calls=%async_computation | async-start | bytes 2097152 | tf_op jit(solution)/shard_map/all_to_all | solution.py:277
  86.1 31.7 %all-gather.2.cloned.1.call-start = ((), (), s32[]{:S(2)}) async-start(), calls=%async_computation.11 | async-start | bytes 1572864 | tf_op jit(solution)/shard_map/all_gather | solution.py:302
  112.2 1.0 copy-start.2
  113.2 20.8 %all-to-all-start.2 = ((bf16[4,1280,128]{2,1,0:T(8,128)(2,1)}), bf16[4,1280,128]{2,1,0:T(8,128)(2,1)S(1)}, u32[]{:S(2)}, u32[]{:S(2)}) async-start(bf16[4,1280,128]{2,1,0:T(8,128)(2,1)} %pad_maximum_fusion), calls=%async_computation.2 | async-start | bytes 2621440 | tf_op jit(solution)/shard_map/all_to_all | solution.py:293
  134.0 1.2 copy-start
  135.2 1.2 copy-start.3
  139.4 1.0 copy-start.6
  140.4 0.7 copy-start.7
  141.1 0.7 copy-start.9
  161.6 12.9 %all-to-all-start.8 = ((bf16[8,128,128]{2,1,0:T(8,128)(2,1)}), bf16[8,128,128]{2,1,0:T(8,128)(2,1)}, u32[]{:S(2)}, u32[]{:S(2)}) async-start(bf16[8,128,128]{2,1,0:T(8,128)(2,1)} %bitcast.57), calls=%async_computation.8 | async-start | bytes 524288 | tf_op jit(solution)/shard_map/all_to_all | solution.py:308
  174.5 21.7 %all-to-all-start.5 = ((bf16[4,1280,128]{2,1,0:T(8,128)(2,1)}), bf16[4,1280,128]{2,1,0:T(8,128)(2,1)}, u32[]{:S(2)}, u32[]{:S(2)}) async-start(bf16[4,1280,128]{2,1,0:T(8,128)(2,1)} %pad_maximum_fusion.1), calls=%async_computation.5 | async-start | bytes 2621440 | tf_op jit(solution)/shard_map/all_to_all | solution.py:320
  196.1 9.4 %all-to-all-start.9 = ((bf16[4,128,256]{2,1,0:T(8,128)(2,1)}), bf16[4,128,256]{2,1,0:T(8,128)(2,1)S(1)}, u32[]{:S(2)}, u32[]{:S(2)}) async-start(bf16[4,128,256]{2,1,0:T(8,128)(2,1)} %bitcast.28), calls=%async_computation.9 | async-start | bytes 524288 | tf_op jit(solution)/shard_map/all_to_all | solution.py:313
  199.7 10.0 %copy-start.1 = (bf16[4,1024,128]{2,1,0:T(8,128)(2,1)S(1)}, bf16[4,1024,128]{2,1,0:T(8,128)(2,1)}, u32[]{:S(2)}) copy-start(bf16[4,1024,128]{2,1,0:T(8,128)(2,1)} %all-gather.2.cloned.1.call-done.agg_ref) | copy-start | bytes 3145732
  199.7 10.0 %copy-start.8 = (bf16[4,256,128]{2,1,0:T(8,128)(2,1)S(1)}, bf16[4,256,128]{2,1,0:T(8,128)(2,1)}, u32[]{:S(2)}) copy-start(bf16[4,256,128]{2,1,0:T(8,128)(2,1)} %copy-done.7) | copy-start | bytes 786436
  205.5 18.7 %all-to-all-start.6 = ((bf16[8,256,128]{2,1,0:T(8,128)(2,1)}), bf16[8,256,128]{2,1,0:T(8,128)(2,1)}, u32[]{:S(2)}, u32[]{:S(2)}) async-start(bf16[8,256,128]{2,1,0:T(8,128)(2,1)} %pad_maximum_fusion.3), calls=%async_computation.6 | async-start | bytes 1048576 | tf_op jit(solution)/shard_map/all_to_all | solution.py:324
  209.7 18.8 %copy-start.15 = (s32[128]{0:T(128)S(1)}, s32[128]{0:T(128)}, u32[]{:S(2)}) copy-start(s32[128]{0:T(128)} %param.13) | copy-start | bytes 1540
  209.7 18.8 %copy-start.14 = (s32[512]{0:T(512)S(1)}, s32[512]{0:T(512)}, u32[]{:S(2)}) copy-start(s32[512]{0:T(512)} %param.12) | copy-start | bytes 6148
  212.0 16.8 %copy-start.10 = (bf16[128,8,128]{0,2,1:T(8,128)(2,1)S(1)}, bf16[128,8,128]{0,2,1:T(8,128)(2,1)}, u32[]{:S(2)}) copy-start(bf16[128,8,128]{0,2,1:T(8,128)(2,1)} %copy.116) | copy-start | bytes 786436
  224.3 31.2 %all-to-all-start.10 = ((bf16[8,32,2176]{2,1,0:T(8,128)(2,1)}), bf16[8,32,2176]{2,1,0:T(8,128)(2,1)}, u32[]{:S(2)}, u32[]{:S(2)}) async-start(bf16[8,32,2176]{2,1,0:T(8,128)(2,1)} %wgrad.1), calls=%async_computation.10 | async-start | bytes 2228224 | tf_op jit(solution)/shard_map/all_to_all | solution.py:317
Sparse Core Ops, SparseCore 0:
  96.3 9.1 all-gather.1

commit v2 on v0

v2 whole, which is shorter than its diff:
```python
import functools

import jax
import jax.numpy as jnp
from jax import lax
from jax.experimental import pallas as pl
from jax.experimental.pallas import tpu as pltpu
from jax.sharding import PartitionSpec as P

T = 128
BF = jnp.bfloat16
F32 = jnp.float32
MIB = 1 << 20
VMEM = pl.BlockSpec(memory_space=pltpu.VMEM)
SMEM = pl.BlockSpec(memory_space=pltpu.SMEM)


def dot(left, right, dims):
    return lax.dot_general(left, right, (dims, ((), ())), preferred_element_type=F32)


def params(mib):
    return pltpu.CompilerParams(vmem_limit_bytes=mib * MIB)


def cost(micros):
    return pl.CostEstimate(flops=0, bytes_accessed=int(micros * 3.0e6), transcendentals=0)


def shape(*dims, kind=BF):
    return jax.ShapeDtypeStruct(dims, kind)


def gather_kernel(x_ref, idx_ref, *out_refs):
    x = x_ref[...]
    rows = lax.broadcasted_iota(jnp.int32, (x.shape[1], T), 0)
    readers = len(out_refs)
    for q in range(readers + 1):
        hot = (rows == idx_ref[q : q + 1, :]).astype(F32).astype(BF)
        got = dot(x, hot, ((1,), (0,))).astype(BF)
        if q < readers:
            out_refs[q][:, :T] = got
        else:
            for r in range(readers):
                out_refs[r][:, T:] = got


def gather_cols(x, idx):
    readers = idx.shape[0] - 1
    return pl.pallas_call(
        gather_kernel,
        out_shape=[shape(x.shape[0], 2 * T)] * readers,
        in_specs=[VMEM] * 2,
        out_specs=[VMEM] * readers,
        compiler_params=params(40),
        cost_estimate=cost(2.5),
        name="gather_cols",
    )(x, idx)


def build_kernel(n_own, order_ref, start_ref, x_ref, vals_hbm, own_ref, ext_ref, agg_ref, vals, sems):
    u = pl.program_id(0)
    slots = vals_hbm.shape[0]
    n_src = n_own + ext_ref.shape[1] // T
    chunks = sems.shape[0]
    per = slots // chunks

    def piece(i):
        span = pl.ds(i * per, per)
        return pltpu.make_async_copy(vals_hbm.at[span], vals.at[span], sems.at[i])

    @pl.when(u == 0)
    def _():
        for i in range(chunks):
            piece(i).start()
        vals[slots] = jnp.zeros((T, T), BF)
        for i in range(chunks):
            piece(i).wait()

    for s in range(n_src):
        p = u * n_src + s
        first, last = start_ref[p], start_ref[p + 1]
        one = jnp.where(last > first, order_ref[first], slots)
        two = jnp.where(last > first + 1, order_ref[first + 1], slots)
        total = vals[one].astype(F32) + vals[two].astype(F32)

        def more(i, total):
            return total + vals[order_ref[i]].astype(F32)

        total = lax.fori_loop(first + 2, last, more, total).astype(BF)
        if s < n_own:
            own_ref[:, s * T : (s + 1) * T] = total
        else:
            ext_ref[:, (s - n_own) * T : (s - n_own + 1) * T] = total
    agg_ref[...] = dot(x_ref[...], own_ref[...], ((1,), (1,)))


def build_dense(vals, order, start, x, n_dst, n_src, n_own):
    slots = vals.shape[0]
    chunks = 8
    return pl.pallas_call(
        functools.partial(build_kernel, n_own),
        out_shape=(
            shape(n_dst * T, n_own * T),
            shape(n_dst * T, (n_src - n_own) * T),
            shape(x.shape[0], n_dst * T, kind=F32),
        ),
        grid_spec=pltpu.PrefetchScalarGridSpec(
            num_scalar_prefetch=2,
            grid=(n_dst,),
            in_specs=[
                pl.BlockSpec(x.shape, lambda u, *_: (0, 0)),
                pl.BlockSpec(memory_space=pl.ANY),
            ],
            out_specs=[
                pl.BlockSpec((T, n_own * T), lambda u, *_: (u, 0)),
                pl.BlockSpec((T, (n_src - n_own) * T), lambda u, *_: (u, 0)),
                pl.BlockSpec((x.shape[0], T), lambda u, *_: (0, u)),
            ],
            scratch_shapes=[
                pltpu.VMEM((slots + 1, T, T), BF),
                pltpu.SemaphoreType.DMA((chunks,)),
            ],
        ),
        compiler_params=params(40),
        cost_estimate=cost(14.0),
        name="build_dense",
    )(order, start, x, vals)


def halo_kernel(own_ref, ext_ref, *refs):
    *in_refs, out_ref = refs
    total = own_ref[...]
    halo = jnp.concatenate([r[...] for r in in_refs], axis=1)
    total = (total + dot(halo, ext_ref[...], ((1,), (1,)))).astype(BF)
    piece = out_ref.shape[2]
    for b in range(out_ref.shape[0]):
        out_ref[b] = total[:, b * piece : (b + 1) * piece]


def add_halo(own, ext, halos, n_feat):
    rows, n = own.shape
    return pl.pallas_call(
        halo_kernel,
        out_shape=shape(n_feat, rows, n // n_feat),
        in_specs=[VMEM] * (2 + len(halos)),
        out_specs=VMEM,
        compiler_params=params(40),
        cost_estimate=cost(2.0),
        name="add_halo",
    )(own, ext, *halos)


def middle_kernel(ny, small, w_ref, bias_ref, *refs):
    even, odd = refs[:ny], refs[ny : 2 * ny]
    agg = refs[2 * ny : 4 * ny]
    g_ref, gagg_even, gagg_odd, back_even, back_odd = refs[4 * ny :]
    width = w_ref.shape[2]
    w_self, w_neigh = w_ref[0], w_ref[1]
    bias = bias_ref[...]
    for k in range(2 * ny):
        j = k // 2
        if k % 2 == 0:
            cot, x = even[j][:small, :], even[j][small : small + width, :]
            gagg_ref, back_ref = gagg_even, back_even
        else:
            x, cot = odd[j][:width, :], odd[j][width:, :]
            gagg_ref, back_ref = gagg_odd, back_odd
        pre = dot(w_self, x, ((1,), (0,)))
        pre += dot(w_neigh, agg[k][...], ((1,), (0,)))
        pre += bias
        sig = 1.0 / (1.0 + jnp.exp(-pre))
        back_ref[j, width:, :] = (pre * sig).astype(BF)
        grad = (cot.astype(F32) * sig * (1.0 + pre * (1.0 - sig))).astype(BF)
        g_ref[k] = grad
        gagg_ref[j] = dot(w_neigh, grad, ((0,), (0,))).astype(BF)
        back_ref[j, :width, :] = dot(w_self, grad, ((0,), (0,))).astype(BF)


def middle(w, bias, even, odd, agg):
    ny, width, small = len(even), w.shape[2], w.shape[1]
    n = agg[0].shape[1]
    return pl.pallas_call(
        functools.partial(middle_kernel, ny, small),
        out_shape=[
            shape(2 * ny, small, n),
            shape(ny, width, n),
            shape(ny, width, n),
            shape(ny, width + small, n),
            shape(ny, width + small, n),
        ],
        in_specs=[VMEM] * (2 + 4 * ny),
        out_specs=[VMEM] * 5,
        compiler_params=params(40),
        cost_estimate=cost(3.0),
        name="middle",
    )(w, bias, *even, *odd, *agg)


def wgrad_kernel(ny, small, me_ref, g_ref, *refs):
    even, odd = refs[:ny], refs[ny : 2 * ny]
    agg = refs[2 * ny : 4 * ny]
    out_ref = refs[4 * ny]
    width = agg[0].shape[0]
    sub = out_ref.shape[2]
    xs = []
    for k in range(2 * ny):
        ref = odd[k // 2] if k % 2 else even[k // 2]
        xs.append(ref[:width, :] if k % 2 else ref[small : small + width, :])
    grad = jnp.concatenate([g_ref[k] for k in range(2 * ny)], axis=1)
    own = dot(grad, jnp.concatenate(xs, axis=1), ((1,), (1,))).astype(BF)
    neigh = dot(grad, jnp.concatenate([r[...] for r in agg], axis=1), ((1,), (1,))).astype(BF)
    total = jnp.sum(grad.astype(F32), axis=1, keepdims=True)
    high = total.astype(BF).astype(F32)
    lane = lax.broadcasted_iota(jnp.int32, (small, T), 1)
    both = jnp.where(lane == 0, high, jnp.where(lane == 1, total - high, 0.0)).astype(BF)
    for i in range(small // sub):
        k = me_ref[0] ^ i
        rows = slice(i * sub, (i + 1) * sub)
        out_ref[k % 2, k // 2, :, :width] = own[rows]
        out_ref[k % 2, k // 2, :, width : 2 * width] = neigh[rows]
        out_ref[k % 2, k // 2, :, 2 * width :] = both[rows]


def wgrad(me, g, even, odd, agg, groups):
    ny, width, small = len(even), agg[0].shape[0], g.shape[1]
    return pl.pallas_call(
        functools.partial(wgrad_kernel, ny, small),
        out_shape=shape(2, groups // 2, small // groups, 2 * width + T),
        in_specs=[SMEM] + [VMEM] * (1 + 4 * ny),
        out_specs=VMEM,
        compiler_params=params(40),
        cost_estimate=cost(2.5),
        name="wgrad",
    )(me, g, *even, *odd, *agg)


def halo_grad_kernel(ga_ref, ext_ref, flat_ref, *out_refs):
    ga = jnp.concatenate([ga_ref[b] for b in range(ga_ref.shape[0])], axis=1)
    flat_ref[...] = ga
    for k, out_ref in enumerate(out_refs):
        span = slice(k * 2 * T, (k + 1) * 2 * T)
        out_ref[...] = dot(ga, ext_ref[:, span], ((1,), (0,))).astype(BF)


def halo_grads(ga, ext, n_dom):
    groups, rows, piece = ga.shape
    return pl.pallas_call(
        halo_grad_kernel,
        out_shape=[shape(rows, groups * piece)] + [shape(rows, 2 * T)] * n_dom,
        in_specs=[VMEM] * 2,
        out_specs=[VMEM] * (1 + n_dom),
        compiler_params=params(40),
        cost_estimate=cost(2.0),
        name="halo_grads",
    )(ga, ext)


def finish_kernel(dst_blocks, base_ref, idx_ref, gself_ref, *refs):
    *ret_refs, out_ref = refs
    step = pl.program_id(0)
    width = out_ref.shape[1]
    total = base_ref[...]
    cols = lax.broadcasted_iota(jnp.int32, (2 * T, width), 1) + step * width
    for q, ret_ref in enumerate(ret_refs):
        hot = (cols == idx_ref[q]).astype(F32).astype(BF)
        total += dot(ret_ref[...], hot, ((1,), (0,)))
    own = gself_ref[...].astype(F32)
    out_ref[...] = total + jnp.where(step < dst_blocks, own, 0.0)


def finish(base, ret, idx, gself):
    rows, n = base.shape
    width = 512
    dst_blocks = gself.shape[1] // width
    return pl.pallas_call(
        functools.partial(finish_kernel, dst_blocks),
        out_shape=shape(rows, n, kind=F32),
        grid=(n // width,),
        in_specs=[
            pl.BlockSpec((rows, width), lambda i: (0, i)),
            pl.BlockSpec(idx.shape, lambda i: (0, 0, 0)),
            pl.BlockSpec((rows, width), lambda i: (0, jnp.minimum(i, dst_blocks - 1))),
        ]
        + [pl.BlockSpec((rows, 2 * T), lambda i: (0, 0))] * len(ret),
        out_specs=pl.BlockSpec((rows, width), lambda i: (0, i)),
        compiler_params=params(40),
        cost_estimate=cost(5.0),
        name="finish",
    )(base, idx, gself, *ret)


def body(
    node_feats,
    send_rows,
    hub_rows,
    tile_dst,
    tile_src,
    tile_count,
    tile_vals,
    w_self,
    w_neigh,
    bias_vec,
    cotangent,
):
    n_dom = lax.axis_size("dom")
    n_feat = lax.axis_size("feat")
    ny, nz = n_dom // 2, n_feat // 2
    rows = node_feats.shape[0]
    own_rows = node_feats.shape[1]
    dst_rows = cotangent.shape[1]
    width = w_self.shape[1]
    n_own, n_dst = own_rows // T, dst_rows // T
    n_src = n_own + 2 * n_dom
    piece = dst_rows // n_feat
    sub = w_self.shape[0] // n_dom
    small = n_feat * sub
    me = lax.axis_index("dom")
    block = lax.axis_index("feat")

    def over_dom(x, k):
        return lax.ppermute(x, "dom", [(i, i ^ k) for i in range(n_dom)])

    def over_feat(x, k):
        return lax.ppermute(x, "feat", [(i, i ^ k) for i in range(n_feat)])

    def relative(x, axis):
        parts = [lax.dynamic_slice_in_dim(x, me ^ k, 1, axis) for k in range(n_dom)]
        return jnp.concatenate(parts, axis=axis)

    def by_piece(x):
        return x.reshape(rows, n_feat, piece).transpose(1, 0, 2)

    mine = jnp.stack(
        [
            lax.dynamic_slice_in_dim(w_self, me * sub, sub, axis=0),
            lax.dynamic_slice_in_dim(w_neigh, me * sub, sub, axis=0),
        ]
    )
    mine = mine.reshape(2 * sub, width // piece, piece).transpose(1, 0, 2).reshape(-1, piece)
    high = bias_vec.astype(BF)
    low = (bias_vec - high.astype(F32)).astype(BF)
    bias_rows = jnp.pad(jnp.stack([high, low]), ((0, 14), (0, 0)))
    first = jnp.concatenate(
        [
            by_piece(node_feats[:, :dst_rows]),
            by_piece(cotangent),
            jnp.broadcast_to(bias_rows[None], (n_feat, 16, piece)),
            jnp.broadcast_to(mine[None], (n_feat,) + mine.shape),
        ],
        axis=1,
    )
    first = lax.all_to_all(first, "feat", 0, 0, tiled=True)

    sends = relative(send_rows.reshape(n_dom, T), 0)
    outgoing = gather_cols(node_feats, jnp.concatenate([sends, hub_rows[None, :]], axis=0))
    incoming = [outgoing[0]] + [over_dom(outgoing[k], k) for k in range(1, n_dom)]

    halo_tile = n_own + 2 * ((tile_src - n_own) ^ me)
    hub_tile = n_own + 2 * ((tile_src - n_own - n_dom) ^ me) + 1
    place = jnp.where(
        tile_src < n_own, tile_src, jnp.where(tile_src < n_own + n_dom, halo_tile, hub_tile)
    )
    n_pos = n_dst * n_src
    slot = jnp.arange(tile_dst.shape[0], dtype=jnp.int32)
    key = jnp.where(slot < tile_count[0], tile_dst * n_src + place, n_pos)
    before = (key[None, :] < key[:, None]) | (
        (key[None, :] == key[:, None]) & (slot[None, :] < slot[:, None])
    )
    rank = jnp.sum(before.astype(jnp.int32), axis=1)
    order = jnp.sum(jnp.where(rank[:, None] == slot[None, :], slot[:, None], 0), axis=0)
    order = jnp.concatenate([order, jnp.zeros((2,), jnp.int32)])
    ends = jnp.arange(n_pos + 1, dtype=jnp.int32)
    start = jnp.sum((key[None, :] < ends[:, None]).astype(jnp.int32), axis=1)
    a_own, a_ext, agg_own = build_dense(tile_vals, order, start, node_feats, n_dst, n_src, n_own)
    agg = add_halo(agg_own, a_ext, incoming, n_feat)

    agg, first = lax.optimization_barrier((agg, first))
    agg = lax.all_to_all(agg, "feat", 0, 0, tiled=True).reshape(width, piece)

    x = first[:, :rows, :].reshape(width, piece)
    cot = first[:, rows : 2 * rows, :].reshape(n_feat, n_dom, sub, piece)
    cot = relative(cot, 1).transpose(1, 0, 2, 3).reshape(n_dom, small, piece)
    even = [jnp.concatenate([cot[0], x, cot[1]], axis=0)]
    for j in range(1, ny):
        even.append(over_dom(jnp.concatenate([cot[2 * j], x, cot[2 * j + 1]], axis=0), 2 * j))
    odd = [over_dom(e[small:], 1) for e in even]
    bias = first[:, 2 * rows, :].astype(F32) + first[:, 2 * rows + 1, :].astype(F32)
    bias = lax.dynamic_slice_in_dim(bias, me * sub, sub, axis=1).reshape(small, 1)
    w = first[:, 2 * rows + 16 :, :].reshape(n_feat, width // piece, 2, sub, piece)
    w = w.transpose(2, 0, 3, 1, 4).reshape(2, small, width)

    agg_even = [agg] + [over_dom(agg, 2 * j) for j in range(1, ny)]
    agg_odd = [over_dom(a, 1) for a in agg_even]
    aggs = [a for pair in zip(agg_even, agg_odd) for a in pair]

    grad, gagg_even, gagg_odd, back_even, back_odd = middle(w, bias, even, odd, aggs)

    got = over_dom(gagg_odd, 1)
    pair = (gagg_even.astype(F32) + got.astype(F32)).astype(BF)
    gagg = pair[0].astype(F32)
    for j in range(1, ny):
        gagg += over_dom(pair[j], 2 * j).astype(F32)
    gagg = gagg.astype(BF).reshape(n_feat, rows, piece)
    gagg = lax.all_to_all(gagg, "feat", 0, 0, tiled=True)
    gagg, *halo_grad = halo_grads(gagg, a_ext, n_dom)
    returned = [halo_grad[0]] + [over_dom(halo_grad[k], k) for k in range(1, n_dom)]
    base = dot(gagg, a_own, ((1,), (0,)))

    parts = wgrad(block.reshape(1), grad, even, odd, aggs, n_feat)
    parts = (parts[0].astype(F32) + over_feat(parts[1], 1).astype(F32)).astype(BF)
    total = parts[0].astype(F32)
    for j in range(1, nz):
        total += over_feat(parts[j], 2 * j).astype(F32)
    bias_grad = total[:, 2 * width] + total[:, 2 * width + 1]
    bias_high = bias_grad.astype(BF).astype(F32)
    tail = jnp.stack([bias_high, bias_grad - bias_high], axis=1)
    total = jnp.concatenate([total[:, : 2 * width], jnp.pad(tail, ((0, 0), (0, T - 2)))], axis=1)
    total = total.astype(BF)
    whole = [total] + [over_dom(total, 2 * j) for j in range(1, ny)]
    whole = [t for e in whole for t in (e, over_dom(e, 1))]
    whole = relative(jnp.stack(whole), 0).reshape(n_dom * sub, -1).astype(F32)
    grad_bias = whole[:, 2 * width] + whole[:, 2 * width + 1]

    got = over_dom(back_odd, 1)
    self_pair = (back_even[:, :width].astype(F32) + got[:, :width].astype(F32)).astype(BF)
    gself = self_pair[0].astype(F32)
    acts = [back_even[0, width:], got[0, width:]]
    for j in range(1, ny):
        back = over_dom(
            jnp.concatenate([self_pair[j], back_even[j, width:], got[j, width:]], axis=0), 2 * j
        )
        gself += back[:width].astype(F32)
        acts += [back[width : width + small], back[width + small :]]
    acts = jnp.stack([a.reshape(n_feat, sub, piece) for a in acts], axis=1)
    acts = relative(acts, 1).reshape(n_feat, rows, piece)
    back = jnp.concatenate([gself.astype(BF).reshape(n_feat, rows, piece), acts], axis=1)
    back = lax.all_to_all(back, "feat", 0, 0, tiled=True)
    gself = back[:, :rows, :].transpose(1, 0, 2).reshape(rows, dst_rows)
    activations = back[:, rows:, :].transpose(1, 0, 2).reshape(rows, dst_rows)

    ret_idx = jnp.concatenate([sends, jnp.broadcast_to(hub_rows[None], (n_dom, T))], axis=1)
    grad_feats = finish(base, returned, ret_idx[:, :, None], gself)
    return (activations, grad_feats, whole[:, :width], whole[:, width : 2 * width], grad_bias)


def solution(mesh):
    return jax.shard_map(
        body,
        mesh=mesh,
        in_specs=(
            P("feat", "dom"),
            P("dom"),
            P("dom"),
            P("dom"),
            P("dom"),
            P("dom"),
            P("dom", None, None),
            P("feat", None),
            P("feat", None),
            P("feat"),
            P("feat", "dom"),
        ),
        out_specs=(P("feat", "dom"), P("feat", "dom"), P("feat", None), P("feat", None), P("feat")),
        check_vma=False,
    )
```

time: 487 us -> 171 us (0.35); the launches traced: 481 us -> 170 us
  waiting for transfers between devices: 219 us -> 56.5 us
  matrix products: 156 us -> 4.64 us
  starting transfers between devices: 7.95 us -> 39.8 us
  Pallas kernels: 0 us -> 30.8 us
  local copies, waits for them, and re-layouts: 48.8 us -> 26.7 us
  blocking collectives: 13.8 us -> 0 us
  between operations: 15.1 us -> 1.91 us
  other arithmetic: 20.1 us -> 9.61 us
    dot_general x10 -> x1, matrix products: 156 us -> 4.64 us  [dot(): lax.dot_general(left, right, (dims, ((), ())), preferred_element_type=F32)]
    reduce_scatter x2 -> x0, waiting for transfers between devices: 145 us -> none  [the longest x1 145 us: body(): lax.psum_scatter(jnp.concatenate([contract_first(w_self, grad_pre), contr...]
    all_gather x2 -> x0, waiting for transfers between devices: 49.2 us -> none  [the longest x1 49.2 us: body(): lax.all_gather(aggregate, 'feat', axis=0, tiled=True)]
    pallas_call x0 -> x7, Pallas kernels: none -> 30.8 us  [the longest x1 15.6 us: build_dense(): pl.pallas_call(functools.partial(build_kernel, n_own), out_shape=(shape(n...]
    all_to_all x2 -> x4, waiting for transfers between devices: 0.01 us -> 30.2 us  [the longest x1 12.3 us: body(): first = lax.all_to_all(first, 'feat', 0, 0, tiled=True)]
    gather x4 -> x0, local copies, waits for them, and re-layouts: 29.8 us -> none  [the longest x1 14 us: body(): picked = source_table.reshape(feat_cols, tile_total, 128)[:, tile_src, :]]
    ppermute x0 -> x23, waiting for transfers between devices: none -> 26.3 us  [the longest x4 18.1 us: over_feat(): return lax.ppermute(x, 'feat', [(i, i ^ k) for i in range(n_feat)])]
    psum x1 -> x0, waiting for transfers between devices: 25.1 us -> none  [body(): lax.psum((local_self, local_neigh, local_bias), 'dom')]
  transfers between devices with their start and end apart: 7 -> 27, of which waited for: 3 -> 9; matrix products, arithmetic and copies ran while one was open for 25% -> 18% of each run, Pallas kernels for 0% -> 13%
where the time goes in v2:
time: 171 us; the launch traced here: 170 us
  waiting for transfers between devices  56.5 us (33%)
  starting transfers between devices  39.8 us (23%)
  Pallas kernels  30.8 us (18%)
  local copies, waits for them, and re-layouts  26.7 us (16%)
  other arithmetic  9.61 us (6%)
  matrix products  4.64 us (3%)
  between operations  1.91 us (1%)
    ppermute x4, waiting for transfers between devices, over_feat(): return lax.ppermute(x, 'feat', [(i, i ^ k) for i in range(n_feat)])  18.1 us
    pallas_call x1, Pallas kernels, build_dense(): pl.pallas_call(functools.partial(build_kernel, n_own), out_shape=(shape(n...  15.6 us
    ppermute x19, starting transfers between devices, over_dom(): return lax.ppermute(x, 'dom', [(i, i ^ k) for i in range(n_dom)])  12.7 us
    all_to_all x1, waiting for transfers between devices, body(): first = lax.all_to_all(first, 'feat', 0, 0, tiled=True)  12.3 us
    unnamed x38, local copies, waits for them, and re-layouts  11 us
    ppermute x19, waiting for transfers between devices, over_dom(): return lax.ppermute(x, 'dom', [(i, i ^ k) for i in range(n_dom)])  8.25 us
    all_to_all x1, starting transfers between devices, body(): first = lax.all_to_all(first, 'feat', 0, 0, tiled=True)  7.4 us
    ppermute x4, starting transfers between devices, over_feat(): return lax.ppermute(x, 'feat', [(i, i ^ k) for i in range(n_feat)])  6.26 us
  transfers between devices with their start and end apart: 27, of which 9 were waited for; matrix products, arithmetic and copies ran while one was open for 18% of the time, Pallas kernels for 13%

profile of v2, /device:TPU:0, one launch (start us, length us, event | category | flops | bytes accessed | tf_op | source)
XLA Modules:
  0.0 169.9 jit_solution(6793622453385544981)
XLA Ops:
  0.7 0.9 dynamic-slice_bitcast_fusion
  3.3 1.3 pad_maximum_fusion
  4.6 7.4 %all-to-all-start = ((bf16[8,784,128]{2,1,0:T(8,128)(2,1)}), bf16[8,784,128]{2,1,0:T(8,128)(2,1)}, u32[]{:S(2)}, u32[]{:S(2)}) async-start(bf16[8,784,128]{2,1,0:T(8,128)(2,1)} %pad_maximum_fusion), calls=%async_computation | async-start | bytes 3211264 | tf_op jit(solution)/shard_map/all_to_all | solution.py:353
  12.1 1.7 gather_cols.1
  13.8 1.6 collective-permute-start.1
  17.1 15.6 %build_dense.1 = (bf16[1024,4096]{1,0:T(8,128)(2,1)S(1)}, bf16[1024,1024]{1,0:T(8,128)(2,1)S(1)}, f32[128,1024]{1,0:T(8,128)S(1)}) custom-call(s32[514]{0:T(1024)S(1)} %concatenate.58.order_ref, s32[321]{0:T(512)S(1)} %convert_reduce_fusion.1.start_ref, bf16[128,4096]{1,0:T(8,128)(2,1)S(1)} %copy-done.1, bf16[512,128,128]{2,1,0:T(8,128)(2,1)} %vals_hbm.1), custom_call_target="tpu_custom_call" | custom-call | bytes 42000000 | tf_op jit(solution)/shard_map/build_dense/pallas_call | solution.py:101
  32.7 3.3 %copy-done = bf16[1024,4096]{1,0:T(8,128)(2,1)} copy-done((bf16[1024,4096]{1,0:T(8,128)(2,1)}, bf16[1024,4096]{1,0:T(8,128)(2,1)S(1)}, u32[]{:S(2)}) %copy-start) | copy-done | bytes 8388632
  36.0 1.5 add_halo.1
  37.6 12.3 %all-to-all-done = bf16[8,784,128]{2,1,0:T(8,128)(2,1)} async-done(((bf16[8,784,128]{2,1,0:T(8,128)(2,1)}), bf16[8,784,128]{2,1,0:T(8,128)(2,1)}, u32[]{:S(2)}, u32[]{:S(2)}) %all-to-all-start) | async-done | bytes 1605664 | tf_op jit(solution)/shard_map/all_to_all | solution.py:353
  49.8 1.1 fusion.21
  50.9 4.2 %all-to-all-start.1 = ((bf16[8,128,128]{2,1,0:T(8,128)(2,1)}), bf16[8,128,128]{2,1,0:T(8,128)(2,1)}, u32[]{:S(2)}, u32[]{:S(2)}) async-start(bf16[8,128,128]{2,1,0:T(8,128)(2,1)} %add_halo.1), calls=%async_computation.1 | async-start | bytes 524288 | tf_op jit(solution)/shard_map/all_to_all | solution.py:379
  56.1 1.5 collective-permute-start.3
  57.6 6.2 %all-to-all-done.1 = bf16[8,128,128]{2,1,0:T(8,128)(2,1)} async-done(((bf16[8,128,128]{2,1,0:T(8,128)(2,1)}), bf16[8,128,128]{2,1,0:T(8,128)(2,1)}, u32[]{:S(2)}, u32[]{:S(2)}) %all-to-all-start.1) | async-done | bytes 262176 | tf_op jit(solution)/shard_map/all_to_all | solution.py:379
  63.8 1.5 collective-permute-start.7
  66.1 2.2 %collective-permute-done.3.refs_1_ = bf16[1536,128]{1,0:T(8,128)(2,1)S(1)} collective-permute-done((bf16[1536,128]{1,0:T(8,128)(2,1)}, bf16[1536,128]{1,0:T(8,128)(2,1)S(1)}, u32[]{:S(2)}, u32[]{:S(2)}) %collective-permute-start.3) | collective-permute-done | bytes 393248 | tf_op jit(solution)/shard_map/ppermute | solution.py:322
  69.6 2.5 %collective-permute-done.7.refs_6_ = bf16[1024,128]{1,0:T(8,128)(2,1)} collective-permute-done((bf16[1024,128]{1,0:T(8,128)(2,1)}, bf16[1024,128]{1,0:T(8,128)(2,1)}, u32[]{:S(2)}, u32[]{:S(2)}) %collective-permute-start.7) | collective-permute-done | bytes 262176 | tf_op jit(solution)/shard_map/ppermute | solution.py:322
  72.2 1.0 copy.74.idx_ref
  73.2 2.3 %slice.124 = bf16[8,512,128]{2,1,0:T(8,128)(2,1)} slice(bf16[8,784,128]{2,1,0:T(8,128)(2,1)} %all-to-all-done), slice={[0:8], [272:784], [0:128]} | slice | bytes 2097152 | tf_op jit(solution)/shard_map/slice | solution.py:390
  75.5 0.8 fusion.22
  77.2 2.9 %copy.82 = bf16[8,8,2,32,128]{4,1,3,0,2:T(8,128)(2,1)} copy(bf16[8,8,2,32,128]{4,3,2,1,0:T(8,128)(2,1)} %bitcast.107) | data formatting | bytes 2097152 | tf_op jit(solution)/shard_map/reshape | solution.py:390
  80.0 1.5 reshape.126.w_ref
  81.6 1.0 copy-done.3
  82.6 0.9 copy-done.6
  83.5 4.4 %middle.1 = (bf16[4,256,128]{2,1,0:T(8,128)(2,1)S(1)}, bf16[2,1024,128]{2,1,0:T(8,128)(2,1)S(1)}, bf16[2,1024,128]{2,1,0:T(8,128)(2,1)S(1)}, bf16[2,1280,128]{2,1,0:T(8,128)(2,1)S(1)}, bf16[2,1280,128]{2,1,0:T(8,128)(2,1)S(1)}) custom-call(bf16[2,256,1024]{2,1,0:T(8,128)(2,1)S(1)} %reshape.126.w_ref, f32[256,1]{1,0:T(8,128)S(1)} %copy-done.6, ...), custom_call_target="tpu_custom_call" | custom-call | bytes 9000000 | tf_op jit(solution)/shard_map/middle/pallas_call | solution.py:183
  88.5 2.1 %wgrad.1 = bf16[2,4,32,2176]{3,2,1,0:T(8,128)(2,1)S(1)} custom-call(s32[1]{0:T(128)} %bitcast.40.me_ref, bf16[4,256,128]{2,1,0:T(8,128)(2,1)S(1)} %get-tuple-element.42.g_ref, bf16[1536,128]{1,0:T(8,128)(2,1)S(1)} %get-tuple-element.79.refs_0_, bf16[1536,128]{1,0:T(8,128)(2,1)S(1)} %copy-done.4, bf16[1280,128]{1,0:T(8,128)(2,1)} %collective-permute-done.4.refs_2_, ...), custom_call_target="tpu_custom_call" | custom-call | bytes 7500000 | tf_op jit(solution)/shard_map/wgrad/pallas_call | solution.py:227
  90.7 1.8 %collective-permute-start.16 = (bf16[4,32,2176]{2,1,0:T(8,128)(2,1)S(1)}, bf16[4,32,2176]{2,1,0:T(8,128)(2,1)S(1)}, u32[]{:S(2)}, u32[]{:S(2)}) collective-permute-start(bf16[4,32,2176]{2,1,0:T(8,128)(2,1)S(1)} %slice_bitcast_fusion), channel_id=1, source_target_pairs={{0,1},{1,0},{2,3},{3,2},{4,5},{5,4},{6,7},{7,6},{8,9},{9,8},{10,11... | collective-permute-start | bytes 1671176 | tf_op jit(solution)/shard_map/ppermute | solution.py:325
  92.7 1.6 collective-permute-start.12
  94.3 11.0 %collective-permute-done.16 = bf16[4,32,2176]{2,1,0:T(8,128)(2,1)S(1)} collective-permute-done((bf16[4,32,2176]{2,1,0:T(8,128)(2,1)S(1)}, bf16[4,32,2176]{2,1,0:T(8,128)(2,1)S(1)}, u32[]{:S(2)}, u32[]{:S(2)}) %collective-permute-start.16) | collective-permute-done | bytes 557088 | tf_op jit(solution)/shard_map/ppermute | solution.py:325
  105.5 1.8 %collective-permute-start.17 = (bf16[32,2176]{1,0:T(8,128)(2,1)S(1)}, bf16[32,2176]{1,0:T(8,128)(2,1)S(1)}, u32[]{:S(2)}, u32[]{:S(2)}) collective-permute-start(bf16[32,2176]{1,0:T(8,128)(2,1)S(1)} %get-tuple-element.67), channel_id=1, source_target_pairs={{0,2},{1,3},{2,0},{3,1},{4,6},{5,7},{6,4},{7,5},{8,10},{9,11},{10,... | collective-permute-start | bytes 417800 | tf_op jit(solution)/shard_map/ppermute | solution.py:325
  107.3 2.4 %collective-permute-start.18 = (bf16[32,2176]{1,0:T(8,128)(2,1)S(1)}, bf16[32,2176]{1,0:T(8,128)(2,1)S(1)}, u32[]{:S(2)}, u32[]{:S(2)}) collective-permute-start(bf16[32,2176]{1,0:T(8,128)(2,1)S(1)} %get-tuple-element.69), channel_id=1, source_target_pairs={{0,4},{1,5},{2,6},{3,7},{4,0},{5,1},{6,2},{7,3},{8,12},{9,13},{10,... | collective-permute-start | bytes 417800 | tf_op jit(solution)/shard_map/ppermute | solution.py:325
  111.6 1.5 collective-permute-start.10
  113.2 7.0 %collective-permute-done.18 = bf16[32,2176]{1,0:T(8,128)(2,1)S(1)} collective-permute-done((bf16[32,2176]{1,0:T(8,128)(2,1)S(1)}, bf16[32,2176]{1,0:T(8,128)(2,1)S(1)}, u32[]{:S(2)}, u32[]{:S(2)}) %collective-permute-start.18) | collective-permute-done | bytes 139296 | tf_op jit(solution)/shard_map/ppermute | solution.py:325
  120.5 1.6 collective-permute-start.21
  122.2 3.4 %collective-permute-done.21 = bf16[32,2176]{1,0:T(8,128)(2,1)S(1)} collective-permute-done((bf16[32,2176]{1,0:T(8,128)(2,1)S(1)}, bf16[32,2176]{1,0:T(8,128)(2,1)S(1)}, u32[]{:S(2)}, u32[]{:S(2)}) %collective-permute-start.21) | collective-permute-done | bytes 139296 | tf_op jit(solution)/shard_map/ppermute | solution.py:322
  126.4 5.1 %all-to-all-start.3 = ((bf16[8,128,128]{2,1,0:T(8,128)(2,1)}), bf16[8,128,128]{2,1,0:T(8,128)(2,1)S(1)}, u32[]{:S(2)}, u32[]{:S(2)}) async-start(bf16[8,128,128]{2,1,0:T(8,128)(2,1)} %bitcast.37), calls=%async_computation.3 | async-start | bytes 524288 | tf_op jit(solution)/shard_map/all_to_all | solution.py:405
  131.9 0.9 fusion.26
  133.0 1.0 fusion.4
  134.0 0.8 pad_maximum_fusion.3
  134.9 6.2 %all-to-all-done.3.ga_ref = bf16[8,128,128]{2,1,0:T(8,128)(2,1)S(1)} async-done(((bf16[8,128,128]{2,1,0:T(8,128)(2,1)}), bf16[8,128,128]{2,1,0:T(8,128)(2,1)S(1)}, u32[]{:S(2)}, u32[]{:S(2)}) %all-to-all-start.3) | async-done | bytes 262176 | tf_op jit(solution)/shard_map/all_to_all | solution.py:405
  141.1 4.2 %all-to-all-start.2 = ((bf16[8,256,128]{2,1,0:T(8,128)(2,1)}), bf16[8,256,128]{2,1,0:T(8,128)(2,1)}, u32[]{:S(2)}, u32[]{:S(2)}) async-start(bf16[8,256,128]{2,1,0:T(8,128)(2,1)} %pad_maximum_fusion.3), calls=%async_computation.2 | async-start | bytes 1048576 | tf_op jit(solution)/shard_map/all_to_all | solution.py:438
  146.0 1.1 fusion.23
  147.6 1.6 collective-permute-start.14
  149.5 4.6 %fusion.28.base_ref = f32[128,4096]{1,0:T(8,128)S(1)} fusion(bf16[128,1024]{1,0:T(8,128)(2,1)S(1)} %get-tuple-element.36, bf16[1024,4096]{1,0:T(8,128)(2,1)} %copy-done), kind=kOutput, calls=%fused_computation.102 | convolution fusion | flops 1073741824 | bytes 10747904 | tf_op jit(solution)/shard_map/dot_general | solution.py:19
  154.1 5.4 %all-to-all-done.2 = bf16[8,256,128]{2,1,0:T(8,128)(2,1)} async-done(((bf16[8,256,128]{2,1,0:T(8,128)(2,1)}), bf16[8,256,128]{2,1,0:T(8,128)(2,1)}, u32[]{:S(2)}, u32[]{:S(2)}) %all-to-all-start.2) | async-done | bytes 524320 | tf_op jit(solution)/shard_map/all_to_all | solution.py:438
  159.5 1.8 %slice_bitcast_fusion.2 = (bf16[8,16,8,128]{3,2,1,0:T(8,128)(2,1)S(1)}, bf16[8,128,128]{2,1,0:T(8,128)(2,1)}) fusion(bf16[8,256,128]{2,1,0:T(8,128)(2,1)} %all-to-all-done.2), kind=kLoop, calls=%fused_computation.35 | loop fusion | bytes 1048576
  161.4 1.8 %copy.77 = bf16[8,128,128]{1,2,0:T(8,128)(2,1)} copy(bf16[8,128,128]{2,1,0:T(8,128)(2,1)} %get-tuple-element.71) | data formatting | bytes 524288
  163.2 1.8 %copy.75 = bf16[128,1024]{1,0:T(8,128)(2,1)} copy(bf16[128,1024]{0,1:T(8,128)(2,1)} %bitcast.113) | data formatting | bytes 524288
  165.0 4.9 %finish.1 = f32[128,4096]{1,0:T(8,128)} custom-call(f32[128,4096]{1,0:T(8,128)S(1)} %fusion.28.base_ref, s32[4,256,1]{2,1,0:T(8,128)S(1)} %copy-done.5, bf16[128,1024]{1,0:T(8,128)(2,1)S(1)} %bitcast.106, bf16[128,256]{1,0:T(8,128)(2,1)S(1)} %get-tuple-element.38.refs_0_, bf16[128,256]{1,0:T(8,128)(2,1)S(1)} %collective-permute-done.13.refs_1_, ...), custom_call_target="tpu_custom_call" | custom-call | bytes 15000000 | tf_op jit(solution)/shard_map/finish/pallas_call | solution.py:276
  (120 shorter events, 12.7 us)
Async XLA Ops:
  0.6 1.8 %slice-start = ((bf16[128,4096]{1,0:T(8,128)(2,1)}), bf16[128,1024]{1,0:T(8,128)(2,1)S(1)}, s32[]{:S(2)}) async-start(bf16[128,4096]{1,0:T(8,128)(2,1)} %x_ref.3), calls=%async_computation.4 | async-start | bytes 524288 | tf_op jit(solution)/shard_map/slice | solution.py:346
  0.6 2.1 %copy-start.9 = (bf16[128,1024]{1,0:T(8,128)(2,1)S(1)}, bf16[128,1024]{1,0:T(8,128)(2,1)}, u32[]{:S(2)}) copy-start(bf16[128,1024]{1,0:T(8,128)(2,1)} %param.21) | copy-start | bytes 786436
  4.6 7.4 %copy-start.11 = (s32[512]{0:T(512)S(1)}, s32[512]{0:T(512)}, u32[]{:S(2)}) copy-start(s32[512]{0:T(512)} %param.12) | copy-start | bytes 6148
  4.6 7.4 %copy-start.14 = (s32[128]{0:T(128)S(1)}, s32[128]{0:T(128)}, u32[]{:S(2)}) copy-start(s32[128]{0:T(128)} %param.13) | copy-start | bytes 1540
  4.6 7.5 %copy-start.1 = (bf16[128,4096]{1,0:T(8,128)(2,1)S(1)}, bf16[128,4096]{1,0:T(8,128)(2,1)}, u32[]{:S(2)}) copy-start(bf16[128,4096]{1,0:T(8,128)(2,1)} %x_ref.3) | copy-start | bytes 3145732
  4.6 11.8 %copy-start.12 = (s32[512]{0:T(512)S(1)}, s32[512]{0:T(512)}, u32[]{:S(2)}) copy-start(s32[512]{0:T(512)} %param.15) | copy-start | bytes 6148
  4.6 11.8 %copy-start.13 = (s32[512]{0:T(512)S(1)}, s32[512]{0:T(512)}, u32[]{:S(2)}) copy-start(s32[512]{0:T(512)} %param.14) | copy-start | bytes 6148
  4.6 45.2 %all-to-all-start = ((bf16[8,784,128]{2,1,0:T(8,128)(2,1)}), bf16[8,784,128]{2,1,0:T(8,128)(2,1)}, u32[]{:S(2)}, u32[]{:S(2)}) async-start(bf16[8,784,128]{2,1,0:T(8,128)(2,1)} %pad_maximum_fusion), calls=%async_computation | async-start | bytes 3211264 | tf_op jit(solution)/shard_map/all_to_all | solution.py:353
  13.8 22.3 %collective-permute-start = (bf16[128,256]{1,0:T(8,128)(2,1)S(1)}, bf16[128,256]{1,0:T(8,128)(2,1)S(1)}, u32[]{:S(2)}, u32[]{:S(2)}) collective-permute-start(bf16[128,256]{1,0:T(8,128)(2,1)S(1)} %get-tuple-element.27), channel_id=1, source_target_pairs={{0,8},{8,0},{16,24},{24,16},{1,9},{9,1},{17,25},{25,17},{2,10},{10... | collective-permute-start | bytes 196616 | tf_op jit(solution)/shard_map/ppermute | solution.py:322
  13.8 22.2 %collective-permute-start.1 = (bf16[128,256]{1,0:T(8,128)(2,1)S(1)}, bf16[128,256]{1,0:T(8,128)(2,1)S(1)}, u32[]{:S(2)}, u32[]{:S(2)}) collective-permute-start(bf16[128,256]{1,0:T(8,128)(2,1)S(1)} %get-tuple-element.28), channel_id=1, source_target_pairs={{0,16},{8,24},{16,0},{24,8},{1,17},{9,25},{17,1},{25,9},{2,18},{10... | collective-permute-start | bytes 196616 | tf_op jit(solution)/shard_map/ppermute | solution.py:322
  15.4 20.6 %collective-permute-start.2 = (bf16[128,256]{1,0:T(8,128)(2,1)S(1)}, bf16[128,256]{1,0:T(8,128)(2,1)S(1)}, u32[]{:S(2)}, u32[]{:S(2)}) collective-permute-start(bf16[128,256]{1,0:T(8,128)(2,1)S(1)} %get-tuple-element.29), channel_id=1, source_target_pairs={{0,24},{8,16},{16,8},{24,0},{1,25},{9,17},{17,9},{25,1},{2,26},{10... | collective-permute-start | bytes 196616 | tf_op jit(solution)/shard_map/ppermute | solution.py:322
  32.7 3.3 %copy-start = (bf16[1024,4096]{1,0:T(8,128)(2,1)}, bf16[1024,4096]{1,0:T(8,128)(2,1)S(1)}, u32[]{:S(2)}) copy-start(bf16[1024,4096]{1,0:T(8,128)(2,1)S(1)} %get-tuple-element.37) | copy-start | bytes 25165828
  50.9 14.4 %copy-start.15 = (s32[128]{0:T(128)S(1)}, s32[128]{0:T(128)}, u32[]{:S(2)}) copy-start(s32[128]{0:T(128)} %param.13) | copy-start | bytes 1540
  50.9 12.9 %all-to-all-start.1 = ((bf16[8,128,128]{2,1,0:T(8,128)(2,1)}), bf16[8,128,128]{2,1,0:T(8,128)(2,1)}, u32[]{:S(2)}, u32[]{:S(2)}) async-start(bf16[8,128,128]{2,1,0:T(8,128)(2,1)} %add_halo.1), calls=%async_computation.1 | async-start | bytes 524288 | tf_op jit(solution)/shard_map/all_to_all | solution.py:379
  56.1 12.3 %collective-permute-start.3 = (bf16[1536,128]{1,0:T(8,128)(2,1)}, bf16[1536,128]{1,0:T(8,128)(2,1)S(1)}, u32[]{:S(2)}, u32[]{:S(2)}) collective-permute-start(bf16[1536,128]{1,0:T(8,128)(2,1)} %get-tuple-element.78), channel_id=1, source_target_pairs={{0,16},{8,24},{16,0},{24,8},{1,17},{9,25},{17,1},{25,9},{2,18},{10... | collective-permute-start | bytes 1179656 | tf_op jit(solution)/shard_map/ppermute | solution.py:322
  63.8 8.3 %collective-permute-start.7 = (bf16[1024,128]{1,0:T(8,128)(2,1)}, bf16[1024,128]{1,0:T(8,128)(2,1)}, u32[]{:S(2)}, u32[]{:S(2)}) collective-permute-start(bf16[1024,128]{1,0:T(8,128)(2,1)} %bitcast.22.refs_4_), channel_id=1, source_target_pairs={{0,16},{8,24},{16,0},{24,8},{1,17},{9,25},{17,1},{25,9},{2,18},{10... | collective-permute-start | bytes 786440 | tf_op jit(solution)/shard_map/ppermute | solution.py:322
  66.1 15.5 %collective-permute-start.4 = (bf16[1280,128]{1,0:T(8,128)(2,1)}, bf16[1280,128]{1,0:T(8,128)(2,1)}, u32[]{:S(2)}, u32[]{:S(2)}) collective-permute-start(bf16[1280,128]{1,0:T(8,128)(2,1)} %pad_maximum_fusion.7), channel_id=1, source_target_pairs={{0,8},{8,0},{16,24},{24,16},{1,9},{9,1},{17,25},{25,17},{2,10},{10... | collective-permute-start | bytes 983048 | tf_op jit(solution)/shard_map/ppermute | solution.py:322
  68.3 7.2 %copy-start.2 = (bf16[1536,128]{1,0:T(8,128)(2,1)}, bf16[1536,128]{1,0:T(8,128)(2,1)S(1)}, u32[]{:S(2)}) copy-start(bf16[1536,128]{1,0:T(8,128)(2,1)S(1)} %collective-permute-done.3.refs_1_) | copy-start | bytes 1179652
  69.1 12.5 %collective-permute-start.5 = (bf16[1280,128]{1,0:T(8,128)(2,1)}, bf16[1280,128]{1,0:T(8,128)(2,1)}, u32[]{:S(2)}, u32[]{:S(2)}) collective-permute-start(bf16[1280,128]{1,0:T(8,128)(2,1)} %slice.166), channel_id=1, source_target_pairs={{0,8},{8,0},{16,24},{24,16},{1,9},{9,1},{17,25},{25,17},{2,10},{10... | collective-permute-start | bytes 983048 | tf_op jit(solution)/shard_map/ppermute | solution.py:322
  69.1 12.5 %collective-permute-start.6 = (bf16[1024,128]{1,0:T(8,128)(2,1)}, bf16[1024,128]{1,0:T(8,128)(2,1)}, u32[]{:S(2)}, u32[]{:S(2)}) collective-permute-start(bf16[1024,128]{1,0:T(8,128)(2,1)} %bitcast.22.refs_4_), channel_id=1, source_target_pairs={{0,8},{8,0},{16,24},{24,16},{1,9},{9,1},{17,25},{25,17},{2,10},{10... | collective-permute-start | bytes 786440 | tf_op jit(solution)/shard_map/ppermute | solution.py:322
  72.2 9.4 %collective-permute-start.8 = (bf16[1024,128]{1,0:T(8,128)(2,1)}, bf16[1024,128]{1,0:T(8,128)(2,1)}, u32[]{:S(2)}, u32[]{:S(2)}) collective-permute-start(bf16[1024,128]{1,0:T(8,128)(2,1)} %collective-permute-done.7.refs_6_), channel_id=1, source_target_pairs={{0,8},{8,0},{16,24},{24,16},{1,9},{9,1},{17,25},{25,17},{2,10},{10... | collective-permute-start | bytes 786440 | tf_op jit(solution)/shard_map/ppermute | solution.py:322
  81.6 1.0 copy-start.3
  82.6 0.9 copy-start.6
  83.5 5.0 %copy-start.4 = (bf16[1536,128]{1,0:T(8,128)(2,1)S(1)}, bf16[1536,128]{1,0:T(8,128)(2,1)}, u32[]{:S(2)}) copy-start(bf16[1536,128]{1,0:T(8,128)(2,1)} %copy-done.2) | copy-start | bytes 1179652
  87.9 4.6 %collective-permute-start.11 = (bf16[2,1024,128]{2,1,0:T(8,128)(2,1)S(1)}, bf16[2,1024,128]{2,1,0:T(8,128)(2,1)S(1)}, u32[]{:S(2)}, u32[]{:S(2)}) collective-permute-start(bf16[2,1024,128]{2,1,0:T(8,128)(2,1)S(1)} %get-tuple-element.35), channel_id=1, source_target_pairs={{0,8},{8,0},{16,24},{24,16},{1,9},{9,1},{17,25},{25,17},{2,10},{10... | collective-permute-start | bytes 1572872 | tf_op jit(solution)/shard_map/ppermute | solution.py:322
  90.7 14.6 %collective-permute-start.16 = (bf16[4,32,2176]{2,1,0:T(8,128)(2,1)S(1)}, bf16[4,32,2176]{2,1,0:T(8,128)(2,1)S(1)}, u32[]{:S(2)}, u32[]{:S(2)}) collective-permute-start(bf16[4,32,2176]{2,1,0:T(8,128)(2,1)S(1)} %slice_bitcast_fusion), channel_id=1, source_target_pairs={{0,1},{1,0},{2,3},{3,2},{4,5},{5,4},{6,7},{7,6},{8,9},{9,8},{10,11... | collective-permute-start | bytes 1671176 | tf_op jit(solution)/shard_map/ppermute | solution.py:325
  92.5 17.4 %collective-permute-start.9 = (bf16[2,1280,128]{2,1,0:T(8,128)(2,1)S(1)}, bf16[2,1280,128]{2,1,0:T(8,128)(2,1)S(1)}, u32[]{:S(2)}, u32[]{:S(2)}) collective-permute-start(bf16[2,1280,128]{2,1,0:T(8,128)(2,1)S(1)} %get-tuple-element.33), channel_id=1, source_target_pairs={{0,8},{8,0},{16,24},{24,16},{1,9},{9,1},{17,25},{25,17},{2,10},{10... | collective-permute-start | bytes 1966088 | tf_op jit(solution)/shard_map/ppermute | solution.py:322
  92.7 32.9 %collective-permute-start.12 = (bf16[1024,128]{1,0:T(8,128)(2,1)S(1)}, bf16[1024,128]{1,0:T(8,128)(2,1)S(1)}, u32[]{:S(2)}, u32[]{:S(2)}) collective-permute-start(bf16[1024,128]{1,0:T(8,128)(2,1)S(1)} %slice_bitcast_fusion.3), channel_id=1, source_target_pairs={{0,16},{8,24},{16,0},{24,8},{1,17},{9,25},{17,1},{25,9},{2,18},{10... | collective-permute-start | bytes 786440 | tf_op jit(solution)/shard_map/ppermute | solution.py:322
  105.5 7.7 %collective-permute-start.17 = (bf16[32,2176]{1,0:T(8,128)(2,1)S(1)}, bf16[32,2176]{1,0:T(8,128)(2,1)S(1)}, u32[]{:S(2)}, u32[]{:S(2)}) collective-permute-start(bf16[32,2176]{1,0:T(8,128)(2,1)S(1)} %get-tuple-element.67), channel_id=1, source_target_pairs={{0,2},{1,3},{2,0},{3,1},{4,6},{5,7},{6,4},{7,5},{8,10},{9,11},{10,... | collective-permute-start | bytes 417800 | tf_op jit(solution)/shard_map/ppermute | solution.py:325
  107.3 12.9 %collective-permute-start.18 = (bf16[32,2176]{1,0:T(8,128)(2,1)S(1)}, bf16[32,2176]{1,0:T(8,128)(2,1)S(1)}, u32[]{:S(2)}, u32[]{:S(2)}) collective-permute-start(bf16[32,2176]{1,0:T(8,128)(2,1)S(1)} %get-tuple-element.69), channel_id=1, source_target_pairs={{0,4},{1,5},{2,6},{3,7},{4,0},{5,1},{6,2},{7,3},{8,12},{9,13},{10,... | collective-permute-start | bytes 417800 | tf_op jit(solution)/shard_map/ppermute | solution.py:325
  109.7 10.5 %collective-permute-start.19 = (bf16[32,2176]{1,0:T(8,128)(2,1)S(1)}, bf16[32,2176]{1,0:T(8,128)(2,1)S(1)}, u32[]{:S(2)}, u32[]{:S(2)}) collective-permute-start(bf16[32,2176]{1,0:T(8,128)(2,1)S(1)} %get-tuple-element.68), channel_id=1, source_target_pairs={{0,6},{1,7},{2,4},{3,5},{4,2},{5,3},{6,0},{7,1},{8,14},{9,15},{10,... | collective-permute-start | bytes 417800 | tf_op jit(solution)/shard_map/ppermute | solution.py:325
  110.1 12.0 %copy-start.7 = (bf16[2,1024,128]{2,1,0:T(8,128)(2,1)}, bf16[2,1024,128]{2,1,0:T(8,128)(2,1)S(1)}, u32[]{:S(2)}) copy-start(bf16[2,1024,128]{2,1,0:T(8,128)(2,1)S(1)} %add_convert_fusion.1) | copy-start | bytes 1572868
  111.6 20.3 %collective-permute-start.10 = (bf16[1536,128]{1,0:T(8,128)(2,1)}, bf16[1536,128]{1,0:T(8,128)(2,1)}, u32[]{:S(2)}, u32[]{:S(2)}) collective-permute-start(bf16[1536,128]{1,0:T(8,128)(2,1)} %pad_maximum_fusion.6), channel_id=1, source_target_pairs={{0,16},{8,24},{16,0},{24,8},{1,17},{9,25},{17,1},{25,9},{2,18},{10... | collective-permute-start | bytes 1179656 | tf_op jit(solution)/shard_map/ppermute | solution.py:322
  120.5 5.1 %collective-permute-start.21 = (bf16[32,2176]{1,0:T(8,128)(2,1)S(1)}, bf16[32,2176]{1,0:T(8,128)(2,1)S(1)}, u32[]{:S(2)}, u32[]{:S(2)}) collective-permute-start(bf16[32,2176]{1,0:T(8,128)(2,1)S(1)} %pad_maximum_fusion.10), channel_id=1, source_target_pairs={{0,16},{8,24},{16,0},{24,8},{1,17},{9,25},{17,1},{25,9},{2,18},{10... | collective-permute-start | bytes 417800 | tf_op jit(solution)/shard_map/ppermute | solution.py:322
  122.1 9.4 %collective-permute-start.20 = (bf16[32,2176]{1,0:T(8,128)(2,1)S(1)}, bf16[32,2176]{1,0:T(8,128)(2,1)S(1)}, u32[]{:S(2)}, u32[]{:S(2)}) collective-permute-start(bf16[32,2176]{1,0:T(8,128)(2,1)S(1)} %pad_maximum_fusion.10), channel_id=1, source_target_pairs={{0,8},{8,0},{16,24},{24,16},{1,9},{9,1},{17,25},{25,17},{2,10},{10... | collective-permute-start | bytes 417800 | tf_op jit(solution)/shard_map/ppermute | solution.py:322
  125.6 5.9 %collective-permute-start.22 = (bf16[32,2176]{1,0:T(8,128)(2,1)S(1)}, bf16[32,2176]{1,0:T(8,128)(2,1)S(1)}, u32[]{:S(2)}, u32[]{:S(2)}) collective-permute-start(bf16[32,2176]{1,0:T(8,128)(2,1)S(1)} %collective-permute-done.21), channel_id=1, source_target_pairs={{0,8},{8,0},{16,24},{24,16},{1,9},{9,1},{17,25},{25,17},{2,10},{10... | collective-permute-start | bytes 417800 | tf_op jit(solution)/shard_map/ppermute | solution.py:322
  126.4 14.7 %all-to-all-start.3 = ((bf16[8,128,128]{2,1,0:T(8,128)(2,1)}), bf16[8,128,128]{2,1,0:T(8,128)(2,1)S(1)}, u32[]{:S(2)}, u32[]{:S(2)}) async-start(bf16[8,128,128]{2,1,0:T(8,128)(2,1)} %bitcast.37), calls=%async_computation.3 | async-start | bytes 524288 | tf_op jit(solution)/shard_map/all_to_all | solution.py:405
  131.7 1.2 copy-start.10
  131.9 1.1 copy-start.8
  141.1 18.4 %all-to-all-start.2 = ((bf16[8,256,128]{2,1,0:T(8,128)(2,1)}), bf16[8,256,128]{2,1,0:T(8,128)(2,1)}, u32[]{:S(2)}, u32[]{:S(2)}) async-start(bf16[8,256,128]{2,1,0:T(8,128)(2,1)} %pad_maximum_fusion.3), calls=%async_computation.2 | async-start | bytes 1048576 | tf_op jit(solution)/shard_map/all_to_all | solution.py:438
  147.5 17.5 %collective-permute-start.13 = (bf16[128,256]{1,0:T(8,128)(2,1)S(1)}, bf16[128,256]{1,0:T(8,128)(2,1)S(1)}, u32[]{:S(2)}, u32[]{:S(2)}) collective-permute-start(bf16[128,256]{1,0:T(8,128)(2,1)S(1)} %get-tuple-element.39), channel_id=1, source_target_pairs={{0,8},{8,0},{16,24},{24,16},{1,9},{9,1},{17,25},{25,17},{2,10},{10... | collective-permute-start | bytes 196616 | tf_op jit(solution)/shard_map/ppermute | solution.py:322
  147.6 17.4 %collective-permute-start.14 = (bf16[128,256]{1,0:T(8,128)(2,1)S(1)}, bf16[128,256]{1,0:T(8,128)(2,1)S(1)}, u32[]{:S(2)}, u32[]{:S(2)}) collective-permute-start(bf16[128,256]{1,0:T(8,128)(2,1)S(1)} %get-tuple-element.40), channel_id=1, source_target_pairs={{0,16},{8,24},{16,0},{24,8},{1,17},{9,25},{17,1},{25,9},{2,18},{10... | collective-permute-start | bytes 196616 | tf_op jit(solution)/shard_map/ppermute | solution.py:322
  149.2 15.8 %collective-permute-start.15 = (bf16[128,256]{1,0:T(8,128)(2,1)S(1)}, bf16[128,256]{1,0:T(8,128)(2,1)S(1)}, u32[]{:S(2)}, u32[]{:S(2)}) collective-permute-start(bf16[128,256]{1,0:T(8,128)(2,1)S(1)} %get-tuple-element.41), channel_id=1, source_target_pairs={{0,24},{8,16},{16,8},{24,0},{1,25},{9,17},{17,9},{25,1},{2,26},{10... | collective-permute-start | bytes 196616 | tf_op jit(solution)/shard_map/ppermute | solution.py:322
  154.1 10.9 %copy-start.5 = (s32[4,256,1]{2,1,0:T(8,128)S(1)}, s32[4,256,1]{2,1,0:T(8,128)}, u32[]{:S(2)}) copy-start(s32[4,256,1]{2,1,0:T(8,128)} %copy.74.idx_ref) | copy-start | bytes 12292

commit v3 on v0

v3 whole, which is shorter than its diff:
```python
import functools

import jax
import jax.numpy as jnp
from jax import lax
from jax.experimental import pallas as pl
from jax.experimental.pallas import tpu as pltpu
from jax.sharding import PartitionSpec as P

T = 128
BF = jnp.bfloat16
F32 = jnp.float32
MIB = 1 << 20
VMEM = pl.BlockSpec(memory_space=pltpu.VMEM)
SMEM = pl.BlockSpec(memory_space=pltpu.SMEM)


def dot(left, right, dims):
    return lax.dot_general(left, right, (dims, ((), ())), preferred_element_type=F32)


def shape(*dims, kind=BF):
    return jax.ShapeDtypeStruct(dims, kind)


def whole_call(kernel, name, micros, out_shape, *args, scalars=0, mib=24):
    many = isinstance(out_shape, (list, tuple))
    return pl.pallas_call(
        kernel,
        out_shape=out_shape,
        in_specs=[SMEM] * scalars + [VMEM] * (len(args) - scalars),
        out_specs=[VMEM] * len(out_shape) if many else VMEM,
        compiler_params=pltpu.CompilerParams(vmem_limit_bytes=mib * MIB),
        cost_estimate=pl.CostEstimate(
            flops=0, bytes_accessed=int(micros * 3.0e6), transcendentals=0
        ),
        name=name,
    )(*args)


def pack_kernel(sub, me_ref, x_ref, cot_ref, bias_ref, send_ref, hub_ref, first_ref, *out_refs):
    groups, chunks, _, piece = first_ref.shape
    n = x_ref.shape[0] // sub
    bias = bias_ref[...]
    high = bias.astype(BF).astype(F32)
    row = lax.broadcasted_iota(jnp.int32, (sub, piece), 0)
    tail = jnp.where(row == 0, high, jnp.where(row == 1, bias - high, 0.0)).astype(BF)
    for b in range(groups):
        cols = slice(b * piece, (b + 1) * piece)
        first_ref[b, :n] = x_ref[:, cols].reshape(n, sub, piece)
        first_ref[b, n : 2 * n] = cot_ref[:, cols].reshape(n, sub, piece)
        first_ref[b, 2 * n] = tail
    x = x_ref[...]
    rows = lax.broadcasted_iota(jnp.int32, (x.shape[1], T), 0)
    readers = len(out_refs)
    for q in range(readers + 1):
        idx = send_ref[pl.ds(me_ref[0] ^ q, 1), :] if q < readers else hub_ref[...]
        hot = (rows == idx).astype(F32).astype(BF)
        got = dot(x, hot, ((1,), (0,))).astype(BF)
        if q < readers:
            out_refs[q][:, :T] = got
        else:
            for r in range(readers):
                out_refs[r][:, T:] = got


def pack(me, x, cot, bias, sends, hubs, sub, n_feat):
    n_dom = sends.shape[0]
    rows = x.shape[0]
    args = (x, cot, bias, sends, hubs)
    outs = [shape(n_feat, 2 * n_dom + 1, sub, cot.shape[1] // n_feat)]
    outs += [shape(rows, 2 * T)] * n_dom
    return pl.pallas_call(
        functools.partial(pack_kernel, sub),
        out_shape=outs,
        grid=(1,),
        in_specs=[SMEM] + [pl.BlockSpec(a.shape, lambda i, n=a.ndim: (0,) * n) for a in args],
        out_specs=[pl.BlockSpec(o.shape, lambda i, n=len(o.shape): (0,) * n) for o in outs],
        compiler_params=pltpu.CompilerParams(vmem_limit_bytes=60 * MIB),
        cost_estimate=pl.CostEstimate(flops=0, bytes_accessed=12000000, transcendentals=0),
        name="pack",
    )(me, *args)


def build_kernel(n_own, order_ref, start_ref, x_ref, vals_hbm, *refs):
    *halo_refs, own_ref, ext_ref, agg_ref, vals, sems = refs
    step = pl.program_id(0)
    slots = vals_hbm.shape[0]
    n_src = n_own + ext_ref.shape[1] // T
    chunks = sems.shape[0]
    per = slots // chunks

    def piece(i):
        span = pl.ds(i * per, per)
        return pltpu.make_async_copy(vals_hbm.at[span], vals.at[span], sems.at[i])

    @pl.when(step == 0)
    def _():
        for i in range(chunks):
            piece(i).start()
        vals[slots] = jnp.zeros((T, T), BF)
        for i in range(chunks):
            piece(i).wait()

    for v in range(own_ref.shape[0] // T):
        rows = slice(v * T, (v + 1) * T)
        for s in range(n_src):
            p = (step * (own_ref.shape[0] // T) + v) * n_src + s
            first, last = start_ref[p], start_ref[p + 1]
            one = jnp.where(last > first, order_ref[first], slots)
            two = jnp.where(last > first + 1, order_ref[first + 1], slots)
            total = vals[one].astype(F32) + vals[two].astype(F32)

            def more(i, total):
                return total + vals[order_ref[i]].astype(F32)

            total = lax.fori_loop(first + 2, last, more, total).astype(BF)
            if s < n_own:
                own_ref[rows, s * T : (s + 1) * T] = total
            else:
                ext_ref[rows, (s - n_own) * T : (s - n_own + 1) * T] = total
    halo = jnp.concatenate([r[...] for r in halo_refs], axis=1)
    total = dot(x_ref[...], own_ref[...], ((1,), (1,)))
    total = (total + dot(halo, ext_ref[...], ((1,), (1,)))).astype(BF)
    piece_n = agg_ref.shape[2]
    for b in range(agg_ref.shape[0]):
        agg_ref[b] = total[:, b * piece_n : (b + 1) * piece_n]


def build_dense(vals, order, start, x, halos, n_dst, n_src, n_own, n_feat):
    rows = x.shape[0]
    piece = n_dst * T // n_feat
    ext = (n_src - n_own) * T
    return pl.pallas_call(
        functools.partial(build_kernel, n_own),
        out_shape=(
            shape(n_dst * T, n_own * T),
            shape(n_dst * T, ext),
            shape(n_feat, rows, piece),
        ),
        grid_spec=pltpu.PrefetchScalarGridSpec(
            num_scalar_prefetch=2,
            grid=(n_dst // 2,),
            in_specs=[VMEM, pl.BlockSpec(memory_space=pl.ANY)] + [VMEM] * len(halos),
            out_specs=[
                pl.BlockSpec((2 * T, n_own * T), lambda u, *_: (u, 0)),
                pl.BlockSpec((2 * T, ext), lambda u, *_: (u, 0)),
                pl.BlockSpec((2 * T // piece, rows, piece), lambda u, *_: (u, 0, 0)),
            ],
            scratch_shapes=[
                pltpu.VMEM((vals.shape[0] + 1, T, T), BF),
                pltpu.SemaphoreType.DMA((8,)),
            ],
        ),
        compiler_params=pltpu.CompilerParams(vmem_limit_bytes=58 * MIB),
        cost_estimate=pl.CostEstimate(flops=0, bytes_accessed=30000000, transcendentals=0),
        name="build_dense",
    )(order, start, x, vals, *halos)


def split_kernel(blocks, n_dom, me_ref, block_ref, first_ref, bias_ref, *out_refs):
    _, _, sub, piece = first_ref.shape
    n = (first_ref.shape[1] - 1) // 2
    small = len(blocks) * sub
    width = len(blocks) * n * sub
    x = first_ref[:, :n].reshape(width, piece)
    row = lax.broadcasted_iota(jnp.int32, (sub, piece), 0) + me_ref[0] * sub
    lane = lax.broadcasted_iota(jnp.int32, (sub, piece), 1)
    for i, k in enumerate(blocks):
        b = block_ref[0] ^ k
        both = first_ref[b, 2 * n, 0:1].astype(F32) + first_ref[b, 2 * n, 1:2].astype(F32)
        mine = jnp.sum(jnp.where(row == lane, both, 0.0), axis=1, keepdims=True)
        bias_ref[i * sub : (i + 1) * sub, :] = jnp.broadcast_to(mine, (sub, T))
    even, odd = out_refs[0], out_refs[1]
    even[small:] = x
    odd[:width] = x
    for i, k in enumerate(blocks):
        b = block_ref[0] ^ k
        even[i * sub : (i + 1) * sub] = first_ref[b, n + me_ref[0]]
        odd[width + i * sub : width + (i + 1) * sub] = first_ref[b, n + (me_ref[0] ^ 1)]
    for j in range(1, n_dom // 2):
        ref = out_refs[1 + j]
        ref[small : small + width] = x
        for i, k in enumerate(blocks):
            b = block_ref[0] ^ k
            at = small + width + i * sub
            ref[i * sub : (i + 1) * sub] = first_ref[b, n + (me_ref[0] ^ (2 * j))]
            ref[at : at + sub] = first_ref[b, n + (me_ref[0] ^ (2 * j + 1))]


def weights(refs):
    return [jnp.concatenate([r[g, m] for r in refs for g in range(r.shape[0])]) for m in (0, 1)]


def dense_kernel(ny, nw, bias_ref, *refs):
    w_refs, refs = refs[:nw], refs[nw:]
    even, odd, agg = refs[:ny], refs[ny : 2 * ny], refs[2 * ny : 4 * ny]
    g_ref, act_even, act_odd, gagg_even, gagg_odd = refs[4 * ny :]
    w_self, w_neigh = weights(w_refs)
    small, width = w_self.shape
    bias = bias_ref[:, :1]
    for k in range(2 * ny):
        j = k // 2
        if k % 2 == 0:
            cot, x = even[j][:small, :], even[j][small : small + width, :]
            act_ref, gagg_ref = act_even, gagg_even
        else:
            x, cot = odd[j][:width, :], odd[j][width:, :]
            act_ref, gagg_ref = act_odd, gagg_odd
        pre = dot(w_self, x, ((1,), (0,)))
        pre += dot(w_neigh, agg[k][...], ((1,), (0,)))
        pre += bias
        sig = 1.0 / (1.0 + jnp.exp(-pre))
        act_ref[j] = (pre * sig).astype(BF)
        grad = (cot.astype(F32) * sig * (1.0 + pre * (1.0 - sig))).astype(BF)
        g_ref[k] = grad
        gagg_ref[j] = dot(w_neigh, grad, ((0,), (0,))).astype(BF)


def grads_kernel(ny, nw, g_ref, act_even, act_odd, *refs):
    w_refs, refs = refs[:nw], refs[nw:]
    even, odd, agg = refs[:ny], refs[ny : 2 * ny], refs[2 * ny : 4 * ny]
    back_even, back_odd, out_ref = refs[4 * ny :]
    w_self, _ = weights(w_refs)
    small, width = w_self.shape
    sub = out_ref.shape[2]
    xs = []
    for k in range(2 * ny):
        j = k // 2
        act_ref, back_ref = (act_odd, back_odd) if k % 2 else (act_even, back_even)
        back_ref[j, :width] = dot(w_self, g_ref[k], ((0,), (0,))).astype(BF)
        back_ref[j, width:] = act_ref[j]
        xs.append(odd[j][:width, :] if k % 2 else even[j][small : small + width, :])
    grad = jnp.concatenate([g_ref[k] for k in range(2 * ny)], axis=1)
    own = dot(grad, jnp.concatenate(xs, axis=1), ((1,), (1,))).astype(BF)
    neigh = dot(grad, jnp.concatenate([r[...] for r in agg], axis=1), ((1,), (1,))).astype(BF)
    total = jnp.sum(grad.astype(F32), axis=1, keepdims=True)
    high = total.astype(BF).astype(F32)
    lane = lax.broadcasted_iota(jnp.int32, (small, T), 1)
    both = jnp.where(lane == 0, high, jnp.where(lane == 1, total - high, 0.0)).astype(BF)
    nz = out_ref.shape[1]
    for i in range(small // sub):
        rows = slice(i * sub, (i + 1) * sub)
        out_ref[i // nz, i % nz, :, :width] = own[rows]
        out_ref[i // nz, i % nz, :, width : 2 * width] = neigh[rows]
        out_ref[i // nz, i % nz, :, 2 * width :] = both[rows]


def pair_kernel(even_ref, got_ref, *out_refs):
    for j, out_ref in enumerate(out_refs):
        out_ref[...] = (even_ref[j].astype(F32) + got_ref[j].astype(F32)).astype(BF)


def back_pair_kernel(width, even_ref, got_ref, *out_refs):
    for j, out_ref in enumerate(out_refs):
        both = even_ref[j, :width].astype(F32) + got_ref[j, :width].astype(F32)
        small = even_ref.shape[1] - width
        out_ref[:width] = both.astype(BF)
        out_ref[width : width + small] = even_ref[j, width:]
        out_ref[width + small :] = got_ref[j, width:]


def back_pack_kernel(blocks, me_ref, block_ref, *refs):
    *in_refs, out_ref = refs
    groups, chunks, sub, piece = out_ref.shape
    n = chunks // 2
    width = groups * n * sub
    small = groups * sub
    total = in_refs[0][:width].astype(F32)
    for r in in_refs[1:]:
        total += r[:width].astype(F32)
    out_ref[:, :n] = total.astype(BF).reshape(groups, n, sub, piece)
    for k in range(2 * len(in_refs)):
        d = me_ref[0] ^ k
        for i, f in enumerate(blocks):
            at = width + (k % 2) * small + i * sub
            out_ref[block_ref[0] ^ f, n + d] = in_refs[k // 2][at : at + sub]


def wsum_kernel(width, *refs):
    *in_refs, out_ref = refs
    total = in_refs[0][...].astype(F32)
    for r in in_refs[1:]:
        total += r[...].astype(F32)
    out_ref[:, : 2 * width] = total[:, : 2 * width].astype(BF)
    bias = jnp.sum(total[:, 2 * width :], axis=1, keepdims=True)
    high = bias.astype(BF).astype(F32)
    lane = lax.broadcasted_iota(jnp.int32, (total.shape[0], T), 1)
    both = jnp.where(lane == 0, high, jnp.where(lane == 1, bias - high, 0.0))
    out_ref[:, 2 * width :] = both.astype(BF)


def wout_kernel(me_ref, *refs):
    *in_refs, self_ref, neigh_ref, bias_ref = refs
    width = self_ref.shape[2]
    for k, ref in enumerate(in_refs):
        d = me_ref[0] ^ k
        self_ref[d] = ref[:, :width].astype(F32)
        neigh_ref[d] = ref[:, width : 2 * width].astype(F32)
        total = jnp.sum(ref[:, 2 * width :].astype(F32), axis=1, keepdims=True)
        bias_ref[d] = jnp.broadcast_to(total, bias_ref.shape[1:])


def halo_grad_kernel(ga_ref, ext_ref, flat_ref, *out_refs):
    ga = jnp.concatenate([ga_ref[b] for b in range(ga_ref.shape[0])], axis=1)
    flat_ref[...] = ga
    for k, out_ref in enumerate(out_refs):
        span = slice(k * 2 * T, (k + 1) * 2 * T)
        out_ref[...] = dot(ga, ext_ref[:, span], ((1,), (0,))).astype(BF)


def add_returned(total, at, me_ref, send_ref, hub_ref, ret_refs):
    rows = lax.broadcasted_iota(jnp.int32, (total.shape[1], T), 0) + at
    hub = (rows == hub_ref[...]).astype(F32).astype(BF)
    for q, ret_ref in enumerate(ret_refs):
        idx = send_ref[pl.ds(me_ref[0] ^ q, 1), :]
        sent = (rows == idx).astype(F32).astype(BF)
        total += dot(ret_ref[:, :T], sent, ((1,), (1,)))
        total += dot(ret_ref[:, T:], hub, ((1,), (1,)))
    return total


def finish_rest_kernel(top, me_ref, base_ref, send_ref, hub_ref, *refs):
    *ret_refs, out_ref = refs
    at = (pl.program_id(0) + top) * out_ref.shape[1]
    out_ref[...] = add_returned(base_ref[...], at, me_ref, send_ref, hub_ref, ret_refs)


def finish_dst_kernel(me_ref, base_ref, send_ref, hub_ref, back_ref, grads_ref, *refs):
    *ret_refs, out_ref, act_ref = refs
    rows = base_ref.shape[0]
    groups = range(back_ref.shape[0])
    own = jnp.concatenate([back_ref[b, :rows] for b in groups], axis=1).astype(F32)
    act_ref[...] = jnp.concatenate([back_ref[b, rows:] for b in groups], axis=1)
    at = pl.program_id(0) * out_ref.shape[1]
    out_ref[...] = add_returned(base_ref[...] + own, at, me_ref, send_ref, hub_ref, ret_refs)


def finish(me, base, ret, sends, hubs, back):
    rows, n = base.shape
    width = 512
    groups, _, piece = back.shape
    n_dst = groups * piece
    per = width // piece
    top = n_dst // width

    def column(first):
        return pl.BlockSpec((rows, width), lambda i: (0, i + first))

    def fixed(x):
        return pl.BlockSpec(x.shape, lambda i: (0, 0))

    grads = pl.pallas_call(
        functools.partial(finish_rest_kernel, top),
        out_shape=shape(rows, n, kind=F32),
        grid=(n // width - top,),
        in_specs=[SMEM, column(top), fixed(sends), fixed(hubs)] + [fixed(r) for r in ret],
        out_specs=column(top),
        compiler_params=pltpu.CompilerParams(vmem_limit_bytes=24 * MIB),
        cost_estimate=pl.CostEstimate(flops=0, bytes_accessed=15000000, transcendentals=0),
        name="finish_rest",
    )(me, base, sends, hubs, *ret)
    return pl.pallas_call(
        finish_dst_kernel,
        out_shape=[shape(rows, n, kind=F32), shape(rows, n_dst)],
        grid=(top,),
        in_specs=[
            SMEM,
            column(0),
            fixed(sends),
            fixed(hubs),
            pl.BlockSpec((per, 2 * rows, piece), lambda i: (i, 0, 0)),
            pl.BlockSpec(memory_space=pl.ANY),
        ]
        + [fixed(r) for r in ret],
        out_specs=[column(0), column(0)],
        input_output_aliases={5: 0},
        compiler_params=pltpu.CompilerParams(vmem_limit_bytes=24 * MIB),
        cost_estimate=pl.CostEstimate(flops=0, bytes_accessed=5000000, transcendentals=0),
        name="finish_dst",
    )(me, base, sends, hubs, back, grads, *ret)


def body(
    node_feats,
    send_rows,
    hub_rows,
    tile_dst,
    tile_src,
    tile_count,
    tile_vals,
    w_self,
    w_neigh,
    bias_vec,
    cotangent,
):
    n_dom = lax.axis_size("dom")
    n_feat = lax.axis_size("feat")
    ny, nz = n_dom // 2, n_feat // 2
    rows = node_feats.shape[0]
    own_rows = node_feats.shape[1]
    dst_rows = cotangent.shape[1]
    width = w_self.shape[1]
    n_own, n_dst = own_rows // T, dst_rows // T
    n_src = n_own + 2 * n_dom
    piece = dst_rows // n_feat
    sub = w_self.shape[0] // n_dom
    small = n_feat * sub
    me = lax.axis_index("dom")
    block = lax.axis_index("feat")
    me_s, block_s = me.reshape(1), block.reshape(1)

    def over_dom(x, k):
        return lax.ppermute(x, "dom", [(i, i ^ k) for i in range(n_dom)])

    def over_feat(x, k):
        return lax.ppermute(x, "feat", [(i, i ^ k) for i in range(n_feat)])

    def after(x, *events):
        return lax.optimization_barrier((x, events))[0]

    mine = jnp.stack(
        [
            lax.dynamic_slice_in_dim(w_self, me * sub, sub, axis=0),
            lax.dynamic_slice_in_dim(w_neigh, me * sub, sub, axis=0),
        ]
    )
    w, blocks = [mine[None]], [0]
    for bit in [1 << i for i in range(1, n_feat.bit_length() - 1)]:
        send = w[0] if len(w) == 1 else jnp.concatenate(w, axis=0)
        w.append(over_feat(send, bit))
        blocks += [k ^ bit for k in blocks]
    blocks += [k ^ 1 for k in blocks]

    sends, hubs = send_rows.reshape(n_dom, T), hub_rows[None, :]
    first, *outgoing = pack(
        me_s, node_feats, cotangent, bias_vec[None, :], sends, hubs, sub, n_feat
    )
    first = after(first, w[1])
    first = lax.all_to_all(first, "feat", 0, 0, tiled=True)
    incoming = [outgoing[0]] + [over_dom(outgoing[k], k) for k in range(1, n_dom)]

    halo_tile = n_own + 2 * ((tile_src - n_own) ^ me)
    hub_tile = n_own + 2 * ((tile_src - n_own - n_dom) ^ me) + 1
    place = jnp.where(
        tile_src < n_own, tile_src, jnp.where(tile_src < n_own + n_dom, halo_tile, hub_tile)
    )
    n_pos = n_dst * n_src
    slot = jnp.arange(tile_dst.shape[0], dtype=jnp.int32)
    key = jnp.where(slot < tile_count[0], tile_dst * n_src + place, n_pos)
    before = (key[None, :] < key[:, None]) | (
        (key[None, :] == key[:, None]) & (slot[None, :] < slot[:, None])
    )
    rank = jnp.sum(before.astype(jnp.int32), axis=1)
    order = jnp.sum(jnp.where(rank[:, None] == slot[None, :], slot[:, None], 0), axis=0)
    order = jnp.concatenate([order, jnp.zeros((2,), jnp.int32)])
    ends = jnp.arange(n_pos + 1, dtype=jnp.int32)
    start = jnp.sum((key[None, :] < ends[:, None]).astype(jnp.int32), axis=1)
    a_own, a_ext, agg = build_dense(
        tile_vals, order, start, node_feats, incoming, n_dst, n_src, n_own, n_feat
    )

    w[-1] = after(w[-1], agg)
    w.append(over_feat(jnp.concatenate(w, axis=0), 1))
    agg = after(agg, first)
    agg = lax.all_to_all(agg, "feat", 0, 0, tiled=True).reshape(width, piece)

    bias, even, odd, *cross = whole_call(
        functools.partial(split_kernel, blocks, n_dom),
        "split",
        1.5,
        [
            shape(small, T, kind=F32),
            shape(small + width, piece),
            shape(small + width, piece),
        ]
        + [shape(2 * small + width, piece)] * (ny - 1),
        me_s,
        block_s,
        first,
        scalars=2,
    )
    cross = [over_dom(c, 2 * (j + 1)) for j, c in enumerate(cross)]
    evens = [even] + cross
    odds = [over_dom(odd, 1)] + [over_dom(c[small:], 1) for c in cross]
    agg_even = [agg] + [over_dom(agg, 2 * j) for j in range(1, ny)]
    agg_odd = [over_dom(a, 1) for a in agg_even]
    aggs = [a for pair in zip(agg_even, agg_odd) for a in pair]

    grad, act_even, act_odd, gagg_even, gagg_odd = whole_call(
        functools.partial(dense_kernel, ny, len(w)),
        "dense",
        3.0,
        [
            shape(n_dom, small, piece),
            shape(ny, small, piece),
            shape(ny, small, piece),
            shape(ny, width, piece),
            shape(ny, width, piece),
        ],
        bias,
        *w,
        *evens,
        *odds,
        *aggs,
    )

    got = over_dom(gagg_odd, 1)
    pair = whole_call(pair_kernel, "pair", 1.0, [shape(width, piece)] * ny, gagg_even, got)

    back_even, back_odd, parts = whole_call(
        functools.partial(grads_kernel, ny, len(w)),
        "grads",
        3.0,
        [
            shape(ny, width + small, piece),
            shape(ny, width + small, piece),
            shape(2, nz, sub, 2 * width + T),
        ],
        grad,
        act_even,
        act_odd,
        *w,
        *evens,
        *odds,
        *aggs,
    )
    parts, back_odd = after((parts, back_odd), pair)

    gagg = pair[0].astype(F32)
    for j in range(1, ny):
        gagg += over_dom(pair[j], 2 * j).astype(F32)
    gagg = gagg.astype(BF).reshape(n_feat, rows, piece)
    from_x = over_feat(parts[1], 1)
    from_core = over_dom(back_odd, 1)
    from_x, from_core = after(from_x, gagg), after(from_core, gagg)

    gagg = lax.all_to_all(gagg, "feat", 0, 0, tiled=True)
    back = whole_call(
        functools.partial(back_pair_kernel, width),
        "back_pair",
        1.0,
        [shape(width + 2 * small, piece)] * ny,
        back_even,
        from_core,
    )
    back = [back[0]] + [over_dom(back[j], 2 * j) for j in range(1, ny)]
    parts = whole_call(pair_kernel, "x_sum", 1.0, [shape(sub, 2 * width + T)] * nz, parts[0], from_x)
    parts = [parts[0]] + [over_feat(parts[j], 2 * j) for j in range(1, nz)]

    gagg, *halo_grad = whole_call(
        halo_grad_kernel,
        "halo_grads",
        1.0,
        [shape(rows, dst_rows)] + [shape(rows, 2 * T)] * n_dom,
        gagg,
        a_ext,
    )
    back, parts = after(back, halo_grad), after(parts, halo_grad)
    returned = [halo_grad[0]] + [over_dom(halo_grad[k], k) for k in range(1, n_dom)]
    parts = after(parts, returned)

    back = whole_call(
        functools.partial(back_pack_kernel, blocks),
        "back_pack",
        1.0,
        shape(n_feat, 2 * n_dom, sub, piece),
        me_s,
        block_s,
        *back,
        scalars=2,
    )
    back = lax.all_to_all(back, "feat", 0, 0, tiled=True).reshape(n_feat, 2 * rows, piece)
    total = whole_call(
        functools.partial(wsum_kernel, width), "w_sum", 1.0, shape(sub, 2 * width + T), *parts
    )
    whole = [total] + [over_dom(total, 2 * j) for j in range(1, ny)]
    whole = [t for e in whole for t in (e, over_dom(e, 1))]
    base = dot(gagg, a_own, ((1,), (0,)))
    grad_self, grad_neigh, grad_bias = whole_call(
        wout_kernel,
        "w_out",
        1.0,
        [
            shape(n_dom, sub, width, kind=F32),
            shape(n_dom, sub, width, kind=F32),
            shape(n_dom, sub, T, kind=F32),
        ],
        me_s,
        *whole,
        scalars=1,
    )

    grad_feats, activations = finish(me_s, base, returned, sends, hubs, back)
    return (
        activations,
        grad_feats,
        grad_self.reshape(n_dom * sub, width),
        grad_neigh.reshape(n_dom * sub, width),
        grad_bias[:, :, 0].reshape(n_dom * sub),
    )


def solution(mesh):
    return jax.shard_map(
        body,
        mesh=mesh,
        in_specs=(
            P("feat", "dom"),
            P("dom"),
            P("dom"),
            P("dom"),
            P("dom"),
            P("dom"),
            P("dom", None, None),
            P("feat", None),
            P("feat", None),
            P("feat"),
            P("feat", "dom"),
        ),
        out_specs=(P("feat", "dom"), P("feat", "dom"), P("feat", None), P("feat", None), P("feat")),
        check_vma=False,
    )
```

time: 487 us -> 147 us (0.30); the launches traced: 481 us -> 146 us
  waiting for transfers between devices: 219 us -> 40.6 us
  matrix products: 156 us -> 4.67 us
  local copies, waits for them, and re-layouts: 48.8 us -> 6.21 us
  Pallas kernels: 0 us -> 41.4 us
  starting transfers between devices: 7.95 us -> 48.8 us
  other arithmetic: 20.1 us -> 2.94 us
  blocking collectives: 13.8 us -> 0 us
  between operations: 15.1 us -> 1.5 us
    dot_general x10 -> x1, matrix products: 156 us -> 4.67 us  [dot(): lax.dot_general(left, right, (dims, ((), ())), preferred_element_type=F32)]
    reduce_scatter x2 -> x0, waiting for transfers between devices: 145 us -> none  [the longest x1 145 us: body(): lax.psum_scatter(jnp.concatenate([contract_first(w_self, grad_pre), contr...]
    all_gather x2 -> x0, waiting for transfers between devices: 49.2 us -> none  [the longest x1 49.2 us: body(): lax.all_gather(aggregate, 'feat', axis=0, tiled=True)]
    pallas_call x0 -> x14, Pallas kernels: none -> 41.4 us  [the longest x1 19.1 us: build_dense(): pl.pallas_call(functools.partial(build_kernel, n_own), out_shape=(shape(n...]
    ppermute x0 -> x26, waiting for transfers between devices: none -> 40.6 us  [the longest x19 21.3 us: over_dom(): return lax.ppermute(x, 'dom', [(i, i ^ k) for i in range(n_dom)])]
    gather x4 -> x0, local copies, waits for them, and re-layouts: 29.8 us -> none  [the longest x1 14 us: body(): picked = source_table.reshape(feat_cols, tile_total, 128)[:, tile_src, :]]
    ppermute x0 -> x26, starting transfers between devices: none -> 27.5 us  [the longest x19 14.1 us: over_dom(): return lax.ppermute(x, 'dom', [(i, i ^ k) for i in range(n_dom)])]
    psum x1 -> x0, waiting for transfers between devices: 25.1 us -> none  [body(): lax.psum((local_self, local_neigh, local_bias), 'dom')]
  transfers between devices with their start and end apart: 7 -> 30, of which waited for: 3 -> 11; matrix products, arithmetic and copies ran while one was open for 25% -> 7% of each run, Pallas kernels for 0% -> 25%
where the time goes in v3:
time: 147 us; the launch traced here: 146 us
  starting transfers between devices  48.8 us (33%)
  Pallas kernels  41.4 us (28%)
  waiting for transfers between devices  40.6 us (28%)
  local copies, waits for them, and re-layouts  6.21 us (4%)
  matrix products  4.67 us (3%)
  other arithmetic  2.94 us (2%)
  between operations  1.5 us (1%)
    ppermute x19, waiting for transfers between devices, over_dom(): return lax.ppermute(x, 'dom', [(i, i ^ k) for i in range(n_dom)])  21.3 us
    ppermute x7, waiting for transfers between devices, over_feat(): return lax.ppermute(x, 'feat', [(i, i ^ k) for i in range(n_feat)])  19.3 us
    pallas_call x1, Pallas kernels, build_dense(): pl.pallas_call(functools.partial(build_kernel, n_own), out_shape=(shape(n...  19.1 us
    ppermute x19, starting transfers between devices, over_dom(): return lax.ppermute(x, 'dom', [(i, i ^ k) for i in range(n_dom)])  14.1 us
    ppermute x7, starting transfers between devices, over_feat(): return lax.ppermute(x, 'feat', [(i, i ^ k) for i in range(n_feat)])  13.4 us
    pallas_call x10, Pallas kernels, whole_call(): pl.pallas_call(kernel, out_shape=out_shape, in_specs=[SMEM] * scalars + [...  12.7 us
    all_to_all x1, starting transfers between devices, body(): agg = lax.all_to_all(agg, 'feat', 0, 0, tiled=True).reshape(width, piece)  5.95 us
    all_to_all x1, starting transfers between devices, body(): lax.all_to_all(back, 'feat', 0, 0, tiled=True)  5.71 us
  transfers between devices with their start and end apart: 30, of which 11 were waited for; matrix products, arithmetic and copies ran while one was open for 7% of the time, Pallas kernels for 25%

profile of v3, /device:TPU:0, one launch (start us, length us, event | category | flops | bytes accessed | tf_op | source)
XLA Modules:
  0.0 146.1 jit_solution(6697701821975653193)
XLA Ops:
  0.7 0.9 dynamic-slice_bitcast_fusion
  1.6 3.1 %collective-permute-start = (bf16[1,2,32,1024]{3,2,1,0:T(8,128)(2,1)S(1)}, bf16[1,2,32,1024]{3,2,1,0:T(8,128)(2,1)S(1)}, u32[]{:S(2)}, u32[]{:S(2)}) collective-permute-start(bf16[1,2,32,1024]{3,2,1,0:T(8,128)(2,1)S(1)} %maximum_bitcast_fusion.refs_0_), channel_id=1, source_target_pairs={{0,2},{1,3},{2,0},{3,1},{4,6},{5,7},{6,4},{7,5},{8,10},{9,11},{10,... | collective-permute-start | bytes 393224 | tf_op jit(solution)/shard_map/ppermute | solution.py:417
  4.7 3.9 %pack.1 = (bf16[8,9,32,128]{3,2,1,0:T(8,128)(2,1)}, bf16[128,256]{1,0:T(8,128)(2,1)}, bf16[128,256]{1,0:T(8,128)(2,1)}, bf16[128,256]{1,0:T(8,128)(2,1)}, bf16[128,256]{1,0:T(8,128)(2,1)}) custom-call(s32[1]{0:T(128)} %bitcast.me_ref, bf16[128,4096]{1,0:T(8,128)(2,1)} %x_ref.3, bf16[128,1024]{1,0:T(8,128)(2,1)} %cot_ref.1, f32[1,128]{1,0:T(1,128)} %bitcast.36, ...), custom_call_target="tpu_custom_call" | custom-call | bytes 12000000 | tf_op jit(solution)/shard_map/pack/pallas_call | solution.py:73
  8.6 5.5 %all-to-all-start = ((bf16[8,9,32,128]{3,2,1,0:T(8,128)(2,1)}), bf16[8,9,32,128]{3,2,1,0:T(8,128)(2,1)S(1)}, u32[]{:S(2)}, u32[]{:S(2)}) async-start(bf16[8,9,32,128]{3,2,1,0:T(8,128)(2,1)} %get-tuple-element.61), calls=%async_computation | async-start | bytes 1179648 | tf_op jit(solution)/shard_map/all_to_all | solution.py:440
  14.1 1.6 %collective-permute-start.3 = (bf16[128,256]{1,0:T(8,128)(2,1)}, bf16[128,256]{1,0:T(8,128)(2,1)S(1)}, u32[]{:S(2)}, u32[]{:S(2)}) collective-permute-start(bf16[128,256]{1,0:T(8,128)(2,1)} %get-tuple-element.65), channel_id=1, source_target_pairs={{0,16},{8,24},{16,0},{24,8},{1,17},{9,25},{17,1},{25,9},{2,18},{10... | collective-permute-start | bytes 196616 | tf_op jit(solution)/shard_map/ppermute | solution.py:414
  17.8 0.8 convert_reduce_fusion.1.start_ref
  18.8 1.1 collective-permute-done.4.refs_3_
  20.0 0.6 copy-done.11
  20.6 19.1 %build_dense.1 = (bf16[1024,4096]{1,0:T(8,128)(2,1)}, bf16[1024,1024]{1,0:T(8,128)(2,1)}, bf16[8,128,128]{2,1,0:T(8,128)(2,1)}) custom-call(s32[514]{0:T(1024)} %concatenate.10.order_ref, s32[321]{0:T(512)} %convert_reduce_fusion.1.start_ref, bf16[128,4096]{1,0:T(8,128)(2,1)} %x_ref.3, bf16[512,128,128]{2,1,0:T(8,128)(2,1)} %vals_hbm.1, ...), custom_call_target="tpu_custom_call" | custom-call | bytes 30000000 | tf_op jit(solution)/shard_map/build_dense/pallas_call | solution.py:134
  39.7 6.0 %all-to-all-start.1 = ((bf16[8,128,128]{2,1,0:T(8,128)(2,1)}), bf16[8,128,128]{2,1,0:T(8,128)(2,1)S(1)}, u32[]{:S(2)}, u32[]{:S(2)}) async-start(bf16[8,128,128]{2,1,0:T(8,128)(2,1)} %get-tuple-element.72), calls=%async_computation.1 | async-start | bytes 524288 | tf_op jit(solution)/shard_map/all_to_all | solution.py:466
  45.7 3.0 %collective-permute-start.1 = (bf16[2,2,32,1024]{3,2,1,0:T(8,128)(2,1)S(1)}, bf16[2,2,32,1024]{3,2,1,0:T(8,128)(2,1)S(1)}, u32[]{:S(2)}, u32[]{:S(2)}) collective-permute-start(bf16[2,2,32,1024]{3,2,1,0:T(8,128)(2,1)S(1)} %pad_maximum_fusion.1), channel_id=1, source_target_pairs={{0,4},{1,5},{2,6},{3,7},{4,0},{5,1},{6,2},{7,3},{8,12},{9,13},{10,... | collective-permute-start | bytes 786440 | tf_op jit(solution)/shard_map/ppermute | solution.py:417
  48.8 0.8 collective-permute-start.6
  49.6 15.7 %collective-permute-done.1.refs_2_ = bf16[2,2,32,1024]{3,2,1,0:T(8,128)(2,1)S(1)} collective-permute-done((bf16[2,2,32,1024]{3,2,1,0:T(8,128)(2,1)S(1)}, bf16[2,2,32,1024]{3,2,1,0:T(8,128)(2,1)S(1)}, u32[]{:S(2)}, u32[]{:S(2)}) %collective-permute-start.1) | collective-permute-done | bytes 262176 | tf_op jit(solution)/shard_map/ppermute | solution.py:417
  65.3 0.8 pad_maximum_fusion
  66.1 1.5 %collective-permute-start.5 = (bf16[4,2,32,1024]{3,2,1,0:T(8,128)(2,1)}, bf16[4,2,32,1024]{3,2,1,0:T(8,128)(2,1)S(1)}, u32[]{:S(2)}, u32[]{:S(2)}) collective-permute-start(bf16[4,2,32,1024]{3,2,1,0:T(8,128)(2,1)} %pad_maximum_fusion), channel_id=1, source_target_pairs={{0,1},{1,0},{2,3},{3,2},{4,5},{5,4},{6,7},{7,6},{8,9},{9,8},{10,11... | collective-permute-start | bytes 1572872 | tf_op jit(solution)/shard_map/ppermute | solution.py:417
  67.7 2.0 %collective-permute-start.10 = (bf16[1024,128]{1,0:T(8,128)(2,1)S(1)}, bf16[1024,128]{1,0:T(8,128)(2,1)S(1)}, u32[]{:S(2)}, u32[]{:S(2)}) collective-permute-start(bf16[1024,128]{1,0:T(8,128)(2,1)S(1)} %bitcast.24), channel_id=1, source_target_pairs={{0,16},{8,24},{16,0},{24,8},{1,17},{9,25},{17,1},{25,9},{2,18},{10... | collective-permute-start | bytes 786440 | tf_op jit(solution)/shard_map/ppermute | solution.py:414
  70.4 5.1 %collective-permute-done.10.refs_10_ = bf16[1024,128]{1,0:T(8,128)(2,1)S(1)} collective-permute-done((bf16[1024,128]{1,0:T(8,128)(2,1)S(1)}, bf16[1024,128]{1,0:T(8,128)(2,1)S(1)}, u32[]{:S(2)}, u32[]{:S(2)}) %collective-permute-start.10) | collective-permute-done | bytes 262176 | tf_op jit(solution)/shard_map/ppermute | solution.py:414
  75.5 3.2 %collective-permute-done.5.refs_3_ = bf16[4,2,32,1024]{3,2,1,0:T(8,128)(2,1)S(1)} collective-permute-done((bf16[4,2,32,1024]{3,2,1,0:T(8,128)(2,1)}, bf16[4,2,32,1024]{3,2,1,0:T(8,128)(2,1)S(1)}, u32[]{:S(2)}, u32[]{:S(2)}) %collective-permute-start.5) | collective-permute-done | bytes 524320 | tf_op jit(solution)/shard_map/ppermute | solution.py:417
  78.8 2.7 %dense.1 = (bf16[4,256,128]{2,1,0:T(8,128)(2,1)S(1)}, bf16[2,256,128]{2,1,0:T(8,128)(2,1)S(1)}, bf16[2,256,128]{2,1,0:T(8,128)(2,1)S(1)}, bf16[2,1024,128]{2,1,0:T(8,128)(2,1)S(1)}, bf16[2,1024,128]{2,1,0:T(8,128)(2,1)S(1)}) custom-call(f32[256,128]{1,0:T(8,128)S(1)} %get-tuple-element.62.bias_ref, bf16[1,2,32,1024]{3,2,1,0:T(8,128)(2,1)S(1)} %maximum_bitcast_fusion.refs_0_, ...), custom_call_target="tpu_custom_call" | custom-call | bytes 9000000 | tf_op jit(solution)/shard_map/dense/pallas_call | solution.py:28
  81.5 2.1 %grads.1 = (bf16[2,1280,128]{2,1,0:T(8,128)(2,1)S(1)}, bf16[2,1280,128]{2,1,0:T(8,128)(2,1)}, bf16[2,4,32,2176]{3,2,1,0:T(8,128)(2,1)S(1)}) custom-call(bf16[4,256,128]{2,1,0:T(8,128)(2,1)S(1)} %get-tuple-element.80.g_ref, bf16[2,256,128]{2,1,0:T(8,128)(2,1)S(1)} %get-tuple-element.81.act_even, bf16[2,256,128]{2,1,0:T(8,128)(2,1)S(1)} %get-tuple-element.82.act_odd, ...), custom_call_target="tpu_custom_call" | custom-call | bytes 9000000 | tf_op jit(solution)/shard_map/grads/pallas_call | solution.py:28
  83.7 3.2 %collective-permute-start.13 = (bf16[1024,128]{1,0:T(8,128)(2,1)S(1)}, bf16[1024,128]{1,0:T(8,128)(2,1)S(1)}, u32[]{:S(2)}, u32[]{:S(2)}) collective-permute-start(bf16[1024,128]{1,0:T(8,128)(2,1)S(1)} %get-tuple-element.76), channel_id=1, source_target_pairs={{0,16},{8,24},{16,0},{24,8},{1,17},{9,25},{17,1},{25,9},{2,18},{10... | collective-permute-start | bytes 786440 | tf_op jit(solution)/shard_map/ppermute | solution.py:414
  87.2 0.9 slice_bitcast_fusion
  88.0 1.5 %collective-permute-start.19 = (bf16[4,32,2176]{2,1,0:T(8,128)(2,1)}, bf16[4,32,2176]{2,1,0:T(8,128)(2,1)S(1)}, u32[]{:S(2)}, u32[]{:S(2)}) collective-permute-start(bf16[4,32,2176]{2,1,0:T(8,128)(2,1)} %get-tuple-element.115), channel_id=1, source_target_pairs={{0,1},{1,0},{2,3},{3,2},{4,5},{5,4},{6,7},{7,6},{8,9},{9,8},{10,11... | collective-permute-start | bytes 1671176 | tf_op jit(solution)/shard_map/ppermute | solution.py:417
  89.5 4.4 %collective-permute-done.13 = bf16[1024,128]{1,0:T(8,128)(2,1)S(1)} collective-permute-done((bf16[1024,128]{1,0:T(8,128)(2,1)S(1)}, bf16[1024,128]{1,0:T(8,128)(2,1)S(1)}, u32[]{:S(2)}, u32[]{:S(2)}) %collective-permute-start.13) | collective-permute-done | bytes 262176 | tf_op jit(solution)/shard_map/ppermute | solution.py:414
  93.9 0.8 add_convert_fusion
  94.7 4.1 %all-to-all-start.2 = ((bf16[8,128,128]{2,1,0:T(8,128)(2,1)}), bf16[8,128,128]{2,1,0:T(8,128)(2,1)S(1)}, u32[]{:S(2)}, u32[]{:S(2)}) async-start(bf16[8,128,128]{2,1,0:T(8,128)(2,1)} %bitcast.35), calls=%async_computation.2 | async-start | bytes 524288 | tf_op jit(solution)/shard_map/all_to_all | solution.py:538
  98.8 1.1 copy-done.2
  99.9 1.9 %back_pair.1 = (bf16[1536,128]{1,0:T(8,128)(2,1)S(1)}, bf16[1536,128]{1,0:T(8,128)(2,1)}) custom-call(bf16[2,1280,128]{2,1,0:T(8,128)(2,1)S(1)} %copy-done.2, bf16[2,1280,128]{2,1,0:T(8,128)(2,1)} %collective-permute-done.14.got_ref), custom_call_target="tpu_custom_call" | custom-call | bytes 3000000 | tf_op jit(solution)/shard_map/back_pair/pallas_call | solution.py:28
  101.7 0.7 copy-done.3
  102.5 1.7 %collective-permute-start.15 = (bf16[1536,128]{1,0:T(8,128)(2,1)}, bf16[1536,128]{1,0:T(8,128)(2,1)}, u32[]{:S(2)}, u32[]{:S(2)}) collective-permute-start(bf16[1536,128]{1,0:T(8,128)(2,1)} %get-tuple-element.89), channel_id=1, source_target_pairs={{0,16},{8,24},{16,0},{24,8},{1,17},{9,25},{17,1},{25,9},{2,18},{10... | collective-permute-start | bytes 1179656 | tf_op jit(solution)/shard_map/ppermute | solution.py:414
  104.6 0.8 x_sum.1
  105.4 0.7 copy-done.5
  106.0 1.7 %collective-permute-start.20 = (bf16[32,2176]{1,0:T(8,128)(2,1)}, bf16[32,2176]{1,0:T(8,128)(2,1)S(1)}, u32[]{:S(2)}, u32[]{:S(2)}) collective-permute-start(bf16[32,2176]{1,0:T(8,128)(2,1)} %get-tuple-element.101), channel_id=1, source_target_pairs={{0,2},{1,3},{2,0},{3,1},{4,6},{5,7},{6,4},{7,5},{8,10},{9,11},{10,... | collective-permute-start | bytes 417800 | tf_op jit(solution)/shard_map/ppermute | solution.py:417
  107.7 2.4 %collective-permute-start.21 = (bf16[32,2176]{1,0:T(8,128)(2,1)}, bf16[32,2176]{1,0:T(8,128)(2,1)}, u32[]{:S(2)}, u32[]{:S(2)}) collective-permute-start(bf16[32,2176]{1,0:T(8,128)(2,1)} %get-tuple-element.102), channel_id=1, source_target_pairs={{0,4},{1,5},{2,6},{3,7},{4,0},{5,1},{6,2},{7,3},{8,12},{9,13},{10,... | collective-permute-start | bytes 417800 | tf_op jit(solution)/shard_map/ppermute | solution.py:417
  110.4 1.1 halo_grads.1
  111.5 1.9 %collective-permute-done.15.refs_1_ = bf16[1536,128]{1,0:T(8,128)(2,1)} collective-permute-done((bf16[1536,128]{1,0:T(8,128)(2,1)}, bf16[1536,128]{1,0:T(8,128)(2,1)}, u32[]{:S(2)}, u32[]{:S(2)}) %collective-permute-start.15) | collective-permute-done | bytes 393248 | tf_op jit(solution)/shard_map/ppermute | solution.py:414
  113.5 1.9 %back_pack.1 = bf16[8,8,32,128]{3,2,1,0:T(8,128)(2,1)} custom-call(s32[1]{0:T(128)} %bitcast.me_ref, s32[1]{0:T(128)} %bitcast.1.block_ref, bf16[1536,128]{1,0:T(8,128)(2,1)S(1)} %copy-done.4, bf16[1536,128]{1,0:T(8,128)(2,1)} %collective-permute-done.15.refs_1_), custom_call_target="tpu_custom_call" | custom-call | bytes 3000000 | tf_op jit(solution)/shard_map/back_pack/pallas_call | solution.py:28
  115.4 5.7 %all-to-all-start.3 = ((bf16[8,8,32,128]{3,2,1,0:T(8,128)(2,1)}), bf16[8,8,32,128]{3,2,1,0:T(8,128)(2,1)S(1)}, u32[]{:S(2)}, u32[]{:S(2)}) async-start(bf16[8,8,32,128]{3,2,1,0:T(8,128)(2,1)} %back_pack.1), calls=%async_computation.3 | async-start | bytes 1048576 | tf_op jit(solution)/shard_map/all_to_all | solution.py:573
  121.1 1.6 %collective-permute-start.17 = (bf16[128,256]{1,0:T(8,128)(2,1)}, bf16[128,256]{1,0:T(8,128)(2,1)S(1)}, u32[]{:S(2)}, u32[]{:S(2)}) collective-permute-start(bf16[128,256]{1,0:T(8,128)(2,1)} %get-tuple-element.92), channel_id=1, source_target_pairs={{0,16},{8,24},{16,0},{24,8},{1,17},{9,25},{17,1},{25,9},{2,18},{10... | collective-permute-start | bytes 196616 | tf_op jit(solution)/shard_map/ppermute | solution.py:414
  123.0 3.0 %collective-permute-done.17.refs_2_ = bf16[128,256]{1,0:T(8,128)(2,1)S(1)} collective-permute-done((bf16[128,256]{1,0:T(8,128)(2,1)}, bf16[128,256]{1,0:T(8,128)(2,1)S(1)}, u32[]{:S(2)}, u32[]{:S(2)}) %collective-permute-start.17) | collective-permute-done | bytes 65568 | tf_op jit(solution)/shard_map/ppermute | solution.py:414
  125.9 1.0 collective-permute-done.18.refs_3_
  127.0 1.1 w_sum.1.refs_0_
  128.0 1.4 collective-permute-start.24
  129.7 4.3 %collective-permute-done.24.refs_2_ = bf16[32,2176]{1,0:T(8,128)(2,1)S(1)} collective-permute-done((bf16[32,2176]{1,0:T(8,128)(2,1)S(1)}, bf16[32,2176]{1,0:T(8,128)(2,1)S(1)}, u32[]{:S(2)}, u32[]{:S(2)}) %collective-permute-start.24) | collective-permute-done | bytes 139296 | tf_op jit(solution)/shard_map/ppermute | solution.py:414
  134.0 4.7 %fusion.4.base_ref = f32[128,4096]{1,0:T(8,128)S(1)} fusion(bf16[128,1024]{1,0:T(8,128)(2,1)S(1)} %get-tuple-element.78, bf16[1024,4096]{1,0:T(8,128)(2,1)} %get-tuple-element.79), kind=kOutput, calls=%fused_computation.21 | convolution fusion | flops 1073741824 | bytes 10747904 | tf_op jit(solution)/shard_map/dot_general | solution.py:19
  138.7 4.0 %finish_rest.1.grads_ref = f32[128,4096]{1,0:T(8,128)} custom-call(s32[1]{0:T(128)} %bitcast.me_ref, f32[128,4096]{1,0:T(8,128)S(1)} %fusion.4.base_ref, s32[4,128]{1,0:T(4,128)S(1)} %bitcast.30, s32[1,128]{1,0:T(1,128)S(1)} %bitcast.33, bf16[128,256]{1,0:T(8,128)(2,1)S(1)} %get-tuple-element.90.refs_0_, ...), custom_call_target="tpu_custom_call" | custom-call | bytes 15000000 | tf_op jit(solution)/shard_map/finish_rest/pallas_call | solution.py:353
  142.8 1.0 w_out.1
  144.5 1.7 %finish_dst.1 = (f32[128,4096]{1,0:T(8,128)}, bf16[128,1024]{1,0:T(8,128)(2,1)}) custom-call(s32[1]{0:T(128)} %bitcast.me_ref, f32[128,4096]{1,0:T(8,128)S(1)} %fusion.4.base_ref, s32[4,128]{1,0:T(4,128)S(1)} %bitcast.31, s32[1,128]{1,0:T(1,128)S(1)} %bitcast.34, bf16[8,256,128]{2,1,0:T(8,128)(2,1)S(1)} %bitcast.28, ...), custom_call_target="tpu_custom_call", output_to_operand_aliasing={{0}: (5, {})} | custom-call | bytes 5000000 | tf_op jit(solution)/shard_map/finish_dst/pallas_call | solution.py:363
  (69 shorter events, 5.0 us)
Async XLA Ops:
  0.6 16.0 %copy-start.12 = (s32[512]{0:T(512)S(1)}, s32[512]{0:T(512)}, u32[]{:S(2)}) copy-start(s32[512]{0:T(512)} %param.15) | copy-start | bytes 6148
  0.6 16.0 %copy-start.13 = (s32[512]{0:T(512)S(1)}, s32[512]{0:T(512)}, u32[]{:S(2)}) copy-start(s32[512]{0:T(512)} %param.14) | copy-start | bytes 6148
  1.6 7.0 %collective-permute-start = (bf16[1,2,32,1024]{3,2,1,0:T(8,128)(2,1)S(1)}, bf16[1,2,32,1024]{3,2,1,0:T(8,128)(2,1)S(1)}, u32[]{:S(2)}, u32[]{:S(2)}) collective-permute-start(bf16[1,2,32,1024]{3,2,1,0:T(8,128)(2,1)S(1)} %maximum_bitcast_fusion.refs_0_), channel_id=1, source_target_pairs={{0,2},{1,3},{2,0},{3,1},{4,6},{5,7},{6,4},{7,5},{8,10},{9,11},{10,... | collective-permute-start | bytes 393224 | tf_op jit(solution)/shard_map/ppermute | solution.py:417
  8.6 31.1 %all-to-all-start = ((bf16[8,9,32,128]{3,2,1,0:T(8,128)(2,1)}), bf16[8,9,32,128]{3,2,1,0:T(8,128)(2,1)S(1)}, u32[]{:S(2)}, u32[]{:S(2)}) async-start(bf16[8,9,32,128]{3,2,1,0:T(8,128)(2,1)} %get-tuple-element.61), calls=%async_computation | async-start | bytes 1179648 | tf_op jit(solution)/shard_map/all_to_all | solution.py:440
  14.1 4.4 %collective-permute-start.2 = (bf16[128,256]{1,0:T(8,128)(2,1)}, bf16[128,256]{1,0:T(8,128)(2,1)S(1)}, u32[]{:S(2)}, u32[]{:S(2)}) collective-permute-start(bf16[128,256]{1,0:T(8,128)(2,1)} %get-tuple-element.64), channel_id=1, source_target_pairs={{0,8},{8,0},{16,24},{24,16},{1,9},{9,1},{17,25},{25,17},{2,10},{10... | collective-permute-start | bytes 196616 | tf_op jit(solution)/shard_map/ppermute | solution.py:414
  14.1 4.7 %collective-permute-start.3 = (bf16[128,256]{1,0:T(8,128)(2,1)}, bf16[128,256]{1,0:T(8,128)(2,1)S(1)}, u32[]{:S(2)}, u32[]{:S(2)}) collective-permute-start(bf16[128,256]{1,0:T(8,128)(2,1)} %get-tuple-element.65), channel_id=1, source_target_pairs={{0,16},{8,24},{16,0},{24,8},{1,17},{9,25},{17,1},{25,9},{2,18},{10... | collective-permute-start | bytes 196616 | tf_op jit(solution)/shard_map/ppermute | solution.py:414
  15.7 4.3 %collective-permute-start.4 = (bf16[128,256]{1,0:T(8,128)(2,1)}, bf16[128,256]{1,0:T(8,128)(2,1)S(1)}, u32[]{:S(2)}, u32[]{:S(2)}) collective-permute-start(bf16[128,256]{1,0:T(8,128)(2,1)} %get-tuple-element.66), channel_id=1, source_target_pairs={{0,24},{8,16},{16,8},{24,0},{1,25},{9,17},{17,9},{25,1},{2,26},{10... | collective-permute-start | bytes 196616 | tf_op jit(solution)/shard_map/ppermute | solution.py:414
  18.5 1.4 copy-start.9
  18.8 1.1 copy-start.10
  20.0 0.6 copy-start.11
  39.7 27.9 %all-to-all-start.1 = ((bf16[8,128,128]{2,1,0:T(8,128)(2,1)}), bf16[8,128,128]{2,1,0:T(8,128)(2,1)S(1)}, u32[]{:S(2)}, u32[]{:S(2)}) async-start(bf16[8,128,128]{2,1,0:T(8,128)(2,1)} %get-tuple-element.72), calls=%async_computation.1 | async-start | bytes 524288 | tf_op jit(solution)/shard_map/all_to_all | solution.py:466
  45.7 19.6 %collective-permute-start.1 = (bf16[2,2,32,1024]{3,2,1,0:T(8,128)(2,1)S(1)}, bf16[2,2,32,1024]{3,2,1,0:T(8,128)(2,1)S(1)}, u32[]{:S(2)}, u32[]{:S(2)}) collective-permute-start(bf16[2,2,32,1024]{3,2,1,0:T(8,128)(2,1)S(1)} %pad_maximum_fusion.1), channel_id=1, source_target_pairs={{0,4},{1,5},{2,6},{3,7},{4,0},{5,1},{6,2},{7,3},{8,12},{9,13},{10,... | collective-permute-start | bytes 786440 | tf_op jit(solution)/shard_map/ppermute | solution.py:417
  48.8 20.9 %collective-permute-start.6 = (bf16[1536,128]{1,0:T(8,128)(2,1)S(1)}, bf16[1536,128]{1,0:T(8,128)(2,1)S(1)}, u32[]{:S(2)}, u32[]{:S(2)}) collective-permute-start(bf16[1536,128]{1,0:T(8,128)(2,1)S(1)} %get-tuple-element.70), channel_id=1, source_target_pairs={{0,16},{8,24},{16,0},{24,8},{1,17},{9,25},{17,1},{25,9},{2,18},{10... | collective-permute-start | bytes 1179656 | tf_op jit(solution)/shard_map/ppermute | solution.py:414
  66.1 12.6 %collective-permute-start.5 = (bf16[4,2,32,1024]{3,2,1,0:T(8,128)(2,1)}, bf16[4,2,32,1024]{3,2,1,0:T(8,128)(2,1)S(1)}, u32[]{:S(2)}, u32[]{:S(2)}) collective-permute-start(bf16[4,2,32,1024]{3,2,1,0:T(8,128)(2,1)} %pad_maximum_fusion), channel_id=1, source_target_pairs={{0,1},{1,0},{2,3},{3,2},{4,5},{5,4},{6,7},{7,6},{8,9},{9,8},{10,11... | collective-permute-start | bytes 1572872 | tf_op jit(solution)/shard_map/ppermute | solution.py:417
  67.7 7.9 %collective-permute-start.10 = (bf16[1024,128]{1,0:T(8,128)(2,1)S(1)}, bf16[1024,128]{1,0:T(8,128)(2,1)S(1)}, u32[]{:S(2)}, u32[]{:S(2)}) collective-permute-start(bf16[1024,128]{1,0:T(8,128)(2,1)S(1)} %bitcast.24), channel_id=1, source_target_pairs={{0,16},{8,24},{16,0},{24,8},{1,17},{9,25},{17,1},{25,9},{2,18},{10... | collective-permute-start | bytes 786440 | tf_op jit(solution)/shard_map/ppermute | solution.py:414
  69.7 9.1 %collective-permute-start.7 = (bf16[1280,128]{1,0:T(8,128)(2,1)S(1)}, bf16[1280,128]{1,0:T(8,128)(2,1)S(1)}, u32[]{:S(2)}, u32[]{:S(2)}) collective-permute-start(bf16[1280,128]{1,0:T(8,128)(2,1)S(1)} %get-tuple-element.71), channel_id=1, source_target_pairs={{0,8},{8,0},{16,24},{24,16},{1,9},{9,1},{17,25},{25,17},{2,10},{10... | collective-permute-start | bytes 983048 | tf_op jit(solution)/shard_map/ppermute | solution.py:414
  69.7 9.0 %collective-permute-start.8 = (bf16[1280,128]{1,0:T(8,128)(2,1)S(1)}, bf16[1280,128]{1,0:T(8,128)(2,1)S(1)}, u32[]{:S(2)}, u32[]{:S(2)}) collective-permute-start(bf16[1280,128]{1,0:T(8,128)(2,1)S(1)} %slice.16), channel_id=1, source_target_pairs={{0,8},{8,0},{16,24},{24,16},{1,9},{9,1},{17,25},{25,17},{2,10},{10... | collective-permute-start | bytes 983048 | tf_op jit(solution)/shard_map/ppermute | solution.py:414
  70.3 8.5 %collective-permute-start.9 = (bf16[1024,128]{1,0:T(8,128)(2,1)S(1)}, bf16[1024,128]{1,0:T(8,128)(2,1)S(1)}, u32[]{:S(2)}, u32[]{:S(2)}) collective-permute-start(bf16[1024,128]{1,0:T(8,128)(2,1)S(1)} %bitcast.25), channel_id=1, source_target_pairs={{0,8},{8,0},{16,24},{24,16},{1,9},{9,1},{17,25},{25,17},{2,10},{10... | collective-permute-start | bytes 786440 | tf_op jit(solution)/shard_map/ppermute | solution.py:414
  75.5 3.2 %collective-permute-start.11 = (bf16[1024,128]{1,0:T(8,128)(2,1)S(1)}, bf16[1024,128]{1,0:T(8,128)(2,1)S(1)}, u32[]{:S(2)}, u32[]{:S(2)}) collective-permute-start(bf16[1024,128]{1,0:T(8,128)(2,1)S(1)} %collective-permute-done.10.refs_10_), channel_id=1, source_target_pairs={{0,8},{8,0},{16,24},{24,16},{1,9},{9,1},{17,25},{25,17},{2,10},{10... | collective-permute-start | bytes 786440 | tf_op jit(solution)/shard_map/ppermute | solution.py:414
  81.4 2.2 %collective-permute-start.12 = (bf16[2,1024,128]{2,1,0:T(8,128)(2,1)S(1)}, bf16[2,1024,128]{2,1,0:T(8,128)(2,1)S(1)}, u32[]{:S(2)}, u32[]{:S(2)}) collective-permute-start(bf16[2,1024,128]{2,1,0:T(8,128)(2,1)S(1)} %get-tuple-element.74), channel_id=1, source_target_pairs={{0,8},{8,0},{16,24},{24,16},{1,9},{9,1},{17,25},{25,17},{2,10},{10... | collective-permute-start | bytes 1572872 | tf_op jit(solution)/shard_map/ppermute | solution.py:414
  83.6 4.4 %copy-start.1 = (bf16[2,1280,128]{2,1,0:T(8,128)(2,1)}, bf16[2,1280,128]{2,1,0:T(8,128)(2,1)S(1)}, u32[]{:S(2)}) copy-start(bf16[2,1280,128]{2,1,0:T(8,128)(2,1)S(1)} %get-tuple-element.83.even_ref) | copy-start | bytes 1966084
  83.7 10.2 %collective-permute-start.13 = (bf16[1024,128]{1,0:T(8,128)(2,1)S(1)}, bf16[1024,128]{1,0:T(8,128)(2,1)S(1)}, u32[]{:S(2)}, u32[]{:S(2)}) collective-permute-start(bf16[1024,128]{1,0:T(8,128)(2,1)S(1)} %get-tuple-element.76), channel_id=1, source_target_pairs={{0,16},{8,24},{16,0},{24,8},{1,17},{9,25},{17,1},{25,9},{2,18},{10... | collective-permute-start | bytes 786440 | tf_op jit(solution)/shard_map/ppermute | solution.py:414
  87.0 11.8 %collective-permute-start.14 = (bf16[2,1280,128]{2,1,0:T(8,128)(2,1)}, bf16[2,1280,128]{2,1,0:T(8,128)(2,1)}, u32[]{:S(2)}, u32[]{:S(2)}) collective-permute-start(bf16[2,1280,128]{2,1,0:T(8,128)(2,1)} %get-tuple-element.86), channel_id=1, source_target_pairs={{0,8},{8,0},{16,24},{24,16},{1,9},{9,1},{17,25},{25,17},{2,10},{10... | collective-permute-start | bytes 1966088 | tf_op jit(solution)/shard_map/ppermute | solution.py:414
  88.0 22.4 %copy-start = (bf16[1024,1024]{1,0:T(8,128)(2,1)S(1)}, bf16[1024,1024]{1,0:T(8,128)(2,1)}, u32[]{:S(2)}) copy-start(bf16[1024,1024]{1,0:T(8,128)(2,1)} %get-tuple-element.77.ext_ref) | copy-start | bytes 6291460
  88.0 16.5 %collective-permute-start.19 = (bf16[4,32,2176]{2,1,0:T(8,128)(2,1)}, bf16[4,32,2176]{2,1,0:T(8,128)(2,1)S(1)}, u32[]{:S(2)}, u32[]{:S(2)}) collective-permute-start(bf16[4,32,2176]{2,1,0:T(8,128)(2,1)} %get-tuple-element.115), channel_id=1, source_target_pairs={{0,1},{1,0},{2,3},{3,2},{4,5},{5,4},{6,7},{7,6},{8,9},{9,8},{10,11... | collective-permute-start | bytes 1671176 | tf_op jit(solution)/shard_map/ppermute | solution.py:417
  94.7 15.7 %all-to-all-start.2 = ((bf16[8,128,128]{2,1,0:T(8,128)(2,1)}), bf16[8,128,128]{2,1,0:T(8,128)(2,1)S(1)}, u32[]{:S(2)}, u32[]{:S(2)}) async-start(bf16[8,128,128]{2,1,0:T(8,128)(2,1)} %bitcast.35), calls=%async_computation.2 | async-start | bytes 524288 | tf_op jit(solution)/shard_map/all_to_all | solution.py:538
  98.8 1.1 copy-start.2
  101.7 0.7 copy-start.3
  102.5 11.0 %collective-permute-start.15 = (bf16[1536,128]{1,0:T(8,128)(2,1)}, bf16[1536,128]{1,0:T(8,128)(2,1)}, u32[]{:S(2)}, u32[]{:S(2)}) collective-permute-start(bf16[1536,128]{1,0:T(8,128)(2,1)} %get-tuple-element.89), channel_id=1, source_target_pairs={{0,16},{8,24},{16,0},{24,8},{1,17},{9,25},{17,1},{25,9},{2,18},{10... | collective-permute-start | bytes 1179656 | tf_op jit(solution)/shard_map/ppermute | solution.py:414
  105.4 0.7 copy-start.5
  106.0 7.4 %copy-start.4 = (bf16[1536,128]{1,0:T(8,128)(2,1)S(1)}, bf16[1536,128]{1,0:T(8,128)(2,1)}, u32[]{:S(2)}) copy-start(bf16[1536,128]{1,0:T(8,128)(2,1)} %copy-done.3) | copy-start | bytes 1179652
  106.0 16.6 %collective-permute-start.20 = (bf16[32,2176]{1,0:T(8,128)(2,1)}, bf16[32,2176]{1,0:T(8,128)(2,1)S(1)}, u32[]{:S(2)}, u32[]{:S(2)}) collective-permute-start(bf16[32,2176]{1,0:T(8,128)(2,1)} %get-tuple-element.101), channel_id=1, source_target_pairs={{0,2},{1,3},{2,0},{3,1},{4,6},{5,7},{6,4},{7,5},{8,10},{9,11},{10,... | collective-permute-start | bytes 417800 | tf_op jit(solution)/shard_map/ppermute | solution.py:417
  107.7 15.2 %collective-permute-start.21 = (bf16[32,2176]{1,0:T(8,128)(2,1)}, bf16[32,2176]{1,0:T(8,128)(2,1)}, u32[]{:S(2)}, u32[]{:S(2)}) collective-permute-start(bf16[32,2176]{1,0:T(8,128)(2,1)} %get-tuple-element.102), channel_id=1, source_target_pairs={{0,4},{1,5},{2,6},{3,7},{4,0},{5,1},{6,2},{7,3},{8,12},{9,13},{10,... | collective-permute-start | bytes 417800 | tf_op jit(solution)/shard_map/ppermute | solution.py:417
  110.1 12.9 %collective-permute-start.22 = (bf16[32,2176]{1,0:T(8,128)(2,1)}, bf16[32,2176]{1,0:T(8,128)(2,1)}, u32[]{:S(2)}, u32[]{:S(2)}) collective-permute-start(bf16[32,2176]{1,0:T(8,128)(2,1)} %get-tuple-element.103), channel_id=1, source_target_pairs={{0,6},{1,7},{2,4},{3,5},{4,2},{5,3},{6,0},{7,1},{8,14},{9,15},{10,... | collective-permute-start | bytes 417800 | tf_op jit(solution)/shard_map/ppermute | solution.py:417
  110.4 16.5 %copy-start.6 = (bf16[32,2176]{1,0:T(8,128)(2,1)S(1)}, bf16[32,2176]{1,0:T(8,128)(2,1)}, u32[]{:S(2)}) copy-start(bf16[32,2176]{1,0:T(8,128)(2,1)} %copy-done.5) | copy-start | bytes 417796
  115.4 29.1 %all-to-all-start.3 = ((bf16[8,8,32,128]{3,2,1,0:T(8,128)(2,1)}), bf16[8,8,32,128]{3,2,1,0:T(8,128)(2,1)S(1)}, u32[]{:S(2)}, u32[]{:S(2)}) async-start(bf16[8,8,32,128]{3,2,1,0:T(8,128)(2,1)} %back_pack.1), calls=%async_computation.3 | async-start | bytes 1048576 | tf_op jit(solution)/shard_map/all_to_all | solution.py:573
  121.1 1.9 %collective-permute-start.16 = (bf16[128,256]{1,0:T(8,128)(2,1)}, bf16[128,256]{1,0:T(8,128)(2,1)S(1)}, u32[]{:S(2)}, u32[]{:S(2)}) collective-permute-start(bf16[128,256]{1,0:T(8,128)(2,1)} %get-tuple-element.91), channel_id=1, source_target_pairs={{0,8},{8,0},{16,24},{24,16},{1,9},{9,1},{17,25},{25,17},{2,10},{10... | collective-permute-start | bytes 196616 | tf_op jit(solution)/shard_map/ppermute | solution.py:414
  121.1 4.9 %collective-permute-start.17 = (bf16[128,256]{1,0:T(8,128)(2,1)}, bf16[128,256]{1,0:T(8,128)(2,1)S(1)}, u32[]{:S(2)}, u32[]{:S(2)}) collective-permute-start(bf16[128,256]{1,0:T(8,128)(2,1)} %get-tuple-element.92), channel_id=1, source_target_pairs={{0,16},{8,24},{16,0},{24,8},{1,17},{9,25},{17,1},{25,9},{2,18},{10... | collective-permute-start | bytes 196616 | tf_op jit(solution)/shard_map/ppermute | solution.py:414
  122.7 4.3 %collective-permute-start.18 = (bf16[128,256]{1,0:T(8,128)(2,1)S(1)}, bf16[128,256]{1,0:T(8,128)(2,1)S(1)}, u32[]{:S(2)}, u32[]{:S(2)}) collective-permute-start(bf16[128,256]{1,0:T(8,128)(2,1)S(1)} %get-tuple-element.93), channel_id=1, source_target_pairs={{0,24},{8,16},{16,8},{24,0},{1,25},{9,17},{17,9},{25,1},{2,26},{10... | collective-permute-start | bytes 196616 | tf_op jit(solution)/shard_map/ppermute | solution.py:414
  128.0 6.0 %collective-permute-start.24 = (bf16[32,2176]{1,0:T(8,128)(2,1)S(1)}, bf16[32,2176]{1,0:T(8,128)(2,1)S(1)}, u32[]{:S(2)}, u32[]{:S(2)}) collective-permute-start(bf16[32,2176]{1,0:T(8,128)(2,1)S(1)} %w_sum.1.refs_0_), channel_id=1, source_target_pairs={{0,16},{8,24},{16,0},{24,8},{1,17},{9,25},{17,1},{25,9},{2,18},{10... | collective-permute-start | bytes 417800 | tf_op jit(solution)/shard_map/ppermute | solution.py:414
  129.4 13.3 %collective-permute-start.23 = (bf16[32,2176]{1,0:T(8,128)(2,1)S(1)}, bf16[32,2176]{1,0:T(8,128)(2,1)S(1)}, u32[]{:S(2)}, u32[]{:S(2)}) collective-permute-start(bf16[32,2176]{1,0:T(8,128)(2,1)S(1)} %w_sum.1.refs_0_), channel_id=1, source_target_pairs={{0,8},{8,0},{16,24},{24,16},{1,9},{9,1},{17,25},{25,17},{2,10},{10... | collective-permute-start | bytes 417800 | tf_op jit(solution)/shard_map/ppermute | solution.py:414
  134.0 8.7 %collective-permute-start.25 = (bf16[32,2176]{1,0:T(8,128)(2,1)S(1)}, bf16[32,2176]{1,0:T(8,128)(2,1)S(1)}, u32[]{:S(2)}, u32[]{:S(2)}) collective-permute-start(bf16[32,2176]{1,0:T(8,128)(2,1)S(1)} %collective-permute-done.24.refs_2_), channel_id=1, source_target_pairs={{0,8},{8,0},{16,24},{24,16},{1,9},{9,1},{17,25},{25,17},{2,10},{10... | collective-permute-start | bytes 417800 | tf_op jit(solution)/shard_map/ppermute | solution.py:414
  134.0 4.7 %copy-start.7 = (s32[512]{0:T(512)S(1)}, s32[512]{0:T(512)}, u32[]{:S(2)}) copy-start(s32[512]{0:T(512)} %param.12) | copy-start | bytes 6148
  134.0 4.7 %copy-start.8 = (s32[128]{0:T(128)S(1)}, s32[128]{0:T(128)}, u32[]{:S(2)}) copy-start(s32[128]{0:T(128)} %param.13) | copy-start | bytes 1540

commit v4 on v3

--- a/solution.py
+++ b/solution.py
@@ -220,10 +220,10 @@
 def grads_kernel(ny, nw, g_ref, act_even, act_odd, *refs):
     w_refs, refs = refs[:nw], refs[nw:]
     even, odd, agg = refs[:ny], refs[ny : 2 * ny], refs[2 * ny : 4 * ny]
-    back_even, back_odd, out_ref = refs[4 * ny :]
+    back_even, back_odd, *out_refs = refs[4 * ny :]
     w_self, _ = weights(w_refs)
     small, width = w_self.shape
-    sub = out_ref.shape[2]
+    sub = out_refs[0].shape[1]
     xs = []
     for k in range(2 * ny):
         j = k // 2
@@ -238,12 +238,12 @@
     high = total.astype(BF).astype(F32)
     lane = lax.broadcasted_iota(jnp.int32, (small, T), 1)
     both = jnp.where(lane == 0, high, jnp.where(lane == 1, total - high, 0.0)).astype(BF)
-    nz = out_ref.shape[1]
+    nz = out_refs[0].shape[0]
     for i in range(small // sub):
-        rows = slice(i * sub, (i + 1) * sub)
-        out_ref[i // nz, i % nz, :, :width] = own[rows]
-        out_ref[i // nz, i % nz, :, width : 2 * width] = neigh[rows]
-        out_ref[i // nz, i % nz, :, 2 * width :] = both[rows]
+        rows, out_ref = slice(i * sub, (i + 1) * sub), out_refs[i // nz]
+        out_ref[i % nz, :, :width] = own[rows]
+        out_ref[i % nz, :, width : 2 * width] = neigh[rows]
+        out_ref[i % nz, :, 2 * width :] = both[rows]
 
 
 def pair_kernel(even_ref, got_ref, *out_refs):
@@ -320,65 +320,74 @@
     return total
 
 
-def finish_rest_kernel(top, me_ref, base_ref, send_ref, hub_ref, *refs):
+def finish_rest_kernel(top, me_ref, ga_ref, own_ref, send_ref, hub_ref, *refs):
     *ret_refs, out_ref = refs
     at = (pl.program_id(0) + top) * out_ref.shape[1]
-    out_ref[...] = add_returned(base_ref[...], at, me_ref, send_ref, hub_ref, ret_refs)
-
-
-def finish_dst_kernel(me_ref, base_ref, send_ref, hub_ref, back_ref, grads_ref, *refs):
+    total = dot(ga_ref[...], own_ref[...], ((1,), (0,)))
+    out_ref[...] = add_returned(total, at, me_ref, send_ref, hub_ref, ret_refs)
+
+
+def finish_dst_kernel(me_ref, ga_ref, own_ref, send_ref, hub_ref, back_ref, grads_ref, *refs):
     *ret_refs, out_ref, act_ref = refs
-    rows = base_ref.shape[0]
+    rows = ga_ref.shape[0]
     groups = range(back_ref.shape[0])
     own = jnp.concatenate([back_ref[b, :rows] for b in groups], axis=1).astype(F32)
     act_ref[...] = jnp.concatenate([back_ref[b, rows:] for b in groups], axis=1)
     at = pl.program_id(0) * out_ref.shape[1]
-    out_ref[...] = add_returned(base_ref[...] + own, at, me_ref, send_ref, hub_ref, ret_refs)
-
-
-def finish(me, base, ret, sends, hubs, back):
-    rows, n = base.shape
-    width = 512
+    total = dot(ga_ref[...], own_ref[...], ((1,), (0,))) + own
+    out_ref[...] = add_returned(total, at, me_ref, send_ref, hub_ref, ret_refs)
+
+
+WIDE = 512
+
+
+def column(rows, first):
+    return pl.BlockSpec((rows, WIDE), lambda i: (0, i + first))
+
+
+def fixed(x):
+    return pl.BlockSpec(x.shape, lambda i: (0, 0))
+
+
+def finish_rest(me, ga, own, ret, sends, hubs, n_dst):
+    rows, n, top = ga.shape[0], own.shape[1], n_dst // WIDE
+    return pl.pallas_call(
+        functools.partial(finish_rest_kernel, top),
+        out_shape=shape(rows, n, kind=F32),
+        grid=(n // WIDE - top,),
+        in_specs=[SMEM, fixed(ga), column(n_dst, top), fixed(sends), fixed(hubs)]
+        + [fixed(r) for r in ret],
+        out_specs=column(rows, top),
+        compiler_params=pltpu.CompilerParams(vmem_limit_bytes=24 * MIB),
+        cost_estimate=pl.CostEstimate(flops=0, bytes_accessed=18000000, transcendentals=0),
+        name="finish_rest",
+    )(me, ga, own, sends, hubs, *ret)
+
+
+def finish_dst(me, ga, own, ret, sends, hubs, back, grads):
+    rows, n = grads.shape
     groups, _, piece = back.shape
     n_dst = groups * piece
-    per = width // piece
-    top = n_dst // width
-
-    def column(first):
-        return pl.BlockSpec((rows, width), lambda i: (0, i + first))
-
-    def fixed(x):
-        return pl.BlockSpec(x.shape, lambda i: (0, 0))
-
-    grads = pl.pallas_call(
-        functools.partial(finish_rest_kernel, top),
-        out_shape=shape(rows, n, kind=F32),
-        grid=(n // width - top,),
-        in_specs=[SMEM, column(top), fixed(sends), fixed(hubs)] + [fixed(r) for r in ret],
-        out_specs=column(top),
-        compiler_params=pltpu.CompilerParams(vmem_limit_bytes=24 * MIB),
-        cost_estimate=pl.CostEstimate(flops=0, bytes_accessed=15000000, transcendentals=0),
-        name="finish_rest",
-    )(me, base, sends, hubs, *ret)
     return pl.pallas_call(
         finish_dst_kernel,
         out_shape=[shape(rows, n, kind=F32), shape(rows, n_dst)],
-        grid=(top,),
+        grid=(n_dst // WIDE,),
         in_specs=[
             SMEM,
-            column(0),
+            fixed(ga),
+            column(n_dst, 0),
             fixed(sends),
             fixed(hubs),
-            pl.BlockSpec((per, 2 * rows, piece), lambda i: (i, 0, 0)),
+            pl.BlockSpec((WIDE // piece, 2 * rows, piece), lambda i: (i, 0, 0)),
             pl.BlockSpec(memory_space=pl.ANY),
         ]
         + [fixed(r) for r in ret],
-        out_specs=[column(0), column(0)],
-        input_output_aliases={5: 0},
+        out_specs=[column(rows, 0), column(rows, 0)],
+        input_output_aliases={6: 0},
         compiler_params=pltpu.CompilerParams(vmem_limit_bytes=24 * MIB),
-        cost_estimate=pl.CostEstimate(flops=0, bytes_accessed=5000000, transcendentals=0),
+        cost_estimate=pl.CostEstimate(flops=0, bytes_accessed=6000000, transcendentals=0),
         name="finish_dst",
-    )(me, base, sends, hubs, back, grads, *ret)
+    )(me, ga, own, sends, hubs, back, grads, *ret)
 
 
 def body(
@@ -426,7 +435,7 @@
         ]
     )
     w, blocks = [mine[None]], [0]
-    for bit in [1 << i for i in range(1, n_feat.bit_length() - 1)]:
+    for bit in [1 << i for i in range(n_feat.bit_length() - 2, 0, -1)]:
         send = w[0] if len(w) == 1 else jnp.concatenate(w, axis=0)
         w.append(over_feat(send, bit))
         blocks += [k ^ bit for k in blocks]
@@ -461,8 +470,9 @@
     )
 
     w[-1] = after(w[-1], agg)
+    agg = after(agg, first)
+    first = after(first, w[-1])
     w.append(over_feat(jnp.concatenate(w, axis=0), 1))
-    agg = after(agg, first)
     agg = lax.all_to_all(agg, "feat", 0, 0, tiled=True).reshape(width, piece)
 
     bias, even, odd, *cross = whole_call(
@@ -508,14 +518,15 @@
     got = over_dom(gagg_odd, 1)
     pair = whole_call(pair_kernel, "pair", 1.0, [shape(width, piece)] * ny, gagg_even, got)
 
-    back_even, back_odd, parts = whole_call(
+    back_even, back_odd, parts, parts_odd = whole_call(
         functools.partial(grads_kernel, ny, len(w)),
         "grads",
         3.0,
         [
             shape(ny, width + small, piece),
             shape(ny, width + small, piece),
-            shape(2, nz, sub, 2 * width + T),
+            shape(nz, sub, 2 * width + T),
+            shape(nz, sub, 2 * width + T),
         ],
         grad,
         act_even,
@@ -525,13 +536,13 @@
         *odds,
         *aggs,
     )
-    parts, back_odd = after((parts, back_odd), pair)
+    parts_odd, back_odd = after(parts_odd, pair), after(back_odd, pair)
 
     gagg = pair[0].astype(F32)
     for j in range(1, ny):
         gagg += over_dom(pair[j], 2 * j).astype(F32)
     gagg = gagg.astype(BF).reshape(n_feat, rows, piece)
-    from_x = over_feat(parts[1], 1)
+    from_x = over_feat(parts_odd, 1)
     from_core = over_dom(back_odd, 1)
     from_x, from_core = after(from_x, gagg), after(from_core, gagg)
 
@@ -545,8 +556,9 @@
         from_core,
     )
     back = [back[0]] + [over_dom(back[j], 2 * j) for j in range(1, ny)]
-    parts = whole_call(pair_kernel, "x_sum", 1.0, [shape(sub, 2 * width + T)] * nz, parts[0], from_x)
-    parts = [parts[0]] + [over_feat(parts[j], 2 * j) for j in range(1, nz)]
+    parts = whole_call(pair_kernel, "x_sum", 1.0, [shape(sub, 2 * width + T)] * nz, parts, from_x)
+    gagg = after(gagg, parts)
+    parts = [parts[0]] + [over_feat(parts[j], blocks[j]) for j in range(1, nz)]
 
     gagg, *halo_grad = whole_call(
         halo_grad_kernel,
@@ -556,9 +568,8 @@
         gagg,
         a_ext,
     )
-    back, parts = after(back, halo_grad), after(parts, halo_grad)
+    back = after(back, halo_grad, parts)
     returned = [halo_grad[0]] + [over_dom(halo_grad[k], k) for k in range(1, n_dom)]
-    parts = after(parts, returned)
 
     back = whole_call(
         functools.partial(back_pack_kernel, blocks),
@@ -575,8 +586,9 @@
         functools.partial(wsum_kernel, width), "w_sum", 1.0, shape(sub, 2 * width + T), *parts
     )
     whole = [total] + [over_dom(total, 2 * j) for j in range(1, ny)]
+    grads = finish_rest(me_s, gagg, a_own, returned, sends, hubs, dst_rows)
+    whole[1:] = [after(e, grads) for e in whole[1:]]
     whole = [t for e in whole for t in (e, over_dom(e, 1))]
-    base = dot(gagg, a_own, ((1,), (0,)))
     grad_self, grad_neigh, grad_bias = whole_call(
         wout_kernel,
         "w_out",
@@ -591,7 +603,9 @@
         scalars=1,
     )
 
-    grad_feats, activations = finish(me_s, base, returned, sends, hubs, back)
+    grad_feats, activations = finish_dst(
+        me_s, gagg, a_own, returned, sends, hubs, back, grads
+    )
     return (
         activations,
         grad_feats,

time: 147 us -> 143 us (0.973)
  local copies, waits for them, and re-layouts: 6.21 us -> 14.1 us
  waiting for transfers between devices: 40.6 us -> 33.8 us
  matrix products: 4.67 us -> 0 us
    ppermute x7, waiting for transfers between devices: 19.3 us -> 9.44 us  [over_feat(): return lax.ppermute(x, 'feat', [(i, i ^ k) for i in range(n_feat)])]
    unnamed x28 -> x40, local copies, waits for them, and re-layouts: 3.14 us -> 11.9 us
    all_to_all x1, waiting for transfers between devices: 0.01 us -> 5.41 us  [body(): agg = lax.all_to_all(agg, 'feat', 0, 0, tiled=True).reshape(width, piece)]
    dot_general x1 -> x0, matrix products: 4.67 us -> none  [dot(): lax.dot_general(left, right, (dims, ((), ())), preferred_element_type=F32)]
    ppermute x19, starting transfers between devices: 14.1 us -> 11.6 us  [over_dom(): return lax.ppermute(x, 'dom', [(i, i ^ k) for i in range(n_dom)])]
    ppermute x19, waiting for transfers between devices: 21.3 us -> 19 us  [over_dom(): return lax.ppermute(x, 'dom', [(i, i ^ k) for i in range(n_dom)])]
  transfers between devices with their start and end apart: 30 -> 30, of which waited for: 11 -> 11; matrix products, arithmetic and copies ran while one was open for 7% -> 3% of each run, Pallas kernels for 25% -> 25%
where the time goes in v4:
time: 143 us; the launch traced here: 142 us
  starting transfers between devices  48.4 us (34%)
  Pallas kernels  41.6 us (29%)
  waiting for transfers between devices  33.8 us (24%)
  local copies, waits for them, and re-layouts  14.1 us (10%)
  other arithmetic  2.93 us (2%)
  between operations  1.52 us (1%)
    ppermute x19, waiting for transfers between devices, over_dom(): return lax.ppermute(x, 'dom', [(i, i ^ k) for i in range(n_dom)])  19 us
    pallas_call x1, Pallas kernels, build_dense(): pl.pallas_call(functools.partial(build_kernel, n_own), out_shape=(shape(n...  18.3 us
    ppermute x7, starting transfers between devices, over_feat(): return lax.ppermute(x, 'feat', [(i, i ^ k) for i in range(n_feat)])  14.3 us
    pallas_call x10, Pallas kernels, whole_call(): pl.pallas_call(kernel, out_shape=out_shape, in_specs=[SMEM] * scalars + [...  12.5 us
    unnamed x40, local copies, waits for them, and re-layouts  11.9 us
    ppermute x19, starting transfers between devices, over_dom(): return lax.ppermute(x, 'dom', [(i, i ^ k) for i in range(n_dom)])  11.6 us
    ppermute x7, waiting for transfers between devices, over_feat(): return lax.ppermute(x, 'feat', [(i, i ^ k) for i in range(n_feat)])  9.44 us
    all_to_all x1, starting transfers between devices, body(): lax.all_to_all(back, 'feat', 0, 0, tiled=True)  6.43 us
  transfers between devices with their start and end apart: 30, of which 11 were waited for; matrix products, arithmetic and copies ran while one was open for 3% of the time, Pallas kernels for 25%

profile of v4, /device:TPU:0, one launch (start us, length us, event | category | flops | bytes accessed | tf_op | source)
XLA Modules:
  0.0 142.4 jit_solution(17750375376819914039)
XLA Ops:
  0.7 0.9 dynamic-slice_bitcast_fusion
  1.6 4.1 %collective-permute-start = (bf16[1,2,32,1024]{3,2,1,0:T(8,128)(2,1)S(1)}, bf16[1,2,32,1024]{3,2,1,0:T(8,128)(2,1)S(1)}, u32[]{:S(2)}, u32[]{:S(2)}) collective-permute-start(bf16[1,2,32,1024]{3,2,1,0:T(8,128)(2,1)S(1)} %maximum_bitcast_fusion.refs_0_), channel_id=1, source_target_pairs={{0,4},{1,5},{2,6},{3,7},{4,0},{5,1},{6,2},{7,3},{8,12},{9,13},{10,... | collective-permute-start | bytes 393224 | tf_op jit(solution)/shard_map/ppermute | solution.py:426
  5.7 3.9 %pack.1 = (bf16[8,9,32,128]{3,2,1,0:T(8,128)(2,1)}, bf16[128,256]{1,0:T(8,128)(2,1)}, bf16[128,256]{1,0:T(8,128)(2,1)}, bf16[128,256]{1,0:T(8,128)(2,1)}, bf16[128,256]{1,0:T(8,128)(2,1)}) custom-call(s32[1]{0:T(128)} %bitcast.me_ref, bf16[128,4096]{1,0:T(8,128)(2,1)} %x_ref.3, bf16[128,1024]{1,0:T(8,128)(2,1)} %cot_ref.1, f32[1,128]{1,0:T(1,128)} %bitcast.29, ...), custom_call_target="tpu_custom_call" | custom-call | bytes 12000000 | tf_op jit(solution)/shard_map/pack/pallas_call | solution.py:73
  9.6 2.4 %collective-permute-done.refs_1_ = bf16[1,2,32,1024]{3,2,1,0:T(8,128)(2,1)S(1)} collective-permute-done((bf16[1,2,32,1024]{3,2,1,0:T(8,128)(2,1)S(1)}, bf16[1,2,32,1024]{3,2,1,0:T(8,128)(2,1)S(1)}, u32[]{:S(2)}, u32[]{:S(2)}) %collective-permute-start) | collective-permute-done | bytes 131104 | tf_op jit(solution)/shard_map/ppermute | solution.py:426
  12.0 5.7 %all-to-all-start = ((bf16[8,9,32,128]{3,2,1,0:T(8,128)(2,1)}), bf16[8,9,32,128]{3,2,1,0:T(8,128)(2,1)S(1)}, u32[]{:S(2)}, u32[]{:S(2)}) async-start(bf16[8,9,32,128]{3,2,1,0:T(8,128)(2,1)} %get-tuple-element.57), calls=%async_computation | async-start | bytes 1179648 | tf_op jit(solution)/shard_map/all_to_all | solution.py:449
  17.7 1.6 %collective-permute-start.3 = (bf16[128,256]{1,0:T(8,128)(2,1)}, bf16[128,256]{1,0:T(8,128)(2,1)S(1)}, u32[]{:S(2)}, u32[]{:S(2)}) collective-permute-start(bf16[128,256]{1,0:T(8,128)(2,1)} %get-tuple-element.60), channel_id=1, source_target_pairs={{0,16},{8,24},{16,0},{24,8},{1,17},{9,25},{17,1},{25,9},{2,18},{10... | collective-permute-start | bytes 196616 | tf_op jit(solution)/shard_map/ppermute | solution.py:423
  21.4 0.8 convert_reduce_fusion.1.start_ref
  22.2 2.1 %collective-permute-start.1 = (bf16[2,2,32,1024]{3,2,1,0:T(8,128)(2,1)S(1)}, bf16[2,2,32,1024]{3,2,1,0:T(8,128)(2,1)S(1)}, u32[]{:S(2)}, u32[]{:S(2)}) collective-permute-start(bf16[2,2,32,1024]{3,2,1,0:T(8,128)(2,1)S(1)} %pad_maximum_fusion.1), channel_id=1, source_target_pairs={{0,2},{1,3},{2,0},{3,1},{4,6},{5,7},{6,4},{7,5},{8,10},{9,11},{10,... | collective-permute-start | bytes 786440 | tf_op jit(solution)/shard_map/ppermute | solution.py:426
  24.9 18.3 %build_dense.1 = (bf16[1024,4096]{1,0:T(8,128)(2,1)}, bf16[1024,1024]{1,0:T(8,128)(2,1)}, bf16[8,128,128]{2,1,0:T(8,128)(2,1)}) custom-call(s32[514]{0:T(1024)} %concatenate.10.order_ref, s32[321]{0:T(512)} %convert_reduce_fusion.1.start_ref, bf16[128,4096]{1,0:T(8,128)(2,1)} %x_ref.3, bf16[512,128,128]{2,1,0:T(8,128)(2,1)} %vals_hbm.1, ...), custom_call_target="tpu_custom_call" | custom-call | bytes 30000000 | tf_op jit(solution)/shard_map/build_dense/pallas_call | solution.py:134
  43.3 5.3 %all-to-all-start.1 = ((bf16[8,128,128]{2,1,0:T(8,128)(2,1)}), bf16[8,128,128]{2,1,0:T(8,128)(2,1)S(1)}, u32[]{:S(2)}, u32[]{:S(2)}) async-start(bf16[8,128,128]{2,1,0:T(8,128)(2,1)} %get-tuple-element.69), calls=%async_computation.1 | async-start | bytes 524288 | tf_op jit(solution)/shard_map/all_to_all | solution.py:476
  48.7 1.8 %collective-permute-start.6 = (bf16[1536,128]{1,0:T(8,128)(2,1)S(1)}, bf16[1536,128]{1,0:T(8,128)(2,1)S(1)}, u32[]{:S(2)}, u32[]{:S(2)}) collective-permute-start(bf16[1536,128]{1,0:T(8,128)(2,1)S(1)} %get-tuple-element.67), channel_id=1, source_target_pairs={{0,16},{8,24},{16,0},{24,8},{1,17},{9,25},{17,1},{25,9},{2,18},{10... | collective-permute-start | bytes 1179656 | tf_op jit(solution)/shard_map/ppermute | solution.py:423
  50.4 0.8 pad_maximum_fusion
  51.3 2.0 %collective-permute-start.5 = (bf16[4,2,32,1024]{3,2,1,0:T(8,128)(2,1)}, bf16[4,2,32,1024]{3,2,1,0:T(8,128)(2,1)S(1)}, u32[]{:S(2)}, u32[]{:S(2)}) collective-permute-start(bf16[4,2,32,1024]{3,2,1,0:T(8,128)(2,1)} %pad_maximum_fusion), channel_id=1, source_target_pairs={{0,1},{1,0},{2,3},{3,2},{4,5},{5,4},{6,7},{7,6},{8,9},{9,8},{10,11... | collective-permute-start | bytes 1572872 | tf_op jit(solution)/shard_map/ppermute | solution.py:426
  53.3 5.4 %all-to-all-done.1 = bf16[8,128,128]{2,1,0:T(8,128)(2,1)S(1)} async-done(((bf16[8,128,128]{2,1,0:T(8,128)(2,1)}), bf16[8,128,128]{2,1,0:T(8,128)(2,1)S(1)}, u32[]{:S(2)}, u32[]{:S(2)}) %all-to-all-start.1) | async-done | bytes 262176 | tf_op jit(solution)/shard_map/all_to_all | solution.py:476
  58.7 1.2 collective-permute-start.10
  59.9 0.7 collective-permute-done.6.refs_5_
  61.2 5.7 %collective-permute-done.10.refs_10_ = bf16[1024,128]{1,0:T(8,128)(2,1)S(1)} collective-permute-done((bf16[1024,128]{1,0:T(8,128)(2,1)S(1)}, bf16[1024,128]{1,0:T(8,128)(2,1)S(1)}, u32[]{:S(2)}, u32[]{:S(2)}) %collective-permute-start.10) | collective-permute-done | bytes 262176 | tf_op jit(solution)/shard_map/ppermute | solution.py:423
  67.1 1.3 collective-permute-done.11.refs_11_
  68.5 2.6 %dense.1 = (bf16[4,256,128]{2,1,0:T(8,128)(2,1)S(1)}, bf16[2,256,128]{2,1,0:T(8,128)(2,1)S(1)}, bf16[2,256,128]{2,1,0:T(8,128)(2,1)S(1)}, bf16[2,1024,128]{2,1,0:T(8,128)(2,1)S(1)}, bf16[2,1024,128]{2,1,0:T(8,128)(2,1)S(1)}) custom-call(f32[256,128]{1,0:T(8,128)S(1)} %get-tuple-element.65.bias_ref, bf16[1,2,32,1024]{3,2,1,0:T(8,128)(2,1)S(1)} %maximum_bitcast_fusion.refs_0_, ...), custom_call_target="tpu_custom_call" | custom-call | bytes 9000000 | tf_op jit(solution)/shard_map/dense/pallas_call | solution.py:28
  71.3 2.3 %grads.1 = (bf16[2,1280,128]{2,1,0:T(8,128)(2,1)S(1)}, bf16[2,1280,128]{2,1,0:T(8,128)(2,1)}, bf16[4,32,2176]{2,1,0:T(8,128)(2,1)S(1)}, bf16[4,32,2176]{2,1,0:T(8,128)(2,1)}) custom-call(bf16[4,256,128]{2,1,0:T(8,128)(2,1)S(1)} %get-tuple-element.74.g_ref, bf16[2,256,128]{2,1,0:T(8,128)(2,1)S(1)} %get-tuple-element.75.act_even, ...), custom_call_target="tpu_custom_call" | custom-call | bytes 9000000 | tf_op jit(solution)/shard_map/grads/pallas_call | solution.py:28
  73.6 0.8 copy-done.3
  75.4 1.7 %collective-permute-start.14 = (bf16[4,32,2176]{2,1,0:T(8,128)(2,1)}, bf16[4,32,2176]{2,1,0:T(8,128)(2,1)}, u32[]{:S(2)}, u32[]{:S(2)}) collective-permute-start(bf16[4,32,2176]{2,1,0:T(8,128)(2,1)} %get-tuple-element.79), channel_id=1, source_target_pairs={{0,1},{1,0},{2,3},{3,2},{4,5},{5,4},{6,7},{7,6},{8,9},{9,8},{10,11... | collective-permute-start | bytes 1671176 | tf_op jit(solution)/shard_map/ppermute | solution.py:426
  77.2 6.2 %collective-permute-done.13 = bf16[1024,128]{1,0:T(8,128)(2,1)S(1)} collective-permute-done((bf16[1024,128]{1,0:T(8,128)(2,1)S(1)}, bf16[1024,128]{1,0:T(8,128)(2,1)S(1)}, u32[]{:S(2)}, u32[]{:S(2)}) %collective-permute-start.13) | collective-permute-done | bytes 262176 | tf_op jit(solution)/shard_map/ppermute | solution.py:423
  83.3 0.8 add_convert_fusion
  84.1 5.0 %all-to-all-start.2 = ((bf16[8,128,128]{2,1,0:T(8,128)(2,1)}), bf16[8,128,128]{2,1,0:T(8,128)(2,1)S(1)}, u32[]{:S(2)}, u32[]{:S(2)}) async-start(bf16[8,128,128]{2,1,0:T(8,128)(2,1)} %bitcast.10), calls=%async_computation.2 | async-start | bytes 524288 | tf_op jit(solution)/shard_map/all_to_all | solution.py:549
  89.1 1.9 %back_pair.1 = (bf16[1536,128]{1,0:T(8,128)(2,1)S(1)}, bf16[1536,128]{1,0:T(8,128)(2,1)}) custom-call(bf16[2,1280,128]{2,1,0:T(8,128)(2,1)S(1)} %get-tuple-element.89.even_ref, bf16[2,1280,128]{2,1,0:T(8,128)(2,1)} %collective-permute-done.15.got_ref), custom_call_target="tpu_custom_call" | custom-call | bytes 3000000 | tf_op jit(solution)/shard_map/back_pair/pallas_call | solution.py:28
  91.0 0.7 copy-done.5
  91.8 1.1 collective-permute-start.16
  92.9 1.1 copy-done.4
  94.0 1.9 %x_sum.1 = (bf16[32,2176]{1,0:T(8,128)(2,1)S(1)}, bf16[32,2176]{1,0:T(8,128)(2,1)}, bf16[32,2176]{1,0:T(8,128)(2,1)}, bf16[32,2176]{1,0:T(8,128)(2,1)}) custom-call(bf16[4,32,2176]{2,1,0:T(8,128)(2,1)S(1)} %copy-done.4, bf16[4,32,2176]{2,1,0:T(8,128)(2,1)} %collective-permute-done.14.got_ref), custom_call_target="tpu_custom_call" | custom-call | bytes 3000000 | tf_op jit(solution)/shard_map/x_sum/pallas_call | solution.py:28
  95.9 0.7 copy-done.7
  96.5 2.9 %collective-permute-start.17 = (bf16[32,2176]{1,0:T(8,128)(2,1)}, bf16[32,2176]{1,0:T(8,128)(2,1)}, u32[]{:S(2)}, u32[]{:S(2)}) collective-permute-start(bf16[32,2176]{1,0:T(8,128)(2,1)} %get-tuple-element.82), channel_id=1, source_target_pairs={{0,4},{1,5},{2,6},{3,7},{4,0},{5,1},{6,2},{7,3},{8,12},{9,13},{10,... | collective-permute-start | bytes 417800 | tf_op jit(solution)/shard_map/ppermute | solution.py:426
  99.5 1.5 %collective-permute-start.18 = (bf16[32,2176]{1,0:T(8,128)(2,1)}, bf16[32,2176]{1,0:T(8,128)(2,1)}, u32[]{:S(2)}, u32[]{:S(2)}) collective-permute-start(bf16[32,2176]{1,0:T(8,128)(2,1)} %get-tuple-element.83), channel_id=1, source_target_pairs={{0,2},{1,3},{2,0},{3,1},{4,6},{5,7},{6,4},{7,5},{8,10},{9,11},{10,... | collective-permute-start | bytes 417800 | tf_op jit(solution)/shard_map/ppermute | solution.py:426
  102.7 5.4 %collective-permute-done.17.refs_1_ = bf16[32,2176]{1,0:T(8,128)(2,1)} collective-permute-done((bf16[32,2176]{1,0:T(8,128)(2,1)}, bf16[32,2176]{1,0:T(8,128)(2,1)}, u32[]{:S(2)}, u32[]{:S(2)}) %collective-permute-start.17) | collective-permute-done | bytes 139296 | tf_op jit(solution)/shard_map/ppermute | solution.py:426
  108.0 1.5 %collective-permute-done.19.refs_3_ = bf16[32,2176]{1,0:T(8,128)(2,1)} collective-permute-done((bf16[32,2176]{1,0:T(8,128)(2,1)}, bf16[32,2176]{1,0:T(8,128)(2,1)}, u32[]{:S(2)}, u32[]{:S(2)}) %collective-permute-start.19) | collective-permute-done | bytes 139296 | tf_op jit(solution)/shard_map/ppermute | solution.py:426
  109.5 0.9 back_pack.1
  110.4 6.4 %all-to-all-start.3 = ((bf16[8,8,32,128]{3,2,1,0:T(8,128)(2,1)}), bf16[8,8,32,128]{3,2,1,0:T(8,128)(2,1)S(1)}, u32[]{:S(2)}, u32[]{:S(2)}) async-start(bf16[8,8,32,128]{3,2,1,0:T(8,128)(2,1)} %back_pack.1), calls=%async_computation.3 | async-start | bytes 1048576 | tf_op jit(solution)/shard_map/all_to_all | solution.py:584
  116.9 1.1 w_sum.1.refs_0_
  118.0 1.0 collective-permute-start.24
  119.0 1.2 collective-permute-start.21
  121.2 4.0 %collective-permute-done.21.refs_2_ = bf16[128,256]{1,0:T(8,128)(2,1)S(1)} collective-permute-done((bf16[128,256]{1,0:T(8,128)(2,1)S(1)}, bf16[128,256]{1,0:T(8,128)(2,1)S(1)}, u32[]{:S(2)}, u32[]{:S(2)}) %collective-permute-start.21) | collective-permute-done | bytes 65568 | tf_op jit(solution)/shard_map/ppermute | solution.py:423
  125.2 3.4 %copy-done = bf16[1024,4096]{1,0:T(8,128)(2,1)S(1)} copy-done((bf16[1024,4096]{1,0:T(8,128)(2,1)S(1)}, bf16[1024,4096]{1,0:T(8,128)(2,1)}, u32[]{:S(2)}) %copy-start) | copy-done | bytes 8388632
  128.6 4.8 %finish_rest.1.grads_ref = f32[128,4096]{1,0:T(8,128)} custom-call(s32[1]{0:T(128)} %bitcast.me_ref, bf16[128,1024]{1,0:T(8,128)(2,1)S(1)} %get-tuple-element.87.ga_ref, bf16[1024,4096]{1,0:T(8,128)(2,1)S(1)} %copy-done, s32[4,128]{1,0:T(4,128)S(1)} %bitcast.24, s32[1,128]{1,0:T(1,128)S(1)} %bitcast.27, bf16[128,256]{1,0:T(8,128)(2,1)S(1)} %get-tuple-element.95.refs_0_, ...), custom_call_target="tpu_custom_call" | custom-call | bytes 18000000 | tf_op jit(solution)/shard_map/finish_rest/pallas_call | solution.py:354
  133.4 0.8 collective-permute-start.25
  134.2 1.0 collective-permute-done.25.refs_3_
  135.2 1.0 w_out.1
  136.9 3.4 %copy-done.1 = bf16[1024,4096]{1,0:T(8,128)(2,1)S(1)} copy-done((bf16[1024,4096]{1,0:T(8,128)(2,1)S(1)}, bf16[1024,4096]{1,0:T(8,128)(2,1)}, u32[]{:S(2)}) %copy-start.1) | copy-done | bytes 8388632
  140.3 2.1 %finish_dst.1 = (f32[128,4096]{1,0:T(8,128)}, bf16[128,1024]{1,0:T(8,128)(2,1)}) custom-call(s32[1]{0:T(128)} %bitcast.me_ref, bf16[128,1024]{1,0:T(8,128)(2,1)S(1)} %get-tuple-element.87.ga_ref, bf16[1024,4096]{1,0:T(8,128)(2,1)S(1)} %copy-done.1, s32[4,128]{1,0:T(4,128)S(1)} %bitcast.25, s32[1,128]{1,0:T(1,128)S(1)} %bitcast.28, ...), custom_call_target="tpu_custom_call", output_to_operand_aliasing={{0}: (6, {})} | custom-call | bytes 6000000 | tf_op jit(solution)/shard_map/finish_dst/pallas_call | solution.py:371
  (79 shorter events, 7.7 us)
Async XLA Ops:
  0.6 19.6 %copy-start.19 = (s32[512]{0:T(512)S(1)}, s32[512]{0:T(512)}, u32[]{:S(2)}) copy-start(s32[512]{0:T(512)} %param.14) | copy-start | bytes 6148
  0.6 19.6 %copy-start.18 = (s32[512]{0:T(512)S(1)}, s32[512]{0:T(512)}, u32[]{:S(2)}) copy-start(s32[512]{0:T(512)} %param.15) | copy-start | bytes 6148
  1.6 10.4 %collective-permute-start = (bf16[1,2,32,1024]{3,2,1,0:T(8,128)(2,1)S(1)}, bf16[1,2,32,1024]{3,2,1,0:T(8,128)(2,1)S(1)}, u32[]{:S(2)}, u32[]{:S(2)}) collective-permute-start(bf16[1,2,32,1024]{3,2,1,0:T(8,128)(2,1)S(1)} %maximum_bitcast_fusion.refs_0_), channel_id=1, source_target_pairs={{0,4},{1,5},{2,6},{3,7},{4,0},{5,1},{6,2},{7,3},{8,12},{9,13},{10,... | collective-permute-start | bytes 393224 | tf_op jit(solution)/shard_map/ppermute | solution.py:426
  12.0 31.3 %all-to-all-start = ((bf16[8,9,32,128]{3,2,1,0:T(8,128)(2,1)}), bf16[8,9,32,128]{3,2,1,0:T(8,128)(2,1)S(1)}, u32[]{:S(2)}, u32[]{:S(2)}) async-start(bf16[8,9,32,128]{3,2,1,0:T(8,128)(2,1)} %get-tuple-element.57), calls=%async_computation | async-start | bytes 1179648 | tf_op jit(solution)/shard_map/all_to_all | solution.py:449
  17.7 6.5 %collective-permute-start.2 = (bf16[128,256]{1,0:T(8,128)(2,1)}, bf16[128,256]{1,0:T(8,128)(2,1)S(1)}, u32[]{:S(2)}, u32[]{:S(2)}) collective-permute-start(bf16[128,256]{1,0:T(8,128)(2,1)} %get-tuple-element.59), channel_id=1, source_target_pairs={{0,8},{8,0},{16,24},{24,16},{1,9},{9,1},{17,25},{25,17},{2,10},{10... | collective-permute-start | bytes 196616 | tf_op jit(solution)/shard_map/ppermute | solution.py:423
  17.7 6.5 %collective-permute-start.3 = (bf16[128,256]{1,0:T(8,128)(2,1)}, bf16[128,256]{1,0:T(8,128)(2,1)S(1)}, u32[]{:S(2)}, u32[]{:S(2)}) collective-permute-start(bf16[128,256]{1,0:T(8,128)(2,1)} %get-tuple-element.60), channel_id=1, source_target_pairs={{0,16},{8,24},{16,0},{24,8},{1,17},{9,25},{17,1},{25,9},{2,18},{10... | collective-permute-start | bytes 196616 | tf_op jit(solution)/shard_map/ppermute | solution.py:423
  19.3 4.9 %collective-permute-start.4 = (bf16[128,256]{1,0:T(8,128)(2,1)}, bf16[128,256]{1,0:T(8,128)(2,1)S(1)}, u32[]{:S(2)}, u32[]{:S(2)}) collective-permute-start(bf16[128,256]{1,0:T(8,128)(2,1)} %get-tuple-element.61), channel_id=1, source_target_pairs={{0,24},{8,16},{16,8},{24,0},{1,25},{9,17},{17,9},{25,1},{2,26},{10... | collective-permute-start | bytes 196616 | tf_op jit(solution)/shard_map/ppermute | solution.py:423
  22.2 26.4 %collective-permute-start.1 = (bf16[2,2,32,1024]{3,2,1,0:T(8,128)(2,1)S(1)}, bf16[2,2,32,1024]{3,2,1,0:T(8,128)(2,1)S(1)}, u32[]{:S(2)}, u32[]{:S(2)}) collective-permute-start(bf16[2,2,32,1024]{3,2,1,0:T(8,128)(2,1)S(1)} %pad_maximum_fusion.1), channel_id=1, source_target_pairs={{0,2},{1,3},{2,0},{3,1},{4,6},{5,7},{6,4},{7,5},{8,10},{9,11},{10,... | collective-permute-start | bytes 786440 | tf_op jit(solution)/shard_map/ppermute | solution.py:426
  24.2 0.6 copy-start.15
  24.2 0.6 copy-start.16
  43.3 15.4 %all-to-all-start.1 = ((bf16[8,128,128]{2,1,0:T(8,128)(2,1)}), bf16[8,128,128]{2,1,0:T(8,128)(2,1)S(1)}, u32[]{:S(2)}, u32[]{:S(2)}) async-start(bf16[8,128,128]{2,1,0:T(8,128)(2,1)} %get-tuple-element.69), calls=%async_computation.1 | async-start | bytes 524288 | tf_op jit(solution)/shard_map/all_to_all | solution.py:476
  48.7 12.0 %collective-permute-start.6 = (bf16[1536,128]{1,0:T(8,128)(2,1)S(1)}, bf16[1536,128]{1,0:T(8,128)(2,1)S(1)}, u32[]{:S(2)}, u32[]{:S(2)}) collective-permute-start(bf16[1536,128]{1,0:T(8,128)(2,1)S(1)} %get-tuple-element.67), channel_id=1, source_target_pairs={{0,16},{8,24},{16,0},{24,8},{1,17},{9,25},{17,1},{25,9},{2,18},{10... | collective-permute-start | bytes 1179656 | tf_op jit(solution)/shard_map/ppermute | solution.py:423
  51.3 15.8 %collective-permute-start.5 = (bf16[4,2,32,1024]{3,2,1,0:T(8,128)(2,1)}, bf16[4,2,32,1024]{3,2,1,0:T(8,128)(2,1)S(1)}, u32[]{:S(2)}, u32[]{:S(2)}) collective-permute-start(bf16[4,2,32,1024]{3,2,1,0:T(8,128)(2,1)} %pad_maximum_fusion), channel_id=1, source_target_pairs={{0,1},{1,0},{2,3},{3,2},{4,5},{5,4},{6,7},{7,6},{8,9},{9,8},{10,11... | collective-permute-start | bytes 1572872 | tf_op jit(solution)/shard_map/ppermute | solution.py:426
  58.7 8.2 %collective-permute-start.10 = (bf16[1024,128]{1,0:T(8,128)(2,1)S(1)}, bf16[1024,128]{1,0:T(8,128)(2,1)S(1)}, u32[]{:S(2)}, u32[]{:S(2)}) collective-permute-start(bf16[1024,128]{1,0:T(8,128)(2,1)S(1)} %bitcast.18), channel_id=1, source_target_pairs={{0,16},{8,24},{16,0},{24,8},{1,17},{9,25},{17,1},{25,9},{2,18},{10... | collective-permute-start | bytes 786440 | tf_op jit(solution)/shard_map/ppermute | solution.py:423
  59.9 7.2 %collective-permute-start.7 = (bf16[1280,128]{1,0:T(8,128)(2,1)S(1)}, bf16[1280,128]{1,0:T(8,128)(2,1)S(1)}, u32[]{:S(2)}, u32[]{:S(2)}) collective-permute-start(bf16[1280,128]{1,0:T(8,128)(2,1)S(1)} %get-tuple-element.68), channel_id=1, source_target_pairs={{0,8},{8,0},{16,24},{24,16},{1,9},{9,1},{17,25},{25,17},{2,10},{10... | collective-permute-start | bytes 983048 | tf_op jit(solution)/shard_map/ppermute | solution.py:423
  60.7 6.5 %collective-permute-start.8 = (bf16[1280,128]{1,0:T(8,128)(2,1)S(1)}, bf16[1280,128]{1,0:T(8,128)(2,1)S(1)}, u32[]{:S(2)}, u32[]{:S(2)}) collective-permute-start(bf16[1280,128]{1,0:T(8,128)(2,1)S(1)} %slice.8), channel_id=1, source_target_pairs={{0,8},{8,0},{16,24},{24,16},{1,9},{9,1},{17,25},{25,17},{2,10},{10... | collective-permute-start | bytes 983048 | tf_op jit(solution)/shard_map/ppermute | solution.py:423
  60.7 6.4 %collective-permute-start.9 = (bf16[1024,128]{1,0:T(8,128)(2,1)S(1)}, bf16[1024,128]{1,0:T(8,128)(2,1)S(1)}, u32[]{:S(2)}, u32[]{:S(2)}) collective-permute-start(bf16[1024,128]{1,0:T(8,128)(2,1)S(1)} %bitcast.19), channel_id=1, source_target_pairs={{0,8},{8,0},{16,24},{24,16},{1,9},{9,1},{17,25},{25,17},{2,10},{10... | collective-permute-start | bytes 786440 | tf_op jit(solution)/shard_map/ppermute | solution.py:423
  66.9 1.5 %collective-permute-start.11 = (bf16[1024,128]{1,0:T(8,128)(2,1)S(1)}, bf16[1024,128]{1,0:T(8,128)(2,1)S(1)}, u32[]{:S(2)}, u32[]{:S(2)}) collective-permute-start(bf16[1024,128]{1,0:T(8,128)(2,1)S(1)} %collective-permute-done.10.refs_10_), channel_id=1, source_target_pairs={{0,8},{8,0},{16,24},{24,16},{1,9},{9,1},{17,25},{25,17},{2,10},{10... | collective-permute-start | bytes 786440 | tf_op jit(solution)/shard_map/ppermute | solution.py:423
  71.1 3.3 %collective-permute-start.12 = (bf16[2,1024,128]{2,1,0:T(8,128)(2,1)S(1)}, bf16[2,1024,128]{2,1,0:T(8,128)(2,1)S(1)}, u32[]{:S(2)}, u32[]{:S(2)}) collective-permute-start(bf16[2,1024,128]{2,1,0:T(8,128)(2,1)S(1)} %get-tuple-element.71), channel_id=1, source_target_pairs={{0,8},{8,0},{16,24},{24,16},{1,9},{9,1},{17,25},{25,17},{2,10},{10... | collective-permute-start | bytes 1572872 | tf_op jit(solution)/shard_map/ppermute | solution.py:423
  73.6 0.8 copy-start.3
  74.5 26.4 %copy-start.2 = (bf16[1024,1024]{1,0:T(8,128)(2,1)S(1)}, bf16[1024,1024]{1,0:T(8,128)(2,1)}, u32[]{:S(2)}) copy-start(bf16[1024,1024]{1,0:T(8,128)(2,1)} %get-tuple-element.86.ext_ref) | copy-start | bytes 6291460
  74.5 14.6 %collective-permute-start.15 = (bf16[2,1280,128]{2,1,0:T(8,128)(2,1)}, bf16[2,1280,128]{2,1,0:T(8,128)(2,1)}, u32[]{:S(2)}, u32[]{:S(2)}) collective-permute-start(bf16[2,1280,128]{2,1,0:T(8,128)(2,1)} %get-tuple-element.91), channel_id=1, source_target_pairs={{0,8},{8,0},{16,24},{24,16},{1,9},{9,1},{17,25},{25,17},{2,10},{10... | collective-permute-start | bytes 1966088 | tf_op jit(solution)/shard_map/ppermute | solution.py:423
  75.0 8.3 %collective-permute-start.13 = (bf16[1024,128]{1,0:T(8,128)(2,1)S(1)}, bf16[1024,128]{1,0:T(8,128)(2,1)S(1)}, u32[]{:S(2)}, u32[]{:S(2)}) collective-permute-start(bf16[1024,128]{1,0:T(8,128)(2,1)S(1)} %get-tuple-element.73), channel_id=1, source_target_pairs={{0,16},{8,24},{16,0},{24,8},{1,17},{9,25},{17,1},{25,9},{2,18},{10... | collective-permute-start | bytes 786440 | tf_op jit(solution)/shard_map/ppermute | solution.py:423
  75.4 17.5 %collective-permute-start.14 = (bf16[4,32,2176]{2,1,0:T(8,128)(2,1)}, bf16[4,32,2176]{2,1,0:T(8,128)(2,1)}, u32[]{:S(2)}, u32[]{:S(2)}) collective-permute-start(bf16[4,32,2176]{2,1,0:T(8,128)(2,1)} %get-tuple-element.79), channel_id=1, source_target_pairs={{0,1},{1,0},{2,3},{3,2},{4,5},{5,4},{6,7},{7,6},{8,9},{9,8},{10,11... | collective-permute-start | bytes 1671176 | tf_op jit(solution)/shard_map/ppermute | solution.py:426
  84.1 16.8 %all-to-all-start.2 = ((bf16[8,128,128]{2,1,0:T(8,128)(2,1)}), bf16[8,128,128]{2,1,0:T(8,128)(2,1)S(1)}, u32[]{:S(2)}, u32[]{:S(2)}) async-start(bf16[8,128,128]{2,1,0:T(8,128)(2,1)} %bitcast.10), calls=%async_computation.2 | async-start | bytes 524288 | tf_op jit(solution)/shard_map/all_to_all | solution.py:549
  91.0 0.7 copy-start.5
  91.8 17.8 %collective-permute-start.16 = (bf16[1536,128]{1,0:T(8,128)(2,1)}, bf16[1536,128]{1,0:T(8,128)(2,1)S(1)}, u32[]{:S(2)}, u32[]{:S(2)}) collective-permute-start(bf16[1536,128]{1,0:T(8,128)(2,1)} %get-tuple-element.94), channel_id=1, source_target_pairs={{0,16},{8,24},{16,0},{24,8},{1,17},{9,25},{17,1},{25,9},{2,18},{10... | collective-permute-start | bytes 1179656 | tf_op jit(solution)/shard_map/ppermute | solution.py:423
  92.9 1.1 copy-start.4
  94.0 15.6 %copy-start.6 = (bf16[1536,128]{1,0:T(8,128)(2,1)S(1)}, bf16[1536,128]{1,0:T(8,128)(2,1)}, u32[]{:S(2)}) copy-start(bf16[1536,128]{1,0:T(8,128)(2,1)} %copy-done.5) | copy-start | bytes 1179652
  95.9 0.7 copy-start.7
  96.5 11.5 %collective-permute-start.17 = (bf16[32,2176]{1,0:T(8,128)(2,1)}, bf16[32,2176]{1,0:T(8,128)(2,1)}, u32[]{:S(2)}, u32[]{:S(2)}) collective-permute-start(bf16[32,2176]{1,0:T(8,128)(2,1)} %get-tuple-element.82), channel_id=1, source_target_pairs={{0,4},{1,5},{2,6},{3,7},{4,0},{5,1},{6,2},{7,3},{8,12},{9,13},{10,... | collective-permute-start | bytes 417800 | tf_op jit(solution)/shard_map/ppermute | solution.py:426
  99.5 8.6 %collective-permute-start.18 = (bf16[32,2176]{1,0:T(8,128)(2,1)}, bf16[32,2176]{1,0:T(8,128)(2,1)}, u32[]{:S(2)}, u32[]{:S(2)}) collective-permute-start(bf16[32,2176]{1,0:T(8,128)(2,1)} %get-tuple-element.83), channel_id=1, source_target_pairs={{0,2},{1,3},{2,0},{3,1},{4,6},{5,7},{6,4},{7,5},{8,10},{9,11},{10,... | collective-permute-start | bytes 417800 | tf_op jit(solution)/shard_map/ppermute | solution.py:426
  100.9 8.6 %collective-permute-start.19 = (bf16[32,2176]{1,0:T(8,128)(2,1)}, bf16[32,2176]{1,0:T(8,128)(2,1)}, u32[]{:S(2)}, u32[]{:S(2)}) collective-permute-start(bf16[32,2176]{1,0:T(8,128)(2,1)} %get-tuple-element.84), channel_id=1, source_target_pairs={{0,6},{1,7},{2,4},{3,5},{4,2},{5,3},{6,0},{7,1},{8,14},{9,15},{10,... | collective-permute-start | bytes 417800 | tf_op jit(solution)/shard_map/ppermute | solution.py:426
  101.4 0.6 copy-start.11
  102.7 14.2 %copy-start.8 = (bf16[32,2176]{1,0:T(8,128)(2,1)S(1)}, bf16[32,2176]{1,0:T(8,128)(2,1)}, u32[]{:S(2)}) copy-start(bf16[32,2176]{1,0:T(8,128)(2,1)} %copy-done.7) | copy-start | bytes 417796
  102.7 22.6 %copy-start.9 = (s32[512]{0:T(512)S(1)}, s32[512]{0:T(512)}, u32[]{:S(2)}) copy-start(s32[512]{0:T(512)} %param.12) | copy-start | bytes 6148
  102.7 22.6 %copy-start.10 = (s32[128]{0:T(128)S(1)}, s32[128]{0:T(128)}, u32[]{:S(2)}) copy-start(s32[128]{0:T(128)} %param.13) | copy-start | bytes 1540
  108.0 10.9 %copy-start.14 = (bf16[128,256]{1,0:T(8,128)(2,1)S(1)}, bf16[128,256]{1,0:T(8,128)(2,1)}, u32[]{:S(2)}) copy-start(bf16[128,256]{1,0:T(8,128)(2,1)} %copy-done.13) | copy-start | bytes 196612
  108.0 10.9 %copy-start.12 = (bf16[128,256]{1,0:T(8,128)(2,1)S(1)}, bf16[128,256]{1,0:T(8,128)(2,1)}, u32[]{:S(2)}) copy-start(bf16[128,256]{1,0:T(8,128)(2,1)} %copy-done.11) | copy-start | bytes 196612
  110.4 26.5 %all-to-all-start.3 = ((bf16[8,8,32,128]{3,2,1,0:T(8,128)(2,1)}), bf16[8,8,32,128]{3,2,1,0:T(8,128)(2,1)S(1)}, u32[]{:S(2)}, u32[]{:S(2)}) async-start(bf16[8,8,32,128]{3,2,1,0:T(8,128)(2,1)} %back_pack.1), calls=%async_computation.3 | async-start | bytes 1048576 | tf_op jit(solution)/shard_map/all_to_all | solution.py:584
  118.0 15.4 %collective-permute-start.24 = (bf16[32,2176]{1,0:T(8,128)(2,1)S(1)}, bf16[32,2176]{1,0:T(8,128)(2,1)S(1)}, u32[]{:S(2)}, u32[]{:S(2)}) collective-permute-start(bf16[32,2176]{1,0:T(8,128)(2,1)S(1)} %w_sum.1.refs_0_), channel_id=1, source_target_pairs={{0,16},{8,24},{16,0},{24,8},{1,17},{9,25},{17,1},{25,9},{2,18},{10... | collective-permute-start | bytes 417800 | tf_op jit(solution)/shard_map/ppermute | solution.py:423
  119.0 2.2 %collective-permute-start.20 = (bf16[128,256]{1,0:T(8,128)(2,1)S(1)}, bf16[128,256]{1,0:T(8,128)(2,1)S(1)}, u32[]{:S(2)}, u32[]{:S(2)}) collective-permute-start(bf16[128,256]{1,0:T(8,128)(2,1)S(1)} %copy-done.14), channel_id=1, source_target_pairs={{0,8},{8,0},{16,24},{24,16},{1,9},{9,1},{17,25},{25,17},{2,10},{10... | collective-permute-start | bytes 196616 | tf_op jit(solution)/shard_map/ppermute | solution.py:423
  119.0 6.3 %collective-permute-start.21 = (bf16[128,256]{1,0:T(8,128)(2,1)S(1)}, bf16[128,256]{1,0:T(8,128)(2,1)S(1)}, u32[]{:S(2)}, u32[]{:S(2)}) collective-permute-start(bf16[128,256]{1,0:T(8,128)(2,1)S(1)} %copy-done.12), channel_id=1, source_target_pairs={{0,16},{8,24},{16,0},{24,8},{1,17},{9,25},{17,1},{25,9},{2,18},{10... | collective-permute-start | bytes 196616 | tf_op jit(solution)/shard_map/ppermute | solution.py:423
  120.2 5.1 %collective-permute-start.22 = (bf16[128,256]{1,0:T(8,128)(2,1)S(1)}, bf16[128,256]{1,0:T(8,128)(2,1)S(1)}, u32[]{:S(2)}, u32[]{:S(2)}) collective-permute-start(bf16[128,256]{1,0:T(8,128)(2,1)S(1)} %get-tuple-element.98), channel_id=1, source_target_pairs={{0,24},{8,16},{16,8},{24,0},{1,25},{9,17},{17,9},{25,1},{2,26},{10... | collective-permute-start | bytes 196616 | tf_op jit(solution)/shard_map/ppermute | solution.py:423
  120.8 13.4 %collective-permute-start.23 = (bf16[32,2176]{1,0:T(8,128)(2,1)S(1)}, bf16[32,2176]{1,0:T(8,128)(2,1)S(1)}, u32[]{:S(2)}, u32[]{:S(2)}) collective-permute-start(bf16[32,2176]{1,0:T(8,128)(2,1)S(1)} %w_sum.1.refs_0_), channel_id=1, source_target_pairs={{0,8},{8,0},{16,24},{24,16},{1,9},{9,1},{17,25},{25,17},{2,10},{10... | collective-permute-start | bytes 417800 | tf_op jit(solution)/shard_map/ppermute | solution.py:423
  125.2 3.4 %copy-start = (bf16[1024,4096]{1,0:T(8,128)(2,1)S(1)}, bf16[1024,4096]{1,0:T(8,128)(2,1)}, u32[]{:S(2)}) copy-start(bf16[1024,4096]{1,0:T(8,128)(2,1)} %get-tuple-element.88.own_ref) | copy-start | bytes 25165828
  133.4 1.8 %collective-permute-start.25 = (bf16[32,2176]{1,0:T(8,128)(2,1)S(1)}, bf16[32,2176]{1,0:T(8,128)(2,1)S(1)}, u32[]{:S(2)}, u32[]{:S(2)}) collective-permute-start(bf16[32,2176]{1,0:T(8,128)(2,1)S(1)} %collective-permute-done.24.refs_2_), channel_id=1, source_target_pairs={{0,8},{8,0},{16,24},{24,16},{1,9},{9,1},{17,25},{25,17},{2,10},{10... | collective-permute-start | bytes 417800 | tf_op jit(solution)/shard_map/ppermute | solution.py:423
  136.9 3.4 %copy-start.1 = (bf16[1024,4096]{1,0:T(8,128)(2,1)S(1)}, bf16[1024,4096]{1,0:T(8,128)(2,1)}, u32[]{:S(2)}) copy-start(bf16[1024,4096]{1,0:T(8,128)(2,1)} %get-tuple-element.88.own_ref) | copy-start | bytes 25165828
  (2 other events, 1.3 us)

commit v5 on v4

--- a/solution.py
+++ b/solution.py
@@ -260,21 +260,24 @@
         out_ref[width + small :] = got_ref[j, width:]
 
 
-def back_pack_kernel(blocks, me_ref, block_ref, *refs):
-    *in_refs, out_ref = refs
+def back_pack_kernel(blocks, ny, me_ref, block_ref, *refs):
+    gagg_refs, in_refs, out_ref = refs[:ny], refs[ny:-1], refs[-1]
     groups, chunks, sub, piece = out_ref.shape
-    n = chunks // 2
+    n = chunks // 3
     width = groups * n * sub
     small = groups * sub
-    total = in_refs[0][:width].astype(F32)
-    for r in in_refs[1:]:
-        total += r[:width].astype(F32)
+    total = gagg_refs[0][...].astype(F32)
+    own = in_refs[0][:width].astype(F32)
+    for j in range(1, ny):
+        total += gagg_refs[j][...].astype(F32)
+        own += in_refs[j][:width].astype(F32)
     out_ref[:, :n] = total.astype(BF).reshape(groups, n, sub, piece)
-    for k in range(2 * len(in_refs)):
+    out_ref[:, n : 2 * n] = own.astype(BF).reshape(groups, n, sub, piece)
+    for k in range(2 * ny):
         d = me_ref[0] ^ k
         for i, f in enumerate(blocks):
             at = width + (k % 2) * small + i * sub
-            out_ref[block_ref[0] ^ f, n + d] = in_refs[k // 2][at : at + sub]
+            out_ref[block_ref[0] ^ f, 2 * n + d] = in_refs[k // 2][at : at + sub]
 
 
 def wsum_kernel(width, *refs):
@@ -302,7 +305,8 @@
 
 
 def halo_grad_kernel(ga_ref, ext_ref, flat_ref, *out_refs):
-    ga = jnp.concatenate([ga_ref[b] for b in range(ga_ref.shape[0])], axis=1)
+    rows = flat_ref.shape[0]
+    ga = jnp.concatenate([ga_ref[b, :rows] for b in range(ga_ref.shape[0])], axis=1)
     flat_ref[...] = ga
     for k, out_ref in enumerate(out_refs):
         span = slice(k * 2 * T, (k + 1) * 2 * T)
@@ -320,74 +324,54 @@
     return total
 
 
-def finish_rest_kernel(top, me_ref, ga_ref, own_ref, send_ref, hub_ref, *refs):
-    *ret_refs, out_ref = refs
-    at = (pl.program_id(0) + top) * out_ref.shape[1]
+def finish_kernel(top, me_ref, ga_ref, own_ref, send_ref, hub_ref, back_ref, *refs):
+    *ret_refs, out_ref, act_ref = refs
+    step = pl.program_id(0)
+    rows, width = out_ref.shape
     total = dot(ga_ref[...], own_ref[...], ((1,), (0,)))
-    out_ref[...] = add_returned(total, at, me_ref, send_ref, hub_ref, ret_refs)
-
-
-def finish_dst_kernel(me_ref, ga_ref, own_ref, send_ref, hub_ref, back_ref, grads_ref, *refs):
-    *ret_refs, out_ref, act_ref = refs
-    rows = ga_ref.shape[0]
-    groups = range(back_ref.shape[0])
-    own = jnp.concatenate([back_ref[b, :rows] for b in groups], axis=1).astype(F32)
-    act_ref[...] = jnp.concatenate([back_ref[b, rows:] for b in groups], axis=1)
-    at = pl.program_id(0) * out_ref.shape[1]
-    total = dot(ga_ref[...], own_ref[...], ((1,), (0,))) + own
-    out_ref[...] = add_returned(total, at, me_ref, send_ref, hub_ref, ret_refs)
-
-
-WIDE = 512
-
-
-def column(rows, first):
-    return pl.BlockSpec((rows, WIDE), lambda i: (0, i + first))
-
-
-def fixed(x):
-    return pl.BlockSpec(x.shape, lambda i: (0, 0))
-
-
-def finish_rest(me, ga, own, ret, sends, hubs, n_dst):
-    rows, n, top = ga.shape[0], own.shape[1], n_dst // WIDE
+    total = add_returned(total, step * width, me_ref, send_ref, hub_ref, ret_refs)
+    out_ref[...] = total
+
+    @pl.when(step < top)
+    def _():
+        groups = range(back_ref.shape[0])
+        own = jnp.concatenate([back_ref[b, rows : 2 * rows] for b in groups], axis=1)
+        act_ref[...] = jnp.concatenate([back_ref[b, 2 * rows :] for b in groups], axis=1)
+        out_ref[...] = total + own.astype(F32)
+
+
+def finish(me, ga, own, ret, sends, hubs, back):
+    rows, n = ga.shape[0], own.shape[1]
+    groups, _, piece = back.shape
+    n_dst, wide = groups * piece, 512
+    top = n_dst // wide
+
+    def fixed(x):
+        return pl.BlockSpec(x.shape, lambda i: (0, 0))
+
     return pl.pallas_call(
-        functools.partial(finish_rest_kernel, top),
-        out_shape=shape(rows, n, kind=F32),
-        grid=(n // WIDE - top,),
-        in_specs=[SMEM, fixed(ga), column(n_dst, top), fixed(sends), fixed(hubs)]
-        + [fixed(r) for r in ret],
-        out_specs=column(rows, top),
-        compiler_params=pltpu.CompilerParams(vmem_limit_bytes=24 * MIB),
-        cost_estimate=pl.CostEstimate(flops=0, bytes_accessed=18000000, transcendentals=0),
-        name="finish_rest",
-    )(me, ga, own, sends, hubs, *ret)
-
-
-def finish_dst(me, ga, own, ret, sends, hubs, back, grads):
-    rows, n = grads.shape
-    groups, _, piece = back.shape
-    n_dst = groups * piece
-    return pl.pallas_call(
-        finish_dst_kernel,
+        functools.partial(finish_kernel, top),
         out_shape=[shape(rows, n, kind=F32), shape(rows, n_dst)],
-        grid=(n_dst // WIDE,),
+        grid=(n // wide,),
         in_specs=[
             SMEM,
             fixed(ga),
-            column(n_dst, 0),
+            pl.BlockSpec((n_dst, wide), lambda i: (0, i)),
             fixed(sends),
             fixed(hubs),
-            pl.BlockSpec((WIDE // piece, 2 * rows, piece), lambda i: (i, 0, 0)),
-            pl.BlockSpec(memory_space=pl.ANY),
+            pl.BlockSpec(
+                (wide // piece, 3 * rows, piece), lambda i: (jnp.minimum(i, top - 1), 0, 0)
+            ),
         ]
         + [fixed(r) for r in ret],
-        out_specs=[column(rows, 0), column(rows, 0)],
-        input_output_aliases={6: 0},
-        compiler_params=pltpu.CompilerParams(vmem_limit_bytes=24 * MIB),
-        cost_estimate=pl.CostEstimate(flops=0, bytes_accessed=6000000, transcendentals=0),
-        name="finish_dst",
-    )(me, ga, own, sends, hubs, back, grads, *ret)
+        out_specs=[
+            pl.BlockSpec((rows, wide), lambda i: (0, i)),
+            pl.BlockSpec((rows, wide), lambda i: (0, jnp.minimum(i, top - 1))),
+        ],
+        compiler_params=pltpu.CompilerParams(vmem_limit_bytes=56 * MIB),
+        cost_estimate=pl.CostEstimate(flops=0, bytes_accessed=24000000, transcendentals=0),
+        name="finish",
+    )(me, ga, own, sends, hubs, back, *ret)
 
 
 def body(
@@ -538,26 +522,32 @@
     )
     parts_odd, back_odd = after(parts_odd, pair), after(back_odd, pair)
 
-    gagg = pair[0].astype(F32)
-    for j in range(1, ny):
-        gagg += over_dom(pair[j], 2 * j).astype(F32)
-    gagg = gagg.astype(BF).reshape(n_feat, rows, piece)
-    from_x = over_feat(parts_odd, 1)
-    from_core = over_dom(back_odd, 1)
-    from_x, from_core = after(from_x, gagg), after(from_core, gagg)
-
-    gagg = lax.all_to_all(gagg, "feat", 0, 0, tiled=True)
+    gaggs = [pair[0]] + [over_dom(pair[j], 2 * j) for j in range(1, ny)]
     back = whole_call(
         functools.partial(back_pair_kernel, width),
         "back_pair",
         1.0,
         [shape(width + 2 * small, piece)] * ny,
         back_even,
-        from_core,
-    )
+        over_dom(back_odd, 1),
+    )
+    back = [back[0]] + [after(b, gaggs) for b in back[1:]]
     back = [back[0]] + [over_dom(back[j], 2 * j) for j in range(1, ny)]
+    from_x = over_feat(parts_odd, 1)
     parts = whole_call(pair_kernel, "x_sum", 1.0, [shape(sub, 2 * width + T)] * nz, parts, from_x)
-    gagg = after(gagg, parts)
+    back[1:] = [after(b, parts) for b in back[1:]]
+    back = whole_call(
+        functools.partial(back_pack_kernel, blocks, ny),
+        "back_pack",
+        1.5,
+        shape(n_feat, 3 * n_dom, sub, piece),
+        me_s,
+        block_s,
+        *gaggs,
+        *back,
+        scalars=2,
+    )
+    back = lax.all_to_all(back, "feat", 0, 0, tiled=True).reshape(n_feat, 3 * rows, piece)
     parts = [parts[0]] + [over_feat(parts[j], blocks[j]) for j in range(1, nz)]
 
     gagg, *halo_grad = whole_call(
@@ -565,29 +555,19 @@
         "halo_grads",
         1.0,
         [shape(rows, dst_rows)] + [shape(rows, 2 * T)] * n_dom,
-        gagg,
+        back,
         a_ext,
     )
-    back = after(back, halo_grad, parts)
+    halo_grad = after(halo_grad, parts)
     returned = [halo_grad[0]] + [over_dom(halo_grad[k], k) for k in range(1, n_dom)]
 
-    back = whole_call(
-        functools.partial(back_pack_kernel, blocks),
-        "back_pack",
-        1.0,
-        shape(n_feat, 2 * n_dom, sub, piece),
-        me_s,
-        block_s,
-        *back,
-        scalars=2,
-    )
-    back = lax.all_to_all(back, "feat", 0, 0, tiled=True).reshape(n_feat, 2 * rows, piece)
     total = whole_call(
         functools.partial(wsum_kernel, width), "w_sum", 1.0, shape(sub, 2 * width + T), *parts
     )
     whole = [total] + [over_dom(total, 2 * j) for j in range(1, ny)]
-    grads = finish_rest(me_s, gagg, a_own, returned, sends, hubs, dst_rows)
-    whole[1:] = [after(e, grads) for e in whole[1:]]
+    gagg = after(gagg, total)
+    grad_feats, activations = finish(me_s, gagg, a_own, returned, sends, hubs, back)
+    whole[1:] = [after(e, grad_feats) for e in whole[1:]]
     whole = [t for e in whole for t in (e, over_dom(e, 1))]
     grad_self, grad_neigh, grad_bias = whole_call(
         wout_kernel,
@@ -603,9 +583,6 @@
         scalars=1,
     )
 
-    grad_feats, activations = finish_dst(
-        me_s, gagg, a_own, returned, sends, hubs, back, grads
-    )
     return (
         activations,
         grad_feats,

time: 143 us -> 151 us (1.056)
  waiting for transfers between devices: 33.8 us -> 59.6 us
  local copies, waits for them, and re-layouts: 14.1 us -> 4.78 us
  starting transfers between devices: 48.4 us -> 42.2 us
  Pallas kernels: 41.6 us -> 38.8 us
    ppermute x7, waiting for transfers between devices: 9.44 us -> 34 us  [over_feat(): return lax.ppermute(x, 'feat', [(i, i ^ k) for i in range(n_feat)])]
    unnamed x40 -> x20, local copies, waits for them, and re-layouts: 11.9 us -> 2.58 us
    pallas_call x10, Pallas kernels: 12.5 us -> 7.08 us  [whole_call(): pl.pallas_call(kernel, out_shape=out_shape, in_specs=[SMEM] * scalars + [...]
    all_to_all x1 -> x0, starting transfers between devices: 5.03 us -> none  [body(): gagg = lax.all_to_all(gagg, 'feat', 0, 0, tiled=True)]
    pallas_call x2 -> x1, Pallas kernels: 6.9 us -> 9.52 us  [finish(): pl.pallas_call(functools.partial(finish_kernel, top), out_shape=[shape(ro...]
    ppermute x19, waiting for transfers between devices: 19 us -> 21.1 us  [over_dom(): return lax.ppermute(x, 'dom', [(i, i ^ k) for i in range(n_dom)])]
  transfers between devices with their start and end apart: 30 -> 29, of which waited for: 11 -> 14; matrix products, arithmetic and copies ran while one was open for 3% -> 2% of each run, Pallas kernels for 25% -> 23%
where the time goes in v5:
time: 151 us; the launch traced here: 150 us
  waiting for transfers between devices  59.6 us (39%)
  starting transfers between devices  42.2 us (28%)
  Pallas kernels  38.8 us (26%)
  local copies, waits for them, and re-layouts  4.78 us (3%)
  other arithmetic  2.85 us (2%)
    ppermute x7, waiting for transfers between devices, over_feat(): return lax.ppermute(x, 'feat', [(i, i ^ k) for i in range(n_feat)])  34 us
    ppermute x19, waiting for transfers between devices, over_dom(): return lax.ppermute(x, 'dom', [(i, i ^ k) for i in range(n_dom)])  21.1 us
    pallas_call x1, Pallas kernels, build_dense(): pl.pallas_call(functools.partial(build_kernel, n_own), out_shape=(shape(n...  18.2 us
    ppermute x7, starting transfers between devices, over_feat(): return lax.ppermute(x, 'feat', [(i, i ^ k) for i in range(n_feat)])  14.3 us
    ppermute x19, starting transfers between devices, over_dom(): return lax.ppermute(x, 'dom', [(i, i ^ k) for i in range(n_dom)])  12.2 us
    pallas_call x1, Pallas kernels, finish(): pl.pallas_call(functools.partial(finish_kernel, top), out_shape=[shape(ro...  9.52 us
    pallas_call x10, Pallas kernels, whole_call(): pl.pallas_call(kernel, out_shape=out_shape, in_specs=[SMEM] * scalars + [...  7.08 us
    all_to_all x1, starting transfers between devices, body(): first = lax.all_to_all(first, 'feat', 0, 0, tiled=True)  5.74 us
  transfers between devices with their start and end apart: 29, of which 14 were waited for; matrix products, arithmetic and copies ran while one was open for 2% of the time, Pallas kernels for 23%

profile of v5, /device:TPU:0, one launch (start us, length us, event | category | flops | bytes accessed | tf_op | source)
XLA Modules:
  0.0 149.7 jit_solution(6388041026012852883)
XLA Ops:
  0.6 0.9 dynamic-slice_bitcast_fusion
  1.5 4.1 %collective-permute-start = (bf16[1,2,32,1024]{3,2,1,0:T(8,128)(2,1)S(1)}, bf16[1,2,32,1024]{3,2,1,0:T(8,128)(2,1)S(1)}, u32[]{:S(2)}, u32[]{:S(2)}) collective-permute-start(bf16[1,2,32,1024]{3,2,1,0:T(8,128)(2,1)S(1)} %maximum_bitcast_fusion.refs_0_), channel_id=1, source_target_pairs={{0,4},{1,5},{2,6},{3,7},{4,0},{5,1},{6,2},{7,3},{8,12},{9,13},{10,... | collective-permute-start | bytes 393224 | tf_op jit(solution)/shard_map/ppermute | solution.py:410
  5.7 3.9 %pack.1 = (bf16[8,9,32,128]{3,2,1,0:T(8,128)(2,1)}, bf16[128,256]{1,0:T(8,128)(2,1)}, bf16[128,256]{1,0:T(8,128)(2,1)}, bf16[128,256]{1,0:T(8,128)(2,1)}, bf16[128,256]{1,0:T(8,128)(2,1)}) custom-call(s32[1]{0:T(128)} %bitcast.me_ref, bf16[128,4096]{1,0:T(8,128)(2,1)} %x_ref.3, bf16[128,1024]{1,0:T(8,128)(2,1)} %cot_ref.1, f32[1,128]{1,0:T(1,128)} %bitcast.27, ...), custom_call_target="tpu_custom_call" | custom-call | bytes 12000000 | tf_op jit(solution)/shard_map/pack/pallas_call | solution.py:73
  9.6 2.4 %collective-permute-done.refs_1_ = bf16[1,2,32,1024]{3,2,1,0:T(8,128)(2,1)S(1)} collective-permute-done((bf16[1,2,32,1024]{3,2,1,0:T(8,128)(2,1)S(1)}, bf16[1,2,32,1024]{3,2,1,0:T(8,128)(2,1)S(1)}, u32[]{:S(2)}, u32[]{:S(2)}) %collective-permute-start) | collective-permute-done | bytes 131104 | tf_op jit(solution)/shard_map/ppermute | solution.py:410
  12.0 5.7 %all-to-all-start = ((bf16[8,9,32,128]{3,2,1,0:T(8,128)(2,1)}), bf16[8,9,32,128]{3,2,1,0:T(8,128)(2,1)S(1)}, u32[]{:S(2)}, u32[]{:S(2)}) async-start(bf16[8,9,32,128]{3,2,1,0:T(8,128)(2,1)} %get-tuple-element.59), calls=%async_computation | async-start | bytes 1179648 | tf_op jit(solution)/shard_map/all_to_all | solution.py:433
  17.7 1.6 %collective-permute-start.3 = (bf16[128,256]{1,0:T(8,128)(2,1)}, bf16[128,256]{1,0:T(8,128)(2,1)S(1)}, u32[]{:S(2)}, u32[]{:S(2)}) collective-permute-start(bf16[128,256]{1,0:T(8,128)(2,1)} %get-tuple-element.62), channel_id=1, source_target_pairs={{0,16},{8,24},{16,0},{24,8},{1,17},{9,25},{17,1},{25,9},{2,18},{10... | collective-permute-start | bytes 196616 | tf_op jit(solution)/shard_map/ppermute | solution.py:407
  20.2 0.7 fusion.3
  21.4 0.6 concatenate.10.order_ref
  22.0 0.7 convert_reduce_fusion.1.start_ref
  22.8 2.1 %collective-permute-start.1 = (bf16[2,2,32,1024]{3,2,1,0:T(8,128)(2,1)S(1)}, bf16[2,2,32,1024]{3,2,1,0:T(8,128)(2,1)S(1)}, u32[]{:S(2)}, u32[]{:S(2)}) collective-permute-start(bf16[2,2,32,1024]{3,2,1,0:T(8,128)(2,1)S(1)} %pad_maximum_fusion.1), channel_id=1, source_target_pairs={{0,2},{1,3},{2,0},{3,1},{4,6},{5,7},{6,4},{7,5},{8,10},{9,11},{10,... | collective-permute-start | bytes 786440 | tf_op jit(solution)/shard_map/ppermute | solution.py:410
  24.9 0.6 copy-done.4
  25.6 18.2 %build_dense.1 = (bf16[1024,4096]{1,0:T(8,128)(2,1)}, bf16[1024,1024]{1,0:T(8,128)(2,1)}, bf16[8,128,128]{2,1,0:T(8,128)(2,1)}) custom-call(s32[514]{0:T(1024)} %concatenate.10.order_ref, s32[321]{0:T(512)} %convert_reduce_fusion.1.start_ref, bf16[128,4096]{1,0:T(8,128)(2,1)} %x_ref.3, bf16[512,128,128]{2,1,0:T(8,128)(2,1)} %vals_hbm.1, ...), custom_call_target="tpu_custom_call" | custom-call | bytes 30000000 | tf_op jit(solution)/shard_map/build_dense/pallas_call | solution.py:134
  43.8 4.6 %all-to-all-start.1 = ((bf16[8,128,128]{2,1,0:T(8,128)(2,1)}), bf16[8,128,128]{2,1,0:T(8,128)(2,1)S(1)}, u32[]{:S(2)}, u32[]{:S(2)}) async-start(bf16[8,128,128]{2,1,0:T(8,128)(2,1)} %get-tuple-element.71), calls=%async_computation.1 | async-start | bytes 524288 | tf_op jit(solution)/shard_map/all_to_all | solution.py:460
  48.5 2.4 %collective-permute-start.6 = (bf16[1536,128]{1,0:T(8,128)(2,1)S(1)}, bf16[1536,128]{1,0:T(8,128)(2,1)S(1)}, u32[]{:S(2)}, u32[]{:S(2)}) collective-permute-start(bf16[1536,128]{1,0:T(8,128)(2,1)S(1)} %get-tuple-element.69), channel_id=1, source_target_pairs={{0,16},{8,24},{16,0},{24,8},{1,17},{9,25},{17,1},{25,9},{2,18},{10... | collective-permute-start | bytes 1179656 | tf_op jit(solution)/shard_map/ppermute | solution.py:407
  50.9 0.8 pad_maximum_fusion
  51.8 2.0 %collective-permute-start.5 = (bf16[4,2,32,1024]{3,2,1,0:T(8,128)(2,1)}, bf16[4,2,32,1024]{3,2,1,0:T(8,128)(2,1)S(1)}, u32[]{:S(2)}, u32[]{:S(2)}) collective-permute-start(bf16[4,2,32,1024]{3,2,1,0:T(8,128)(2,1)} %pad_maximum_fusion), channel_id=1, source_target_pairs={{0,1},{1,0},{2,3},{3,2},{4,5},{5,4},{6,7},{7,6},{8,9},{9,8},{10,11... | collective-permute-start | bytes 1572872 | tf_op jit(solution)/shard_map/ppermute | solution.py:410
  53.8 4.5 %all-to-all-done.1 = bf16[8,128,128]{2,1,0:T(8,128)(2,1)S(1)} async-done(((bf16[8,128,128]{2,1,0:T(8,128)(2,1)}), bf16[8,128,128]{2,1,0:T(8,128)(2,1)S(1)}, u32[]{:S(2)}, u32[]{:S(2)}) %all-to-all-start.1) | async-done | bytes 262176 | tf_op jit(solution)/shard_map/all_to_all | solution.py:460
  58.3 1.3 collective-permute-start.10
  59.6 0.5 collective-permute-done.6.refs_5_
  60.2 0.5 collective-permute-start.9
  60.7 5.4 %collective-permute-done.10.refs_10_ = bf16[1024,128]{1,0:T(8,128)(2,1)S(1)} collective-permute-done((bf16[1024,128]{1,0:T(8,128)(2,1)S(1)}, bf16[1024,128]{1,0:T(8,128)(2,1)S(1)}, u32[]{:S(2)}, u32[]{:S(2)}) %collective-permute-start.10) | collective-permute-done | bytes 262176 | tf_op jit(solution)/shard_map/ppermute | solution.py:407
  66.1 0.5 collective-permute-done.5.refs_3_
  66.5 1.1 collective-permute-done.11.refs_11_
  67.6 2.6 %dense.1 = (bf16[4,256,128]{2,1,0:T(8,128)(2,1)S(1)}, bf16[2,256,128]{2,1,0:T(8,128)(2,1)S(1)}, bf16[2,256,128]{2,1,0:T(8,128)(2,1)S(1)}, bf16[2,1024,128]{2,1,0:T(8,128)(2,1)S(1)}, bf16[2,1024,128]{2,1,0:T(8,128)(2,1)S(1)}) custom-call(f32[256,128]{1,0:T(8,128)S(1)} %get-tuple-element.67.bias_ref, bf16[1,2,32,1024]{3,2,1,0:T(8,128)(2,1)S(1)} %maximum_bitcast_fusion.refs_0_, ...), custom_call_target="tpu_custom_call" | custom-call | bytes 9000000 | tf_op jit(solution)/shard_map/dense/pallas_call | solution.py:28
  70.4 1.3 grads.1
  72.5 1.0 collective-permute-start.13
  73.5 1.7 %collective-permute-start.16 = (bf16[4,32,2176]{2,1,0:T(8,128)(2,1)S(1)}, bf16[4,32,2176]{2,1,0:T(8,128)(2,1)S(1)}, u32[]{:S(2)}, u32[]{:S(2)}) collective-permute-start(bf16[4,32,2176]{2,1,0:T(8,128)(2,1)S(1)} %get-tuple-element.87), channel_id=1, source_target_pairs={{0,1},{1,0},{2,3},{3,2},{4,5},{5,4},{6,7},{7,6},{8,9},{9,8},{10,11... | collective-permute-start | bytes 1671176 | tf_op jit(solution)/shard_map/ppermute | solution.py:410
  75.4 5.8 %collective-permute-done.13.refs_1_ = bf16[1024,128]{1,0:T(8,128)(2,1)S(1)} collective-permute-done((bf16[1024,128]{1,0:T(8,128)(2,1)S(1)}, bf16[1024,128]{1,0:T(8,128)(2,1)S(1)}, u32[]{:S(2)}, u32[]{:S(2)}) %collective-permute-start.13) | collective-permute-done | bytes 262176 | tf_op jit(solution)/shard_map/ppermute | solution.py:407
  81.1 0.9 collective-permute-start.15
  82.1 6.0 %collective-permute-done.16.got_ref = bf16[4,32,2176]{2,1,0:T(8,128)(2,1)S(1)} collective-permute-done((bf16[4,32,2176]{2,1,0:T(8,128)(2,1)S(1)}, bf16[4,32,2176]{2,1,0:T(8,128)(2,1)S(1)}, u32[]{:S(2)}, u32[]{:S(2)}) %collective-permute-start.16) | collective-permute-done | bytes 557088 | tf_op jit(solution)/shard_map/ppermute | solution.py:410
  88.3 3.5 %collective-permute-done.15.refs_3_ = bf16[1536,128]{1,0:T(8,128)(2,1)S(1)} collective-permute-done((bf16[1536,128]{1,0:T(8,128)(2,1)S(1)}, bf16[1536,128]{1,0:T(8,128)(2,1)S(1)}, u32[]{:S(2)}, u32[]{:S(2)}) %collective-permute-start.15) | collective-permute-done | bytes 393248 | tf_op jit(solution)/shard_map/ppermute | solution.py:407
  91.7 1.1 back_pack.1
  92.8 5.4 %all-to-all-start.2 = ((bf16[8,12,32,128]{3,2,1,0:T(8,128)(2,1)}), bf16[8,12,32,128]{3,2,1,0:T(8,128)(2,1)S(1)}, u32[]{:S(2)}, u32[]{:S(2)}) async-start(bf16[8,12,32,128]{3,2,1,0:T(8,128)(2,1)} %back_pack.1), calls=%async_computation.2 | async-start | bytes 1572864 | tf_op jit(solution)/shard_map/all_to_all | solution.py:550
  98.1 2.9 %collective-permute-start.17 = (bf16[32,2176]{1,0:T(8,128)(2,1)S(1)}, bf16[32,2176]{1,0:T(8,128)(2,1)S(1)}, u32[]{:S(2)}, u32[]{:S(2)}) collective-permute-start(bf16[32,2176]{1,0:T(8,128)(2,1)S(1)} %get-tuple-element.89), channel_id=1, source_target_pairs={{0,4},{1,5},{2,6},{3,7},{4,0},{5,1},{6,2},{7,3},{8,12},{9,13},{10,... | collective-permute-start | bytes 417800 | tf_op jit(solution)/shard_map/ppermute | solution.py:410
  101.1 1.5 collective-permute-start.18
  102.6 25.1 %collective-permute-done.17.refs_1_ = bf16[32,2176]{1,0:T(8,128)(2,1)S(1)} collective-permute-done((bf16[32,2176]{1,0:T(8,128)(2,1)S(1)}, bf16[32,2176]{1,0:T(8,128)(2,1)S(1)}, u32[]{:S(2)}, u32[]{:S(2)}) %collective-permute-start.17) | collective-permute-done | bytes 139296 | tf_op jit(solution)/shard_map/ppermute | solution.py:410
  127.8 1.4 collective-permute-start.24
  129.6 0.7 copy-done.2
  130.3 0.6 copy-done.3
  130.9 0.7 collective-permute-start.21
  131.6 1.1 collective-permute-start.22
  133.1 2.7 %collective-permute-done.21.refs_2_ = bf16[128,256]{1,0:T(8,128)(2,1)S(1)} collective-permute-done((bf16[128,256]{1,0:T(8,128)(2,1)S(1)}, bf16[128,256]{1,0:T(8,128)(2,1)S(1)}, u32[]{:S(2)}, u32[]{:S(2)}) %collective-permute-start.21) | collective-permute-done | bytes 65568 | tf_op jit(solution)/shard_map/ppermute | solution.py:407
  135.8 0.6 collective-permute-done.22.refs_3_
  136.5 0.6 copy-done.9
  137.1 9.5 %finish.1 = (f32[128,4096]{1,0:T(8,128)}, bf16[128,1024]{1,0:T(8,128)(2,1)}) custom-call(s32[1]{0:T(128)} %bitcast.me_ref, bf16[128,1024]{1,0:T(8,128)(2,1)} %copy-done.2, bf16[1024,4096]{1,0:T(8,128)(2,1)} %get-tuple-element.96.own_ref, s32[4,128]{1,0:T(4,128)} %bitcast.24, s32[1,128]{1,0:T(1,128)} %bitcast.26, bf16[8,384,128]{2,1,0:T(8,128)(2,1)} %bitcast.18, ...), custom_call_target="tpu_custom_call" | custom-call | bytes 24000000 | tf_op jit(solution)/shard_map/finish/pallas_call | solution.py:352
  146.9 1.1 collective-permute-done.25.refs_3_
  148.0 1.0 w_out.1
  149.1 0.6 reshape_squeeze.3
  (55 shorter events, 3.7 us)
Async XLA Ops:
  1.5 10.4 %collective-permute-start = (bf16[1,2,32,1024]{3,2,1,0:T(8,128)(2,1)S(1)}, bf16[1,2,32,1024]{3,2,1,0:T(8,128)(2,1)S(1)}, u32[]{:S(2)}, u32[]{:S(2)}) collective-permute-start(bf16[1,2,32,1024]{3,2,1,0:T(8,128)(2,1)S(1)} %maximum_bitcast_fusion.refs_0_), channel_id=1, source_target_pairs={{0,4},{1,5},{2,6},{3,7},{4,0},{5,1},{6,2},{7,3},{8,12},{9,13},{10,... | collective-permute-start | bytes 393224 | tf_op jit(solution)/shard_map/ppermute | solution.py:410
  12.0 31.8 %all-to-all-start = ((bf16[8,9,32,128]{3,2,1,0:T(8,128)(2,1)}), bf16[8,9,32,128]{3,2,1,0:T(8,128)(2,1)S(1)}, u32[]{:S(2)}, u32[]{:S(2)}) async-start(bf16[8,9,32,128]{3,2,1,0:T(8,128)(2,1)} %get-tuple-element.59), calls=%async_computation | async-start | bytes 1179648 | tf_op jit(solution)/shard_map/all_to_all | solution.py:433
  17.7 7.2 %collective-permute-start.2 = (bf16[128,256]{1,0:T(8,128)(2,1)}, bf16[128,256]{1,0:T(8,128)(2,1)S(1)}, u32[]{:S(2)}, u32[]{:S(2)}) collective-permute-start(bf16[128,256]{1,0:T(8,128)(2,1)} %get-tuple-element.61), channel_id=1, source_target_pairs={{0,8},{8,0},{16,24},{24,16},{1,9},{9,1},{17,25},{25,17},{2,10},{10... | collective-permute-start | bytes 196616 | tf_op jit(solution)/shard_map/ppermute | solution.py:407
  17.7 7.2 %collective-permute-start.3 = (bf16[128,256]{1,0:T(8,128)(2,1)}, bf16[128,256]{1,0:T(8,128)(2,1)S(1)}, u32[]{:S(2)}, u32[]{:S(2)}) collective-permute-start(bf16[128,256]{1,0:T(8,128)(2,1)} %get-tuple-element.62), channel_id=1, source_target_pairs={{0,16},{8,24},{16,0},{24,8},{1,17},{9,25},{17,1},{25,9},{2,18},{10... | collective-permute-start | bytes 196616 | tf_op jit(solution)/shard_map/ppermute | solution.py:407
  19.3 5.6 %collective-permute-start.4 = (bf16[128,256]{1,0:T(8,128)(2,1)}, bf16[128,256]{1,0:T(8,128)(2,1)S(1)}, u32[]{:S(2)}, u32[]{:S(2)}) collective-permute-start(bf16[128,256]{1,0:T(8,128)(2,1)} %get-tuple-element.63), channel_id=1, source_target_pairs={{0,24},{8,16},{16,8},{24,0},{1,25},{9,17},{17,9},{25,1},{2,26},{10... | collective-permute-start | bytes 196616 | tf_op jit(solution)/shard_map/ppermute | solution.py:407
  22.8 25.6 %collective-permute-start.1 = (bf16[2,2,32,1024]{3,2,1,0:T(8,128)(2,1)S(1)}, bf16[2,2,32,1024]{3,2,1,0:T(8,128)(2,1)S(1)}, u32[]{:S(2)}, u32[]{:S(2)}) collective-permute-start(bf16[2,2,32,1024]{3,2,1,0:T(8,128)(2,1)S(1)} %pad_maximum_fusion.1), channel_id=1, source_target_pairs={{0,2},{1,3},{2,0},{3,1},{4,6},{5,7},{6,4},{7,5},{8,10},{9,11},{10,... | collective-permute-start | bytes 786440 | tf_op jit(solution)/shard_map/ppermute | solution.py:410
  24.9 0.6 copy-start.4
  24.9 0.6 copy-start.5
  24.9 0.6 copy-start.6
  43.8 14.5 %all-to-all-start.1 = ((bf16[8,128,128]{2,1,0:T(8,128)(2,1)}), bf16[8,128,128]{2,1,0:T(8,128)(2,1)S(1)}, u32[]{:S(2)}, u32[]{:S(2)}) async-start(bf16[8,128,128]{2,1,0:T(8,128)(2,1)} %get-tuple-element.71), calls=%async_computation.1 | async-start | bytes 524288 | tf_op jit(solution)/shard_map/all_to_all | solution.py:460
  48.5 11.6 %collective-permute-start.6 = (bf16[1536,128]{1,0:T(8,128)(2,1)S(1)}, bf16[1536,128]{1,0:T(8,128)(2,1)S(1)}, u32[]{:S(2)}, u32[]{:S(2)}) collective-permute-start(bf16[1536,128]{1,0:T(8,128)(2,1)S(1)} %get-tuple-element.69), channel_id=1, source_target_pairs={{0,16},{8,24},{16,0},{24,8},{1,17},{9,25},{17,1},{25,9},{2,18},{10... | collective-permute-start | bytes 1179656 | tf_op jit(solution)/shard_map/ppermute | solution.py:407
  51.8 14.8 %collective-permute-start.5 = (bf16[4,2,32,1024]{3,2,1,0:T(8,128)(2,1)}, bf16[4,2,32,1024]{3,2,1,0:T(8,128)(2,1)S(1)}, u32[]{:S(2)}, u32[]{:S(2)}) collective-permute-start(bf16[4,2,32,1024]{3,2,1,0:T(8,128)(2,1)} %pad_maximum_fusion), channel_id=1, source_target_pairs={{0,1},{1,0},{2,3},{3,2},{4,5},{5,4},{6,7},{7,6},{8,9},{9,8},{10,11... | collective-permute-start | bytes 1572872 | tf_op jit(solution)/shard_map/ppermute | solution.py:410
  58.3 7.7 %collective-permute-start.10 = (bf16[1024,128]{1,0:T(8,128)(2,1)S(1)}, bf16[1024,128]{1,0:T(8,128)(2,1)S(1)}, u32[]{:S(2)}, u32[]{:S(2)}) collective-permute-start(bf16[1024,128]{1,0:T(8,128)(2,1)S(1)} %bitcast.19), channel_id=1, source_target_pairs={{0,16},{8,24},{16,0},{24,8},{1,17},{9,25},{17,1},{25,9},{2,18},{10... | collective-permute-start | bytes 786440 | tf_op jit(solution)/shard_map/ppermute | solution.py:407
  59.6 6.9 %collective-permute-start.7 = (bf16[1280,128]{1,0:T(8,128)(2,1)S(1)}, bf16[1280,128]{1,0:T(8,128)(2,1)S(1)}, u32[]{:S(2)}, u32[]{:S(2)}) collective-permute-start(bf16[1280,128]{1,0:T(8,128)(2,1)S(1)} %get-tuple-element.70), channel_id=1, source_target_pairs={{0,8},{8,0},{16,24},{24,16},{1,9},{9,1},{17,25},{25,17},{2,10},{10... | collective-permute-start | bytes 983048 | tf_op jit(solution)/shard_map/ppermute | solution.py:407
  60.1 6.4 %collective-permute-start.8 = (bf16[1280,128]{1,0:T(8,128)(2,1)S(1)}, bf16[1280,128]{1,0:T(8,128)(2,1)S(1)}, u32[]{:S(2)}, u32[]{:S(2)}) collective-permute-start(bf16[1280,128]{1,0:T(8,128)(2,1)S(1)} %slice.8), channel_id=1, source_target_pairs={{0,8},{8,0},{16,24},{24,16},{1,9},{9,1},{17,25},{25,17},{2,10},{10... | collective-permute-start | bytes 983048 | tf_op jit(solution)/shard_map/ppermute | solution.py:407
  60.2 6.3 %collective-permute-start.9 = (bf16[1024,128]{1,0:T(8,128)(2,1)S(1)}, bf16[1024,128]{1,0:T(8,128)(2,1)S(1)}, u32[]{:S(2)}, u32[]{:S(2)}) collective-permute-start(bf16[1024,128]{1,0:T(8,128)(2,1)S(1)} %bitcast.20), channel_id=1, source_target_pairs={{0,8},{8,0},{16,24},{24,16},{1,9},{9,1},{17,25},{25,17},{2,10},{10... | collective-permute-start | bytes 786440 | tf_op jit(solution)/shard_map/ppermute | solution.py:407
  66.1 1.5 %collective-permute-start.11 = (bf16[1024,128]{1,0:T(8,128)(2,1)S(1)}, bf16[1024,128]{1,0:T(8,128)(2,1)S(1)}, u32[]{:S(2)}, u32[]{:S(2)}) collective-permute-start(bf16[1024,128]{1,0:T(8,128)(2,1)S(1)} %collective-permute-done.10.refs_10_), channel_id=1, source_target_pairs={{0,8},{8,0},{16,24},{24,16},{1,9},{9,1},{17,25},{25,17},{2,10},{10... | collective-permute-start | bytes 786440 | tf_op jit(solution)/shard_map/ppermute | solution.py:407
  70.2 2.0 %collective-permute-start.12 = (bf16[2,1024,128]{2,1,0:T(8,128)(2,1)S(1)}, bf16[2,1024,128]{2,1,0:T(8,128)(2,1)S(1)}, u32[]{:S(2)}, u32[]{:S(2)}) collective-permute-start(bf16[2,1024,128]{2,1,0:T(8,128)(2,1)S(1)} %get-tuple-element.73), channel_id=1, source_target_pairs={{0,8},{8,0},{16,24},{24,16},{1,9},{9,1},{17,25},{25,17},{2,10},{10... | collective-permute-start | bytes 1572872 | tf_op jit(solution)/shard_map/ppermute | solution.py:407
  71.7 57.4 %copy-start.1 = (bf16[1024,1024]{1,0:T(8,128)(2,1)S(1)}, bf16[1024,1024]{1,0:T(8,128)(2,1)}, u32[]{:S(2)}) copy-start(bf16[1024,1024]{1,0:T(8,128)(2,1)} %get-tuple-element.93.ext_ref) | copy-start | bytes 6291460
  72.3 2.9 %collective-permute-start.14 = (bf16[2,1280,128]{2,1,0:T(8,128)(2,1)S(1)}, bf16[2,1280,128]{2,1,0:T(8,128)(2,1)S(1)}, u32[]{:S(2)}, u32[]{:S(2)}) collective-permute-start(bf16[2,1280,128]{2,1,0:T(8,128)(2,1)S(1)} %get-tuple-element.81), channel_id=1, source_target_pairs={{0,8},{8,0},{16,24},{24,16},{1,9},{9,1},{17,25},{25,17},{2,10},{10... | collective-permute-start | bytes 1966088 | tf_op jit(solution)/shard_map/ppermute | solution.py:407
  72.5 8.6 %collective-permute-start.13 = (bf16[1024,128]{1,0:T(8,128)(2,1)S(1)}, bf16[1024,128]{1,0:T(8,128)(2,1)S(1)}, u32[]{:S(2)}, u32[]{:S(2)}) collective-permute-start(bf16[1024,128]{1,0:T(8,128)(2,1)S(1)} %get-tuple-element.75), channel_id=1, source_target_pairs={{0,16},{8,24},{16,0},{24,8},{1,17},{9,25},{17,1},{25,9},{2,18},{10... | collective-permute-start | bytes 786440 | tf_op jit(solution)/shard_map/ppermute | solution.py:407
  73.5 14.6 %collective-permute-start.16 = (bf16[4,32,2176]{2,1,0:T(8,128)(2,1)S(1)}, bf16[4,32,2176]{2,1,0:T(8,128)(2,1)S(1)}, u32[]{:S(2)}, u32[]{:S(2)}) collective-permute-start(bf16[4,32,2176]{2,1,0:T(8,128)(2,1)S(1)} %get-tuple-element.87), channel_id=1, source_target_pairs={{0,1},{1,0},{2,3},{3,2},{4,5},{5,4},{6,7},{7,6},{8,9},{9,8},{10,11... | collective-permute-start | bytes 1671176 | tf_op jit(solution)/shard_map/ppermute | solution.py:410
  81.1 10.6 %collective-permute-start.15 = (bf16[1536,128]{1,0:T(8,128)(2,1)S(1)}, bf16[1536,128]{1,0:T(8,128)(2,1)S(1)}, u32[]{:S(2)}, u32[]{:S(2)}) collective-permute-start(bf16[1536,128]{1,0:T(8,128)(2,1)S(1)} %get-tuple-element.84), channel_id=1, source_target_pairs={{0,16},{8,24},{16,0},{24,8},{1,17},{9,25},{17,1},{25,9},{2,18},{10... | collective-permute-start | bytes 1179656 | tf_op jit(solution)/shard_map/ppermute | solution.py:407
  92.8 36.3 %all-to-all-start.2 = ((bf16[8,12,32,128]{3,2,1,0:T(8,128)(2,1)}), bf16[8,12,32,128]{3,2,1,0:T(8,128)(2,1)S(1)}, u32[]{:S(2)}, u32[]{:S(2)}) async-start(bf16[8,12,32,128]{3,2,1,0:T(8,128)(2,1)} %back_pack.1), calls=%async_computation.2 | async-start | bytes 1572864 | tf_op jit(solution)/shard_map/all_to_all | solution.py:550
  98.1 29.5 %collective-permute-start.17 = (bf16[32,2176]{1,0:T(8,128)(2,1)S(1)}, bf16[32,2176]{1,0:T(8,128)(2,1)S(1)}, u32[]{:S(2)}, u32[]{:S(2)}) collective-permute-start(bf16[32,2176]{1,0:T(8,128)(2,1)S(1)} %get-tuple-element.89), channel_id=1, source_target_pairs={{0,4},{1,5},{2,6},{3,7},{4,0},{5,1},{6,2},{7,3},{8,12},{9,13},{10,... | collective-permute-start | bytes 417800 | tf_op jit(solution)/shard_map/ppermute | solution.py:410
  101.1 26.6 %collective-permute-start.18 = (bf16[32,2176]{1,0:T(8,128)(2,1)S(1)}, bf16[32,2176]{1,0:T(8,128)(2,1)S(1)}, u32[]{:S(2)}, u32[]{:S(2)}) collective-permute-start(bf16[32,2176]{1,0:T(8,128)(2,1)S(1)} %get-tuple-element.90), channel_id=1, source_target_pairs={{0,2},{1,3},{2,0},{3,1},{4,6},{5,7},{6,4},{7,5},{8,10},{9,11},{10,... | collective-permute-start | bytes 417800 | tf_op jit(solution)/shard_map/ppermute | solution.py:410
  102.5 25.1 %collective-permute-start.19 = (bf16[32,2176]{1,0:T(8,128)(2,1)S(1)}, bf16[32,2176]{1,0:T(8,128)(2,1)S(1)}, u32[]{:S(2)}, u32[]{:S(2)}) collective-permute-start(bf16[32,2176]{1,0:T(8,128)(2,1)S(1)} %get-tuple-element.91), channel_id=1, source_target_pairs={{0,6},{1,7},{2,4},{3,5},{4,2},{5,3},{6,0},{7,1},{8,14},{9,15},{10,... | collective-permute-start | bytes 417800 | tf_op jit(solution)/shard_map/ppermute | solution.py:410
  127.8 18.8 %collective-permute-start.24 = (bf16[32,2176]{1,0:T(8,128)(2,1)S(1)}, bf16[32,2176]{1,0:T(8,128)(2,1)S(1)}, u32[]{:S(2)}, u32[]{:S(2)}) collective-permute-start(bf16[32,2176]{1,0:T(8,128)(2,1)S(1)} %w_sum.1.refs_0_), channel_id=1, source_target_pairs={{0,16},{8,24},{16,0},{24,8},{1,17},{9,25},{17,1},{25,9},{2,18},{10... | collective-permute-start | bytes 417800 | tf_op jit(solution)/shard_map/ppermute | solution.py:407
  129.1 7.3 %copy-start = (bf16[8,12,32,128]{3,2,1,0:T(8,128)(2,1)}, bf16[8,12,32,128]{3,2,1,0:T(8,128)(2,1)S(1)}, u32[]{:S(2)}) copy-start(bf16[8,12,32,128]{3,2,1,0:T(8,128)(2,1)S(1)} %all-to-all-done.2) | copy-start | bytes 2359300
  129.6 0.7 copy-start.2
  130.3 0.6 copy-start.3
  130.9 2.1 %collective-permute-start.20 = (bf16[128,256]{1,0:T(8,128)(2,1)S(1)}, bf16[128,256]{1,0:T(8,128)(2,1)S(1)}, u32[]{:S(2)}, u32[]{:S(2)}) collective-permute-start(bf16[128,256]{1,0:T(8,128)(2,1)S(1)} %get-tuple-element.102), channel_id=1, source_target_pairs={{0,8},{8,0},{16,24},{24,16},{1,9},{9,1},{17,25},{25,17},{2,10},{10... | collective-permute-start | bytes 196616 | tf_op jit(solution)/shard_map/ppermute | solution.py:407
  130.9 4.9 %collective-permute-start.21 = (bf16[128,256]{1,0:T(8,128)(2,1)S(1)}, bf16[128,256]{1,0:T(8,128)(2,1)S(1)}, u32[]{:S(2)}, u32[]{:S(2)}) collective-permute-start(bf16[128,256]{1,0:T(8,128)(2,1)S(1)} %get-tuple-element.103), channel_id=1, source_target_pairs={{0,16},{8,24},{16,0},{24,8},{1,17},{9,25},{17,1},{25,9},{2,18},{10... | collective-permute-start | bytes 196616 | tf_op jit(solution)/shard_map/ppermute | solution.py:407
  131.6 4.8 %collective-permute-start.22 = (bf16[128,256]{1,0:T(8,128)(2,1)S(1)}, bf16[128,256]{1,0:T(8,128)(2,1)S(1)}, u32[]{:S(2)}, u32[]{:S(2)}) collective-permute-start(bf16[128,256]{1,0:T(8,128)(2,1)S(1)} %get-tuple-element.104), channel_id=1, source_target_pairs={{0,24},{8,16},{16,8},{24,0},{1,25},{9,17},{17,9},{25,1},{2,26},{10... | collective-permute-start | bytes 196616 | tf_op jit(solution)/shard_map/ppermute | solution.py:407
  132.8 14.1 %collective-permute-start.23 = (bf16[32,2176]{1,0:T(8,128)(2,1)S(1)}, bf16[32,2176]{1,0:T(8,128)(2,1)S(1)}, u32[]{:S(2)}, u32[]{:S(2)}) collective-permute-start(bf16[32,2176]{1,0:T(8,128)(2,1)S(1)} %w_sum.1.refs_0_), channel_id=1, source_target_pairs={{0,8},{8,0},{16,24},{24,16},{1,9},{9,1},{17,25},{25,17},{2,10},{10... | collective-permute-start | bytes 417800 | tf_op jit(solution)/shard_map/ppermute | solution.py:407
  133.1 3.4 %copy-start.7 = (bf16[128,256]{1,0:T(8,128)(2,1)}, bf16[128,256]{1,0:T(8,128)(2,1)S(1)}, u32[]{:S(2)}) copy-start(bf16[128,256]{1,0:T(8,128)(2,1)S(1)} %collective-permute-done.20.refs_1_) | copy-start | bytes 196612
  135.8 0.6 copy-start.8
  136.4 0.6 copy-start.9
  146.6 1.4 collective-permute-start.25

commit v6 on v4

--- a/solution.py
+++ b/solution.py
@@ -312,12 +312,16 @@
 def add_returned(total, at, me_ref, send_ref, hub_ref, ret_refs):
     rows = lax.broadcasted_iota(jnp.int32, (total.shape[1], T), 0) + at
     hub = (rows == hub_ref[...]).astype(F32).astype(BF)
+    hots, cols, hubs = [], [], 0.0
     for q, ret_ref in enumerate(ret_refs):
         idx = send_ref[pl.ds(me_ref[0] ^ q, 1), :]
-        sent = (rows == idx).astype(F32).astype(BF)
-        total += dot(ret_ref[:, :T], sent, ((1,), (1,)))
-        total += dot(ret_ref[:, T:], hub, ((1,), (1,)))
-    return total
+        hots.append((rows == idx).astype(F32).astype(BF))
+        cols.append(ret_ref[:, :T])
+        hubs += ret_ref[:, T:].astype(F32)
+    high = hubs.astype(BF)
+    cols += [high, (hubs - high.astype(F32)).astype(BF)]
+    hots += [hub, hub]
+    return total + dot(jnp.concatenate(cols, axis=1), jnp.concatenate(hots, axis=1), ((1,), (1,)))
 
 
 def finish_rest_kernel(top, me_ref, ga_ref, own_ref, send_ref, hub_ref, *refs):
@@ -358,7 +362,7 @@
         in_specs=[SMEM, fixed(ga), column(n_dst, top), fixed(sends), fixed(hubs)]
         + [fixed(r) for r in ret],
         out_specs=column(rows, top),
-        compiler_params=pltpu.CompilerParams(vmem_limit_bytes=24 * MIB),
+        compiler_params=pltpu.CompilerParams(vmem_limit_bytes=56 * MIB),
         cost_estimate=pl.CostEstimate(flops=0, bytes_accessed=18000000, transcendentals=0),
         name="finish_rest",
     )(me, ga, own, sends, hubs, *ret)
@@ -384,7 +388,7 @@
         + [fixed(r) for r in ret],
         out_specs=[column(rows, 0), column(rows, 0)],
         input_output_aliases={6: 0},
-        compiler_params=pltpu.CompilerParams(vmem_limit_bytes=24 * MIB),
+        compiler_params=pltpu.CompilerParams(vmem_limit_bytes=56 * MIB),
         cost_estimate=pl.CostEstimate(flops=0, bytes_accessed=6000000, transcendentals=0),
         name="finish_dst",
     )(me, ga, own, sends, hubs, back, grads, *ret)
@@ -568,8 +572,8 @@
         gagg,
         a_ext,
     )
-    back = after(back, halo_grad, parts)
     returned = [halo_grad[0]] + [over_dom(halo_grad[k], k) for k in range(1, n_dom)]
+    back = after(back, returned, parts)
 
     back = whole_call(
         functools.partial(back_pack_kernel, blocks),

time: 143 us -> 139 us (0.972)
  local copies, waits for them, and re-layouts: 14.1 us -> 6.84 us
  Pallas kernels: 41.6 us -> 46 us
  waiting for transfers between devices: 33.8 us -> 32.1 us
    unnamed x40 -> x28, local copies, waits for them, and re-layouts: 11.9 us -> 4.64 us
    ppermute x19, waiting for transfers between devices: 19 us -> 15.1 us  [over_dom(): return lax.ppermute(x, 'dom', [(i, i ^ k) for i in range(n_dom)])]
    pallas_call x1, Pallas kernels: 4.81 us -> 7.2 us  [finish_rest(): pl.pallas_call(functools.partial(finish_rest_kernel, top), out_shape=shap...]
    all_to_all x1, waiting for transfers between devices: 0.01 us -> 2.34 us  [body(): lax.all_to_all(back, 'feat', 0, 0, tiled=True)]
  transfers between devices with their start and end apart: 30 -> 30, of which waited for: 11 -> 12; matrix products, arithmetic and copies ran while one was open for 3% -> 3% of each run, Pallas kernels for 25% -> 28%
where the time goes in v6:
time: 139 us; the launch traced here: 138 us
  starting transfers between devices  48.3 us (35%)
  Pallas kernels  46 us (33%)
  waiting for transfers between devices  32.1 us (23%)
  local copies, waits for them, and re-layouts  6.84 us (5%)
  other arithmetic  2.93 us (2%)
  between operations  1.52 us (1%)
    pallas_call x1, Pallas kernels, build_dense(): pl.pallas_call(functools.partial(build_kernel, n_own), out_shape=(shape(n...  19.2 us
    ppermute x19, waiting for transfers between devices, over_dom(): return lax.ppermute(x, 'dom', [(i, i ^ k) for i in range(n_dom)])  15.1 us
    ppermute x7, starting transfers between devices, over_feat(): return lax.ppermute(x, 'feat', [(i, i ^ k) for i in range(n_feat)])  14.3 us
    pallas_call x10, Pallas kernels, whole_call(): pl.pallas_call(kernel, out_shape=out_shape, in_specs=[SMEM] * scalars + [...  12.4 us
    ppermute x19, starting transfers between devices, over_dom(): return lax.ppermute(x, 'dom', [(i, i ^ k) for i in range(n_dom)])  10.5 us
    ppermute x7, waiting for transfers between devices, over_feat(): return lax.ppermute(x, 'feat', [(i, i ^ k) for i in range(n_feat)])  9.74 us
    pallas_call x1, Pallas kernels, finish_rest(): pl.pallas_call(functools.partial(finish_rest_kernel, top), out_shape=shap...  7.2 us
    all_to_all x1, starting transfers between devices, body(): lax.all_to_all(back, 'feat', 0, 0, tiled=True)  6.82 us
  transfers between devices with their start and end apart: 30, of which 12 were waited for; matrix products, arithmetic and copies ran while one was open for 3% of the time, Pallas kernels for 28%

profile of v6, /device:TPU:0, one launch (start us, length us, event | category | flops | bytes accessed | tf_op | source)
XLA Modules:
  0.0 137.7 jit_solution(9287283136630369549)
XLA Ops:
  0.7 0.9 dynamic-slice_bitcast_fusion
  1.6 4.1 %collective-permute-start = (bf16[1,2,32,1024]{3,2,1,0:T(8,128)(2,1)S(1)}, bf16[1,2,32,1024]{3,2,1,0:T(8,128)(2,1)S(1)}, u32[]{:S(2)}, u32[]{:S(2)}) collective-permute-start(bf16[1,2,32,1024]{3,2,1,0:T(8,128)(2,1)S(1)} %maximum_bitcast_fusion.refs_0_), channel_id=1, source_target_pairs={{0,4},{1,5},{2,6},{3,7},{4,0},{5,1},{6,2},{7,3},{8,12},{9,13},{10,... | collective-permute-start | bytes 393224 | tf_op jit(solution)/shard_map/ppermute | solution.py:430
  5.7 3.9 %pack.1 = (bf16[8,9,32,128]{3,2,1,0:T(8,128)(2,1)}, bf16[128,256]{1,0:T(8,128)(2,1)}, bf16[128,256]{1,0:T(8,128)(2,1)}, bf16[128,256]{1,0:T(8,128)(2,1)}, bf16[128,256]{1,0:T(8,128)(2,1)}) custom-call(s32[1]{0:T(128)} %bitcast.me_ref, bf16[128,4096]{1,0:T(8,128)(2,1)} %x_ref.3, bf16[128,1024]{1,0:T(8,128)(2,1)} %cot_ref.1, f32[1,128]{1,0:T(1,128)} %bitcast.29, ...), custom_call_target="tpu_custom_call" | custom-call | bytes 12000000 | tf_op jit(solution)/shard_map/pack/pallas_call | solution.py:73
  9.6 2.4 %collective-permute-done.refs_1_ = bf16[1,2,32,1024]{3,2,1,0:T(8,128)(2,1)S(1)} collective-permute-done((bf16[1,2,32,1024]{3,2,1,0:T(8,128)(2,1)S(1)}, bf16[1,2,32,1024]{3,2,1,0:T(8,128)(2,1)S(1)}, u32[]{:S(2)}, u32[]{:S(2)}) %collective-permute-start) | collective-permute-done | bytes 131104 | tf_op jit(solution)/shard_map/ppermute | solution.py:430
  12.0 5.7 %all-to-all-start = ((bf16[8,9,32,128]{3,2,1,0:T(8,128)(2,1)}), bf16[8,9,32,128]{3,2,1,0:T(8,128)(2,1)S(1)}, u32[]{:S(2)}, u32[]{:S(2)}) async-start(bf16[8,9,32,128]{3,2,1,0:T(8,128)(2,1)} %get-tuple-element.57), calls=%async_computation | async-start | bytes 1179648 | tf_op jit(solution)/shard_map/all_to_all | solution.py:453
  17.7 1.6 %collective-permute-start.3 = (bf16[128,256]{1,0:T(8,128)(2,1)}, bf16[128,256]{1,0:T(8,128)(2,1)S(1)}, u32[]{:S(2)}, u32[]{:S(2)}) collective-permute-start(bf16[128,256]{1,0:T(8,128)(2,1)} %get-tuple-element.60), channel_id=1, source_target_pairs={{0,16},{8,24},{16,0},{24,8},{1,17},{9,25},{17,1},{25,9},{2,18},{10... | collective-permute-start | bytes 196616 | tf_op jit(solution)/shard_map/ppermute | solution.py:427
  20.8 0.6 concatenate.10.order_ref
  21.4 0.8 convert_reduce_fusion.1.start_ref
  22.2 2.1 %collective-permute-start.1 = (bf16[2,2,32,1024]{3,2,1,0:T(8,128)(2,1)S(1)}, bf16[2,2,32,1024]{3,2,1,0:T(8,128)(2,1)S(1)}, u32[]{:S(2)}, u32[]{:S(2)}) collective-permute-start(bf16[2,2,32,1024]{3,2,1,0:T(8,128)(2,1)S(1)} %pad_maximum_fusion.1), channel_id=1, source_target_pairs={{0,2},{1,3},{2,0},{3,1},{4,6},{5,7},{6,4},{7,5},{8,10},{9,11},{10,... | collective-permute-start | bytes 786440 | tf_op jit(solution)/shard_map/ppermute | solution.py:430
  24.9 19.2 %build_dense.1 = (bf16[1024,4096]{1,0:T(8,128)(2,1)}, bf16[1024,1024]{1,0:T(8,128)(2,1)}, bf16[8,128,128]{2,1,0:T(8,128)(2,1)}) custom-call(s32[514]{0:T(1024)} %concatenate.10.order_ref, s32[321]{0:T(512)} %convert_reduce_fusion.1.start_ref, bf16[128,4096]{1,0:T(8,128)(2,1)} %x_ref.3, bf16[512,128,128]{2,1,0:T(8,128)(2,1)} %vals_hbm.1, ...), custom_call_target="tpu_custom_call" | custom-call | bytes 30000000 | tf_op jit(solution)/shard_map/build_dense/pallas_call | solution.py:134
  44.1 5.2 %all-to-all-start.1 = ((bf16[8,128,128]{2,1,0:T(8,128)(2,1)}), bf16[8,128,128]{2,1,0:T(8,128)(2,1)S(1)}, u32[]{:S(2)}, u32[]{:S(2)}) async-start(bf16[8,128,128]{2,1,0:T(8,128)(2,1)} %get-tuple-element.69), calls=%async_computation.1 | async-start | bytes 524288 | tf_op jit(solution)/shard_map/all_to_all | solution.py:480
  50.1 0.8 pad_maximum_fusion
  50.9 2.0 %collective-permute-start.5 = (bf16[4,2,32,1024]{3,2,1,0:T(8,128)(2,1)}, bf16[4,2,32,1024]{3,2,1,0:T(8,128)(2,1)S(1)}, u32[]{:S(2)}, u32[]{:S(2)}) collective-permute-start(bf16[4,2,32,1024]{3,2,1,0:T(8,128)(2,1)} %pad_maximum_fusion), channel_id=1, source_target_pairs={{0,1},{1,0},{2,3},{3,2},{4,5},{5,4},{6,7},{7,6},{8,9},{9,8},{10,11... | collective-permute-start | bytes 1572872 | tf_op jit(solution)/shard_map/ppermute | solution.py:430
  52.9 4.9 %all-to-all-done.1 = bf16[8,128,128]{2,1,0:T(8,128)(2,1)S(1)} async-done(((bf16[8,128,128]{2,1,0:T(8,128)(2,1)}), bf16[8,128,128]{2,1,0:T(8,128)(2,1)S(1)}, u32[]{:S(2)}, u32[]{:S(2)}) %all-to-all-start.1) | async-done | bytes 262176 | tf_op jit(solution)/shard_map/all_to_all | solution.py:480
  57.8 1.5 %collective-permute-start.10 = (bf16[1024,128]{1,0:T(8,128)(2,1)S(1)}, bf16[1024,128]{1,0:T(8,128)(2,1)S(1)}, u32[]{:S(2)}, u32[]{:S(2)}) collective-permute-start(bf16[1024,128]{1,0:T(8,128)(2,1)S(1)} %bitcast.18), channel_id=1, source_target_pairs={{0,16},{8,24},{16,0},{24,8},{1,17},{9,25},{17,1},{25,9},{2,18},{10... | collective-permute-start | bytes 786440 | tf_op jit(solution)/shard_map/ppermute | solution.py:427
  59.3 1.2 collective-permute-done.6.refs_5_
  61.1 4.0 %collective-permute-done.10.refs_10_ = bf16[1024,128]{1,0:T(8,128)(2,1)S(1)} collective-permute-done((bf16[1024,128]{1,0:T(8,128)(2,1)S(1)}, bf16[1024,128]{1,0:T(8,128)(2,1)S(1)}, u32[]{:S(2)}, u32[]{:S(2)}) %collective-permute-start.10) | collective-permute-done | bytes 262176 | tf_op jit(solution)/shard_map/ppermute | solution.py:427
  65.2 1.1 collective-permute-done.5.refs_3_
  66.7 2.6 %dense.1 = (bf16[4,256,128]{2,1,0:T(8,128)(2,1)S(1)}, bf16[2,256,128]{2,1,0:T(8,128)(2,1)S(1)}, bf16[2,256,128]{2,1,0:T(8,128)(2,1)S(1)}, bf16[2,1024,128]{2,1,0:T(8,128)(2,1)S(1)}, bf16[2,1024,128]{2,1,0:T(8,128)(2,1)S(1)}) custom-call(f32[256,128]{1,0:T(8,128)S(1)} %get-tuple-element.65.bias_ref, bf16[1,2,32,1024]{3,2,1,0:T(8,128)(2,1)S(1)} %maximum_bitcast_fusion.refs_0_, ...), custom_call_target="tpu_custom_call" | custom-call | bytes 9000000 | tf_op jit(solution)/shard_map/dense/pallas_call | solution.py:28
  69.5 2.3 %grads.1 = (bf16[2,1280,128]{2,1,0:T(8,128)(2,1)S(1)}, bf16[2,1280,128]{2,1,0:T(8,128)(2,1)}, bf16[4,32,2176]{2,1,0:T(8,128)(2,1)S(1)}, bf16[4,32,2176]{2,1,0:T(8,128)(2,1)}) custom-call(bf16[4,256,128]{2,1,0:T(8,128)(2,1)S(1)} %get-tuple-element.74.g_ref, bf16[2,256,128]{2,1,0:T(8,128)(2,1)S(1)} %get-tuple-element.75.act_even, ...), custom_call_target="tpu_custom_call" | custom-call | bytes 9000000 | tf_op jit(solution)/shard_map/grads/pallas_call | solution.py:28
  71.9 0.8 copy-done.2
  73.2 1.5 %collective-permute-start.13 = (bf16[1024,128]{1,0:T(8,128)(2,1)S(1)}, bf16[1024,128]{1,0:T(8,128)(2,1)S(1)}, u32[]{:S(2)}, u32[]{:S(2)}) collective-permute-start(bf16[1024,128]{1,0:T(8,128)(2,1)S(1)} %get-tuple-element.73), channel_id=1, source_target_pairs={{0,16},{8,24},{16,0},{24,8},{1,17},{9,25},{17,1},{25,9},{2,18},{10... | collective-permute-start | bytes 786440 | tf_op jit(solution)/shard_map/ppermute | solution.py:427
  74.7 1.7 %collective-permute-start.14 = (bf16[4,32,2176]{2,1,0:T(8,128)(2,1)}, bf16[4,32,2176]{2,1,0:T(8,128)(2,1)}, u32[]{:S(2)}, u32[]{:S(2)}) collective-permute-start(bf16[4,32,2176]{2,1,0:T(8,128)(2,1)} %get-tuple-element.79), channel_id=1, source_target_pairs={{0,1},{1,0},{2,3},{3,2},{4,5},{5,4},{6,7},{7,6},{8,9},{9,8},{10,11... | collective-permute-start | bytes 1671176 | tf_op jit(solution)/shard_map/ppermute | solution.py:430
  76.5 5.1 %collective-permute-done.13 = bf16[1024,128]{1,0:T(8,128)(2,1)S(1)} collective-permute-done((bf16[1024,128]{1,0:T(8,128)(2,1)S(1)}, bf16[1024,128]{1,0:T(8,128)(2,1)S(1)}, u32[]{:S(2)}, u32[]{:S(2)}) %collective-permute-start.13) | collective-permute-done | bytes 262176 | tf_op jit(solution)/shard_map/ppermute | solution.py:427
  81.6 0.8 add_convert_fusion
  82.3 5.7 %all-to-all-start.2 = ((bf16[8,128,128]{2,1,0:T(8,128)(2,1)}), bf16[8,128,128]{2,1,0:T(8,128)(2,1)S(1)}, u32[]{:S(2)}, u32[]{:S(2)}) async-start(bf16[8,128,128]{2,1,0:T(8,128)(2,1)} %bitcast.10), calls=%async_computation.2 | async-start | bytes 524288 | tf_op jit(solution)/shard_map/all_to_all | solution.py:553
  88.1 1.9 %back_pair.1 = (bf16[1536,128]{1,0:T(8,128)(2,1)S(1)}, bf16[1536,128]{1,0:T(8,128)(2,1)}) custom-call(bf16[2,1280,128]{2,1,0:T(8,128)(2,1)S(1)} %get-tuple-element.89.even_ref, bf16[2,1280,128]{2,1,0:T(8,128)(2,1)} %collective-permute-done.15.got_ref), custom_call_target="tpu_custom_call" | custom-call | bytes 3000000 | tf_op jit(solution)/shard_map/back_pair/pallas_call | solution.py:28
  90.0 1.5 %collective-permute-start.16 = (bf16[1536,128]{1,0:T(8,128)(2,1)}, bf16[1536,128]{1,0:T(8,128)(2,1)S(1)}, u32[]{:S(2)}, u32[]{:S(2)}) collective-permute-start(bf16[1536,128]{1,0:T(8,128)(2,1)} %get-tuple-element.94), channel_id=1, source_target_pairs={{0,16},{8,24},{16,0},{24,8},{1,17},{9,25},{17,1},{25,9},{2,18},{10... | collective-permute-start | bytes 1179656 | tf_op jit(solution)/shard_map/ppermute | solution.py:427
  91.5 1.1 copy-done.3
  92.5 1.8 %x_sum.1 = (bf16[32,2176]{1,0:T(8,128)(2,1)S(1)}, bf16[32,2176]{1,0:T(8,128)(2,1)}, bf16[32,2176]{1,0:T(8,128)(2,1)}, bf16[32,2176]{1,0:T(8,128)(2,1)}) custom-call(bf16[4,32,2176]{2,1,0:T(8,128)(2,1)S(1)} %copy-done.3, bf16[4,32,2176]{2,1,0:T(8,128)(2,1)} %collective-permute-done.14.got_ref), custom_call_target="tpu_custom_call" | custom-call | bytes 3000000 | tf_op jit(solution)/shard_map/x_sum/pallas_call | solution.py:28
  94.4 2.9 %collective-permute-start.20 = (bf16[32,2176]{1,0:T(8,128)(2,1)}, bf16[32,2176]{1,0:T(8,128)(2,1)S(1)}, u32[]{:S(2)}, u32[]{:S(2)}) collective-permute-start(bf16[32,2176]{1,0:T(8,128)(2,1)} %get-tuple-element.82), channel_id=1, source_target_pairs={{0,4},{1,5},{2,6},{3,7},{4,0},{5,1},{6,2},{7,3},{8,12},{9,13},{10,... | collective-permute-start | bytes 417800 | tf_op jit(solution)/shard_map/ppermute | solution.py:430
  97.3 1.5 %collective-permute-start.21 = (bf16[32,2176]{1,0:T(8,128)(2,1)}, bf16[32,2176]{1,0:T(8,128)(2,1)}, u32[]{:S(2)}, u32[]{:S(2)}) collective-permute-start(bf16[32,2176]{1,0:T(8,128)(2,1)} %get-tuple-element.83), channel_id=1, source_target_pairs={{0,2},{1,3},{2,0},{3,1},{4,6},{5,7},{6,4},{7,5},{8,10},{9,11},{10,... | collective-permute-start | bytes 417800 | tf_op jit(solution)/shard_map/ppermute | solution.py:430
  99.2 0.7 copy-done.1
  99.9 0.6 copy-done.4
  100.6 5.2 %collective-permute-done.20.refs_1_ = bf16[32,2176]{1,0:T(8,128)(2,1)S(1)} collective-permute-done((bf16[32,2176]{1,0:T(8,128)(2,1)}, bf16[32,2176]{1,0:T(8,128)(2,1)S(1)}, u32[]{:S(2)}, u32[]{:S(2)}) %collective-permute-start.20) | collective-permute-done | bytes 139296 | tf_op jit(solution)/shard_map/ppermute | solution.py:430
  106.3 1.1 collective-permute-done.22.refs_3_
  107.4 3.3 %collective-permute-done.18.refs_2_ = bf16[128,256]{1,0:T(8,128)(2,1)S(1)} collective-permute-done((bf16[128,256]{1,0:T(8,128)(2,1)S(1)}, bf16[128,256]{1,0:T(8,128)(2,1)S(1)}, u32[]{:S(2)}, u32[]{:S(2)}) %collective-permute-start.18) | collective-permute-done | bytes 65568 | tf_op jit(solution)/shard_map/ppermute | solution.py:427
  110.7 0.9 back_pack.1
  111.6 6.8 %all-to-all-start.3 = ((bf16[8,8,32,128]{3,2,1,0:T(8,128)(2,1)}), bf16[8,8,32,128]{3,2,1,0:T(8,128)(2,1)S(1)}, u32[]{:S(2)}, u32[]{:S(2)}) async-start(bf16[8,8,32,128]{3,2,1,0:T(8,128)(2,1)} %back_pack.1), calls=%async_computation.3 | async-start | bytes 1048576 | tf_op jit(solution)/shard_map/all_to_all | solution.py:588
  118.4 1.1 w_sum.1.refs_0_
  119.5 1.3 collective-permute-start.24
  120.8 7.2 %finish_rest.1.grads_ref = f32[128,4096]{1,0:T(8,128)} custom-call(s32[1]{0:T(128)} %bitcast.me_ref, bf16[128,1024]{1,0:T(8,128)(2,1)} %copy-done.1, bf16[1024,4096]{1,0:T(8,128)(2,1)} %get-tuple-element.88.own_ref, s32[4,128]{1,0:T(4,128)} %bitcast.24, s32[1,128]{1,0:T(1,128)} %bitcast.27, bf16[128,256]{1,0:T(8,128)(2,1)} %copy-done.4, ...), custom_call_target="tpu_custom_call" | custom-call | bytes 18000000 | tf_op jit(solution)/shard_map/finish_rest/pallas_call | solution.py:358
  128.5 1.0 collective-permute-done.25.refs_3_
  129.5 1.0 w_out.1
  130.6 0.6 reshape_squeeze.3
  131.2 2.3 %all-to-all-done.3 = bf16[8,8,32,128]{3,2,1,0:T(8,128)(2,1)S(1)} async-done(((bf16[8,8,32,128]{3,2,1,0:T(8,128)(2,1)}), bf16[8,8,32,128]{3,2,1,0:T(8,128)(2,1)S(1)}, u32[]{:S(2)}, u32[]{:S(2)}) %all-to-all-start.3) | async-done | bytes 524320 | tf_op jit(solution)/shard_map/all_to_all | solution.py:588
  133.6 0.8 copy-done.5
  134.4 3.3 %finish_dst.1 = (f32[128,4096]{1,0:T(8,128)}, bf16[128,1024]{1,0:T(8,128)(2,1)}) custom-call(s32[1]{0:T(128)} %bitcast.me_ref, bf16[128,1024]{1,0:T(8,128)(2,1)} %copy-done.1, bf16[1024,4096]{1,0:T(8,128)(2,1)} %get-tuple-element.88.own_ref, s32[4,128]{1,0:T(4,128)} %bitcast.25, s32[1,128]{1,0:T(1,128)} %bitcast.28, ...), custom_call_target="tpu_custom_call", output_to_operand_aliasing={{0}: (6, {})} | custom-call | bytes 6000000 | tf_op jit(solution)/shard_map/finish_dst/pallas_call | solution.py:375
  (67 shorter events, 5.6 us)
Async XLA Ops:
  0.6 19.6 %copy-start.13 = (s32[512]{0:T(512)S(1)}, s32[512]{0:T(512)}, u32[]{:S(2)}) copy-start(s32[512]{0:T(512)} %param.14) | copy-start | bytes 6148
  0.6 19.6 %copy-start.12 = (s32[512]{0:T(512)S(1)}, s32[512]{0:T(512)}, u32[]{:S(2)}) copy-start(s32[512]{0:T(512)} %param.15) | copy-start | bytes 6148
  1.6 10.4 %collective-permute-start = (bf16[1,2,32,1024]{3,2,1,0:T(8,128)(2,1)S(1)}, bf16[1,2,32,1024]{3,2,1,0:T(8,128)(2,1)S(1)}, u32[]{:S(2)}, u32[]{:S(2)}) collective-permute-start(bf16[1,2,32,1024]{3,2,1,0:T(8,128)(2,1)S(1)} %maximum_bitcast_fusion.refs_0_), channel_id=1, source_target_pairs={{0,4},{1,5},{2,6},{3,7},{4,0},{5,1},{6,2},{7,3},{8,12},{9,13},{10,... | collective-permute-start | bytes 393224 | tf_op jit(solution)/shard_map/ppermute | solution.py:430
  12.0 32.2 %all-to-all-start = ((bf16[8,9,32,128]{3,2,1,0:T(8,128)(2,1)}), bf16[8,9,32,128]{3,2,1,0:T(8,128)(2,1)S(1)}, u32[]{:S(2)}, u32[]{:S(2)}) async-start(bf16[8,9,32,128]{3,2,1,0:T(8,128)(2,1)} %get-tuple-element.57), calls=%async_computation | async-start | bytes 1179648 | tf_op jit(solution)/shard_map/all_to_all | solution.py:453
  17.7 6.5 %collective-permute-start.2 = (bf16[128,256]{1,0:T(8,128)(2,1)}, bf16[128,256]{1,0:T(8,128)(2,1)S(1)}, u32[]{:S(2)}, u32[]{:S(2)}) collective-permute-start(bf16[128,256]{1,0:T(8,128)(2,1)} %get-tuple-element.59), channel_id=1, source_target_pairs={{0,8},{8,0},{16,24},{24,16},{1,9},{9,1},{17,25},{25,17},{2,10},{10... | collective-permute-start | bytes 196616 | tf_op jit(solution)/shard_map/ppermute | solution.py:427
  17.7 6.5 %collective-permute-start.3 = (bf16[128,256]{1,0:T(8,128)(2,1)}, bf16[128,256]{1,0:T(8,128)(2,1)S(1)}, u32[]{:S(2)}, u32[]{:S(2)}) collective-permute-start(bf16[128,256]{1,0:T(8,128)(2,1)} %get-tuple-element.60), channel_id=1, source_target_pairs={{0,16},{8,24},{16,0},{24,8},{1,17},{9,25},{17,1},{25,9},{2,18},{10... | collective-permute-start | bytes 196616 | tf_op jit(solution)/shard_map/ppermute | solution.py:427
  19.3 5.0 %collective-permute-start.4 = (bf16[128,256]{1,0:T(8,128)(2,1)}, bf16[128,256]{1,0:T(8,128)(2,1)S(1)}, u32[]{:S(2)}, u32[]{:S(2)}) collective-permute-start(bf16[128,256]{1,0:T(8,128)(2,1)} %get-tuple-element.61), channel_id=1, source_target_pairs={{0,24},{8,16},{16,8},{24,0},{1,25},{9,17},{17,9},{25,1},{2,26},{10... | collective-permute-start | bytes 196616 | tf_op jit(solution)/shard_map/ppermute | solution.py:427
  22.2 27.2 %collective-permute-start.1 = (bf16[2,2,32,1024]{3,2,1,0:T(8,128)(2,1)S(1)}, bf16[2,2,32,1024]{3,2,1,0:T(8,128)(2,1)S(1)}, u32[]{:S(2)}, u32[]{:S(2)}) collective-permute-start(bf16[2,2,32,1024]{3,2,1,0:T(8,128)(2,1)S(1)} %pad_maximum_fusion.1), channel_id=1, source_target_pairs={{0,2},{1,3},{2,0},{3,1},{4,6},{5,7},{6,4},{7,5},{8,10},{9,11},{10,... | collective-permute-start | bytes 786440 | tf_op jit(solution)/shard_map/ppermute | solution.py:430
  24.3 0.6 copy-start.9
  24.3 0.6 copy-start.10
  24.3 0.6 copy-start.11
  44.1 13.7 %all-to-all-start.1 = ((bf16[8,128,128]{2,1,0:T(8,128)(2,1)}), bf16[8,128,128]{2,1,0:T(8,128)(2,1)S(1)}, u32[]{:S(2)}, u32[]{:S(2)}) async-start(bf16[8,128,128]{2,1,0:T(8,128)(2,1)} %get-tuple-element.69), calls=%async_computation.1 | async-start | bytes 524288 | tf_op jit(solution)/shard_map/all_to_all | solution.py:480
  49.5 11.0 %collective-permute-start.6 = (bf16[1536,128]{1,0:T(8,128)(2,1)S(1)}, bf16[1536,128]{1,0:T(8,128)(2,1)S(1)}, u32[]{:S(2)}, u32[]{:S(2)}) collective-permute-start(bf16[1536,128]{1,0:T(8,128)(2,1)S(1)} %get-tuple-element.67), channel_id=1, source_target_pairs={{0,16},{8,24},{16,0},{24,8},{1,17},{9,25},{17,1},{25,9},{2,18},{10... | collective-permute-start | bytes 1179656 | tf_op jit(solution)/shard_map/ppermute | solution.py:427
  50.9 15.3 %collective-permute-start.5 = (bf16[4,2,32,1024]{3,2,1,0:T(8,128)(2,1)}, bf16[4,2,32,1024]{3,2,1,0:T(8,128)(2,1)S(1)}, u32[]{:S(2)}, u32[]{:S(2)}) collective-permute-start(bf16[4,2,32,1024]{3,2,1,0:T(8,128)(2,1)} %pad_maximum_fusion), channel_id=1, source_target_pairs={{0,1},{1,0},{2,3},{3,2},{4,5},{5,4},{6,7},{7,6},{8,9},{9,8},{10,11... | collective-permute-start | bytes 1572872 | tf_op jit(solution)/shard_map/ppermute | solution.py:430
  57.8 7.3 %collective-permute-start.10 = (bf16[1024,128]{1,0:T(8,128)(2,1)S(1)}, bf16[1024,128]{1,0:T(8,128)(2,1)S(1)}, u32[]{:S(2)}, u32[]{:S(2)}) collective-permute-start(bf16[1024,128]{1,0:T(8,128)(2,1)S(1)} %bitcast.18), channel_id=1, source_target_pairs={{0,16},{8,24},{16,0},{24,8},{1,17},{9,25},{17,1},{25,9},{2,18},{10... | collective-permute-start | bytes 786440 | tf_op jit(solution)/shard_map/ppermute | solution.py:427
  59.3 7.0 %collective-permute-start.7 = (bf16[1280,128]{1,0:T(8,128)(2,1)S(1)}, bf16[1280,128]{1,0:T(8,128)(2,1)S(1)}, u32[]{:S(2)}, u32[]{:S(2)}) collective-permute-start(bf16[1280,128]{1,0:T(8,128)(2,1)S(1)} %get-tuple-element.68), channel_id=1, source_target_pairs={{0,8},{8,0},{16,24},{24,16},{1,9},{9,1},{17,25},{25,17},{2,10},{10... | collective-permute-start | bytes 983048 | tf_op jit(solution)/shard_map/ppermute | solution.py:427
  60.5 5.7 %collective-permute-start.8 = (bf16[1280,128]{1,0:T(8,128)(2,1)S(1)}, bf16[1280,128]{1,0:T(8,128)(2,1)S(1)}, u32[]{:S(2)}, u32[]{:S(2)}) collective-permute-start(bf16[1280,128]{1,0:T(8,128)(2,1)S(1)} %slice.8), channel_id=1, source_target_pairs={{0,8},{8,0},{16,24},{24,16},{1,9},{9,1},{17,25},{25,17},{2,10},{10... | collective-permute-start | bytes 983048 | tf_op jit(solution)/shard_map/ppermute | solution.py:427
  60.6 5.6 %collective-permute-start.9 = (bf16[1024,128]{1,0:T(8,128)(2,1)S(1)}, bf16[1024,128]{1,0:T(8,128)(2,1)S(1)}, u32[]{:S(2)}, u32[]{:S(2)}) collective-permute-start(bf16[1024,128]{1,0:T(8,128)(2,1)S(1)} %bitcast.19), channel_id=1, source_target_pairs={{0,8},{8,0},{16,24},{24,16},{1,9},{9,1},{17,25},{25,17},{2,10},{10... | collective-permute-start | bytes 786440 | tf_op jit(solution)/shard_map/ppermute | solution.py:427
  65.1 1.5 %collective-permute-start.11 = (bf16[1024,128]{1,0:T(8,128)(2,1)S(1)}, bf16[1024,128]{1,0:T(8,128)(2,1)S(1)}, u32[]{:S(2)}, u32[]{:S(2)}) collective-permute-start(bf16[1024,128]{1,0:T(8,128)(2,1)S(1)} %collective-permute-done.10.refs_10_), channel_id=1, source_target_pairs={{0,8},{8,0},{16,24},{24,16},{1,9},{9,1},{17,25},{25,17},{2,10},{10... | collective-permute-start | bytes 786440 | tf_op jit(solution)/shard_map/ppermute | solution.py:427
  69.3 3.3 %collective-permute-start.12 = (bf16[2,1024,128]{2,1,0:T(8,128)(2,1)S(1)}, bf16[2,1024,128]{2,1,0:T(8,128)(2,1)S(1)}, u32[]{:S(2)}, u32[]{:S(2)}) collective-permute-start(bf16[2,1024,128]{2,1,0:T(8,128)(2,1)S(1)} %get-tuple-element.71), channel_id=1, source_target_pairs={{0,8},{8,0},{16,24},{24,16},{1,9},{9,1},{17,25},{25,17},{2,10},{10... | collective-permute-start | bytes 1572872 | tf_op jit(solution)/shard_map/ppermute | solution.py:427
  71.9 0.8 copy-start.2
  72.8 26.0 %copy-start = (bf16[1024,1024]{1,0:T(8,128)(2,1)S(1)}, bf16[1024,1024]{1,0:T(8,128)(2,1)}, u32[]{:S(2)}) copy-start(bf16[1024,1024]{1,0:T(8,128)(2,1)} %get-tuple-element.86.ext_ref) | copy-start | bytes 6291460
  72.8 15.3 %collective-permute-start.15 = (bf16[2,1280,128]{2,1,0:T(8,128)(2,1)}, bf16[2,1280,128]{2,1,0:T(8,128)(2,1)}, u32[]{:S(2)}, u32[]{:S(2)}) collective-permute-start(bf16[2,1280,128]{2,1,0:T(8,128)(2,1)} %get-tuple-element.91), channel_id=1, source_target_pairs={{0,8},{8,0},{16,24},{24,16},{1,9},{9,1},{17,25},{25,17},{2,10},{10... | collective-permute-start | bytes 1966088 | tf_op jit(solution)/shard_map/ppermute | solution.py:427
  73.2 8.3 %collective-permute-start.13 = (bf16[1024,128]{1,0:T(8,128)(2,1)S(1)}, bf16[1024,128]{1,0:T(8,128)(2,1)S(1)}, u32[]{:S(2)}, u32[]{:S(2)}) collective-permute-start(bf16[1024,128]{1,0:T(8,128)(2,1)S(1)} %get-tuple-element.73), channel_id=1, source_target_pairs={{0,16},{8,24},{16,0},{24,8},{1,17},{9,25},{17,1},{25,9},{2,18},{10... | collective-permute-start | bytes 786440 | tf_op jit(solution)/shard_map/ppermute | solution.py:427
  74.7 16.7 %collective-permute-start.14 = (bf16[4,32,2176]{2,1,0:T(8,128)(2,1)}, bf16[4,32,2176]{2,1,0:T(8,128)(2,1)}, u32[]{:S(2)}, u32[]{:S(2)}) collective-permute-start(bf16[4,32,2176]{2,1,0:T(8,128)(2,1)} %get-tuple-element.79), channel_id=1, source_target_pairs={{0,1},{1,0},{2,3},{3,2},{4,5},{5,4},{6,7},{7,6},{8,9},{9,8},{10,11... | collective-permute-start | bytes 1671176 | tf_op jit(solution)/shard_map/ppermute | solution.py:430
  82.3 16.4 %all-to-all-start.2 = ((bf16[8,128,128]{2,1,0:T(8,128)(2,1)}), bf16[8,128,128]{2,1,0:T(8,128)(2,1)S(1)}, u32[]{:S(2)}, u32[]{:S(2)}) async-start(bf16[8,128,128]{2,1,0:T(8,128)(2,1)} %bitcast.10), calls=%async_computation.2 | async-start | bytes 524288 | tf_op jit(solution)/shard_map/all_to_all | solution.py:553
  90.0 20.7 %collective-permute-start.16 = (bf16[1536,128]{1,0:T(8,128)(2,1)}, bf16[1536,128]{1,0:T(8,128)(2,1)S(1)}, u32[]{:S(2)}, u32[]{:S(2)}) collective-permute-start(bf16[1536,128]{1,0:T(8,128)(2,1)} %get-tuple-element.94), channel_id=1, source_target_pairs={{0,16},{8,24},{16,0},{24,8},{1,17},{9,25},{17,1},{25,9},{2,18},{10... | collective-permute-start | bytes 1179656 | tf_op jit(solution)/shard_map/ppermute | solution.py:427
  91.5 1.1 copy-start.3
  94.4 11.4 %collective-permute-start.20 = (bf16[32,2176]{1,0:T(8,128)(2,1)}, bf16[32,2176]{1,0:T(8,128)(2,1)S(1)}, u32[]{:S(2)}, u32[]{:S(2)}) collective-permute-start(bf16[32,2176]{1,0:T(8,128)(2,1)} %get-tuple-element.82), channel_id=1, source_target_pairs={{0,4},{1,5},{2,6},{3,7},{4,0},{5,1},{6,2},{7,3},{8,12},{9,13},{10,... | collective-permute-start | bytes 417800 | tf_op jit(solution)/shard_map/ppermute | solution.py:430
  97.3 9.0 %collective-permute-start.21 = (bf16[32,2176]{1,0:T(8,128)(2,1)}, bf16[32,2176]{1,0:T(8,128)(2,1)}, u32[]{:S(2)}, u32[]{:S(2)}) collective-permute-start(bf16[32,2176]{1,0:T(8,128)(2,1)} %get-tuple-element.83), channel_id=1, source_target_pairs={{0,2},{1,3},{2,0},{3,1},{4,6},{5,7},{6,4},{7,5},{8,10},{9,11},{10,... | collective-permute-start | bytes 417800 | tf_op jit(solution)/shard_map/ppermute | solution.py:430
  98.8 8.6 %collective-permute-start.22 = (bf16[32,2176]{1,0:T(8,128)(2,1)}, bf16[32,2176]{1,0:T(8,128)(2,1)}, u32[]{:S(2)}, u32[]{:S(2)}) collective-permute-start(bf16[32,2176]{1,0:T(8,128)(2,1)} %get-tuple-element.84), channel_id=1, source_target_pairs={{0,6},{1,7},{2,4},{3,5},{4,2},{5,3},{6,0},{7,1},{8,14},{9,15},{10,... | collective-permute-start | bytes 417800 | tf_op jit(solution)/shard_map/ppermute | solution.py:430
  99.2 0.7 copy-start.1
  99.9 0.6 copy-start.4
  100.6 6.8 %collective-permute-start.17 = (bf16[128,256]{1,0:T(8,128)(2,1)S(1)}, bf16[128,256]{1,0:T(8,128)(2,1)S(1)}, u32[]{:S(2)}, u32[]{:S(2)}) collective-permute-start(bf16[128,256]{1,0:T(8,128)(2,1)S(1)} %get-tuple-element.96), channel_id=1, source_target_pairs={{0,8},{8,0},{16,24},{24,16},{1,9},{9,1},{17,25},{25,17},{2,10},{10... | collective-permute-start | bytes 196616 | tf_op jit(solution)/shard_map/ppermute | solution.py:427
  105.7 4.9 %collective-permute-start.18 = (bf16[128,256]{1,0:T(8,128)(2,1)S(1)}, bf16[128,256]{1,0:T(8,128)(2,1)S(1)}, u32[]{:S(2)}, u32[]{:S(2)}) collective-permute-start(bf16[128,256]{1,0:T(8,128)(2,1)S(1)} %get-tuple-element.97), channel_id=1, source_target_pairs={{0,16},{8,24},{16,0},{24,8},{1,17},{9,25},{17,1},{25,9},{2,18},{10... | collective-permute-start | bytes 196616 | tf_op jit(solution)/shard_map/ppermute | solution.py:427
  106.3 4.4 %collective-permute-start.19 = (bf16[128,256]{1,0:T(8,128)(2,1)S(1)}, bf16[128,256]{1,0:T(8,128)(2,1)S(1)}, u32[]{:S(2)}, u32[]{:S(2)}) collective-permute-start(bf16[128,256]{1,0:T(8,128)(2,1)S(1)} %get-tuple-element.98), channel_id=1, source_target_pairs={{0,24},{8,16},{16,8},{24,0},{1,25},{9,17},{17,9},{25,1},{2,26},{10... | collective-permute-start | bytes 196616 | tf_op jit(solution)/shard_map/ppermute | solution.py:427
  107.4 13.4 %copy-start.6 = (bf16[128,256]{1,0:T(8,128)(2,1)}, bf16[128,256]{1,0:T(8,128)(2,1)S(1)}, u32[]{:S(2)}) copy-start(bf16[128,256]{1,0:T(8,128)(2,1)S(1)} %collective-permute-done.17.refs_1_) | copy-start | bytes 196612
  110.7 10.2 %copy-start.7 = (bf16[128,256]{1,0:T(8,128)(2,1)}, bf16[128,256]{1,0:T(8,128)(2,1)S(1)}, u32[]{:S(2)}) copy-start(bf16[128,256]{1,0:T(8,128)(2,1)S(1)} %collective-permute-done.18.refs_2_) | copy-start | bytes 196612
  110.7 10.2 %copy-start.8 = (bf16[128,256]{1,0:T(8,128)(2,1)}, bf16[128,256]{1,0:T(8,128)(2,1)S(1)}, u32[]{:S(2)}) copy-start(bf16[128,256]{1,0:T(8,128)(2,1)S(1)} %collective-permute-done.19.refs_3_) | copy-start | bytes 196612
  111.6 22.0 %all-to-all-start.3 = ((bf16[8,8,32,128]{3,2,1,0:T(8,128)(2,1)}), bf16[8,8,32,128]{3,2,1,0:T(8,128)(2,1)S(1)}, u32[]{:S(2)}, u32[]{:S(2)}) async-start(bf16[8,8,32,128]{3,2,1,0:T(8,128)(2,1)} %back_pack.1), calls=%async_computation.3 | async-start | bytes 1048576 | tf_op jit(solution)/shard_map/all_to_all | solution.py:588
  119.5 8.6 %collective-permute-start.24 = (bf16[32,2176]{1,0:T(8,128)(2,1)S(1)}, bf16[32,2176]{1,0:T(8,128)(2,1)S(1)}, u32[]{:S(2)}, u32[]{:S(2)}) collective-permute-start(bf16[32,2176]{1,0:T(8,128)(2,1)S(1)} %w_sum.1.refs_0_), channel_id=1, source_target_pairs={{0,16},{8,24},{16,0},{24,8},{1,17},{9,25},{17,1},{25,9},{2,18},{10... | collective-permute-start | bytes 417800 | tf_op jit(solution)/shard_map/ppermute | solution.py:427
  120.8 7.7 %collective-permute-start.23 = (bf16[32,2176]{1,0:T(8,128)(2,1)S(1)}, bf16[32,2176]{1,0:T(8,128)(2,1)S(1)}, u32[]{:S(2)}, u32[]{:S(2)}) collective-permute-start(bf16[32,2176]{1,0:T(8,128)(2,1)S(1)} %w_sum.1.refs_0_), channel_id=1, source_target_pairs={{0,8},{8,0},{16,24},{24,16},{1,9},{9,1},{17,25},{25,17},{2,10},{10... | collective-permute-start | bytes 417800 | tf_op jit(solution)/shard_map/ppermute | solution.py:427
  128.0 1.5 %collective-permute-start.25 = (bf16[32,2176]{1,0:T(8,128)(2,1)S(1)}, bf16[32,2176]{1,0:T(8,128)(2,1)S(1)}, u32[]{:S(2)}, u32[]{:S(2)}) collective-permute-start(bf16[32,2176]{1,0:T(8,128)(2,1)S(1)} %collective-permute-done.24.refs_2_), channel_id=1, source_target_pairs={{0,8},{8,0},{16,24},{24,16},{1,9},{9,1},{17,25},{25,17},{2,10},{10... | collective-permute-start | bytes 417800 | tf_op jit(solution)/shard_map/ppermute | solution.py:427
  133.6 0.8 copy-start.5

commit v7 on v6

--- a/solution.py
+++ b/solution.py
@@ -324,29 +324,44 @@
     return total + dot(jnp.concatenate(cols, axis=1), jnp.concatenate(hots, axis=1), ((1,), (1,)))
 
 
-def finish_rest_kernel(top, me_ref, ga_ref, own_ref, send_ref, hub_ref, *refs):
-    *ret_refs, out_ref = refs
+SPLIT = 4
+
+
+def times_owned(ga_ref, own_refs):
+    depth = own_refs[0].shape[0]
+    total = 0.0
+    for r, ref in enumerate(own_refs):
+        total += dot(ga_ref[:, r * depth : (r + 1) * depth], ref[...], ((1,), (0,)))
+    return total
+
+
+def finish_rest_kernel(top, me_ref, ga_ref, send_ref, hub_ref, *refs):
+    own_refs, ret_refs, out_ref = refs[:SPLIT], refs[SPLIT:-1], refs[-1]
     at = (pl.program_id(0) + top) * out_ref.shape[1]
-    total = dot(ga_ref[...], own_ref[...], ((1,), (0,)))
+    total = times_owned(ga_ref, own_refs)
     out_ref[...] = add_returned(total, at, me_ref, send_ref, hub_ref, ret_refs)
 
 
-def finish_dst_kernel(me_ref, ga_ref, own_ref, send_ref, hub_ref, back_ref, grads_ref, *refs):
-    *ret_refs, out_ref, act_ref = refs
+def finish_dst_kernel(me_ref, ga_ref, send_ref, hub_ref, back_ref, grads_ref, *refs):
+    own_refs, ret_refs, out_ref, act_ref = refs[:SPLIT], refs[SPLIT:-2], refs[-2], refs[-1]
     rows = ga_ref.shape[0]
     groups = range(back_ref.shape[0])
     own = jnp.concatenate([back_ref[b, :rows] for b in groups], axis=1).astype(F32)
     act_ref[...] = jnp.concatenate([back_ref[b, rows:] for b in groups], axis=1)
     at = pl.program_id(0) * out_ref.shape[1]
-    total = dot(ga_ref[...], own_ref[...], ((1,), (0,))) + own
+    total = times_owned(ga_ref, own_refs) + own
     out_ref[...] = add_returned(total, at, me_ref, send_ref, hub_ref, ret_refs)
 
 
 WIDE = 512
 
 
-def column(rows, first):
-    return pl.BlockSpec((rows, WIDE), lambda i: (0, i + first))
+def column(rows, first, at=0):
+    return pl.BlockSpec((rows, WIDE), lambda i: (at, i + first))
+
+
+def row_blocks(n_dst, first):
+    return [column(n_dst // SPLIT, first, r) for r in range(SPLIT)]
 
 
 def fixed(x):
@@ -359,13 +374,14 @@
         functools.partial(finish_rest_kernel, top),
         out_shape=shape(rows, n, kind=F32),
         grid=(n // WIDE - top,),
-        in_specs=[SMEM, fixed(ga), column(n_dst, top), fixed(sends), fixed(hubs)]
+        in_specs=[SMEM, fixed(ga), fixed(sends), fixed(hubs)]
+        + row_blocks(n_dst, top)
         + [fixed(r) for r in ret],
         out_specs=column(rows, top),
         compiler_params=pltpu.CompilerParams(vmem_limit_bytes=56 * MIB),
         cost_estimate=pl.CostEstimate(flops=0, bytes_accessed=18000000, transcendentals=0),
         name="finish_rest",
-    )(me, ga, own, sends, hubs, *ret)
+    )(me, ga, sends, hubs, *[own] * SPLIT, *ret)
 
 
 def finish_dst(me, ga, own, ret, sends, hubs, back, grads):
@@ -379,19 +395,19 @@
         in_specs=[
             SMEM,
             fixed(ga),
-            column(n_dst, 0),
             fixed(sends),
             fixed(hubs),
             pl.BlockSpec((WIDE // piece, 2 * rows, piece), lambda i: (i, 0, 0)),
             pl.BlockSpec(memory_space=pl.ANY),
         ]
+        + row_blocks(n_dst, 0)
         + [fixed(r) for r in ret],
         out_specs=[column(rows, 0), column(rows, 0)],
-        input_output_aliases={6: 0},
+        input_output_aliases={5: 0},
         compiler_params=pltpu.CompilerParams(vmem_limit_bytes=56 * MIB),
         cost_estimate=pl.CostEstimate(flops=0, bytes_accessed=6000000, transcendentals=0),
         name="finish_dst",
-    )(me, ga, own, sends, hubs, back, grads, *ret)
+    )(me, ga, sends, hubs, back, grads, *[own] * SPLIT, *ret)
 
 
 def body(
@@ -551,6 +567,8 @@
     from_x, from_core = after(from_x, gagg), after(from_core, gagg)
 
     gagg = lax.all_to_all(gagg, "feat", 0, 0, tiled=True)
+    parts = whole_call(pair_kernel, "x_sum", 1.0, [shape(sub, 2 * width + T)] * nz, parts, from_x)
+    from_core = after(from_core, parts)
     back = whole_call(
         functools.partial(back_pair_kernel, width),
         "back_pair",
@@ -560,7 +578,6 @@
         from_core,
     )
     back = [back[0]] + [over_dom(back[j], 2 * j) for j in range(1, ny)]
-    parts = whole_call(pair_kernel, "x_sum", 1.0, [shape(sub, 2 * width + T)] * nz, parts, from_x)
     gagg = after(gagg, parts)
     parts = [parts[0]] + [over_feat(parts[j], blocks[j]) for j in range(1, nz)]
 

time: 139 us -> 140 us (level)
  transfers between devices with their start and end apart: 30 -> 30, of which waited for: 12 -> 13; matrix products, arithmetic and copies ran while one was open for 3% -> 3% of each run, Pallas kernels for 28% -> 28%
where the time goes in v7:
time: 140 us; the launch traced here: 139 us
  starting transfers between devices  49.6 us (35%)
  Pallas kernels  46.1 us (33%)
  waiting for transfers between devices  31.9 us (23%)
  local copies, waits for them, and re-layouts  6.85 us (5%)
  other arithmetic  2.93 us (2%)
  between operations  1.52 us (1%)
    pallas_call x1, Pallas kernels, build_dense(): pl.pallas_call(functools.partial(build_kernel, n_own), out_shape=(shape(n...  19.1 us
    ppermute x19, waiting for transfers between devices, over_dom(): return lax.ppermute(x, 'dom', [(i, i ^ k) for i in range(n_dom)])  15.3 us
    ppermute x7, starting transfers between devices, over_feat(): return lax.ppermute(x, 'feat', [(i, i ^ k) for i in range(n_feat)])  14.3 us
    pallas_call x10, Pallas kernels, whole_call(): pl.pallas_call(kernel, out_shape=out_shape, in_specs=[SMEM] * scalars + [...  12.4 us
    ppermute x19, starting transfers between devices, over_dom(): return lax.ppermute(x, 'dom', [(i, i ^ k) for i in range(n_dom)])  11.2 us
    ppermute x7, waiting for transfers between devices, over_feat(): return lax.ppermute(x, 'feat', [(i, i ^ k) for i in range(n_feat)])  10.1 us
    all_to_all x1, starting transfers between devices, body(): lax.all_to_all(back, 'feat', 0, 0, tiled=True)  7.35 us
    pallas_call x1, Pallas kernels, finish_rest(): pl.pallas_call(functools.partial(finish_rest_kernel, top), out_shape=shap...  7.22 us
  transfers between devices with their start and end apart: 30, of which 13 were waited for; matrix products, arithmetic and copies ran while one was open for 3% of the time, Pallas kernels for 28%

profile of v7, /device:TPU:0, one launch (start us, length us, event | category | flops | bytes accessed | tf_op | source)
XLA Modules:
  0.0 138.9 jit_solution(18400526087790988413)
XLA Ops:
  0.7 0.9 dynamic-slice_bitcast_fusion
  1.6 4.1 %collective-permute-start = (bf16[1,2,32,1024]{3,2,1,0:T(8,128)(2,1)S(1)}, bf16[1,2,32,1024]{3,2,1,0:T(8,128)(2,1)S(1)}, u32[]{:S(2)}, u32[]{:S(2)}) collective-permute-start(bf16[1,2,32,1024]{3,2,1,0:T(8,128)(2,1)S(1)} %maximum_bitcast_fusion.refs_0_), channel_id=1, source_target_pairs={{0,4},{1,5},{2,6},{3,7},{4,0},{5,1},{6,2},{7,3},{8,12},{9,13},{10,... | collective-permute-start | bytes 393224 | tf_op jit(solution)/shard_map/ppermute | solution.py:446
  5.7 3.9 %pack.1 = (bf16[8,9,32,128]{3,2,1,0:T(8,128)(2,1)}, bf16[128,256]{1,0:T(8,128)(2,1)}, bf16[128,256]{1,0:T(8,128)(2,1)}, bf16[128,256]{1,0:T(8,128)(2,1)}, bf16[128,256]{1,0:T(8,128)(2,1)}) custom-call(s32[1]{0:T(128)} %bitcast.me_ref, bf16[128,4096]{1,0:T(8,128)(2,1)} %x_ref.3, bf16[128,1024]{1,0:T(8,128)(2,1)} %cot_ref.1, f32[1,128]{1,0:T(1,128)} %bitcast.29, ...), custom_call_target="tpu_custom_call" | custom-call | bytes 12000000 | tf_op jit(solution)/shard_map/pack/pallas_call | solution.py:73
  9.6 2.4 %collective-permute-done.refs_1_ = bf16[1,2,32,1024]{3,2,1,0:T(8,128)(2,1)S(1)} collective-permute-done((bf16[1,2,32,1024]{3,2,1,0:T(8,128)(2,1)S(1)}, bf16[1,2,32,1024]{3,2,1,0:T(8,128)(2,1)S(1)}, u32[]{:S(2)}, u32[]{:S(2)}) %collective-permute-start) | collective-permute-done | bytes 131104 | tf_op jit(solution)/shard_map/ppermute | solution.py:446
  12.0 5.7 %all-to-all-start = ((bf16[8,9,32,128]{3,2,1,0:T(8,128)(2,1)}), bf16[8,9,32,128]{3,2,1,0:T(8,128)(2,1)S(1)}, u32[]{:S(2)}, u32[]{:S(2)}) async-start(bf16[8,9,32,128]{3,2,1,0:T(8,128)(2,1)} %get-tuple-element.58), calls=%async_computation | async-start | bytes 1179648 | tf_op jit(solution)/shard_map/all_to_all | solution.py:469
  17.7 1.6 %collective-permute-start.3 = (bf16[128,256]{1,0:T(8,128)(2,1)}, bf16[128,256]{1,0:T(8,128)(2,1)S(1)}, u32[]{:S(2)}, u32[]{:S(2)}) collective-permute-start(bf16[128,256]{1,0:T(8,128)(2,1)} %get-tuple-element.61), channel_id=1, source_target_pairs={{0,16},{8,24},{16,0},{24,8},{1,17},{9,25},{17,1},{25,9},{2,18},{10... | collective-permute-start | bytes 196616 | tf_op jit(solution)/shard_map/ppermute | solution.py:443
  21.4 0.8 convert_reduce_fusion.1.start_ref
  22.2 2.1 %collective-permute-start.1 = (bf16[2,2,32,1024]{3,2,1,0:T(8,128)(2,1)S(1)}, bf16[2,2,32,1024]{3,2,1,0:T(8,128)(2,1)S(1)}, u32[]{:S(2)}, u32[]{:S(2)}) collective-permute-start(bf16[2,2,32,1024]{3,2,1,0:T(8,128)(2,1)S(1)} %pad_maximum_fusion.1), channel_id=1, source_target_pairs={{0,2},{1,3},{2,0},{3,1},{4,6},{5,7},{6,4},{7,5},{8,10},{9,11},{10,... | collective-permute-start | bytes 786440 | tf_op jit(solution)/shard_map/ppermute | solution.py:446
  24.9 19.1 %build_dense.1 = (bf16[1024,4096]{1,0:T(8,128)(2,1)}, bf16[1024,1024]{1,0:T(8,128)(2,1)}, bf16[8,128,128]{2,1,0:T(8,128)(2,1)}) custom-call(s32[514]{0:T(1024)} %concatenate.10.order_ref, s32[321]{0:T(512)} %convert_reduce_fusion.1.start_ref, bf16[128,4096]{1,0:T(8,128)(2,1)} %x_ref.3, bf16[512,128,128]{2,1,0:T(8,128)(2,1)} %vals_hbm.1, ...), custom_call_target="tpu_custom_call" | custom-call | bytes 30000000 | tf_op jit(solution)/shard_map/build_dense/pallas_call | solution.py:134
  44.1 5.2 %all-to-all-start.1 = ((bf16[8,128,128]{2,1,0:T(8,128)(2,1)}), bf16[8,128,128]{2,1,0:T(8,128)(2,1)S(1)}, u32[]{:S(2)}, u32[]{:S(2)}) async-start(bf16[8,128,128]{2,1,0:T(8,128)(2,1)} %get-tuple-element.70), calls=%async_computation.1 | async-start | bytes 524288 | tf_op jit(solution)/shard_map/all_to_all | solution.py:496
  49.5 0.9 collective-permute-start.6
  50.4 0.8 pad_maximum_fusion
  51.3 2.0 %collective-permute-start.5 = (bf16[4,2,32,1024]{3,2,1,0:T(8,128)(2,1)}, bf16[4,2,32,1024]{3,2,1,0:T(8,128)(2,1)S(1)}, u32[]{:S(2)}, u32[]{:S(2)}) collective-permute-start(bf16[4,2,32,1024]{3,2,1,0:T(8,128)(2,1)} %pad_maximum_fusion), channel_id=1, source_target_pairs={{0,1},{1,0},{2,3},{3,2},{4,5},{5,4},{6,7},{7,6},{8,9},{9,8},{10,11... | collective-permute-start | bytes 1572872 | tf_op jit(solution)/shard_map/ppermute | solution.py:446
  53.3 4.5 %all-to-all-done.1 = bf16[8,128,128]{2,1,0:T(8,128)(2,1)S(1)} async-done(((bf16[8,128,128]{2,1,0:T(8,128)(2,1)}), bf16[8,128,128]{2,1,0:T(8,128)(2,1)S(1)}, u32[]{:S(2)}, u32[]{:S(2)}) %all-to-all-start.1) | async-done | bytes 262176 | tf_op jit(solution)/shard_map/all_to_all | solution.py:496
  57.8 2.0 %collective-permute-start.10 = (bf16[1024,128]{1,0:T(8,128)(2,1)S(1)}, bf16[1024,128]{1,0:T(8,128)(2,1)S(1)}, u32[]{:S(2)}, u32[]{:S(2)}) collective-permute-start(bf16[1024,128]{1,0:T(8,128)(2,1)S(1)} %bitcast.18), channel_id=1, source_target_pairs={{0,16},{8,24},{16,0},{24,8},{1,17},{9,25},{17,1},{25,9},{2,18},{10... | collective-permute-start | bytes 786440 | tf_op jit(solution)/shard_map/ppermute | solution.py:443
  60.9 4.6 %collective-permute-done.10.refs_10_ = bf16[1024,128]{1,0:T(8,128)(2,1)S(1)} collective-permute-done((bf16[1024,128]{1,0:T(8,128)(2,1)S(1)}, bf16[1024,128]{1,0:T(8,128)(2,1)S(1)}, u32[]{:S(2)}, u32[]{:S(2)}) %collective-permute-start.10) | collective-permute-done | bytes 262176 | tf_op jit(solution)/shard_map/ppermute | solution.py:443
  65.5 1.1 collective-permute-done.5.refs_3_
  67.0 2.6 %dense.1 = (bf16[4,256,128]{2,1,0:T(8,128)(2,1)S(1)}, bf16[2,256,128]{2,1,0:T(8,128)(2,1)S(1)}, bf16[2,256,128]{2,1,0:T(8,128)(2,1)S(1)}, bf16[2,1024,128]{2,1,0:T(8,128)(2,1)S(1)}, bf16[2,1024,128]{2,1,0:T(8,128)(2,1)S(1)}) custom-call(f32[256,128]{1,0:T(8,128)S(1)} %get-tuple-element.66.bias_ref, bf16[1,2,32,1024]{3,2,1,0:T(8,128)(2,1)S(1)} %maximum_bitcast_fusion.refs_0_, ...), custom_call_target="tpu_custom_call" | custom-call | bytes 9000000 | tf_op jit(solution)/shard_map/dense/pallas_call | solution.py:28
  69.9 2.3 %grads.1 = (bf16[2,1280,128]{2,1,0:T(8,128)(2,1)S(1)}, bf16[2,1280,128]{2,1,0:T(8,128)(2,1)}, bf16[4,32,2176]{2,1,0:T(8,128)(2,1)S(1)}, bf16[4,32,2176]{2,1,0:T(8,128)(2,1)}) custom-call(bf16[4,256,128]{2,1,0:T(8,128)(2,1)S(1)} %get-tuple-element.75.g_ref, bf16[2,256,128]{2,1,0:T(8,128)(2,1)S(1)} %get-tuple-element.76.act_even, ...), custom_call_target="tpu_custom_call" | custom-call | bytes 9000000 | tf_op jit(solution)/shard_map/grads/pallas_call | solution.py:28
  72.1 0.8 copy-done.2
  73.5 1.7 %collective-permute-start.13 = (bf16[1024,128]{1,0:T(8,128)(2,1)S(1)}, bf16[1024,128]{1,0:T(8,128)(2,1)S(1)}, u32[]{:S(2)}, u32[]{:S(2)}) collective-permute-start(bf16[1024,128]{1,0:T(8,128)(2,1)S(1)} %get-tuple-element.74), channel_id=1, source_target_pairs={{0,16},{8,24},{16,0},{24,8},{1,17},{9,25},{17,1},{25,9},{2,18},{10... | collective-permute-start | bytes 786440 | tf_op jit(solution)/shard_map/ppermute | solution.py:443
  75.2 1.7 %collective-permute-start.14 = (bf16[4,32,2176]{2,1,0:T(8,128)(2,1)}, bf16[4,32,2176]{2,1,0:T(8,128)(2,1)}, u32[]{:S(2)}, u32[]{:S(2)}) collective-permute-start(bf16[4,32,2176]{2,1,0:T(8,128)(2,1)} %get-tuple-element.80), channel_id=1, source_target_pairs={{0,1},{1,0},{2,3},{3,2},{4,5},{5,4},{6,7},{7,6},{8,9},{9,8},{10,11... | collective-permute-start | bytes 1671176 | tf_op jit(solution)/shard_map/ppermute | solution.py:446
  77.0 4.9 %collective-permute-done.13 = bf16[1024,128]{1,0:T(8,128)(2,1)S(1)} collective-permute-done((bf16[1024,128]{1,0:T(8,128)(2,1)S(1)}, bf16[1024,128]{1,0:T(8,128)(2,1)S(1)}, u32[]{:S(2)}, u32[]{:S(2)}) %collective-permute-start.13) | collective-permute-done | bytes 262176 | tf_op jit(solution)/shard_map/ppermute | solution.py:443
  81.9 0.8 add_convert_fusion
  82.6 5.7 %all-to-all-start.2 = ((bf16[8,128,128]{2,1,0:T(8,128)(2,1)}), bf16[8,128,128]{2,1,0:T(8,128)(2,1)S(1)}, u32[]{:S(2)}, u32[]{:S(2)}) async-start(bf16[8,128,128]{2,1,0:T(8,128)(2,1)} %bitcast.10), calls=%async_computation.2 | async-start | bytes 524288 | tf_op jit(solution)/shard_map/all_to_all | solution.py:569
  88.3 1.6 %collective-permute-done.14.got_ref = bf16[4,32,2176]{2,1,0:T(8,128)(2,1)} collective-permute-done((bf16[4,32,2176]{2,1,0:T(8,128)(2,1)}, bf16[4,32,2176]{2,1,0:T(8,128)(2,1)}, u32[]{:S(2)}, u32[]{:S(2)}) %collective-permute-start.14) | collective-permute-done | bytes 557088 | tf_op jit(solution)/shard_map/ppermute | solution.py:446
  89.9 1.1 copy-done.3
  91.0 1.9 %x_sum.1 = (bf16[32,2176]{1,0:T(8,128)(2,1)S(1)}, bf16[32,2176]{1,0:T(8,128)(2,1)}, bf16[32,2176]{1,0:T(8,128)(2,1)}, bf16[32,2176]{1,0:T(8,128)(2,1)}) custom-call(bf16[4,32,2176]{2,1,0:T(8,128)(2,1)S(1)} %copy-done.3, bf16[4,32,2176]{2,1,0:T(8,128)(2,1)} %collective-permute-done.14.got_ref), custom_call_target="tpu_custom_call" | custom-call | bytes 3000000 | tf_op jit(solution)/shard_map/x_sum/pallas_call | solution.py:28
  92.9 1.9 %back_pair.1 = (bf16[1536,128]{1,0:T(8,128)(2,1)S(1)}, bf16[1536,128]{1,0:T(8,128)(2,1)}) custom-call(bf16[2,1280,128]{2,1,0:T(8,128)(2,1)S(1)} %get-tuple-element.89.even_ref, bf16[2,1280,128]{2,1,0:T(8,128)(2,1)} %collective-permute-done.15.got_ref), custom_call_target="tpu_custom_call" | custom-call | bytes 3000000 | tf_op jit(solution)/shard_map/back_pair/pallas_call | solution.py:28
  95.1 2.8 %collective-permute-start.20 = (bf16[32,2176]{1,0:T(8,128)(2,1)}, bf16[32,2176]{1,0:T(8,128)(2,1)S(1)}, u32[]{:S(2)}, u32[]{:S(2)}) collective-permute-start(bf16[32,2176]{1,0:T(8,128)(2,1)} %get-tuple-element.83), channel_id=1, source_target_pairs={{0,4},{1,5},{2,6},{3,7},{4,0},{5,1},{6,2},{7,3},{8,12},{9,13},{10,... | collective-permute-start | bytes 417800 | tf_op jit(solution)/shard_map/ppermute | solution.py:446
  97.8 1.5 %collective-permute-start.21 = (bf16[32,2176]{1,0:T(8,128)(2,1)}, bf16[32,2176]{1,0:T(8,128)(2,1)}, u32[]{:S(2)}, u32[]{:S(2)}) collective-permute-start(bf16[32,2176]{1,0:T(8,128)(2,1)} %get-tuple-element.84), channel_id=1, source_target_pairs={{0,2},{1,3},{2,0},{3,1},{4,6},{5,7},{6,4},{7,5},{8,10},{9,11},{10,... | collective-permute-start | bytes 417800 | tf_op jit(solution)/shard_map/ppermute | solution.py:446
  99.9 0.7 copy-done.1
  100.6 0.6 copy-done.4
  101.3 5.0 %collective-permute-done.20.refs_1_ = bf16[32,2176]{1,0:T(8,128)(2,1)S(1)} collective-permute-done((bf16[32,2176]{1,0:T(8,128)(2,1)}, bf16[32,2176]{1,0:T(8,128)(2,1)S(1)}, u32[]{:S(2)}, u32[]{:S(2)}) %collective-permute-start.20) | collective-permute-done | bytes 139296 | tf_op jit(solution)/shard_map/ppermute | solution.py:446
  106.3 1.7 %collective-permute-start.18 = (bf16[128,256]{1,0:T(8,128)(2,1)S(1)}, bf16[128,256]{1,0:T(8,128)(2,1)S(1)}, u32[]{:S(2)}, u32[]{:S(2)}) collective-permute-start(bf16[128,256]{1,0:T(8,128)(2,1)S(1)} %get-tuple-element.98), channel_id=1, source_target_pairs={{0,16},{8,24},{16,0},{24,8},{1,17},{9,25},{17,1},{25,9},{2,18},{10... | collective-permute-start | bytes 196616 | tf_op jit(solution)/shard_map/ppermute | solution.py:443
  108.0 2.5 %collective-permute-done.18.refs_6_ = bf16[128,256]{1,0:T(8,128)(2,1)S(1)} collective-permute-done((bf16[128,256]{1,0:T(8,128)(2,1)S(1)}, bf16[128,256]{1,0:T(8,128)(2,1)S(1)}, u32[]{:S(2)}, u32[]{:S(2)}) %collective-permute-start.18) | collective-permute-done | bytes 65568 | tf_op jit(solution)/shard_map/ppermute | solution.py:443
  110.6 1.4 %collective-permute-done.19.refs_7_ = bf16[128,256]{1,0:T(8,128)(2,1)S(1)} collective-permute-done((bf16[128,256]{1,0:T(8,128)(2,1)S(1)}, bf16[128,256]{1,0:T(8,128)(2,1)S(1)}, u32[]{:S(2)}, u32[]{:S(2)}) %collective-permute-start.19) | collective-permute-done | bytes 65568 | tf_op jit(solution)/shard_map/ppermute | solution.py:443
  112.0 0.9 back_pack.1
  112.9 7.3 %all-to-all-start.3 = ((bf16[8,8,32,128]{3,2,1,0:T(8,128)(2,1)}), bf16[8,8,32,128]{3,2,1,0:T(8,128)(2,1)S(1)}, u32[]{:S(2)}, u32[]{:S(2)}) async-start(bf16[8,8,32,128]{3,2,1,0:T(8,128)(2,1)} %back_pack.1), calls=%async_computation.3 | async-start | bytes 1048576 | tf_op jit(solution)/shard_map/all_to_all | solution.py:605
  120.2 1.1 w_sum.1.refs_0_
  121.3 0.8 collective-permute-start.24
  122.1 7.2 %finish_rest.1.grads_ref = f32[128,4096]{1,0:T(8,128)} custom-call(s32[1]{0:T(128)} %bitcast.me_ref, bf16[128,1024]{1,0:T(8,128)(2,1)} %copy-done.1, s32[4,128]{1,0:T(4,128)} %bitcast.24, s32[1,128]{1,0:T(1,128)} %bitcast.27, bf16[1024,4096]{1,0:T(8,128)(2,1)} %get-tuple-element.102.refs_0_.refs_1_.refs_2_.refs_3_, ...), custom_call_target="tpu_custom_call" | custom-call | bytes 18000000 | tf_op jit(solution)/shard_map/finish_rest/pallas_call | solution.py:373
  129.9 1.0 collective-permute-done.25.refs_3_
  130.9 1.0 w_out.1
  132.0 0.6 reshape_squeeze.3
  132.6 1.9 %all-to-all-done.3 = bf16[8,8,32,128]{3,2,1,0:T(8,128)(2,1)S(1)} async-done(((bf16[8,8,32,128]{3,2,1,0:T(8,128)(2,1)}), bf16[8,8,32,128]{3,2,1,0:T(8,128)(2,1)S(1)}, u32[]{:S(2)}, u32[]{:S(2)}) %all-to-all-start.3) | async-done | bytes 524320 | tf_op jit(solution)/shard_map/all_to_all | solution.py:605
  134.5 0.8 copy-done.5
  135.4 3.5 %finish_dst.1 = (f32[128,4096]{1,0:T(8,128)}, bf16[128,1024]{1,0:T(8,128)(2,1)}) custom-call(s32[1]{0:T(128)} %bitcast.me_ref, bf16[128,1024]{1,0:T(8,128)(2,1)} %copy-done.1, s32[4,128]{1,0:T(4,128)} %bitcast.25, s32[1,128]{1,0:T(1,128)} %bitcast.28, bf16[8,256,128]{2,1,0:T(8,128)(2,1)} %bitcast.22, ...), custom_call_target="tpu_custom_call", output_to_operand_aliasing={{0}: (5, {})} | custom-call | bytes 6000000 | tf_op jit(solution)/shard_map/finish_dst/pallas_call | solution.py:391
  (67 shorter events, 6.1 us)
Async XLA Ops:
  0.6 19.6 %copy-start.13 = (s32[512]{0:T(512)S(1)}, s32[512]{0:T(512)}, u32[]{:S(2)}) copy-start(s32[512]{0:T(512)} %param.14) | copy-start | bytes 6148
  0.6 19.6 %copy-start.12 = (s32[512]{0:T(512)S(1)}, s32[512]{0:T(512)}, u32[]{:S(2)}) copy-start(s32[512]{0:T(512)} %param.15) | copy-start | bytes 6148
  1.6 10.4 %collective-permute-start = (bf16[1,2,32,1024]{3,2,1,0:T(8,128)(2,1)S(1)}, bf16[1,2,32,1024]{3,2,1,0:T(8,128)(2,1)S(1)}, u32[]{:S(2)}, u32[]{:S(2)}) collective-permute-start(bf16[1,2,32,1024]{3,2,1,0:T(8,128)(2,1)S(1)} %maximum_bitcast_fusion.refs_0_), channel_id=1, source_target_pairs={{0,4},{1,5},{2,6},{3,7},{4,0},{5,1},{6,2},{7,3},{8,12},{9,13},{10,... | collective-permute-start | bytes 393224 | tf_op jit(solution)/shard_map/ppermute | solution.py:446
  12.0 32.1 %all-to-all-start = ((bf16[8,9,32,128]{3,2,1,0:T(8,128)(2,1)}), bf16[8,9,32,128]{3,2,1,0:T(8,128)(2,1)S(1)}, u32[]{:S(2)}, u32[]{:S(2)}) async-start(bf16[8,9,32,128]{3,2,1,0:T(8,128)(2,1)} %get-tuple-element.58), calls=%async_computation | async-start | bytes 1179648 | tf_op jit(solution)/shard_map/all_to_all | solution.py:469
  17.7 6.5 %collective-permute-start.2 = (bf16[128,256]{1,0:T(8,128)(2,1)}, bf16[128,256]{1,0:T(8,128)(2,1)S(1)}, u32[]{:S(2)}, u32[]{:S(2)}) collective-permute-start(bf16[128,256]{1,0:T(8,128)(2,1)} %get-tuple-element.60), channel_id=1, source_target_pairs={{0,8},{8,0},{16,24},{24,16},{1,9},{9,1},{17,25},{25,17},{2,10},{10... | collective-permute-start | bytes 196616 | tf_op jit(solution)/shard_map/ppermute | solution.py:443
  17.7 6.5 %collective-permute-start.3 = (bf16[128,256]{1,0:T(8,128)(2,1)}, bf16[128,256]{1,0:T(8,128)(2,1)S(1)}, u32[]{:S(2)}, u32[]{:S(2)}) collective-permute-start(bf16[128,256]{1,0:T(8,128)(2,1)} %get-tuple-element.61), channel_id=1, source_target_pairs={{0,16},{8,24},{16,0},{24,8},{1,17},{9,25},{17,1},{25,9},{2,18},{10... | collective-permute-start | bytes 196616 | tf_op jit(solution)/shard_map/ppermute | solution.py:443
  19.3 5.0 %collective-permute-start.4 = (bf16[128,256]{1,0:T(8,128)(2,1)}, bf16[128,256]{1,0:T(8,128)(2,1)S(1)}, u32[]{:S(2)}, u32[]{:S(2)}) collective-permute-start(bf16[128,256]{1,0:T(8,128)(2,1)} %get-tuple-element.62), channel_id=1, source_target_pairs={{0,24},{8,16},{16,8},{24,0},{1,25},{9,17},{17,9},{25,1},{2,26},{10... | collective-permute-start | bytes 196616 | tf_op jit(solution)/shard_map/ppermute | solution.py:443
  22.2 27.2 %collective-permute-start.1 = (bf16[2,2,32,1024]{3,2,1,0:T(8,128)(2,1)S(1)}, bf16[2,2,32,1024]{3,2,1,0:T(8,128)(2,1)S(1)}, u32[]{:S(2)}, u32[]{:S(2)}) collective-permute-start(bf16[2,2,32,1024]{3,2,1,0:T(8,128)(2,1)S(1)} %pad_maximum_fusion.1), channel_id=1, source_target_pairs={{0,2},{1,3},{2,0},{3,1},{4,6},{5,7},{6,4},{7,5},{8,10},{9,11},{10,... | collective-permute-start | bytes 786440 | tf_op jit(solution)/shard_map/ppermute | solution.py:446
  24.3 0.6 copy-start.9
  24.3 0.6 copy-start.10
  24.3 0.6 copy-start.11
  44.1 13.7 %all-to-all-start.1 = ((bf16[8,128,128]{2,1,0:T(8,128)(2,1)}), bf16[8,128,128]{2,1,0:T(8,128)(2,1)S(1)}, u32[]{:S(2)}, u32[]{:S(2)}) async-start(bf16[8,128,128]{2,1,0:T(8,128)(2,1)} %get-tuple-element.70), calls=%async_computation.1 | async-start | bytes 524288 | tf_op jit(solution)/shard_map/all_to_all | solution.py:496
  49.5 10.8 %collective-permute-start.6 = (bf16[1536,128]{1,0:T(8,128)(2,1)S(1)}, bf16[1536,128]{1,0:T(8,128)(2,1)S(1)}, u32[]{:S(2)}, u32[]{:S(2)}) collective-permute-start(bf16[1536,128]{1,0:T(8,128)(2,1)S(1)} %get-tuple-element.68), channel_id=1, source_target_pairs={{0,16},{8,24},{16,0},{24,8},{1,17},{9,25},{17,1},{25,9},{2,18},{10... | collective-permute-start | bytes 1179656 | tf_op jit(solution)/shard_map/ppermute | solution.py:443
  51.3 15.3 %collective-permute-start.5 = (bf16[4,2,32,1024]{3,2,1,0:T(8,128)(2,1)}, bf16[4,2,32,1024]{3,2,1,0:T(8,128)(2,1)S(1)}, u32[]{:S(2)}, u32[]{:S(2)}) collective-permute-start(bf16[4,2,32,1024]{3,2,1,0:T(8,128)(2,1)} %pad_maximum_fusion), channel_id=1, source_target_pairs={{0,1},{1,0},{2,3},{3,2},{4,5},{5,4},{6,7},{7,6},{8,9},{9,8},{10,11... | collective-permute-start | bytes 1572872 | tf_op jit(solution)/shard_map/ppermute | solution.py:446
  57.8 7.7 %collective-permute-start.10 = (bf16[1024,128]{1,0:T(8,128)(2,1)S(1)}, bf16[1024,128]{1,0:T(8,128)(2,1)S(1)}, u32[]{:S(2)}, u32[]{:S(2)}) collective-permute-start(bf16[1024,128]{1,0:T(8,128)(2,1)S(1)} %bitcast.18), channel_id=1, source_target_pairs={{0,16},{8,24},{16,0},{24,8},{1,17},{9,25},{17,1},{25,9},{2,18},{10... | collective-permute-start | bytes 786440 | tf_op jit(solution)/shard_map/ppermute | solution.py:443
  59.8 6.8 %collective-permute-start.7 = (bf16[1280,128]{1,0:T(8,128)(2,1)S(1)}, bf16[1280,128]{1,0:T(8,128)(2,1)S(1)}, u32[]{:S(2)}, u32[]{:S(2)}) collective-permute-start(bf16[1280,128]{1,0:T(8,128)(2,1)S(1)} %get-tuple-element.69), channel_id=1, source_target_pairs={{0,8},{8,0},{16,24},{24,16},{1,9},{9,1},{17,25},{25,17},{2,10},{10... | collective-permute-start | bytes 983048 | tf_op jit(solution)/shard_map/ppermute | solution.py:443
  60.3 6.3 %collective-permute-start.8 = (bf16[1280,128]{1,0:T(8,128)(2,1)S(1)}, bf16[1280,128]{1,0:T(8,128)(2,1)S(1)}, u32[]{:S(2)}, u32[]{:S(2)}) collective-permute-start(bf16[1280,128]{1,0:T(8,128)(2,1)S(1)} %slice.8), channel_id=1, source_target_pairs={{0,8},{8,0},{16,24},{24,16},{1,9},{9,1},{17,25},{25,17},{2,10},{10... | collective-permute-start | bytes 983048 | tf_op jit(solution)/shard_map/ppermute | solution.py:443
  60.4 6.2 %collective-permute-start.9 = (bf16[1024,128]{1,0:T(8,128)(2,1)S(1)}, bf16[1024,128]{1,0:T(8,128)(2,1)S(1)}, u32[]{:S(2)}, u32[]{:S(2)}) collective-permute-start(bf16[1024,128]{1,0:T(8,128)(2,1)S(1)} %bitcast.19), channel_id=1, source_target_pairs={{0,8},{8,0},{16,24},{24,16},{1,9},{9,1},{17,25},{25,17},{2,10},{10... | collective-permute-start | bytes 786440 | tf_op jit(solution)/shard_map/ppermute | solution.py:443
  65.5 1.5 %collective-permute-start.11 = (bf16[1024,128]{1,0:T(8,128)(2,1)S(1)}, bf16[1024,128]{1,0:T(8,128)(2,1)S(1)}, u32[]{:S(2)}, u32[]{:S(2)}) collective-permute-start(bf16[1024,128]{1,0:T(8,128)(2,1)S(1)} %collective-permute-done.10.refs_10_), channel_id=1, source_target_pairs={{0,8},{8,0},{16,24},{24,16},{1,9},{9,1},{17,25},{25,17},{2,10},{10... | collective-permute-start | bytes 786440 | tf_op jit(solution)/shard_map/ppermute | solution.py:443
  69.7 3.3 %collective-permute-start.12 = (bf16[2,1024,128]{2,1,0:T(8,128)(2,1)S(1)}, bf16[2,1024,128]{2,1,0:T(8,128)(2,1)S(1)}, u32[]{:S(2)}, u32[]{:S(2)}) collective-permute-start(bf16[2,1024,128]{2,1,0:T(8,128)(2,1)S(1)} %get-tuple-element.72), channel_id=1, source_target_pairs={{0,8},{8,0},{16,24},{24,16},{1,9},{9,1},{17,25},{25,17},{2,10},{10... | collective-permute-start | bytes 1572872 | tf_op jit(solution)/shard_map/ppermute | solution.py:443
  72.1 0.8 copy-start.2
  73.1 26.4 %copy-start = (bf16[1024,1024]{1,0:T(8,128)(2,1)S(1)}, bf16[1024,1024]{1,0:T(8,128)(2,1)}, u32[]{:S(2)}) copy-start(bf16[1024,1024]{1,0:T(8,128)(2,1)} %get-tuple-element.87.ext_ref) | copy-start | bytes 6291460
  73.1 19.8 %collective-permute-start.15 = (bf16[2,1280,128]{2,1,0:T(8,128)(2,1)}, bf16[2,1280,128]{2,1,0:T(8,128)(2,1)}, u32[]{:S(2)}, u32[]{:S(2)}) collective-permute-start(bf16[2,1280,128]{2,1,0:T(8,128)(2,1)} %get-tuple-element.91), channel_id=1, source_target_pairs={{0,8},{8,0},{16,24},{24,16},{1,9},{9,1},{17,25},{25,17},{2,10},{10... | collective-permute-start | bytes 1966088 | tf_op jit(solution)/shard_map/ppermute | solution.py:443
  73.5 8.4 %collective-permute-start.13 = (bf16[1024,128]{1,0:T(8,128)(2,1)S(1)}, bf16[1024,128]{1,0:T(8,128)(2,1)S(1)}, u32[]{:S(2)}, u32[]{:S(2)}) collective-permute-start(bf16[1024,128]{1,0:T(8,128)(2,1)S(1)} %get-tuple-element.74), channel_id=1, source_target_pairs={{0,16},{8,24},{16,0},{24,8},{1,17},{9,25},{17,1},{25,9},{2,18},{10... | collective-permute-start | bytes 786440 | tf_op jit(solution)/shard_map/ppermute | solution.py:443
  75.2 14.7 %collective-permute-start.14 = (bf16[4,32,2176]{2,1,0:T(8,128)(2,1)}, bf16[4,32,2176]{2,1,0:T(8,128)(2,1)}, u32[]{:S(2)}, u32[]{:S(2)}) collective-permute-start(bf16[4,32,2176]{2,1,0:T(8,128)(2,1)} %get-tuple-element.80), channel_id=1, source_target_pairs={{0,1},{1,0},{2,3},{3,2},{4,5},{5,4},{6,7},{7,6},{8,9},{9,8},{10,11... | collective-permute-start | bytes 1671176 | tf_op jit(solution)/shard_map/ppermute | solution.py:446
  82.6 16.8 %all-to-all-start.2 = ((bf16[8,128,128]{2,1,0:T(8,128)(2,1)}), bf16[8,128,128]{2,1,0:T(8,128)(2,1)S(1)}, u32[]{:S(2)}, u32[]{:S(2)}) async-start(bf16[8,128,128]{2,1,0:T(8,128)(2,1)} %bitcast.10), calls=%async_computation.2 | async-start | bytes 524288 | tf_op jit(solution)/shard_map/all_to_all | solution.py:569
  89.9 1.1 copy-start.3
  94.8 17.2 %collective-permute-start.16 = (bf16[1536,128]{1,0:T(8,128)(2,1)}, bf16[1536,128]{1,0:T(8,128)(2,1)S(1)}, u32[]{:S(2)}, u32[]{:S(2)}) collective-permute-start(bf16[1536,128]{1,0:T(8,128)(2,1)} %get-tuple-element.95), channel_id=1, source_target_pairs={{0,16},{8,24},{16,0},{24,8},{1,17},{9,25},{17,1},{25,9},{2,18},{10... | collective-permute-start | bytes 1179656 | tf_op jit(solution)/shard_map/ppermute | solution.py:443
  95.1 11.2 %collective-permute-start.20 = (bf16[32,2176]{1,0:T(8,128)(2,1)}, bf16[32,2176]{1,0:T(8,128)(2,1)S(1)}, u32[]{:S(2)}, u32[]{:S(2)}) collective-permute-start(bf16[32,2176]{1,0:T(8,128)(2,1)} %get-tuple-element.83), channel_id=1, source_target_pairs={{0,4},{1,5},{2,6},{3,7},{4,0},{5,1},{6,2},{7,3},{8,12},{9,13},{10,... | collective-permute-start | bytes 417800 | tf_op jit(solution)/shard_map/ppermute | solution.py:446
  97.8 10.2 %collective-permute-start.21 = (bf16[32,2176]{1,0:T(8,128)(2,1)}, bf16[32,2176]{1,0:T(8,128)(2,1)}, u32[]{:S(2)}, u32[]{:S(2)}) collective-permute-start(bf16[32,2176]{1,0:T(8,128)(2,1)} %get-tuple-element.84), channel_id=1, source_target_pairs={{0,2},{1,3},{2,0},{3,1},{4,6},{5,7},{6,4},{7,5},{8,10},{9,11},{10,... | collective-permute-start | bytes 417800 | tf_op jit(solution)/shard_map/ppermute | solution.py:446
  99.3 8.7 %collective-permute-start.22 = (bf16[32,2176]{1,0:T(8,128)(2,1)}, bf16[32,2176]{1,0:T(8,128)(2,1)}, u32[]{:S(2)}, u32[]{:S(2)}) collective-permute-start(bf16[32,2176]{1,0:T(8,128)(2,1)} %get-tuple-element.85), channel_id=1, source_target_pairs={{0,6},{1,7},{2,4},{3,5},{4,2},{5,3},{6,0},{7,1},{8,14},{9,15},{10,... | collective-permute-start | bytes 417800 | tf_op jit(solution)/shard_map/ppermute | solution.py:446
  99.9 0.7 copy-start.1
  100.6 0.6 copy-start.4
  101.2 6.8 %collective-permute-start.17 = (bf16[128,256]{1,0:T(8,128)(2,1)S(1)}, bf16[128,256]{1,0:T(8,128)(2,1)S(1)}, u32[]{:S(2)}, u32[]{:S(2)}) collective-permute-start(bf16[128,256]{1,0:T(8,128)(2,1)S(1)} %get-tuple-element.97), channel_id=1, source_target_pairs={{0,8},{8,0},{16,24},{24,16},{1,9},{9,1},{17,25},{25,17},{2,10},{10... | collective-permute-start | bytes 196616 | tf_op jit(solution)/shard_map/ppermute | solution.py:443
  106.3 4.3 %collective-permute-start.18 = (bf16[128,256]{1,0:T(8,128)(2,1)S(1)}, bf16[128,256]{1,0:T(8,128)(2,1)S(1)}, u32[]{:S(2)}, u32[]{:S(2)}) collective-permute-start(bf16[128,256]{1,0:T(8,128)(2,1)S(1)} %get-tuple-element.98), channel_id=1, source_target_pairs={{0,16},{8,24},{16,0},{24,8},{1,17},{9,25},{17,1},{25,9},{2,18},{10... | collective-permute-start | bytes 196616 | tf_op jit(solution)/shard_map/ppermute | solution.py:443
  108.0 3.9 %collective-permute-start.19 = (bf16[128,256]{1,0:T(8,128)(2,1)S(1)}, bf16[128,256]{1,0:T(8,128)(2,1)S(1)}, u32[]{:S(2)}, u32[]{:S(2)}) collective-permute-start(bf16[128,256]{1,0:T(8,128)(2,1)S(1)} %get-tuple-element.99), channel_id=1, source_target_pairs={{0,24},{8,16},{16,8},{24,0},{1,25},{9,17},{17,9},{25,1},{2,26},{10... | collective-permute-start | bytes 196616 | tf_op jit(solution)/shard_map/ppermute | solution.py:443
  108.0 14.1 %copy-start.6 = (bf16[128,256]{1,0:T(8,128)(2,1)}, bf16[128,256]{1,0:T(8,128)(2,1)S(1)}, u32[]{:S(2)}) copy-start(bf16[128,256]{1,0:T(8,128)(2,1)S(1)} %collective-permute-done.17.refs_5_) | copy-start | bytes 196612
  110.5 11.6 %copy-start.7 = (bf16[128,256]{1,0:T(8,128)(2,1)}, bf16[128,256]{1,0:T(8,128)(2,1)S(1)}, u32[]{:S(2)}) copy-start(bf16[128,256]{1,0:T(8,128)(2,1)S(1)} %collective-permute-done.18.refs_6_) | copy-start | bytes 196612
  112.0 10.2 %copy-start.8 = (bf16[128,256]{1,0:T(8,128)(2,1)}, bf16[128,256]{1,0:T(8,128)(2,1)S(1)}, u32[]{:S(2)}) copy-start(bf16[128,256]{1,0:T(8,128)(2,1)S(1)} %collective-permute-done.19.refs_7_) | copy-start | bytes 196612
  112.9 21.7 %all-to-all-start.3 = ((bf16[8,8,32,128]{3,2,1,0:T(8,128)(2,1)}), bf16[8,8,32,128]{3,2,1,0:T(8,128)(2,1)S(1)}, u32[]{:S(2)}, u32[]{:S(2)}) async-start(bf16[8,8,32,128]{3,2,1,0:T(8,128)(2,1)} %back_pack.1), calls=%async_computation.3 | async-start | bytes 1048576 | tf_op jit(solution)/shard_map/all_to_all | solution.py:605
  121.3 8.1 %collective-permute-start.24 = (bf16[32,2176]{1,0:T(8,128)(2,1)S(1)}, bf16[32,2176]{1,0:T(8,128)(2,1)S(1)}, u32[]{:S(2)}, u32[]{:S(2)}) collective-permute-start(bf16[32,2176]{1,0:T(8,128)(2,1)S(1)} %w_sum.1.refs_0_), channel_id=1, source_target_pairs={{0,16},{8,24},{16,0},{24,8},{1,17},{9,25},{17,1},{25,9},{2,18},{10... | collective-permute-start | bytes 417800 | tf_op jit(solution)/shard_map/ppermute | solution.py:443
  122.1 7.8 %collective-permute-start.23 = (bf16[32,2176]{1,0:T(8,128)(2,1)S(1)}, bf16[32,2176]{1,0:T(8,128)(2,1)S(1)}, u32[]{:S(2)}, u32[]{:S(2)}) collective-permute-start(bf16[32,2176]{1,0:T(8,128)(2,1)S(1)} %w_sum.1.refs_0_), channel_id=1, source_target_pairs={{0,8},{8,0},{16,24},{24,16},{1,9},{9,1},{17,25},{25,17},{2,10},{10... | collective-permute-start | bytes 417800 | tf_op jit(solution)/shard_map/ppermute | solution.py:443
  129.4 1.6 %collective-permute-start.25 = (bf16[32,2176]{1,0:T(8,128)(2,1)S(1)}, bf16[32,2176]{1,0:T(8,128)(2,1)S(1)}, u32[]{:S(2)}, u32[]{:S(2)}) collective-permute-start(bf16[32,2176]{1,0:T(8,128)(2,1)S(1)} %collective-permute-done.24.refs_2_), channel_id=1, source_target_pairs={{0,8},{8,0},{16,24},{24,16},{1,9},{9,1},{17,25},{25,17},{2,10},{10... | collective-permute-start | bytes 417800 | tf_op jit(solution)/shard_map/ppermute | solution.py:443
  134.5 0.8 copy-start.5

commit v8 on v7

--- a/solution.py
+++ b/solution.py
@@ -11,6 +11,7 @@
 BF = jnp.bfloat16
 F32 = jnp.float32
 MIB = 1 << 20
+WIDE = 512
 VMEM = pl.BlockSpec(memory_space=pltpu.VMEM)
 SMEM = pl.BlockSpec(memory_space=pltpu.SMEM)
 
@@ -87,6 +88,7 @@
     step = pl.program_id(0)
     slots = vals_hbm.shape[0]
     n_src = n_own + ext_ref.shape[1] // T
+    tiles, wide = own_ref.shape[1] // T, own_ref.shape[2]
     chunks = sems.shape[0]
     per = slots // chunks
 
@@ -102,10 +104,10 @@
         for i in range(chunks):
             piece(i).wait()
 
-    for v in range(own_ref.shape[0] // T):
+    for v in range(tiles):
         rows = slice(v * T, (v + 1) * T)
         for s in range(n_src):
-            p = (step * (own_ref.shape[0] // T) + v) * n_src + s
+            p = (step * tiles + v) * n_src + s
             first, last = start_ref[p], start_ref[p + 1]
             one = jnp.where(last > first, order_ref[first], slots)
             two = jnp.where(last > first + 1, order_ref[first + 1], slots)
@@ -116,11 +118,14 @@
 
             total = lax.fori_loop(first + 2, last, more, total).astype(BF)
             if s < n_own:
-                own_ref[rows, s * T : (s + 1) * T] = total
+                at = s * T % wide
+                own_ref[s * T // wide, rows, at : at + T] = total
             else:
                 ext_ref[rows, (s - n_own) * T : (s - n_own + 1) * T] = total
     halo = jnp.concatenate([r[...] for r in halo_refs], axis=1)
-    total = dot(x_ref[...], own_ref[...], ((1,), (1,)))
+    total = 0.0
+    for b in range(own_ref.shape[0]):
+        total += dot(x_ref[:, b * wide : (b + 1) * wide], own_ref[b], ((1,), (1,)))
     total = (total + dot(halo, ext_ref[...], ((1,), (1,)))).astype(BF)
     piece_n = agg_ref.shape[2]
     for b in range(agg_ref.shape[0]):
@@ -134,7 +139,7 @@
     return pl.pallas_call(
         functools.partial(build_kernel, n_own),
         out_shape=(
-            shape(n_dst * T, n_own * T),
+            shape(n_own * T // WIDE, n_dst * T, WIDE),
             shape(n_dst * T, ext),
             shape(n_feat, rows, piece),
         ),
@@ -143,7 +148,7 @@
             grid=(n_dst // 2,),
             in_specs=[VMEM, pl.BlockSpec(memory_space=pl.ANY)] + [VMEM] * len(halos),
             out_specs=[
-                pl.BlockSpec((2 * T, n_own * T), lambda u, *_: (u, 0)),
+                pl.BlockSpec((n_own * T // WIDE, 2 * T, WIDE), lambda u, *_: (0, u, 0)),
                 pl.BlockSpec((2 * T, ext), lambda u, *_: (u, 0)),
                 pl.BlockSpec((2 * T // piece, rows, piece), lambda u, *_: (u, 0, 0)),
             ],
@@ -353,15 +358,13 @@
     out_ref[...] = add_returned(total, at, me_ref, send_ref, hub_ref, ret_refs)
 
 
-WIDE = 512
-
-
-def column(rows, first, at=0):
-    return pl.BlockSpec((rows, WIDE), lambda i: (at, i + first))
+def column(rows, first):
+    return pl.BlockSpec((rows, WIDE), lambda i: (0, i + first))
 
 
 def row_blocks(n_dst, first):
-    return [column(n_dst // SPLIT, first, r) for r in range(SPLIT)]
+    block = (None, n_dst // SPLIT, WIDE)
+    return [pl.BlockSpec(block, lambda i, r=r: (i + first, r, 0)) for r in range(SPLIT)]
 
 
 def fixed(x):
@@ -369,7 +372,7 @@
 
 
 def finish_rest(me, ga, own, ret, sends, hubs, n_dst):
-    rows, n, top = ga.shape[0], own.shape[1], n_dst // WIDE
+    rows, n, top = ga.shape[0], own.shape[0] * WIDE, n_dst // WIDE
     return pl.pallas_call(
         functools.partial(finish_rest_kernel, top),
         out_shape=shape(rows, n, kind=F32),
@@ -568,7 +571,6 @@
 
     gagg = lax.all_to_all(gagg, "feat", 0, 0, tiled=True)
     parts = whole_call(pair_kernel, "x_sum", 1.0, [shape(sub, 2 * width + T)] * nz, parts, from_x)
-    from_core = after(from_core, parts)
     back = whole_call(
         functools.partial(back_pair_kernel, width),
         "back_pair",
@@ -590,7 +592,7 @@
         a_ext,
     )
     returned = [halo_grad[0]] + [over_dom(halo_grad[k], k) for k in range(1, n_dom)]
-    back = after(back, returned, parts)
+    back = after(back, halo_grad, parts)
 
     back = whole_call(
         functools.partial(back_pack_kernel, blocks),

time: 140 us -> 141 us (level)
  starting transfers between devices: 49.6 us -> 46.6 us
  local copies, waits for them, and re-layouts: 6.85 us -> 8.73 us
  waiting for transfers between devices: 31.9 us -> 33.4 us
    ppermute x19, waiting for transfers between devices: 15.3 us -> 19.8 us  [over_dom(): return lax.ppermute(x, 'dom', [(i, i ^ k) for i in range(n_dom)])]
    ppermute x7, waiting for transfers between devices: 10.1 us -> 6.77 us  [over_feat(): return lax.ppermute(x, 'feat', [(i, i ^ k) for i in range(n_feat)])]
    all_to_all x1, waiting for transfers between devices: 1.92 us -> 0.01 us  [body(): lax.all_to_all(back, 'feat', 0, 0, tiled=True)]
    unnamed x28 -> x36, local copies, waits for them, and re-layouts: 4.65 us -> 6.53 us
  transfers between devices with their start and end apart: 30 -> 30, of which waited for: 13 -> 12; matrix products, arithmetic and copies ran while one was open for 3% -> 3% of each run, Pallas kernels for 28% -> 28%
where the time goes in v8:
time: 141 us; the launch traced here: 140 us
  starting transfers between devices  46.6 us (33%)
  Pallas kernels  46.5 us (33%)
  waiting for transfers between devices  33.4 us (24%)
  local copies, waits for them, and re-layouts  8.73 us (6%)
  other arithmetic  2.93 us (2%)
  between operations  1.53 us (1%)
    ppermute x19, waiting for transfers between devices, over_dom(): return lax.ppermute(x, 'dom', [(i, i ^ k) for i in range(n_dom)])  19.8 us
    pallas_call x1, Pallas kernels, build_dense(): pl.pallas_call(functools.partial(build_kernel, n_own), out_shape=(shape(n...  19.5 us
    ppermute x7, starting transfers between devices, over_feat(): return lax.ppermute(x, 'feat', [(i, i ^ k) for i in range(n_feat)])  14 us
    pallas_call x10, Pallas kernels, whole_call(): pl.pallas_call(kernel, out_shape=out_shape, in_specs=[SMEM] * scalars + [...  12.4 us
    ppermute x19, starting transfers between devices, over_dom(): return lax.ppermute(x, 'dom', [(i, i ^ k) for i in range(n_dom)])  9.97 us
    pallas_call x1, Pallas kernels, finish_rest(): pl.pallas_call(functools.partial(finish_rest_kernel, top), out_shape=shap...  7.16 us
    ppermute x7, waiting for transfers between devices, over_feat(): return lax.ppermute(x, 'feat', [(i, i ^ k) for i in range(n_feat)])  6.77 us
    unnamed x36, local copies, waits for them, and re-layouts  6.53 us
  transfers between devices with their start and end apart: 30, of which 12 were waited for; matrix products, arithmetic and copies ran while one was open for 3% of the time, Pallas kernels for 28%

profile of v8, /device:TPU:0, one launch (start us, length us, event | category | flops | bytes accessed | tf_op | source)
XLA Modules:
  0.0 139.7 jit_solution(5983547121209392285)
XLA Ops:
  0.7 0.9 dynamic-slice_bitcast_fusion
  1.6 4.1 %collective-permute-start = (bf16[1,2,32,1024]{3,2,1,0:T(8,128)(2,1)S(1)}, bf16[1,2,32,1024]{3,2,1,0:T(8,128)(2,1)S(1)}, u32[]{:S(2)}, u32[]{:S(2)}) collective-permute-start(bf16[1,2,32,1024]{3,2,1,0:T(8,128)(2,1)S(1)} %maximum_bitcast_fusion.refs_0_), channel_id=1, source_target_pairs={{0,4},{1,5},{2,6},{3,7},{4,0},{5,1},{6,2},{7,3},{8,12},{9,13},{10,... | collective-permute-start | bytes 393224 | tf_op jit(solution)/shard_map/ppermute | solution.py:449
  5.7 3.9 %pack.1 = (bf16[8,9,32,128]{3,2,1,0:T(8,128)(2,1)}, bf16[128,256]{1,0:T(8,128)(2,1)}, bf16[128,256]{1,0:T(8,128)(2,1)}, bf16[128,256]{1,0:T(8,128)(2,1)}, bf16[128,256]{1,0:T(8,128)(2,1)}) custom-call(s32[1]{0:T(128)} %bitcast.me_ref, bf16[128,4096]{1,0:T(8,128)(2,1)} %x_ref.3, bf16[128,1024]{1,0:T(8,128)(2,1)} %cot_ref.1, f32[1,128]{1,0:T(1,128)} %bitcast.29, ...), custom_call_target="tpu_custom_call" | custom-call | bytes 12000000 | tf_op jit(solution)/shard_map/pack/pallas_call | solution.py:74
  9.6 2.4 %collective-permute-done.refs_1_ = bf16[1,2,32,1024]{3,2,1,0:T(8,128)(2,1)S(1)} collective-permute-done((bf16[1,2,32,1024]{3,2,1,0:T(8,128)(2,1)S(1)}, bf16[1,2,32,1024]{3,2,1,0:T(8,128)(2,1)S(1)}, u32[]{:S(2)}, u32[]{:S(2)}) %collective-permute-start) | collective-permute-done | bytes 131104 | tf_op jit(solution)/shard_map/ppermute | solution.py:449
  12.0 5.7 %all-to-all-start = ((bf16[8,9,32,128]{3,2,1,0:T(8,128)(2,1)}), bf16[8,9,32,128]{3,2,1,0:T(8,128)(2,1)S(1)}, u32[]{:S(2)}, u32[]{:S(2)}) async-start(bf16[8,9,32,128]{3,2,1,0:T(8,128)(2,1)} %get-tuple-element.57), calls=%async_computation | async-start | bytes 1179648 | tf_op jit(solution)/shard_map/all_to_all | solution.py:472
  17.7 1.6 %collective-permute-start.3 = (bf16[128,256]{1,0:T(8,128)(2,1)}, bf16[128,256]{1,0:T(8,128)(2,1)S(1)}, u32[]{:S(2)}, u32[]{:S(2)}) collective-permute-start(bf16[128,256]{1,0:T(8,128)(2,1)} %get-tuple-element.60), channel_id=1, source_target_pairs={{0,16},{8,24},{16,0},{24,8},{1,17},{9,25},{17,1},{25,9},{2,18},{10... | collective-permute-start | bytes 196616 | tf_op jit(solution)/shard_map/ppermute | solution.py:446
  21.4 0.8 convert_reduce_fusion.1.start_ref
  22.2 2.1 %collective-permute-start.1 = (bf16[2,2,32,1024]{3,2,1,0:T(8,128)(2,1)S(1)}, bf16[2,2,32,1024]{3,2,1,0:T(8,128)(2,1)S(1)}, u32[]{:S(2)}, u32[]{:S(2)}) collective-permute-start(bf16[2,2,32,1024]{3,2,1,0:T(8,128)(2,1)S(1)} %pad_maximum_fusion.1), channel_id=1, source_target_pairs={{0,2},{1,3},{2,0},{3,1},{4,6},{5,7},{6,4},{7,5},{8,10},{9,11},{10,... | collective-permute-start | bytes 786440 | tf_op jit(solution)/shard_map/ppermute | solution.py:449
  24.9 19.5 %build_dense.1 = (bf16[8,1024,512]{2,1,0:T(8,128)(2,1)}, bf16[1024,1024]{1,0:T(8,128)(2,1)}, bf16[8,128,128]{2,1,0:T(8,128)(2,1)}) custom-call(s32[514]{0:T(1024)} %concatenate.10.order_ref, s32[321]{0:T(512)} %convert_reduce_fusion.1.start_ref, bf16[128,4096]{1,0:T(8,128)(2,1)} %x_ref.3, bf16[512,128,128]{2,1,0:T(8,128)(2,1)} %vals_hbm.1, ...), custom_call_target="tpu_custom_call" | custom-call | bytes 30000000 | tf_op jit(solution)/shard_map/build_dense/pallas_call | solution.py:139
  44.5 5.2 %all-to-all-start.1 = ((bf16[8,128,128]{2,1,0:T(8,128)(2,1)}), bf16[8,128,128]{2,1,0:T(8,128)(2,1)S(1)}, u32[]{:S(2)}, u32[]{:S(2)}) async-start(bf16[8,128,128]{2,1,0:T(8,128)(2,1)} %get-tuple-element.69), calls=%async_computation.1 | async-start | bytes 524288 | tf_op jit(solution)/shard_map/all_to_all | solution.py:499
  49.9 1.4 collective-permute-start.6
  51.2 0.8 pad_maximum_fusion
  52.1 2.0 %collective-permute-start.5 = (bf16[4,2,32,1024]{3,2,1,0:T(8,128)(2,1)}, bf16[4,2,32,1024]{3,2,1,0:T(8,128)(2,1)S(1)}, u32[]{:S(2)}, u32[]{:S(2)}) collective-permute-start(bf16[4,2,32,1024]{3,2,1,0:T(8,128)(2,1)} %pad_maximum_fusion), channel_id=1, source_target_pairs={{0,1},{1,0},{2,3},{3,2},{4,5},{5,4},{6,7},{7,6},{8,9},{9,8},{10,11... | collective-permute-start | bytes 1572872 | tf_op jit(solution)/shard_map/ppermute | solution.py:449
  54.1 5.7 %all-to-all-done.1 = bf16[8,128,128]{2,1,0:T(8,128)(2,1)S(1)} async-done(((bf16[8,128,128]{2,1,0:T(8,128)(2,1)}), bf16[8,128,128]{2,1,0:T(8,128)(2,1)S(1)}, u32[]{:S(2)}, u32[]{:S(2)}) %all-to-all-start.1) | async-done | bytes 262176 | tf_op jit(solution)/shard_map/all_to_all | solution.py:499
  60.3 1.5 %collective-permute-done.6.refs_5_ = bf16[1536,128]{1,0:T(8,128)(2,1)S(1)} collective-permute-done((bf16[1536,128]{1,0:T(8,128)(2,1)S(1)}, bf16[1536,128]{1,0:T(8,128)(2,1)S(1)}, u32[]{:S(2)}, u32[]{:S(2)}) %collective-permute-start.6) | collective-permute-done | bytes 393248 | tf_op jit(solution)/shard_map/ppermute | solution.py:446
  62.3 5.6 %collective-permute-done.10.refs_10_ = bf16[1024,128]{1,0:T(8,128)(2,1)S(1)} collective-permute-done((bf16[1024,128]{1,0:T(8,128)(2,1)S(1)}, bf16[1024,128]{1,0:T(8,128)(2,1)S(1)}, u32[]{:S(2)}, u32[]{:S(2)}) %collective-permute-start.10) | collective-permute-done | bytes 262176 | tf_op jit(solution)/shard_map/ppermute | solution.py:446
  68.0 1.5 %collective-permute-done.11.refs_11_ = bf16[1024,128]{1,0:T(8,128)(2,1)S(1)} collective-permute-done((bf16[1024,128]{1,0:T(8,128)(2,1)S(1)}, bf16[1024,128]{1,0:T(8,128)(2,1)S(1)}, u32[]{:S(2)}, u32[]{:S(2)}) %collective-permute-start.11) | collective-permute-done | bytes 262176 | tf_op jit(solution)/shard_map/ppermute | solution.py:446
  69.5 2.6 %dense.1 = (bf16[4,256,128]{2,1,0:T(8,128)(2,1)S(1)}, bf16[2,256,128]{2,1,0:T(8,128)(2,1)S(1)}, bf16[2,256,128]{2,1,0:T(8,128)(2,1)S(1)}, bf16[2,1024,128]{2,1,0:T(8,128)(2,1)S(1)}, bf16[2,1024,128]{2,1,0:T(8,128)(2,1)S(1)}) custom-call(f32[256,128]{1,0:T(8,128)S(1)} %get-tuple-element.65.bias_ref, bf16[1,2,32,1024]{3,2,1,0:T(8,128)(2,1)S(1)} %maximum_bitcast_fusion.refs_0_, ...), custom_call_target="tpu_custom_call" | custom-call | bytes 9000000 | tf_op jit(solution)/shard_map/dense/pallas_call | solution.py:29
  72.3 2.3 %grads.1 = (bf16[2,1280,128]{2,1,0:T(8,128)(2,1)S(1)}, bf16[2,1280,128]{2,1,0:T(8,128)(2,1)}, bf16[4,32,2176]{2,1,0:T(8,128)(2,1)S(1)}, bf16[4,32,2176]{2,1,0:T(8,128)(2,1)}) custom-call(bf16[4,256,128]{2,1,0:T(8,128)(2,1)S(1)} %get-tuple-element.74.g_ref, bf16[2,256,128]{2,1,0:T(8,128)(2,1)S(1)} %get-tuple-element.75.act_even, ...), custom_call_target="tpu_custom_call" | custom-call | bytes 9000000 | tf_op jit(solution)/shard_map/grads/pallas_call | solution.py:29
  74.6 0.8 copy-done.2
  76.3 1.5 %collective-permute-start.14 = (bf16[4,32,2176]{2,1,0:T(8,128)(2,1)}, bf16[4,32,2176]{2,1,0:T(8,128)(2,1)}, u32[]{:S(2)}, u32[]{:S(2)}) collective-permute-start(bf16[4,32,2176]{2,1,0:T(8,128)(2,1)} %get-tuple-element.79), channel_id=1, source_target_pairs={{0,1},{1,0},{2,3},{3,2},{4,5},{5,4},{6,7},{7,6},{8,9},{9,8},{10,11... | collective-permute-start | bytes 1671176 | tf_op jit(solution)/shard_map/ppermute | solution.py:449
  77.7 6.6 %collective-permute-done.13 = bf16[1024,128]{1,0:T(8,128)(2,1)S(1)} collective-permute-done((bf16[1024,128]{1,0:T(8,128)(2,1)S(1)}, bf16[1024,128]{1,0:T(8,128)(2,1)S(1)}, u32[]{:S(2)}, u32[]{:S(2)}) %collective-permute-start.13) | collective-permute-done | bytes 262176 | tf_op jit(solution)/shard_map/ppermute | solution.py:446
  84.3 0.8 add_convert_fusion
  85.1 5.1 %all-to-all-start.2 = ((bf16[8,128,128]{2,1,0:T(8,128)(2,1)}), bf16[8,128,128]{2,1,0:T(8,128)(2,1)S(1)}, u32[]{:S(2)}, u32[]{:S(2)}) async-start(bf16[8,128,128]{2,1,0:T(8,128)(2,1)} %bitcast.10), calls=%async_computation.2 | async-start | bytes 524288 | tf_op jit(solution)/shard_map/all_to_all | solution.py:572
  90.3 1.9 %back_pair.1 = (bf16[1536,128]{1,0:T(8,128)(2,1)S(1)}, bf16[1536,128]{1,0:T(8,128)(2,1)}) custom-call(bf16[2,1280,128]{2,1,0:T(8,128)(2,1)S(1)} %get-tuple-element.88.even_ref, bf16[2,1280,128]{2,1,0:T(8,128)(2,1)} %collective-permute-done.15.got_ref), custom_call_target="tpu_custom_call" | custom-call | bytes 3000000 | tf_op jit(solution)/shard_map/back_pair/pallas_call | solution.py:29
  92.5 1.1 copy-done.3
  93.5 1.8 %x_sum.1 = (bf16[32,2176]{1,0:T(8,128)(2,1)S(1)}, bf16[32,2176]{1,0:T(8,128)(2,1)}, bf16[32,2176]{1,0:T(8,128)(2,1)}, bf16[32,2176]{1,0:T(8,128)(2,1)}) custom-call(bf16[4,32,2176]{2,1,0:T(8,128)(2,1)S(1)} %copy-done.3, bf16[4,32,2176]{2,1,0:T(8,128)(2,1)} %collective-permute-done.14.got_ref), custom_call_target="tpu_custom_call" | custom-call | bytes 3000000 | tf_op jit(solution)/shard_map/x_sum/pallas_call | solution.py:29
  95.4 2.9 %collective-permute-start.17 = (bf16[32,2176]{1,0:T(8,128)(2,1)}, bf16[32,2176]{1,0:T(8,128)(2,1)S(1)}, u32[]{:S(2)}, u32[]{:S(2)}) collective-permute-start(bf16[32,2176]{1,0:T(8,128)(2,1)} %get-tuple-element.82), channel_id=1, source_target_pairs={{0,4},{1,5},{2,6},{3,7},{4,0},{5,1},{6,2},{7,3},{8,12},{9,13},{10,... | collective-permute-start | bytes 417800 | tf_op jit(solution)/shard_map/ppermute | solution.py:449
  98.3 1.5 %collective-permute-start.18 = (bf16[32,2176]{1,0:T(8,128)(2,1)}, bf16[32,2176]{1,0:T(8,128)(2,1)}, u32[]{:S(2)}, u32[]{:S(2)}) collective-permute-start(bf16[32,2176]{1,0:T(8,128)(2,1)} %get-tuple-element.83), channel_id=1, source_target_pairs={{0,2},{1,3},{2,0},{3,1},{4,6},{5,7},{6,4},{7,5},{8,10},{9,11},{10,... | collective-permute-start | bytes 417800 | tf_op jit(solution)/shard_map/ppermute | solution.py:449
  99.7 1.1 all-to-all-done.2.ga_ref
  101.4 0.7 copy-done.1
  102.1 0.6 copy-done.4
  102.7 0.6 copy-done.5
  103.3 0.6 copy-done.7
  103.9 4.3 %collective-permute-done.17.refs_1_ = bf16[32,2176]{1,0:T(8,128)(2,1)S(1)} collective-permute-done((bf16[32,2176]{1,0:T(8,128)(2,1)}, bf16[32,2176]{1,0:T(8,128)(2,1)S(1)}, u32[]{:S(2)}, u32[]{:S(2)}) %collective-permute-start.17) | collective-permute-done | bytes 139296 | tf_op jit(solution)/shard_map/ppermute | solution.py:449
  108.3 0.9 back_pack.1
  109.2 6.4 %all-to-all-start.3 = ((bf16[8,8,32,128]{3,2,1,0:T(8,128)(2,1)}), bf16[8,8,32,128]{3,2,1,0:T(8,128)(2,1)S(1)}, u32[]{:S(2)}, u32[]{:S(2)}) async-start(bf16[8,8,32,128]{3,2,1,0:T(8,128)(2,1)} %back_pack.1), calls=%async_computation.3 | async-start | bytes 1048576 | tf_op jit(solution)/shard_map/all_to_all | solution.py:607
  115.7 1.1 w_sum.1.refs_0_
  116.7 1.8 %collective-permute-start.24 = (bf16[32,2176]{1,0:T(8,128)(2,1)S(1)}, bf16[32,2176]{1,0:T(8,128)(2,1)S(1)}, u32[]{:S(2)}, u32[]{:S(2)}) collective-permute-start(bf16[32,2176]{1,0:T(8,128)(2,1)S(1)} %w_sum.1.refs_0_), channel_id=1, source_target_pairs={{0,16},{8,24},{16,0},{24,8},{1,17},{9,25},{17,1},{25,9},{2,18},{10... | collective-permute-start | bytes 417800 | tf_op jit(solution)/shard_map/ppermute | solution.py:446
  118.9 1.5 %collective-permute-start.22 = (bf16[128,256]{1,0:T(8,128)(2,1)S(1)}, bf16[128,256]{1,0:T(8,128)(2,1)S(1)}, u32[]{:S(2)}, u32[]{:S(2)}) collective-permute-start(bf16[128,256]{1,0:T(8,128)(2,1)S(1)} %get-tuple-element.97), channel_id=1, source_target_pairs={{0,24},{8,16},{16,8},{24,0},{1,25},{9,17},{17,9},{25,1},{2,26},{10... | collective-permute-start | bytes 196616 | tf_op jit(solution)/shard_map/ppermute | solution.py:446
  120.7 2.8 %collective-permute-done.21.refs_6_ = bf16[128,256]{1,0:T(8,128)(2,1)S(1)} collective-permute-done((bf16[128,256]{1,0:T(8,128)(2,1)S(1)}, bf16[128,256]{1,0:T(8,128)(2,1)S(1)}, u32[]{:S(2)}, u32[]{:S(2)}) %collective-permute-start.21) | collective-permute-done | bytes 65568 | tf_op jit(solution)/shard_map/ppermute | solution.py:446
  123.6 0.8 collective-permute-done.22.refs_7_
  124.4 0.6 copy-done.12
  125.0 7.2 %finish_rest.1.grads_ref = f32[128,4096]{1,0:T(8,128)} custom-call(s32[1]{0:T(128)} %bitcast.me_ref, bf16[128,1024]{1,0:T(8,128)(2,1)} %copy-done.1, s32[4,128]{1,0:T(4,128)} %bitcast.24, s32[1,128]{1,0:T(1,128)} %bitcast.27, bf16[8,1024,512]{2,1,0:T(8,128)(2,1)} %get-tuple-element.100.refs_0_.refs_1_.refs_2_.refs_3_, ...), custom_call_target="tpu_custom_call" | custom-call | bytes 18000000 | tf_op jit(solution)/shard_map/finish_rest/pallas_call | solution.py:376
  132.7 1.0 collective-permute-done.25.refs_3_
  133.7 1.0 w_out.1
  135.4 0.8 copy-done.9
  136.2 3.5 %finish_dst.1 = (f32[128,4096]{1,0:T(8,128)}, bf16[128,1024]{1,0:T(8,128)(2,1)}) custom-call(s32[1]{0:T(128)} %bitcast.me_ref, bf16[128,1024]{1,0:T(8,128)(2,1)} %copy-done.1, s32[4,128]{1,0:T(4,128)} %bitcast.25, s32[1,128]{1,0:T(1,128)} %bitcast.28, bf16[8,256,128]{2,1,0:T(8,128)(2,1)} %bitcast.22, ...), custom_call_target="tpu_custom_call", output_to_operand_aliasing={{0}: (5, {})} | custom-call | bytes 6000000 | tf_op jit(solution)/shard_map/finish_dst/pallas_call | solution.py:394
  (75 shorter events, 7.2 us)
Async XLA Ops:
  0.6 19.6 %copy-start.17 = (s32[512]{0:T(512)S(1)}, s32[512]{0:T(512)}, u32[]{:S(2)}) copy-start(s32[512]{0:T(512)} %param.14) | copy-start | bytes 6148
  0.6 19.6 %copy-start.16 = (s32[512]{0:T(512)S(1)}, s32[512]{0:T(512)}, u32[]{:S(2)}) copy-start(s32[512]{0:T(512)} %param.15) | copy-start | bytes 6148
  1.6 10.4 %collective-permute-start = (bf16[1,2,32,1024]{3,2,1,0:T(8,128)(2,1)S(1)}, bf16[1,2,32,1024]{3,2,1,0:T(8,128)(2,1)S(1)}, u32[]{:S(2)}, u32[]{:S(2)}) collective-permute-start(bf16[1,2,32,1024]{3,2,1,0:T(8,128)(2,1)S(1)} %maximum_bitcast_fusion.refs_0_), channel_id=1, source_target_pairs={{0,4},{1,5},{2,6},{3,7},{4,0},{5,1},{6,2},{7,3},{8,12},{9,13},{10,... | collective-permute-start | bytes 393224 | tf_op jit(solution)/shard_map/ppermute | solution.py:449
  12.0 32.5 %all-to-all-start = ((bf16[8,9,32,128]{3,2,1,0:T(8,128)(2,1)}), bf16[8,9,32,128]{3,2,1,0:T(8,128)(2,1)S(1)}, u32[]{:S(2)}, u32[]{:S(2)}) async-start(bf16[8,9,32,128]{3,2,1,0:T(8,128)(2,1)} %get-tuple-element.57), calls=%async_computation | async-start | bytes 1179648 | tf_op jit(solution)/shard_map/all_to_all | solution.py:472
  17.7 6.5 %collective-permute-start.2 = (bf16[128,256]{1,0:T(8,128)(2,1)}, bf16[128,256]{1,0:T(8,128)(2,1)S(1)}, u32[]{:S(2)}, u32[]{:S(2)}) collective-permute-start(bf16[128,256]{1,0:T(8,128)(2,1)} %get-tuple-element.59), channel_id=1, source_target_pairs={{0,8},{8,0},{16,24},{24,16},{1,9},{9,1},{17,25},{25,17},{2,10},{10... | collective-permute-start | bytes 196616 | tf_op jit(solution)/shard_map/ppermute | solution.py:446
  17.7 6.5 %collective-permute-start.3 = (bf16[128,256]{1,0:T(8,128)(2,1)}, bf16[128,256]{1,0:T(8,128)(2,1)S(1)}, u32[]{:S(2)}, u32[]{:S(2)}) collective-permute-start(bf16[128,256]{1,0:T(8,128)(2,1)} %get-tuple-element.60), channel_id=1, source_target_pairs={{0,16},{8,24},{16,0},{24,8},{1,17},{9,25},{17,1},{25,9},{2,18},{10... | collective-permute-start | bytes 196616 | tf_op jit(solution)/shard_map/ppermute | solution.py:446
  19.3 5.0 %collective-permute-start.4 = (bf16[128,256]{1,0:T(8,128)(2,1)}, bf16[128,256]{1,0:T(8,128)(2,1)S(1)}, u32[]{:S(2)}, u32[]{:S(2)}) collective-permute-start(bf16[128,256]{1,0:T(8,128)(2,1)} %get-tuple-element.61), channel_id=1, source_target_pairs={{0,24},{8,16},{16,8},{24,0},{1,25},{9,17},{17,9},{25,1},{2,26},{10... | collective-permute-start | bytes 196616 | tf_op jit(solution)/shard_map/ppermute | solution.py:446
  22.2 27.6 %collective-permute-start.1 = (bf16[2,2,32,1024]{3,2,1,0:T(8,128)(2,1)S(1)}, bf16[2,2,32,1024]{3,2,1,0:T(8,128)(2,1)S(1)}, u32[]{:S(2)}, u32[]{:S(2)}) collective-permute-start(bf16[2,2,32,1024]{3,2,1,0:T(8,128)(2,1)S(1)} %pad_maximum_fusion.1), channel_id=1, source_target_pairs={{0,2},{1,3},{2,0},{3,1},{4,6},{5,7},{6,4},{7,5},{8,10},{9,11},{10,... | collective-permute-start | bytes 786440 | tf_op jit(solution)/shard_map/ppermute | solution.py:449
  24.3 0.6 copy-start.13
  24.3 0.6 copy-start.14
  24.3 0.6 copy-start.15
  44.5 15.3 %all-to-all-start.1 = ((bf16[8,128,128]{2,1,0:T(8,128)(2,1)}), bf16[8,128,128]{2,1,0:T(8,128)(2,1)S(1)}, u32[]{:S(2)}, u32[]{:S(2)}) async-start(bf16[8,128,128]{2,1,0:T(8,128)(2,1)} %get-tuple-element.69), calls=%async_computation.1 | async-start | bytes 524288 | tf_op jit(solution)/shard_map/all_to_all | solution.py:499
  49.9 11.8 %collective-permute-start.6 = (bf16[1536,128]{1,0:T(8,128)(2,1)S(1)}, bf16[1536,128]{1,0:T(8,128)(2,1)S(1)}, u32[]{:S(2)}, u32[]{:S(2)}) collective-permute-start(bf16[1536,128]{1,0:T(8,128)(2,1)S(1)} %get-tuple-element.67), channel_id=1, source_target_pairs={{0,16},{8,24},{16,0},{24,8},{1,17},{9,25},{17,1},{25,9},{2,18},{10... | collective-permute-start | bytes 1179656 | tf_op jit(solution)/shard_map/ppermute | solution.py:446
  52.1 15.8 %collective-permute-start.5 = (bf16[4,2,32,1024]{3,2,1,0:T(8,128)(2,1)}, bf16[4,2,32,1024]{3,2,1,0:T(8,128)(2,1)S(1)}, u32[]{:S(2)}, u32[]{:S(2)}) collective-permute-start(bf16[4,2,32,1024]{3,2,1,0:T(8,128)(2,1)} %pad_maximum_fusion), channel_id=1, source_target_pairs={{0,1},{1,0},{2,3},{3,2},{4,5},{5,4},{6,7},{7,6},{8,9},{9,8},{10,11... | collective-permute-start | bytes 1572872 | tf_op jit(solution)/shard_map/ppermute | solution.py:449
  59.8 8.1 %collective-permute-start.10 = (bf16[1024,128]{1,0:T(8,128)(2,1)S(1)}, bf16[1024,128]{1,0:T(8,128)(2,1)S(1)}, u32[]{:S(2)}, u32[]{:S(2)}) collective-permute-start(bf16[1024,128]{1,0:T(8,128)(2,1)S(1)} %bitcast.18), channel_id=1, source_target_pairs={{0,16},{8,24},{16,0},{24,8},{1,17},{9,25},{17,1},{25,9},{2,18},{10... | collective-permute-start | bytes 786440 | tf_op jit(solution)/shard_map/ppermute | solution.py:446
  60.3 7.7 %collective-permute-start.7 = (bf16[1280,128]{1,0:T(8,128)(2,1)S(1)}, bf16[1280,128]{1,0:T(8,128)(2,1)S(1)}, u32[]{:S(2)}, u32[]{:S(2)}) collective-permute-start(bf16[1280,128]{1,0:T(8,128)(2,1)S(1)} %get-tuple-element.68), channel_id=1, source_target_pairs={{0,8},{8,0},{16,24},{24,16},{1,9},{9,1},{17,25},{25,17},{2,10},{10... | collective-permute-start | bytes 983048 | tf_op jit(solution)/shard_map/ppermute | solution.py:446
  61.8 6.2 %collective-permute-start.8 = (bf16[1280,128]{1,0:T(8,128)(2,1)S(1)}, bf16[1280,128]{1,0:T(8,128)(2,1)S(1)}, u32[]{:S(2)}, u32[]{:S(2)}) collective-permute-start(bf16[1280,128]{1,0:T(8,128)(2,1)S(1)} %slice.8), channel_id=1, source_target_pairs={{0,8},{8,0},{16,24},{24,16},{1,9},{9,1},{17,25},{25,17},{2,10},{10... | collective-permute-start | bytes 983048 | tf_op jit(solution)/shard_map/ppermute | solution.py:446
  61.8 6.1 %collective-permute-start.9 = (bf16[1024,128]{1,0:T(8,128)(2,1)S(1)}, bf16[1024,128]{1,0:T(8,128)(2,1)S(1)}, u32[]{:S(2)}, u32[]{:S(2)}) collective-permute-start(bf16[1024,128]{1,0:T(8,128)(2,1)S(1)} %bitcast.19), channel_id=1, source_target_pairs={{0,8},{8,0},{16,24},{24,16},{1,9},{9,1},{17,25},{25,17},{2,10},{10... | collective-permute-start | bytes 786440 | tf_op jit(solution)/shard_map/ppermute | solution.py:446
  67.9 1.5 %collective-permute-start.11 = (bf16[1024,128]{1,0:T(8,128)(2,1)S(1)}, bf16[1024,128]{1,0:T(8,128)(2,1)S(1)}, u32[]{:S(2)}, u32[]{:S(2)}) collective-permute-start(bf16[1024,128]{1,0:T(8,128)(2,1)S(1)} %collective-permute-done.10.refs_10_), channel_id=1, source_target_pairs={{0,8},{8,0},{16,24},{24,16},{1,9},{9,1},{17,25},{25,17},{2,10},{10... | collective-permute-start | bytes 786440 | tf_op jit(solution)/shard_map/ppermute | solution.py:446
  72.1 3.3 %collective-permute-start.12 = (bf16[2,1024,128]{2,1,0:T(8,128)(2,1)S(1)}, bf16[2,1024,128]{2,1,0:T(8,128)(2,1)S(1)}, u32[]{:S(2)}, u32[]{:S(2)}) collective-permute-start(bf16[2,1024,128]{2,1,0:T(8,128)(2,1)S(1)} %get-tuple-element.71), channel_id=1, source_target_pairs={{0,8},{8,0},{16,24},{24,16},{1,9},{9,1},{17,25},{25,17},{2,10},{10... | collective-permute-start | bytes 1572872 | tf_op jit(solution)/shard_map/ppermute | solution.py:446
  74.6 0.8 copy-start.2
  75.5 25.4 %copy-start = (bf16[1024,1024]{1,0:T(8,128)(2,1)S(1)}, bf16[1024,1024]{1,0:T(8,128)(2,1)}, u32[]{:S(2)}) copy-start(bf16[1024,1024]{1,0:T(8,128)(2,1)} %get-tuple-element.86.ext_ref) | copy-start | bytes 6291460
  75.5 14.7 %collective-permute-start.15 = (bf16[2,1280,128]{2,1,0:T(8,128)(2,1)}, bf16[2,1280,128]{2,1,0:T(8,128)(2,1)}, u32[]{:S(2)}, u32[]{:S(2)}) collective-permute-start(bf16[2,1280,128]{2,1,0:T(8,128)(2,1)} %get-tuple-element.90), channel_id=1, source_target_pairs={{0,8},{8,0},{16,24},{24,16},{1,9},{9,1},{17,25},{25,17},{2,10},{10... | collective-permute-start | bytes 1966088 | tf_op jit(solution)/shard_map/ppermute | solution.py:446
  76.0 8.3 %collective-permute-start.13 = (bf16[1024,128]{1,0:T(8,128)(2,1)S(1)}, bf16[1024,128]{1,0:T(8,128)(2,1)S(1)}, u32[]{:S(2)}, u32[]{:S(2)}) collective-permute-start(bf16[1024,128]{1,0:T(8,128)(2,1)S(1)} %get-tuple-element.73), channel_id=1, source_target_pairs={{0,16},{8,24},{16,0},{24,8},{1,17},{9,25},{17,1},{25,9},{2,18},{10... | collective-permute-start | bytes 786440 | tf_op jit(solution)/shard_map/ppermute | solution.py:446
  76.3 16.2 %collective-permute-start.14 = (bf16[4,32,2176]{2,1,0:T(8,128)(2,1)}, bf16[4,32,2176]{2,1,0:T(8,128)(2,1)}, u32[]{:S(2)}, u32[]{:S(2)}) collective-permute-start(bf16[4,32,2176]{2,1,0:T(8,128)(2,1)} %get-tuple-element.79), channel_id=1, source_target_pairs={{0,1},{1,0},{2,3},{3,2},{4,5},{5,4},{6,7},{7,6},{8,9},{9,8},{10,11... | collective-permute-start | bytes 1671176 | tf_op jit(solution)/shard_map/ppermute | solution.py:449
  85.1 15.8 %all-to-all-start.2 = ((bf16[8,128,128]{2,1,0:T(8,128)(2,1)}), bf16[8,128,128]{2,1,0:T(8,128)(2,1)S(1)}, u32[]{:S(2)}, u32[]{:S(2)}) async-start(bf16[8,128,128]{2,1,0:T(8,128)(2,1)} %bitcast.10), calls=%async_computation.2 | async-start | bytes 524288 | tf_op jit(solution)/shard_map/all_to_all | solution.py:572
  92.1 16.2 %collective-permute-start.16 = (bf16[1536,128]{1,0:T(8,128)(2,1)}, bf16[1536,128]{1,0:T(8,128)(2,1)S(1)}, u32[]{:S(2)}, u32[]{:S(2)}) collective-permute-start(bf16[1536,128]{1,0:T(8,128)(2,1)} %get-tuple-element.93), channel_id=1, source_target_pairs={{0,16},{8,24},{16,0},{24,8},{1,17},{9,25},{17,1},{25,9},{2,18},{10... | collective-permute-start | bytes 1179656 | tf_op jit(solution)/shard_map/ppermute | solution.py:446
  92.5 1.1 copy-start.3
  95.4 12.9 %collective-permute-start.17 = (bf16[32,2176]{1,0:T(8,128)(2,1)}, bf16[32,2176]{1,0:T(8,128)(2,1)S(1)}, u32[]{:S(2)}, u32[]{:S(2)}) collective-permute-start(bf16[32,2176]{1,0:T(8,128)(2,1)} %get-tuple-element.82), channel_id=1, source_target_pairs={{0,4},{1,5},{2,6},{3,7},{4,0},{5,1},{6,2},{7,3},{8,12},{9,13},{10,... | collective-permute-start | bytes 417800 | tf_op jit(solution)/shard_map/ppermute | solution.py:449
  98.3 10.0 %collective-permute-start.18 = (bf16[32,2176]{1,0:T(8,128)(2,1)}, bf16[32,2176]{1,0:T(8,128)(2,1)}, u32[]{:S(2)}, u32[]{:S(2)}) collective-permute-start(bf16[32,2176]{1,0:T(8,128)(2,1)} %get-tuple-element.83), channel_id=1, source_target_pairs={{0,2},{1,3},{2,0},{3,1},{4,6},{5,7},{6,4},{7,5},{8,10},{9,11},{10,... | collective-permute-start | bytes 417800 | tf_op jit(solution)/shard_map/ppermute | solution.py:449
  99.7 8.6 %collective-permute-start.19 = (bf16[32,2176]{1,0:T(8,128)(2,1)}, bf16[32,2176]{1,0:T(8,128)(2,1)}, u32[]{:S(2)}, u32[]{:S(2)}) collective-permute-start(bf16[32,2176]{1,0:T(8,128)(2,1)} %get-tuple-element.84), channel_id=1, source_target_pairs={{0,6},{1,7},{2,4},{3,5},{4,2},{5,3},{6,0},{7,1},{8,14},{9,15},{10,... | collective-permute-start | bytes 417800 | tf_op jit(solution)/shard_map/ppermute | solution.py:449
  101.4 0.7 copy-start.1
  102.1 0.6 copy-start.4
  102.7 0.6 copy-start.5
  103.3 0.6 copy-start.7
  108.2 10.3 %copy-start.8 = (bf16[128,256]{1,0:T(8,128)(2,1)S(1)}, bf16[128,256]{1,0:T(8,128)(2,1)}, u32[]{:S(2)}) copy-start(bf16[128,256]{1,0:T(8,128)(2,1)} %copy-done.7) | copy-start | bytes 196612
  108.3 10.3 %copy-start.6 = (bf16[128,256]{1,0:T(8,128)(2,1)S(1)}, bf16[128,256]{1,0:T(8,128)(2,1)}, u32[]{:S(2)}) copy-start(bf16[128,256]{1,0:T(8,128)(2,1)} %copy-done.5) | copy-start | bytes 196612
  109.2 26.1 %all-to-all-start.3 = ((bf16[8,8,32,128]{3,2,1,0:T(8,128)(2,1)}), bf16[8,8,32,128]{3,2,1,0:T(8,128)(2,1)S(1)}, u32[]{:S(2)}, u32[]{:S(2)}) async-start(bf16[8,8,32,128]{3,2,1,0:T(8,128)(2,1)} %back_pack.1), calls=%async_computation.3 | async-start | bytes 1048576 | tf_op jit(solution)/shard_map/all_to_all | solution.py:607
  116.7 15.4 %collective-permute-start.24 = (bf16[32,2176]{1,0:T(8,128)(2,1)S(1)}, bf16[32,2176]{1,0:T(8,128)(2,1)S(1)}, u32[]{:S(2)}, u32[]{:S(2)}) collective-permute-start(bf16[32,2176]{1,0:T(8,128)(2,1)S(1)} %w_sum.1.refs_0_), channel_id=1, source_target_pairs={{0,16},{8,24},{16,0},{24,8},{1,17},{9,25},{17,1},{25,9},{2,18},{10... | collective-permute-start | bytes 417800 | tf_op jit(solution)/shard_map/ppermute | solution.py:446
  118.5 2.2 %collective-permute-start.20 = (bf16[128,256]{1,0:T(8,128)(2,1)S(1)}, bf16[128,256]{1,0:T(8,128)(2,1)S(1)}, u32[]{:S(2)}, u32[]{:S(2)}) collective-permute-start(bf16[128,256]{1,0:T(8,128)(2,1)S(1)} %copy-done.8), channel_id=1, source_target_pairs={{0,8},{8,0},{16,24},{24,16},{1,9},{9,1},{17,25},{25,17},{2,10},{10... | collective-permute-start | bytes 196616 | tf_op jit(solution)/shard_map/ppermute | solution.py:446
  118.5 5.0 %collective-permute-start.21 = (bf16[128,256]{1,0:T(8,128)(2,1)S(1)}, bf16[128,256]{1,0:T(8,128)(2,1)S(1)}, u32[]{:S(2)}, u32[]{:S(2)}) collective-permute-start(bf16[128,256]{1,0:T(8,128)(2,1)S(1)} %copy-done.6), channel_id=1, source_target_pairs={{0,16},{8,24},{16,0},{24,8},{1,17},{9,25},{17,1},{25,9},{2,18},{10... | collective-permute-start | bytes 196616 | tf_op jit(solution)/shard_map/ppermute | solution.py:446
  118.9 5.5 %collective-permute-start.22 = (bf16[128,256]{1,0:T(8,128)(2,1)S(1)}, bf16[128,256]{1,0:T(8,128)(2,1)S(1)}, u32[]{:S(2)}, u32[]{:S(2)}) collective-permute-start(bf16[128,256]{1,0:T(8,128)(2,1)S(1)} %get-tuple-element.97), channel_id=1, source_target_pairs={{0,24},{8,16},{16,8},{24,0},{1,25},{9,17},{17,9},{25,1},{2,26},{10... | collective-permute-start | bytes 196616 | tf_op jit(solution)/shard_map/ppermute | solution.py:446
  120.4 12.3 %collective-permute-start.23 = (bf16[32,2176]{1,0:T(8,128)(2,1)S(1)}, bf16[32,2176]{1,0:T(8,128)(2,1)S(1)}, u32[]{:S(2)}, u32[]{:S(2)}) collective-permute-start(bf16[32,2176]{1,0:T(8,128)(2,1)S(1)} %w_sum.1.refs_0_), channel_id=1, source_target_pairs={{0,8},{8,0},{16,24},{24,16},{1,9},{9,1},{17,25},{25,17},{2,10},{10... | collective-permute-start | bytes 417800 | tf_op jit(solution)/shard_map/ppermute | solution.py:446
  120.7 3.6 %copy-start.10 = (bf16[128,256]{1,0:T(8,128)(2,1)}, bf16[128,256]{1,0:T(8,128)(2,1)S(1)}, u32[]{:S(2)}) copy-start(bf16[128,256]{1,0:T(8,128)(2,1)S(1)} %collective-permute-done.20.refs_5_) | copy-start | bytes 196612
  123.6 0.8 copy-start.11
  124.4 0.6 copy-start.12
  132.2 1.5 %collective-permute-start.25 = (bf16[32,2176]{1,0:T(8,128)(2,1)S(1)}, bf16[32,2176]{1,0:T(8,128)(2,1)S(1)}, u32[]{:S(2)}, u32[]{:S(2)}) collective-permute-start(bf16[32,2176]{1,0:T(8,128)(2,1)S(1)} %collective-permute-done.24.refs_2_), channel_id=1, source_target_pairs={{0,8},{8,0},{16,24},{24,16},{1,9},{9,1},{17,25},{25,17},{2,10},{10... | collective-permute-start | bytes 417800 | tf_op jit(solution)/shard_map/ppermute | solution.py:446
  135.4 0.8 copy-start.9

commit v9 on v8

--- a/solution.py
+++ b/solution.py
@@ -591,6 +591,7 @@
         gagg,
         a_ext,
     )
+    halo_grad = after(halo_grad, back)
     returned = [halo_grad[0]] + [over_dom(halo_grad[k], k) for k in range(1, n_dom)]
     back = after(back, halo_grad, parts)
 
@@ -604,6 +605,7 @@
         *back,
         scalars=2,
     )
+    back = after(back, returned[2:])
     back = lax.all_to_all(back, "feat", 0, 0, tiled=True).reshape(n_feat, 2 * rows, piece)
     total = whole_call(
         functools.partial(wsum_kernel, width), "w_sum", 1.0, shape(sub, 2 * width + T), *parts

time: 141 us -> 136 us (0.965)
  waiting for transfers between devices: 33.4 us -> 30.5 us
  local copies, waits for them, and re-layouts: 8.73 us -> 6.84 us
    ppermute x19, waiting for transfers between devices: 19.8 us -> 17.1 us  [over_dom(): return lax.ppermute(x, 'dom', [(i, i ^ k) for i in range(n_dom)])]
    unnamed x36 -> x28, local copies, waits for them, and re-layouts: 6.53 us -> 4.64 us
    ppermute x7, waiting for transfers between devices: 6.77 us -> 8.38 us  [over_feat(): return lax.ppermute(x, 'feat', [(i, i ^ k) for i in range(n_feat)])]
  transfers between devices with their start and end apart: 30 -> 30, of which waited for: 12 -> 12; matrix products, arithmetic and copies ran while one was open for 3% -> 3% of each run, Pallas kernels for 28% -> 30%
where the time goes in v9:
time: 136 us; the launch traced here: 135 us
  Pallas kernels  46.9 us (34%)
  starting transfers between devices  46.3 us (34%)
  waiting for transfers between devices  30.5 us (22%)
  local copies, waits for them, and re-layouts  6.84 us (5%)
  other arithmetic  2.93 us (2%)
  between operations  1.52 us (1%)
    pallas_call x1, Pallas kernels, build_dense(): pl.pallas_call(functools.partial(build_kernel, n_own), out_shape=(shape(n...  19.9 us
    ppermute x19, waiting for transfers between devices, over_dom(): return lax.ppermute(x, 'dom', [(i, i ^ k) for i in range(n_dom)])  17.1 us
    ppermute x7, starting transfers between devices, over_feat(): return lax.ppermute(x, 'feat', [(i, i ^ k) for i in range(n_feat)])  14.3 us
    pallas_call x10, Pallas kernels, whole_call(): pl.pallas_call(kernel, out_shape=out_shape, in_specs=[SMEM] * scalars + [...  12.4 us
    ppermute x19, starting transfers between devices, over_dom(): return lax.ppermute(x, 'dom', [(i, i ^ k) for i in range(n_dom)])  8.87 us
    ppermute x7, waiting for transfers between devices, over_feat(): return lax.ppermute(x, 'feat', [(i, i ^ k) for i in range(n_feat)])  8.38 us
    pallas_call x1, Pallas kernels, finish_rest(): pl.pallas_call(functools.partial(finish_rest_kernel, top), out_shape=shap...  7.16 us
    all_to_all x1, starting transfers between devices, body(): lax.all_to_all(back, 'feat', 0, 0, tiled=True)  6.44 us
  transfers between devices with their start and end apart: 30, of which 12 were waited for; matrix products, arithmetic and copies ran while one was open for 3% of the time, Pallas kernels for 30%

profile of v9, /device:TPU:0, one launch (start us, length us, event | category | flops | bytes accessed | tf_op | source)
XLA Modules:
  0.0 135.0 jit_solution(2782480363858506252)
XLA Ops:
  0.7 0.9 dynamic-slice_bitcast_fusion
  1.6 4.1 %collective-permute-start = (bf16[1,2,32,1024]{3,2,1,0:T(8,128)(2,1)S(1)}, bf16[1,2,32,1024]{3,2,1,0:T(8,128)(2,1)S(1)}, u32[]{:S(2)}, u32[]{:S(2)}) collective-permute-start(bf16[1,2,32,1024]{3,2,1,0:T(8,128)(2,1)S(1)} %maximum_bitcast_fusion.refs_0_), channel_id=1, source_target_pairs={{0,4},{1,5},{2,6},{3,7},{4,0},{5,1},{6,2},{7,3},{8,12},{9,13},{10,... | collective-permute-start | bytes 393224 | tf_op jit(solution)/shard_map/ppermute | solution.py:449
  5.7 3.9 %pack.1 = (bf16[8,9,32,128]{3,2,1,0:T(8,128)(2,1)}, bf16[128,256]{1,0:T(8,128)(2,1)}, bf16[128,256]{1,0:T(8,128)(2,1)}, bf16[128,256]{1,0:T(8,128)(2,1)}, bf16[128,256]{1,0:T(8,128)(2,1)}) custom-call(s32[1]{0:T(128)} %bitcast.me_ref, bf16[128,4096]{1,0:T(8,128)(2,1)} %x_ref.3, bf16[128,1024]{1,0:T(8,128)(2,1)} %cot_ref.1, f32[1,128]{1,0:T(1,128)} %bitcast.29, ...), custom_call_target="tpu_custom_call" | custom-call | bytes 12000000 | tf_op jit(solution)/shard_map/pack/pallas_call | solution.py:74
  9.6 2.4 %collective-permute-done.refs_1_ = bf16[1,2,32,1024]{3,2,1,0:T(8,128)(2,1)S(1)} collective-permute-done((bf16[1,2,32,1024]{3,2,1,0:T(8,128)(2,1)S(1)}, bf16[1,2,32,1024]{3,2,1,0:T(8,128)(2,1)S(1)}, u32[]{:S(2)}, u32[]{:S(2)}) %collective-permute-start) | collective-permute-done | bytes 131104 | tf_op jit(solution)/shard_map/ppermute | solution.py:449
  12.0 5.7 %all-to-all-start = ((bf16[8,9,32,128]{3,2,1,0:T(8,128)(2,1)}), bf16[8,9,32,128]{3,2,1,0:T(8,128)(2,1)S(1)}, u32[]{:S(2)}, u32[]{:S(2)}) async-start(bf16[8,9,32,128]{3,2,1,0:T(8,128)(2,1)} %get-tuple-element.62), calls=%async_computation | async-start | bytes 1179648 | tf_op jit(solution)/shard_map/all_to_all | solution.py:472
  17.7 1.6 %collective-permute-start.3 = (bf16[128,256]{1,0:T(8,128)(2,1)}, bf16[128,256]{1,0:T(8,128)(2,1)S(1)}, u32[]{:S(2)}, u32[]{:S(2)}) collective-permute-start(bf16[128,256]{1,0:T(8,128)(2,1)} %get-tuple-element.65), channel_id=1, source_target_pairs={{0,16},{8,24},{16,0},{24,8},{1,17},{9,25},{17,1},{25,9},{2,18},{10... | collective-permute-start | bytes 196616 | tf_op jit(solution)/shard_map/ppermute | solution.py:446
  20.8 0.6 concatenate.10.order_ref
  21.4 0.8 convert_reduce_fusion.1.start_ref
  22.2 2.1 %collective-permute-start.1 = (bf16[2,2,32,1024]{3,2,1,0:T(8,128)(2,1)S(1)}, bf16[2,2,32,1024]{3,2,1,0:T(8,128)(2,1)S(1)}, u32[]{:S(2)}, u32[]{:S(2)}) collective-permute-start(bf16[2,2,32,1024]{3,2,1,0:T(8,128)(2,1)S(1)} %pad_maximum_fusion.1), channel_id=1, source_target_pairs={{0,2},{1,3},{2,0},{3,1},{4,6},{5,7},{6,4},{7,5},{8,10},{9,11},{10,... | collective-permute-start | bytes 786440 | tf_op jit(solution)/shard_map/ppermute | solution.py:449
  24.3 0.6 copy-done.9
  24.9 19.9 %build_dense.1 = (bf16[8,1024,512]{2,1,0:T(8,128)(2,1)}, bf16[1024,1024]{1,0:T(8,128)(2,1)}, bf16[8,128,128]{2,1,0:T(8,128)(2,1)}) custom-call(s32[514]{0:T(1024)} %concatenate.10.order_ref, s32[321]{0:T(512)} %convert_reduce_fusion.1.start_ref, bf16[128,4096]{1,0:T(8,128)(2,1)} %x_ref.3, bf16[512,128,128]{2,1,0:T(8,128)(2,1)} %vals_hbm.1, ...), custom_call_target="tpu_custom_call" | custom-call | bytes 30000000 | tf_op jit(solution)/shard_map/build_dense/pallas_call | solution.py:139
  44.8 5.2 %all-to-all-start.1 = ((bf16[8,128,128]{2,1,0:T(8,128)(2,1)}), bf16[8,128,128]{2,1,0:T(8,128)(2,1)S(1)}, u32[]{:S(2)}, u32[]{:S(2)}) async-start(bf16[8,128,128]{2,1,0:T(8,128)(2,1)} %get-tuple-element.74), calls=%async_computation.1 | async-start | bytes 524288 | tf_op jit(solution)/shard_map/all_to_all | solution.py:499
  50.2 1.7 %collective-permute-start.6 = (bf16[1536,128]{1,0:T(8,128)(2,1)S(1)}, bf16[1536,128]{1,0:T(8,128)(2,1)S(1)}, u32[]{:S(2)}, u32[]{:S(2)}) collective-permute-start(bf16[1536,128]{1,0:T(8,128)(2,1)S(1)} %get-tuple-element.72), channel_id=1, source_target_pairs={{0,16},{8,24},{16,0},{24,8},{1,17},{9,25},{17,1},{25,9},{2,18},{10... | collective-permute-start | bytes 1179656 | tf_op jit(solution)/shard_map/ppermute | solution.py:446
  51.9 0.8 pad_maximum_fusion
  52.7 2.0 %collective-permute-start.5 = (bf16[4,2,32,1024]{3,2,1,0:T(8,128)(2,1)}, bf16[4,2,32,1024]{3,2,1,0:T(8,128)(2,1)S(1)}, u32[]{:S(2)}, u32[]{:S(2)}) collective-permute-start(bf16[4,2,32,1024]{3,2,1,0:T(8,128)(2,1)} %pad_maximum_fusion), channel_id=1, source_target_pairs={{0,1},{1,0},{2,3},{3,2},{4,5},{5,4},{6,7},{7,6},{8,9},{9,8},{10,11... | collective-permute-start | bytes 1572872 | tf_op jit(solution)/shard_map/ppermute | solution.py:449
  54.7 5.0 %all-to-all-done.1 = bf16[8,128,128]{2,1,0:T(8,128)(2,1)S(1)} async-done(((bf16[8,128,128]{2,1,0:T(8,128)(2,1)}), bf16[8,128,128]{2,1,0:T(8,128)(2,1)S(1)}, u32[]{:S(2)}, u32[]{:S(2)}) %all-to-all-start.1) | async-done | bytes 262176 | tf_op jit(solution)/shard_map/all_to_all | solution.py:499
  60.3 1.6 %collective-permute-done.6.refs_5_ = bf16[1536,128]{1,0:T(8,128)(2,1)S(1)} collective-permute-done((bf16[1536,128]{1,0:T(8,128)(2,1)S(1)}, bf16[1536,128]{1,0:T(8,128)(2,1)S(1)}, u32[]{:S(2)}, u32[]{:S(2)}) %collective-permute-start.6) | collective-permute-done | bytes 393248 | tf_op jit(solution)/shard_map/ppermute | solution.py:446
  62.5 4.8 %collective-permute-done.10.refs_10_ = bf16[1024,128]{1,0:T(8,128)(2,1)S(1)} collective-permute-done((bf16[1024,128]{1,0:T(8,128)(2,1)S(1)}, bf16[1024,128]{1,0:T(8,128)(2,1)S(1)}, u32[]{:S(2)}, u32[]{:S(2)}) %collective-permute-start.10) | collective-permute-done | bytes 262176 | tf_op jit(solution)/shard_map/ppermute | solution.py:446
  67.7 1.0 collective-permute-done.11.refs_11_
  68.8 2.6 %dense.1 = (bf16[4,256,128]{2,1,0:T(8,128)(2,1)S(1)}, bf16[2,256,128]{2,1,0:T(8,128)(2,1)S(1)}, bf16[2,256,128]{2,1,0:T(8,128)(2,1)S(1)}, bf16[2,1024,128]{2,1,0:T(8,128)(2,1)S(1)}, bf16[2,1024,128]{2,1,0:T(8,128)(2,1)S(1)}) custom-call(f32[256,128]{1,0:T(8,128)S(1)} %get-tuple-element.70.bias_ref, bf16[1,2,32,1024]{3,2,1,0:T(8,128)(2,1)S(1)} %maximum_bitcast_fusion.refs_0_, ...), custom_call_target="tpu_custom_call" | custom-call | bytes 9000000 | tf_op jit(solution)/shard_map/dense/pallas_call | solution.py:29
  71.6 2.3 %grads.1 = (bf16[2,1280,128]{2,1,0:T(8,128)(2,1)S(1)}, bf16[2,1280,128]{2,1,0:T(8,128)(2,1)}, bf16[4,32,2176]{2,1,0:T(8,128)(2,1)S(1)}, bf16[4,32,2176]{2,1,0:T(8,128)(2,1)}) custom-call(bf16[4,256,128]{2,1,0:T(8,128)(2,1)S(1)} %get-tuple-element.79.g_ref, bf16[2,256,128]{2,1,0:T(8,128)(2,1)S(1)} %get-tuple-element.80.act_even, ...), custom_call_target="tpu_custom_call" | custom-call | bytes 9000000 | tf_op jit(solution)/shard_map/grads/pallas_call | solution.py:29
  74.0 0.8 copy-done.2
  75.7 1.7 %collective-permute-start.14 = (bf16[4,32,2176]{2,1,0:T(8,128)(2,1)}, bf16[4,32,2176]{2,1,0:T(8,128)(2,1)}, u32[]{:S(2)}, u32[]{:S(2)}) collective-permute-start(bf16[4,32,2176]{2,1,0:T(8,128)(2,1)} %get-tuple-element.84), channel_id=1, source_target_pairs={{0,1},{1,0},{2,3},{3,2},{4,5},{5,4},{6,7},{7,6},{8,9},{9,8},{10,11... | collective-permute-start | bytes 1671176 | tf_op jit(solution)/shard_map/ppermute | solution.py:449
  77.5 6.2 %collective-permute-done.13 = bf16[1024,128]{1,0:T(8,128)(2,1)S(1)} collective-permute-done((bf16[1024,128]{1,0:T(8,128)(2,1)S(1)}, bf16[1024,128]{1,0:T(8,128)(2,1)S(1)}, u32[]{:S(2)}, u32[]{:S(2)}) %collective-permute-start.13) | collective-permute-done | bytes 262176 | tf_op jit(solution)/shard_map/ppermute | solution.py:446
  83.7 0.8 add_convert_fusion
  84.5 5.7 %all-to-all-start.2 = ((bf16[8,128,128]{2,1,0:T(8,128)(2,1)}), bf16[8,128,128]{2,1,0:T(8,128)(2,1)S(1)}, u32[]{:S(2)}, u32[]{:S(2)}) async-start(bf16[8,128,128]{2,1,0:T(8,128)(2,1)} %bitcast.10), calls=%async_computation.2 | async-start | bytes 524288 | tf_op jit(solution)/shard_map/all_to_all | solution.py:572
  90.2 1.9 %back_pair.1 = (bf16[1536,128]{1,0:T(8,128)(2,1)S(1)}, bf16[1536,128]{1,0:T(8,128)(2,1)}) custom-call(bf16[2,1280,128]{2,1,0:T(8,128)(2,1)S(1)} %get-tuple-element.93.even_ref, bf16[2,1280,128]{2,1,0:T(8,128)(2,1)} %collective-permute-done.15.got_ref), custom_call_target="tpu_custom_call" | custom-call | bytes 3000000 | tf_op jit(solution)/shard_map/back_pair/pallas_call | solution.py:29
  92.5 1.1 copy-done.3
  93.5 1.8 %x_sum.1 = (bf16[32,2176]{1,0:T(8,128)(2,1)S(1)}, bf16[32,2176]{1,0:T(8,128)(2,1)}, bf16[32,2176]{1,0:T(8,128)(2,1)}, bf16[32,2176]{1,0:T(8,128)(2,1)}) custom-call(bf16[4,32,2176]{2,1,0:T(8,128)(2,1)S(1)} %copy-done.3, bf16[4,32,2176]{2,1,0:T(8,128)(2,1)} %collective-permute-done.14.got_ref), custom_call_target="tpu_custom_call" | custom-call | bytes 3000000 | tf_op jit(solution)/shard_map/x_sum/pallas_call | solution.py:29
  95.4 2.9 %collective-permute-start.17 = (bf16[32,2176]{1,0:T(8,128)(2,1)}, bf16[32,2176]{1,0:T(8,128)(2,1)S(1)}, u32[]{:S(2)}, u32[]{:S(2)}) collective-permute-start(bf16[32,2176]{1,0:T(8,128)(2,1)} %get-tuple-element.87), channel_id=1, source_target_pairs={{0,4},{1,5},{2,6},{3,7},{4,0},{5,1},{6,2},{7,3},{8,12},{9,13},{10,... | collective-permute-start | bytes 417800 | tf_op jit(solution)/shard_map/ppermute | solution.py:449
  98.3 1.5 %collective-permute-start.18 = (bf16[32,2176]{1,0:T(8,128)(2,1)}, bf16[32,2176]{1,0:T(8,128)(2,1)}, u32[]{:S(2)}, u32[]{:S(2)}) collective-permute-start(bf16[32,2176]{1,0:T(8,128)(2,1)} %get-tuple-element.88), channel_id=1, source_target_pairs={{0,2},{1,3},{2,0},{3,1},{4,6},{5,7},{6,4},{7,5},{8,10},{9,11},{10,... | collective-permute-start | bytes 417800 | tf_op jit(solution)/shard_map/ppermute | solution.py:449
  100.2 0.7 copy-done.1
  100.9 1.5 %collective-permute-done.16.refs_1_ = bf16[1536,128]{1,0:T(8,128)(2,1)S(1)} collective-permute-done((bf16[1536,128]{1,0:T(8,128)(2,1)}, bf16[1536,128]{1,0:T(8,128)(2,1)S(1)}, u32[]{:S(2)}, u32[]{:S(2)}) %collective-permute-start.16) | collective-permute-done | bytes 393248 | tf_op jit(solution)/shard_map/ppermute | solution.py:446
  102.8 3.9 %collective-permute-done.17.refs_1_ = bf16[32,2176]{1,0:T(8,128)(2,1)S(1)} collective-permute-done((bf16[32,2176]{1,0:T(8,128)(2,1)}, bf16[32,2176]{1,0:T(8,128)(2,1)S(1)}, u32[]{:S(2)}, u32[]{:S(2)}) %collective-permute-start.17) | collective-permute-done | bytes 139296 | tf_op jit(solution)/shard_map/ppermute | solution.py:449
  106.7 1.6 %collective-permute-done.19.refs_3_ = bf16[32,2176]{1,0:T(8,128)(2,1)} collective-permute-done((bf16[32,2176]{1,0:T(8,128)(2,1)}, bf16[32,2176]{1,0:T(8,128)(2,1)}, u32[]{:S(2)}, u32[]{:S(2)}) %collective-permute-start.19) | collective-permute-done | bytes 139296 | tf_op jit(solution)/shard_map/ppermute | solution.py:449
  108.4 0.9 back_pack.1
  109.3 6.4 %all-to-all-start.3 = ((bf16[8,8,32,128]{3,2,1,0:T(8,128)(2,1)}), bf16[8,8,32,128]{3,2,1,0:T(8,128)(2,1)S(1)}, u32[]{:S(2)}, u32[]{:S(2)}) async-start(bf16[8,8,32,128]{3,2,1,0:T(8,128)(2,1)} %back_pack.1), calls=%async_computation.3 | async-start | bytes 1048576 | tf_op jit(solution)/shard_map/all_to_all | solution.py:609
  115.7 1.1 w_sum.1.refs_0_
  116.8 1.7 %collective-permute-start.24 = (bf16[32,2176]{1,0:T(8,128)(2,1)S(1)}, bf16[32,2176]{1,0:T(8,128)(2,1)S(1)}, u32[]{:S(2)}, u32[]{:S(2)}) collective-permute-start(bf16[32,2176]{1,0:T(8,128)(2,1)S(1)} %w_sum.1.refs_0_), channel_id=1, source_target_pairs={{0,16},{8,24},{16,0},{24,8},{1,17},{9,25},{17,1},{25,9},{2,18},{10... | collective-permute-start | bytes 417800 | tf_op jit(solution)/shard_map/ppermute | solution.py:446
  118.5 0.5 collective-permute-start.23
  119.0 0.7 collective-permute-done.22.refs_5_
  119.8 0.6 copy-done.8
  120.4 7.2 %finish_rest.1.grads_ref = f32[128,4096]{1,0:T(8,128)} custom-call(s32[1]{0:T(128)} %bitcast.me_ref, bf16[128,1024]{1,0:T(8,128)(2,1)} %copy-done.1, s32[4,128]{1,0:T(4,128)} %bitcast.24, s32[1,128]{1,0:T(1,128)} %bitcast.27, bf16[8,1024,512]{2,1,0:T(8,128)(2,1)} %get-tuple-element.110.refs_0_.refs_1_.refs_2_.refs_3_, ...), custom_call_target="tpu_custom_call" | custom-call | bytes 18000000 | tf_op jit(solution)/shard_map/finish_rest/pallas_call | solution.py:376
  127.8 1.2 collective-permute-done.25.refs_3_
  129.0 1.0 w_out.1
  130.1 0.6 reshape_squeeze.3
  130.7 0.8 copy-done.5
  131.5 3.5 %finish_dst.1 = (f32[128,4096]{1,0:T(8,128)}, bf16[128,1024]{1,0:T(8,128)(2,1)}) custom-call(s32[1]{0:T(128)} %bitcast.me_ref, bf16[128,1024]{1,0:T(8,128)(2,1)} %copy-done.1, s32[4,128]{1,0:T(4,128)} %bitcast.25, s32[1,128]{1,0:T(1,128)} %bitcast.28, bf16[8,256,128]{2,1,0:T(8,128)(2,1)} %bitcast.22, ...), custom_call_target="tpu_custom_call", output_to_operand_aliasing={{0}: (5, {})} | custom-call | bytes 6000000 | tf_op jit(solution)/shard_map/finish_dst/pallas_call | solution.py:394
  (67 shorter events, 5.4 us)
Async XLA Ops:
  0.6 19.6 %copy-start.13 = (s32[512]{0:T(512)S(1)}, s32[512]{0:T(512)}, u32[]{:S(2)}) copy-start(s32[512]{0:T(512)} %param.14) | copy-start | bytes 6148
  0.6 19.6 %copy-start.12 = (s32[512]{0:T(512)S(1)}, s32[512]{0:T(512)}, u32[]{:S(2)}) copy-start(s32[512]{0:T(512)} %param.15) | copy-start | bytes 6148
  1.6 10.4 %collective-permute-start = (bf16[1,2,32,1024]{3,2,1,0:T(8,128)(2,1)S(1)}, bf16[1,2,32,1024]{3,2,1,0:T(8,128)(2,1)S(1)}, u32[]{:S(2)}, u32[]{:S(2)}) collective-permute-start(bf16[1,2,32,1024]{3,2,1,0:T(8,128)(2,1)S(1)} %maximum_bitcast_fusion.refs_0_), channel_id=1, source_target_pairs={{0,4},{1,5},{2,6},{3,7},{4,0},{5,1},{6,2},{7,3},{8,12},{9,13},{10,... | collective-permute-start | bytes 393224 | tf_op jit(solution)/shard_map/ppermute | solution.py:449
  12.0 32.8 %all-to-all-start = ((bf16[8,9,32,128]{3,2,1,0:T(8,128)(2,1)}), bf16[8,9,32,128]{3,2,1,0:T(8,128)(2,1)S(1)}, u32[]{:S(2)}, u32[]{:S(2)}) async-start(bf16[8,9,32,128]{3,2,1,0:T(8,128)(2,1)} %get-tuple-element.62), calls=%async_computation | async-start | bytes 1179648 | tf_op jit(solution)/shard_map/all_to_all | solution.py:472
  17.7 6.5 %collective-permute-start.2 = (bf16[128,256]{1,0:T(8,128)(2,1)}, bf16[128,256]{1,0:T(8,128)(2,1)S(1)}, u32[]{:S(2)}, u32[]{:S(2)}) collective-permute-start(bf16[128,256]{1,0:T(8,128)(2,1)} %get-tuple-element.64), channel_id=1, source_target_pairs={{0,8},{8,0},{16,24},{24,16},{1,9},{9,1},{17,25},{25,17},{2,10},{10... | collective-permute-start | bytes 196616 | tf_op jit(solution)/shard_map/ppermute | solution.py:446
  17.7 6.5 %collective-permute-start.3 = (bf16[128,256]{1,0:T(8,128)(2,1)}, bf16[128,256]{1,0:T(8,128)(2,1)S(1)}, u32[]{:S(2)}, u32[]{:S(2)}) collective-permute-start(bf16[128,256]{1,0:T(8,128)(2,1)} %get-tuple-element.65), channel_id=1, source_target_pairs={{0,16},{8,24},{16,0},{24,8},{1,17},{9,25},{17,1},{25,9},{2,18},{10... | collective-permute-start | bytes 196616 | tf_op jit(solution)/shard_map/ppermute | solution.py:446
  19.3 5.0 %collective-permute-start.4 = (bf16[128,256]{1,0:T(8,128)(2,1)}, bf16[128,256]{1,0:T(8,128)(2,1)S(1)}, u32[]{:S(2)}, u32[]{:S(2)}) collective-permute-start(bf16[128,256]{1,0:T(8,128)(2,1)} %get-tuple-element.66), channel_id=1, source_target_pairs={{0,24},{8,16},{16,8},{24,0},{1,25},{9,17},{17,9},{25,1},{2,26},{10... | collective-permute-start | bytes 196616 | tf_op jit(solution)/shard_map/ppermute | solution.py:446
  22.2 27.9 %collective-permute-start.1 = (bf16[2,2,32,1024]{3,2,1,0:T(8,128)(2,1)S(1)}, bf16[2,2,32,1024]{3,2,1,0:T(8,128)(2,1)S(1)}, u32[]{:S(2)}, u32[]{:S(2)}) collective-permute-start(bf16[2,2,32,1024]{3,2,1,0:T(8,128)(2,1)S(1)} %pad_maximum_fusion.1), channel_id=1, source_target_pairs={{0,2},{1,3},{2,0},{3,1},{4,6},{5,7},{6,4},{7,5},{8,10},{9,11},{10,... | collective-permute-start | bytes 786440 | tf_op jit(solution)/shard_map/ppermute | solution.py:449
  24.3 0.6 copy-start.9
  24.3 0.6 copy-start.10
  24.3 0.6 copy-start.11
  44.8 14.9 %all-to-all-start.1 = ((bf16[8,128,128]{2,1,0:T(8,128)(2,1)}), bf16[8,128,128]{2,1,0:T(8,128)(2,1)S(1)}, u32[]{:S(2)}, u32[]{:S(2)}) async-start(bf16[8,128,128]{2,1,0:T(8,128)(2,1)} %get-tuple-element.74), calls=%async_computation.1 | async-start | bytes 524288 | tf_op jit(solution)/shard_map/all_to_all | solution.py:499
  50.2 11.7 %collective-permute-start.6 = (bf16[1536,128]{1,0:T(8,128)(2,1)S(1)}, bf16[1536,128]{1,0:T(8,128)(2,1)S(1)}, u32[]{:S(2)}, u32[]{:S(2)}) collective-permute-start(bf16[1536,128]{1,0:T(8,128)(2,1)S(1)} %get-tuple-element.72), channel_id=1, source_target_pairs={{0,16},{8,24},{16,0},{24,8},{1,17},{9,25},{17,1},{25,9},{2,18},{10... | collective-permute-start | bytes 1179656 | tf_op jit(solution)/shard_map/ppermute | solution.py:446
  52.7 15.0 %collective-permute-start.5 = (bf16[4,2,32,1024]{3,2,1,0:T(8,128)(2,1)}, bf16[4,2,32,1024]{3,2,1,0:T(8,128)(2,1)S(1)}, u32[]{:S(2)}, u32[]{:S(2)}) collective-permute-start(bf16[4,2,32,1024]{3,2,1,0:T(8,128)(2,1)} %pad_maximum_fusion), channel_id=1, source_target_pairs={{0,1},{1,0},{2,3},{3,2},{4,5},{5,4},{6,7},{7,6},{8,9},{9,8},{10,11... | collective-permute-start | bytes 1572872 | tf_op jit(solution)/shard_map/ppermute | solution.py:449
  59.8 7.5 %collective-permute-start.10 = (bf16[1024,128]{1,0:T(8,128)(2,1)S(1)}, bf16[1024,128]{1,0:T(8,128)(2,1)S(1)}, u32[]{:S(2)}, u32[]{:S(2)}) collective-permute-start(bf16[1024,128]{1,0:T(8,128)(2,1)S(1)} %bitcast.18), channel_id=1, source_target_pairs={{0,16},{8,24},{16,0},{24,8},{1,17},{9,25},{17,1},{25,9},{2,18},{10... | collective-permute-start | bytes 786440 | tf_op jit(solution)/shard_map/ppermute | solution.py:446
  60.3 7.5 %collective-permute-start.7 = (bf16[1280,128]{1,0:T(8,128)(2,1)S(1)}, bf16[1280,128]{1,0:T(8,128)(2,1)S(1)}, u32[]{:S(2)}, u32[]{:S(2)}) collective-permute-start(bf16[1280,128]{1,0:T(8,128)(2,1)S(1)} %get-tuple-element.73), channel_id=1, source_target_pairs={{0,8},{8,0},{16,24},{24,16},{1,9},{9,1},{17,25},{25,17},{2,10},{10... | collective-permute-start | bytes 983048 | tf_op jit(solution)/shard_map/ppermute | solution.py:446
  61.9 5.8 %collective-permute-start.8 = (bf16[1280,128]{1,0:T(8,128)(2,1)S(1)}, bf16[1280,128]{1,0:T(8,128)(2,1)S(1)}, u32[]{:S(2)}, u32[]{:S(2)}) collective-permute-start(bf16[1280,128]{1,0:T(8,128)(2,1)S(1)} %slice.8), channel_id=1, source_target_pairs={{0,8},{8,0},{16,24},{24,16},{1,9},{9,1},{17,25},{25,17},{2,10},{10... | collective-permute-start | bytes 983048 | tf_op jit(solution)/shard_map/ppermute | solution.py:446
  62.0 5.8 %collective-permute-start.9 = (bf16[1024,128]{1,0:T(8,128)(2,1)S(1)}, bf16[1024,128]{1,0:T(8,128)(2,1)S(1)}, u32[]{:S(2)}, u32[]{:S(2)}) collective-permute-start(bf16[1024,128]{1,0:T(8,128)(2,1)S(1)} %bitcast.19), channel_id=1, source_target_pairs={{0,8},{8,0},{16,24},{24,16},{1,9},{9,1},{17,25},{25,17},{2,10},{10... | collective-permute-start | bytes 786440 | tf_op jit(solution)/shard_map/ppermute | solution.py:446
  67.3 1.5 %collective-permute-start.11 = (bf16[1024,128]{1,0:T(8,128)(2,1)S(1)}, bf16[1024,128]{1,0:T(8,128)(2,1)S(1)}, u32[]{:S(2)}, u32[]{:S(2)}) collective-permute-start(bf16[1024,128]{1,0:T(8,128)(2,1)S(1)} %collective-permute-done.10.refs_10_), channel_id=1, source_target_pairs={{0,8},{8,0},{16,24},{24,16},{1,9},{9,1},{17,25},{25,17},{2,10},{10... | collective-permute-start | bytes 786440 | tf_op jit(solution)/shard_map/ppermute | solution.py:446
  71.4 3.3 %collective-permute-start.12 = (bf16[2,1024,128]{2,1,0:T(8,128)(2,1)S(1)}, bf16[2,1024,128]{2,1,0:T(8,128)(2,1)S(1)}, u32[]{:S(2)}, u32[]{:S(2)}) collective-permute-start(bf16[2,1024,128]{2,1,0:T(8,128)(2,1)S(1)} %get-tuple-element.76), channel_id=1, source_target_pairs={{0,8},{8,0},{16,24},{24,16},{1,9},{9,1},{17,25},{25,17},{2,10},{10... | collective-permute-start | bytes 1572872 | tf_op jit(solution)/shard_map/ppermute | solution.py:446
  74.0 0.8 copy-start.2
  74.9 24.9 %copy-start = (bf16[1024,1024]{1,0:T(8,128)(2,1)S(1)}, bf16[1024,1024]{1,0:T(8,128)(2,1)}, u32[]{:S(2)}) copy-start(bf16[1024,1024]{1,0:T(8,128)(2,1)} %get-tuple-element.91.ext_ref) | copy-start | bytes 6291460
  74.9 15.3 %collective-permute-start.15 = (bf16[2,1280,128]{2,1,0:T(8,128)(2,1)}, bf16[2,1280,128]{2,1,0:T(8,128)(2,1)}, u32[]{:S(2)}, u32[]{:S(2)}) collective-permute-start(bf16[2,1280,128]{2,1,0:T(8,128)(2,1)} %get-tuple-element.95), channel_id=1, source_target_pairs={{0,8},{8,0},{16,24},{24,16},{1,9},{9,1},{17,25},{25,17},{2,10},{10... | collective-permute-start | bytes 1966088 | tf_op jit(solution)/shard_map/ppermute | solution.py:446
  75.3 8.3 %collective-permute-start.13 = (bf16[1024,128]{1,0:T(8,128)(2,1)S(1)}, bf16[1024,128]{1,0:T(8,128)(2,1)S(1)}, u32[]{:S(2)}, u32[]{:S(2)}) collective-permute-start(bf16[1024,128]{1,0:T(8,128)(2,1)S(1)} %get-tuple-element.78), channel_id=1, source_target_pairs={{0,16},{8,24},{16,0},{24,8},{1,17},{9,25},{17,1},{25,9},{2,18},{10... | collective-permute-start | bytes 786440 | tf_op jit(solution)/shard_map/ppermute | solution.py:446
  75.7 16.7 %collective-permute-start.14 = (bf16[4,32,2176]{2,1,0:T(8,128)(2,1)}, bf16[4,32,2176]{2,1,0:T(8,128)(2,1)}, u32[]{:S(2)}, u32[]{:S(2)}) collective-permute-start(bf16[4,32,2176]{2,1,0:T(8,128)(2,1)} %get-tuple-element.84), channel_id=1, source_target_pairs={{0,1},{1,0},{2,3},{3,2},{4,5},{5,4},{6,7},{7,6},{8,9},{9,8},{10,11... | collective-permute-start | bytes 1671176 | tf_op jit(solution)/shard_map/ppermute | solution.py:449
  84.5 15.3 %all-to-all-start.2 = ((bf16[8,128,128]{2,1,0:T(8,128)(2,1)}), bf16[8,128,128]{2,1,0:T(8,128)(2,1)S(1)}, u32[]{:S(2)}, u32[]{:S(2)}) async-start(bf16[8,128,128]{2,1,0:T(8,128)(2,1)} %bitcast.10), calls=%async_computation.2 | async-start | bytes 524288 | tf_op jit(solution)/shard_map/all_to_all | solution.py:572
  92.1 10.4 %collective-permute-start.16 = (bf16[1536,128]{1,0:T(8,128)(2,1)}, bf16[1536,128]{1,0:T(8,128)(2,1)S(1)}, u32[]{:S(2)}, u32[]{:S(2)}) collective-permute-start(bf16[1536,128]{1,0:T(8,128)(2,1)} %get-tuple-element.98), channel_id=1, source_target_pairs={{0,16},{8,24},{16,0},{24,8},{1,17},{9,25},{17,1},{25,9},{2,18},{10... | collective-permute-start | bytes 1179656 | tf_op jit(solution)/shard_map/ppermute | solution.py:446
  92.5 1.1 copy-start.3
  95.4 11.4 %collective-permute-start.17 = (bf16[32,2176]{1,0:T(8,128)(2,1)}, bf16[32,2176]{1,0:T(8,128)(2,1)S(1)}, u32[]{:S(2)}, u32[]{:S(2)}) collective-permute-start(bf16[32,2176]{1,0:T(8,128)(2,1)} %get-tuple-element.87), channel_id=1, source_target_pairs={{0,4},{1,5},{2,6},{3,7},{4,0},{5,1},{6,2},{7,3},{8,12},{9,13},{10,... | collective-permute-start | bytes 417800 | tf_op jit(solution)/shard_map/ppermute | solution.py:449
  98.3 8.4 %collective-permute-start.18 = (bf16[32,2176]{1,0:T(8,128)(2,1)}, bf16[32,2176]{1,0:T(8,128)(2,1)}, u32[]{:S(2)}, u32[]{:S(2)}) collective-permute-start(bf16[32,2176]{1,0:T(8,128)(2,1)} %get-tuple-element.88), channel_id=1, source_target_pairs={{0,2},{1,3},{2,0},{3,1},{4,6},{5,7},{6,4},{7,5},{8,10},{9,11},{10,... | collective-permute-start | bytes 417800 | tf_op jit(solution)/shard_map/ppermute | solution.py:449
  99.8 8.6 %collective-permute-start.19 = (bf16[32,2176]{1,0:T(8,128)(2,1)}, bf16[32,2176]{1,0:T(8,128)(2,1)}, u32[]{:S(2)}, u32[]{:S(2)}) collective-permute-start(bf16[32,2176]{1,0:T(8,128)(2,1)} %get-tuple-element.89), channel_id=1, source_target_pairs={{0,6},{1,7},{2,4},{3,5},{4,2},{5,3},{6,0},{7,1},{8,14},{9,15},{10,... | collective-permute-start | bytes 417800 | tf_op jit(solution)/shard_map/ppermute | solution.py:449
  100.2 0.7 copy-start.1
  100.9 8.3 %copy-start.4 = (bf16[128,256]{1,0:T(8,128)(2,1)}, bf16[128,256]{1,0:T(8,128)(2,1)S(1)}, u32[]{:S(2)}) copy-start(bf16[128,256]{1,0:T(8,128)(2,1)S(1)} %get-tuple-element.103.refs_4_) | copy-start | bytes 196612
  102.4 6.8 %collective-permute-start.20 = (bf16[128,256]{1,0:T(8,128)(2,1)S(1)}, bf16[128,256]{1,0:T(8,128)(2,1)S(1)}, u32[]{:S(2)}, u32[]{:S(2)}) collective-permute-start(bf16[128,256]{1,0:T(8,128)(2,1)S(1)} %get-tuple-element.105), channel_id=1, source_target_pairs={{0,16},{8,24},{16,0},{24,8},{1,17},{9,25},{17,1},{25,9},{2,18},{10... | collective-permute-start | bytes 196616 | tf_op jit(solution)/shard_map/ppermute | solution.py:446
  102.8 6.4 %collective-permute-start.21 = (bf16[128,256]{1,0:T(8,128)(2,1)S(1)}, bf16[128,256]{1,0:T(8,128)(2,1)S(1)}, u32[]{:S(2)}, u32[]{:S(2)}) collective-permute-start(bf16[128,256]{1,0:T(8,128)(2,1)S(1)} %get-tuple-element.106), channel_id=1, source_target_pairs={{0,24},{8,16},{16,8},{24,0},{1,25},{9,17},{17,9},{25,1},{2,26},{10... | collective-permute-start | bytes 196616 | tf_op jit(solution)/shard_map/ppermute | solution.py:446
  109.3 10.5 %copy-start.6 = (bf16[128,256]{1,0:T(8,128)(2,1)}, bf16[128,256]{1,0:T(8,128)(2,1)S(1)}, u32[]{:S(2)}) copy-start(bf16[128,256]{1,0:T(8,128)(2,1)S(1)} %collective-permute-done.20.refs_6_) | copy-start | bytes 196612
  109.3 10.5 %copy-start.7 = (bf16[128,256]{1,0:T(8,128)(2,1)}, bf16[128,256]{1,0:T(8,128)(2,1)S(1)}, u32[]{:S(2)}) copy-start(bf16[128,256]{1,0:T(8,128)(2,1)S(1)} %collective-permute-done.21.refs_7_) | copy-start | bytes 196612
  109.3 21.4 %all-to-all-start.3 = ((bf16[8,8,32,128]{3,2,1,0:T(8,128)(2,1)}), bf16[8,8,32,128]{3,2,1,0:T(8,128)(2,1)S(1)}, u32[]{:S(2)}, u32[]{:S(2)}) async-start(bf16[8,8,32,128]{3,2,1,0:T(8,128)(2,1)} %back_pack.1), calls=%async_computation.3 | async-start | bytes 1048576 | tf_op jit(solution)/shard_map/all_to_all | solution.py:609
  116.8 10.7 %collective-permute-start.24 = (bf16[32,2176]{1,0:T(8,128)(2,1)S(1)}, bf16[32,2176]{1,0:T(8,128)(2,1)S(1)}, u32[]{:S(2)}, u32[]{:S(2)}) collective-permute-start(bf16[32,2176]{1,0:T(8,128)(2,1)S(1)} %w_sum.1.refs_0_), channel_id=1, source_target_pairs={{0,16},{8,24},{16,0},{24,8},{1,17},{9,25},{17,1},{25,9},{2,18},{10... | collective-permute-start | bytes 417800 | tf_op jit(solution)/shard_map/ppermute | solution.py:446
  118.5 1.3 collective-permute-start.22
  118.5 9.3 %collective-permute-start.23 = (bf16[32,2176]{1,0:T(8,128)(2,1)S(1)}, bf16[32,2176]{1,0:T(8,128)(2,1)S(1)}, u32[]{:S(2)}, u32[]{:S(2)}) collective-permute-start(bf16[32,2176]{1,0:T(8,128)(2,1)S(1)} %w_sum.1.refs_0_), channel_id=1, source_target_pairs={{0,8},{8,0},{16,24},{24,16},{1,9},{9,1},{17,25},{25,17},{2,10},{10... | collective-permute-start | bytes 417800 | tf_op jit(solution)/shard_map/ppermute | solution.py:446
  119.7 0.6 copy-start.8
  127.5 1.4 %collective-permute-start.25 = (bf16[32,2176]{1,0:T(8,128)(2,1)S(1)}, bf16[32,2176]{1,0:T(8,128)(2,1)S(1)}, u32[]{:S(2)}, u32[]{:S(2)}) collective-permute-start(bf16[32,2176]{1,0:T(8,128)(2,1)S(1)} %collective-permute-done.24.refs_2_), channel_id=1, source_target_pairs={{0,8},{8,0},{16,24},{24,16},{1,9},{9,1},{17,25},{25,17},{2,10},{10... | collective-permute-start | bytes 417800 | tf_op jit(solution)/shard_map/ppermute | solution.py:446
  130.7 0.8 copy-start.5

commit v10 on v9

--- a/solution.py
+++ b/solution.py
@@ -340,22 +340,19 @@
     return total
 
 
-def finish_rest_kernel(top, me_ref, ga_ref, send_ref, hub_ref, *refs):
+def finish_rest_kernel(me_ref, ga_ref, send_ref, hub_ref, *refs):
     own_refs, ret_refs, out_ref = refs[:SPLIT], refs[SPLIT:-1], refs[-1]
-    at = (pl.program_id(0) + top) * out_ref.shape[1]
+    at = pl.program_id(0) * out_ref.shape[1]
     total = times_owned(ga_ref, own_refs)
     out_ref[...] = add_returned(total, at, me_ref, send_ref, hub_ref, ret_refs)
 
 
-def finish_dst_kernel(me_ref, ga_ref, send_ref, hub_ref, back_ref, grads_ref, *refs):
-    own_refs, ret_refs, out_ref, act_ref = refs[:SPLIT], refs[SPLIT:-2], refs[-2], refs[-1]
-    rows = ga_ref.shape[0]
+def finish_dst_kernel(back_ref, grads_ref, out_ref, act_ref):
+    rows = out_ref.shape[0]
     groups = range(back_ref.shape[0])
     own = jnp.concatenate([back_ref[b, :rows] for b in groups], axis=1).astype(F32)
     act_ref[...] = jnp.concatenate([back_ref[b, rows:] for b in groups], axis=1)
-    at = pl.program_id(0) * out_ref.shape[1]
-    total = times_owned(ga_ref, own_refs) + own
-    out_ref[...] = add_returned(total, at, me_ref, send_ref, hub_ref, ret_refs)
+    out_ref[...] = grads_ref[...] + own
 
 
 def column(rows, first):
@@ -372,22 +369,22 @@
 
 
 def finish_rest(me, ga, own, ret, sends, hubs, n_dst):
-    rows, n, top = ga.shape[0], own.shape[0] * WIDE, n_dst // WIDE
+    rows, n = ga.shape[0], own.shape[0] * WIDE
     return pl.pallas_call(
-        functools.partial(finish_rest_kernel, top),
+        finish_rest_kernel,
         out_shape=shape(rows, n, kind=F32),
-        grid=(n // WIDE - top,),
+        grid=(n // WIDE,),
         in_specs=[SMEM, fixed(ga), fixed(sends), fixed(hubs)]
-        + row_blocks(n_dst, top)
+        + row_blocks(n_dst, 0)
         + [fixed(r) for r in ret],
-        out_specs=column(rows, top),
+        out_specs=column(rows, 0),
         compiler_params=pltpu.CompilerParams(vmem_limit_bytes=56 * MIB),
         cost_estimate=pl.CostEstimate(flops=0, bytes_accessed=18000000, transcendentals=0),
         name="finish_rest",
     )(me, ga, sends, hubs, *[own] * SPLIT, *ret)
 
 
-def finish_dst(me, ga, own, ret, sends, hubs, back, grads):
+def finish_dst(back, grads):
     rows, n = grads.shape
     groups, _, piece = back.shape
     n_dst = groups * piece
@@ -396,21 +393,15 @@
         out_shape=[shape(rows, n, kind=F32), shape(rows, n_dst)],
         grid=(n_dst // WIDE,),
         in_specs=[
-            SMEM,
-            fixed(ga),
-            fixed(sends),
-            fixed(hubs),
             pl.BlockSpec((WIDE // piece, 2 * rows, piece), lambda i: (i, 0, 0)),
-            pl.BlockSpec(memory_space=pl.ANY),
-        ]
-        + row_blocks(n_dst, 0)
-        + [fixed(r) for r in ret],
+            column(rows, 0),
+        ],
         out_specs=[column(rows, 0), column(rows, 0)],
-        input_output_aliases={5: 0},
+        input_output_aliases={1: 0},
         compiler_params=pltpu.CompilerParams(vmem_limit_bytes=56 * MIB),
         cost_estimate=pl.CostEstimate(flops=0, bytes_accessed=6000000, transcendentals=0),
         name="finish_dst",
-    )(me, ga, sends, hubs, back, grads, *[own] * SPLIT, *ret)
+    )(back, grads)
 
 
 def body(
@@ -628,9 +619,7 @@
         scalars=1,
     )
 
-    grad_feats, activations = finish_dst(
-        me_s, gagg, a_own, returned, sends, hubs, back, grads
-    )
+    grad_feats, activations = finish_dst(back, grads)
     return (
         activations,
         grad_feats,

time: 136 us -> 136 us (level)
  waiting for transfers between devices: 30.5 us -> 26.8 us
  starting transfers between devices: 46.3 us -> 49.2 us
    ppermute x19, waiting for transfers between devices: 17.1 us -> 13.2 us  [over_dom(): return lax.ppermute(x, 'dom', [(i, i ^ k) for i in range(n_dom)])]
    ppermute x19, starting transfers between devices: 8.87 us -> 11.8 us  [over_dom(): return lax.ppermute(x, 'dom', [(i, i ^ k) for i in range(n_dom)])]
    pallas_call x1, Pallas kernels: 7.16 us -> 9.1 us  [finish_rest(): pl.pallas_call(finish_rest_kernel, out_shape=shape(rows, n, kind=F32), gr...]
    pallas_call x1, Pallas kernels: 3.47 us -> 1.97 us  [finish_dst(): pl.pallas_call(finish_dst_kernel, out_shape=[shape(rows, n, kind=F32), sh...]
    unnamed x28 -> x30, local copies, waits for them, and re-layouts: 4.64 us -> 4.55 us
  transfers between devices with their start and end apart: 30 -> 30, of which waited for: 12 -> 12; matrix products, arithmetic and copies ran while one was open for 3% -> 3% of each run, Pallas kernels for 30% -> 32%
where the time goes in v10:
time: 136 us; the launch traced here: 135 us
  starting transfers between devices  49.2 us (36%)
  Pallas kernels  47.6 us (35%)
  waiting for transfers between devices  26.8 us (20%)
  local copies, waits for them, and re-layouts  6.74 us (5%)
  other arithmetic  2.94 us (2%)
  between operations  1.52 us (1%)
    pallas_call x1, Pallas kernels, build_dense(): pl.pallas_call(functools.partial(build_kernel, n_own), out_shape=(shape(n...  20.2 us
    ppermute x7, starting transfers between devices, over_feat(): return lax.ppermute(x, 'feat', [(i, i ^ k) for i in range(n_feat)])  14.3 us
    ppermute x19, waiting for transfers between devices, over_dom(): return lax.ppermute(x, 'dom', [(i, i ^ k) for i in range(n_dom)])  13.2 us
    pallas_call x10, Pallas kernels, whole_call(): pl.pallas_call(kernel, out_shape=out_shape, in_specs=[SMEM] * scalars + [...  12.4 us
    ppermute x19, starting transfers between devices, over_dom(): return lax.ppermute(x, 'dom', [(i, i ^ k) for i in range(n_dom)])  11.8 us
    pallas_call x1, Pallas kernels, finish_rest(): pl.pallas_call(finish_rest_kernel, out_shape=shape(rows, n, kind=F32), gr...  9.1 us
    ppermute x7, waiting for transfers between devices, over_feat(): return lax.ppermute(x, 'feat', [(i, i ^ k) for i in range(n_feat)])  8.93 us
    all_to_all x1, starting transfers between devices, body(): lax.all_to_all(back, 'feat', 0, 0, tiled=True)  6.44 us
  transfers between devices with their start and end apart: 30, of which 12 were waited for; matrix products, arithmetic and copies ran while one was open for 3% of the time, Pallas kernels for 32%

profile of v10, /device:TPU:0, one launch (start us, length us, event | category | flops | bytes accessed | tf_op | source)
XLA Modules:
  0.0 134.8 jit_solution(12104015528522737273)
XLA Ops:
  0.7 0.9 dynamic-slice_bitcast_fusion
  1.6 4.1 %collective-permute-start = (bf16[1,2,32,1024]{3,2,1,0:T(8,128)(2,1)S(1)}, bf16[1,2,32,1024]{3,2,1,0:T(8,128)(2,1)S(1)}, u32[]{:S(2)}, u32[]{:S(2)}) collective-permute-start(bf16[1,2,32,1024]{3,2,1,0:T(8,128)(2,1)S(1)} %maximum_bitcast_fusion.refs_0_), channel_id=1, source_target_pairs={{0,4},{1,5},{2,6},{3,7},{4,0},{5,1},{6,2},{7,3},{8,12},{9,13},{10,... | collective-permute-start | bytes 393224 | tf_op jit(solution)/shard_map/ppermute | solution.py:440
  5.7 3.9 %pack.1 = (bf16[8,9,32,128]{3,2,1,0:T(8,128)(2,1)}, bf16[128,256]{1,0:T(8,128)(2,1)}, bf16[128,256]{1,0:T(8,128)(2,1)}, bf16[128,256]{1,0:T(8,128)(2,1)}, bf16[128,256]{1,0:T(8,128)(2,1)}) custom-call(s32[1]{0:T(128)} %bitcast.me_ref, bf16[128,4096]{1,0:T(8,128)(2,1)} %x_ref.3, bf16[128,1024]{1,0:T(8,128)(2,1)} %cot_ref.1, f32[1,128]{1,0:T(1,128)} %bitcast.27, ...), custom_call_target="tpu_custom_call" | custom-call | bytes 12000000 | tf_op jit(solution)/shard_map/pack/pallas_call | solution.py:74
  9.6 2.4 %collective-permute-done.refs_1_ = bf16[1,2,32,1024]{3,2,1,0:T(8,128)(2,1)S(1)} collective-permute-done((bf16[1,2,32,1024]{3,2,1,0:T(8,128)(2,1)S(1)}, bf16[1,2,32,1024]{3,2,1,0:T(8,128)(2,1)S(1)}, u32[]{:S(2)}, u32[]{:S(2)}) %collective-permute-start) | collective-permute-done | bytes 131104 | tf_op jit(solution)/shard_map/ppermute | solution.py:440
  12.0 5.7 %all-to-all-start = ((bf16[8,9,32,128]{3,2,1,0:T(8,128)(2,1)}), bf16[8,9,32,128]{3,2,1,0:T(8,128)(2,1)S(1)}, u32[]{:S(2)}, u32[]{:S(2)}) async-start(bf16[8,9,32,128]{3,2,1,0:T(8,128)(2,1)} %get-tuple-element.62), calls=%async_computation | async-start | bytes 1179648 | tf_op jit(solution)/shard_map/all_to_all | solution.py:463
  17.7 1.6 %collective-permute-start.3 = (bf16[128,256]{1,0:T(8,128)(2,1)}, bf16[128,256]{1,0:T(8,128)(2,1)S(1)}, u32[]{:S(2)}, u32[]{:S(2)}) collective-permute-start(bf16[128,256]{1,0:T(8,128)(2,1)} %get-tuple-element.65), channel_id=1, source_target_pairs={{0,16},{8,24},{16,0},{24,8},{1,17},{9,25},{17,1},{25,9},{2,18},{10... | collective-permute-start | bytes 196616 | tf_op jit(solution)/shard_map/ppermute | solution.py:437
  20.8 0.6 concatenate.10.order_ref
  21.4 0.8 convert_reduce_fusion.1.start_ref
  22.2 2.1 %collective-permute-start.1 = (bf16[2,2,32,1024]{3,2,1,0:T(8,128)(2,1)S(1)}, bf16[2,2,32,1024]{3,2,1,0:T(8,128)(2,1)S(1)}, u32[]{:S(2)}, u32[]{:S(2)}) collective-permute-start(bf16[2,2,32,1024]{3,2,1,0:T(8,128)(2,1)S(1)} %pad_maximum_fusion.1), channel_id=1, source_target_pairs={{0,2},{1,3},{2,0},{3,1},{4,6},{5,7},{6,4},{7,5},{8,10},{9,11},{10,... | collective-permute-start | bytes 786440 | tf_op jit(solution)/shard_map/ppermute | solution.py:440
  24.9 20.2 %build_dense.1 = (bf16[8,1024,512]{2,1,0:T(8,128)(2,1)}, bf16[1024,1024]{1,0:T(8,128)(2,1)}, bf16[8,128,128]{2,1,0:T(8,128)(2,1)}) custom-call(s32[514]{0:T(1024)} %concatenate.10.order_ref, s32[321]{0:T(512)} %convert_reduce_fusion.1.start_ref, bf16[128,4096]{1,0:T(8,128)(2,1)} %x_ref.3, bf16[512,128,128]{2,1,0:T(8,128)(2,1)} %vals_hbm.1, ...), custom_call_target="tpu_custom_call" | custom-call | bytes 30000000 | tf_op jit(solution)/shard_map/build_dense/pallas_call | solution.py:139
  45.1 5.2 %all-to-all-start.1 = ((bf16[8,128,128]{2,1,0:T(8,128)(2,1)}), bf16[8,128,128]{2,1,0:T(8,128)(2,1)S(1)}, u32[]{:S(2)}, u32[]{:S(2)}) async-start(bf16[8,128,128]{2,1,0:T(8,128)(2,1)} %get-tuple-element.74), calls=%async_computation.1 | async-start | bytes 524288 | tf_op jit(solution)/shard_map/all_to_all | solution.py:490
  50.5 1.0 collective-permute-start.6
  51.5 0.8 pad_maximum_fusion
  52.3 2.0 %collective-permute-start.5 = (bf16[4,2,32,1024]{3,2,1,0:T(8,128)(2,1)}, bf16[4,2,32,1024]{3,2,1,0:T(8,128)(2,1)S(1)}, u32[]{:S(2)}, u32[]{:S(2)}) collective-permute-start(bf16[4,2,32,1024]{3,2,1,0:T(8,128)(2,1)} %pad_maximum_fusion), channel_id=1, source_target_pairs={{0,1},{1,0},{2,3},{3,2},{4,5},{5,4},{6,7},{7,6},{8,9},{9,8},{10,11... | collective-permute-start | bytes 1572872 | tf_op jit(solution)/shard_map/ppermute | solution.py:440
  54.3 4.7 %all-to-all-done.1 = bf16[8,128,128]{2,1,0:T(8,128)(2,1)S(1)} async-done(((bf16[8,128,128]{2,1,0:T(8,128)(2,1)}), bf16[8,128,128]{2,1,0:T(8,128)(2,1)S(1)}, u32[]{:S(2)}, u32[]{:S(2)}) %all-to-all-start.1) | async-done | bytes 262176 | tf_op jit(solution)/shard_map/all_to_all | solution.py:490
  59.0 1.7 %collective-permute-start.10 = (bf16[1024,128]{1,0:T(8,128)(2,1)S(1)}, bf16[1024,128]{1,0:T(8,128)(2,1)S(1)}, u32[]{:S(2)}, u32[]{:S(2)}) collective-permute-start(bf16[1024,128]{1,0:T(8,128)(2,1)S(1)} %bitcast.18), channel_id=1, source_target_pairs={{0,16},{8,24},{16,0},{24,8},{1,17},{9,25},{17,1},{25,9},{2,18},{10... | collective-permute-start | bytes 786440 | tf_op jit(solution)/shard_map/ppermute | solution.py:437
  60.7 1.0 collective-permute-done.6.refs_5_
  62.2 4.1 %collective-permute-done.10.refs_10_ = bf16[1024,128]{1,0:T(8,128)(2,1)S(1)} collective-permute-done((bf16[1024,128]{1,0:T(8,128)(2,1)S(1)}, bf16[1024,128]{1,0:T(8,128)(2,1)S(1)}, u32[]{:S(2)}, u32[]{:S(2)}) %collective-permute-start.10) | collective-permute-done | bytes 262176 | tf_op jit(solution)/shard_map/ppermute | solution.py:437
  66.4 1.0 collective-permute-done.5.refs_3_
  67.9 2.6 %dense.1 = (bf16[4,256,128]{2,1,0:T(8,128)(2,1)S(1)}, bf16[2,256,128]{2,1,0:T(8,128)(2,1)S(1)}, bf16[2,256,128]{2,1,0:T(8,128)(2,1)S(1)}, bf16[2,1024,128]{2,1,0:T(8,128)(2,1)S(1)}, bf16[2,1024,128]{2,1,0:T(8,128)(2,1)S(1)}) custom-call(f32[256,128]{1,0:T(8,128)S(1)} %get-tuple-element.70.bias_ref, bf16[1,2,32,1024]{3,2,1,0:T(8,128)(2,1)S(1)} %maximum_bitcast_fusion.refs_0_, ...), custom_call_target="tpu_custom_call" | custom-call | bytes 9000000 | tf_op jit(solution)/shard_map/dense/pallas_call | solution.py:29
  70.8 2.3 %grads.1 = (bf16[2,1280,128]{2,1,0:T(8,128)(2,1)S(1)}, bf16[2,1280,128]{2,1,0:T(8,128)(2,1)}, bf16[4,32,2176]{2,1,0:T(8,128)(2,1)S(1)}, bf16[4,32,2176]{2,1,0:T(8,128)(2,1)}) custom-call(bf16[4,256,128]{2,1,0:T(8,128)(2,1)S(1)} %get-tuple-element.75.g_ref, bf16[2,256,128]{2,1,0:T(8,128)(2,1)S(1)} %get-tuple-element.76.act_even, ...), custom_call_target="tpu_custom_call" | custom-call | bytes 9000000 | tf_op jit(solution)/shard_map/grads/pallas_call | solution.py:29
  73.1 0.8 copy-done.1
  74.5 1.6 %collective-permute-start.14 = (bf16[1024,128]{1,0:T(8,128)(2,1)S(1)}, bf16[1024,128]{1,0:T(8,128)(2,1)S(1)}, u32[]{:S(2)}, u32[]{:S(2)}) collective-permute-start(bf16[1024,128]{1,0:T(8,128)(2,1)S(1)} %get-tuple-element.83), channel_id=1, source_target_pairs={{0,16},{8,24},{16,0},{24,8},{1,17},{9,25},{17,1},{25,9},{2,18},{10... | collective-permute-start | bytes 786440 | tf_op jit(solution)/shard_map/ppermute | solution.py:437
  76.1 1.7 %collective-permute-start.16 = (bf16[4,32,2176]{2,1,0:T(8,128)(2,1)}, bf16[4,32,2176]{2,1,0:T(8,128)(2,1)}, u32[]{:S(2)}, u32[]{:S(2)}) collective-permute-start(bf16[4,32,2176]{2,1,0:T(8,128)(2,1)} %get-tuple-element.90), channel_id=1, source_target_pairs={{0,1},{1,0},{2,3},{3,2},{4,5},{5,4},{6,7},{7,6},{8,9},{9,8},{10,11... | collective-permute-start | bytes 1671176 | tf_op jit(solution)/shard_map/ppermute | solution.py:440
  77.8 5.0 %collective-permute-done.14 = bf16[1024,128]{1,0:T(8,128)(2,1)S(1)} collective-permute-done((bf16[1024,128]{1,0:T(8,128)(2,1)S(1)}, bf16[1024,128]{1,0:T(8,128)(2,1)S(1)}, u32[]{:S(2)}, u32[]{:S(2)}) %collective-permute-start.14) | collective-permute-done | bytes 262176 | tf_op jit(solution)/shard_map/ppermute | solution.py:437
  82.8 0.8 add_convert_fusion
  83.6 5.7 %all-to-all-start.2 = ((bf16[8,128,128]{2,1,0:T(8,128)(2,1)}), bf16[8,128,128]{2,1,0:T(8,128)(2,1)S(1)}, u32[]{:S(2)}, u32[]{:S(2)}) async-start(bf16[8,128,128]{2,1,0:T(8,128)(2,1)} %bitcast.10), calls=%async_computation.2 | async-start | bytes 524288 | tf_op jit(solution)/shard_map/all_to_all | solution.py:563
  89.3 1.9 %back_pair.1 = (bf16[1536,128]{1,0:T(8,128)(2,1)S(1)}, bf16[1536,128]{1,0:T(8,128)(2,1)}) custom-call(bf16[2,1280,128]{2,1,0:T(8,128)(2,1)S(1)} %get-tuple-element.78.even_ref, bf16[2,1280,128]{2,1,0:T(8,128)(2,1)} %collective-permute-done.13.got_ref), custom_call_target="tpu_custom_call" | custom-call | bytes 3000000 | tf_op jit(solution)/shard_map/back_pair/pallas_call | solution.py:29
  91.2 1.6 %collective-permute-start.15 = (bf16[1536,128]{1,0:T(8,128)(2,1)}, bf16[1536,128]{1,0:T(8,128)(2,1)S(1)}, u32[]{:S(2)}, u32[]{:S(2)}) collective-permute-start(bf16[1536,128]{1,0:T(8,128)(2,1)} %get-tuple-element.87), channel_id=1, source_target_pairs={{0,16},{8,24},{16,0},{24,8},{1,17},{9,25},{17,1},{25,9},{2,18},{10... | collective-permute-start | bytes 1179656 | tf_op jit(solution)/shard_map/ppermute | solution.py:437
  92.8 1.1 copy-done.2
  93.9 1.8 %x_sum.1 = (bf16[32,2176]{1,0:T(8,128)(2,1)S(1)}, bf16[32,2176]{1,0:T(8,128)(2,1)}, bf16[32,2176]{1,0:T(8,128)(2,1)}, bf16[32,2176]{1,0:T(8,128)(2,1)}) custom-call(bf16[4,32,2176]{2,1,0:T(8,128)(2,1)S(1)} %copy-done.2, bf16[4,32,2176]{2,1,0:T(8,128)(2,1)} %collective-permute-done.16.got_ref), custom_call_target="tpu_custom_call" | custom-call | bytes 3000000 | tf_op jit(solution)/shard_map/x_sum/pallas_call | solution.py:29
  95.7 2.9 %collective-permute-start.17 = (bf16[32,2176]{1,0:T(8,128)(2,1)}, bf16[32,2176]{1,0:T(8,128)(2,1)}, u32[]{:S(2)}, u32[]{:S(2)}) collective-permute-start(bf16[32,2176]{1,0:T(8,128)(2,1)} %get-tuple-element.93), channel_id=1, source_target_pairs={{0,4},{1,5},{2,6},{3,7},{4,0},{5,1},{6,2},{7,3},{8,12},{9,13},{10,... | collective-permute-start | bytes 417800 | tf_op jit(solution)/shard_map/ppermute | solution.py:440
  98.7 1.5 %collective-permute-start.18 = (bf16[32,2176]{1,0:T(8,128)(2,1)}, bf16[32,2176]{1,0:T(8,128)(2,1)}, u32[]{:S(2)}, u32[]{:S(2)}) collective-permute-start(bf16[32,2176]{1,0:T(8,128)(2,1)} %get-tuple-element.94), channel_id=1, source_target_pairs={{0,2},{1,3},{2,0},{3,1},{4,6},{5,7},{6,4},{7,5},{8,10},{9,11},{10,... | collective-permute-start | bytes 417800 | tf_op jit(solution)/shard_map/ppermute | solution.py:440
  100.6 0.6 copy-done.4
  101.6 1.6 %collective-permute-start.20 = (bf16[128,256]{1,0:T(8,128)(2,1)S(1)}, bf16[128,256]{1,0:T(8,128)(2,1)S(1)}, u32[]{:S(2)}, u32[]{:S(2)}) collective-permute-start(bf16[128,256]{1,0:T(8,128)(2,1)S(1)} %get-tuple-element.104), channel_id=1, source_target_pairs={{0,16},{8,24},{16,0},{24,8},{1,17},{9,25},{17,1},{25,9},{2,18},{10... | collective-permute-start | bytes 196616 | tf_op jit(solution)/shard_map/ppermute | solution.py:437
  103.2 4.0 %collective-permute-done.17.refs_1_ = bf16[32,2176]{1,0:T(8,128)(2,1)} collective-permute-done((bf16[32,2176]{1,0:T(8,128)(2,1)}, bf16[32,2176]{1,0:T(8,128)(2,1)}, u32[]{:S(2)}, u32[]{:S(2)}) %collective-permute-start.17) | collective-permute-done | bytes 139296 | tf_op jit(solution)/shard_map/ppermute | solution.py:440
  107.2 1.5 %collective-permute-done.19.refs_3_ = bf16[32,2176]{1,0:T(8,128)(2,1)} collective-permute-done((bf16[32,2176]{1,0:T(8,128)(2,1)}, bf16[32,2176]{1,0:T(8,128)(2,1)}, u32[]{:S(2)}, u32[]{:S(2)}) %collective-permute-start.19) | collective-permute-done | bytes 139296 | tf_op jit(solution)/shard_map/ppermute | solution.py:440
  108.7 0.9 back_pack.1
  109.6 6.4 %all-to-all-start.3 = ((bf16[8,8,32,128]{3,2,1,0:T(8,128)(2,1)}), bf16[8,8,32,128]{3,2,1,0:T(8,128)(2,1)S(1)}, u32[]{:S(2)}, u32[]{:S(2)}) async-start(bf16[8,8,32,128]{3,2,1,0:T(8,128)(2,1)} %back_pack.1), calls=%async_computation.3 | async-start | bytes 1048576 | tf_op jit(solution)/shard_map/all_to_all | solution.py:600
  116.1 1.1 w_sum.1.refs_0_
  118.2 1.0 collective-permute-done.22.refs_5_
  119.2 0.6 copy-done.12
  119.8 9.1 %finish_rest.1.grads_ref = f32[128,4096]{1,0:T(8,128)} custom-call(s32[1]{0:T(128)} %bitcast.me_ref, bf16[128,1024]{1,0:T(8,128)(2,1)} %copy-done.3, s32[4,128]{1,0:T(4,128)} %bitcast.24, s32[1,128]{1,0:T(1,128)} %bitcast.26, bf16[8,1024,512]{2,1,0:T(8,128)(2,1)} %get-tuple-element.110.refs_0_.refs_1_.refs_2_.refs_3_, ...), custom_call_target="tpu_custom_call" | custom-call | bytes 18000000 | tf_op jit(solution)/shard_map/finish_rest/pallas_call | solution.py:373
  129.1 1.2 collective-permute-done.25.refs_3_
  130.3 1.0 w_out.1
  131.4 0.6 reshape_squeeze.3
  132.1 0.8 copy-done.6
  132.9 2.0 %finish_dst.1 = (f32[128,4096]{1,0:T(8,128)}, bf16[128,1024]{1,0:T(8,128)(2,1)}) custom-call(bf16[8,256,128]{2,1,0:T(8,128)(2,1)} %bitcast.22, f32[128,4096]{1,0:T(8,128)} %finish_rest.1.grads_ref), custom_call_target="tpu_custom_call", output_to_operand_aliasing={{0}: (1, {})} | custom-call | bytes 6000000 | tf_op jit(solution)/shard_map/finish_dst/pallas_call | solution.py:391
  (69 shorter events, 5.6 us)
Async XLA Ops:
  0.6 19.6 %copy-start.14 = (s32[512]{0:T(512)S(1)}, s32[512]{0:T(512)}, u32[]{:S(2)}) copy-start(s32[512]{0:T(512)} %param.14) | copy-start | bytes 6148
  0.6 19.6 %copy-start.13 = (s32[512]{0:T(512)S(1)}, s32[512]{0:T(512)}, u32[]{:S(2)}) copy-start(s32[512]{0:T(512)} %param.15) | copy-start | bytes 6148
  1.6 10.4 %collective-permute-start = (bf16[1,2,32,1024]{3,2,1,0:T(8,128)(2,1)S(1)}, bf16[1,2,32,1024]{3,2,1,0:T(8,128)(2,1)S(1)}, u32[]{:S(2)}, u32[]{:S(2)}) collective-permute-start(bf16[1,2,32,1024]{3,2,1,0:T(8,128)(2,1)S(1)} %maximum_bitcast_fusion.refs_0_), channel_id=1, source_target_pairs={{0,4},{1,5},{2,6},{3,7},{4,0},{5,1},{6,2},{7,3},{8,12},{9,13},{10,... | collective-permute-start | bytes 393224 | tf_op jit(solution)/shard_map/ppermute | solution.py:440
  12.0 33.1 %all-to-all-start = ((bf16[8,9,32,128]{3,2,1,0:T(8,128)(2,1)}), bf16[8,9,32,128]{3,2,1,0:T(8,128)(2,1)S(1)}, u32[]{:S(2)}, u32[]{:S(2)}) async-start(bf16[8,9,32,128]{3,2,1,0:T(8,128)(2,1)} %get-tuple-element.62), calls=%async_computation | async-start | bytes 1179648 | tf_op jit(solution)/shard_map/all_to_all | solution.py:463
  17.7 6.5 %collective-permute-start.2 = (bf16[128,256]{1,0:T(8,128)(2,1)}, bf16[128,256]{1,0:T(8,128)(2,1)S(1)}, u32[]{:S(2)}, u32[]{:S(2)}) collective-permute-start(bf16[128,256]{1,0:T(8,128)(2,1)} %get-tuple-element.64), channel_id=1, source_target_pairs={{0,8},{8,0},{16,24},{24,16},{1,9},{9,1},{17,25},{25,17},{2,10},{10... | collective-permute-start | bytes 196616 | tf_op jit(solution)/shard_map/ppermute | solution.py:437
  17.7 6.5 %collective-permute-start.3 = (bf16[128,256]{1,0:T(8,128)(2,1)}, bf16[128,256]{1,0:T(8,128)(2,1)S(1)}, u32[]{:S(2)}, u32[]{:S(2)}) collective-permute-start(bf16[128,256]{1,0:T(8,128)(2,1)} %get-tuple-element.65), channel_id=1, source_target_pairs={{0,16},{8,24},{16,0},{24,8},{1,17},{9,25},{17,1},{25,9},{2,18},{10... | collective-permute-start | bytes 196616 | tf_op jit(solution)/shard_map/ppermute | solution.py:437
  19.3 5.0 %collective-permute-start.4 = (bf16[128,256]{1,0:T(8,128)(2,1)}, bf16[128,256]{1,0:T(8,128)(2,1)S(1)}, u32[]{:S(2)}, u32[]{:S(2)}) collective-permute-start(bf16[128,256]{1,0:T(8,128)(2,1)} %get-tuple-element.66), channel_id=1, source_target_pairs={{0,24},{8,16},{16,8},{24,0},{1,25},{9,17},{17,9},{25,1},{2,26},{10... | collective-permute-start | bytes 196616 | tf_op jit(solution)/shard_map/ppermute | solution.py:437
  22.2 28.2 %collective-permute-start.1 = (bf16[2,2,32,1024]{3,2,1,0:T(8,128)(2,1)S(1)}, bf16[2,2,32,1024]{3,2,1,0:T(8,128)(2,1)S(1)}, u32[]{:S(2)}, u32[]{:S(2)}) collective-permute-start(bf16[2,2,32,1024]{3,2,1,0:T(8,128)(2,1)S(1)} %pad_maximum_fusion.1), channel_id=1, source_target_pairs={{0,2},{1,3},{2,0},{3,1},{4,6},{5,7},{6,4},{7,5},{8,10},{9,11},{10,... | collective-permute-start | bytes 786440 | tf_op jit(solution)/shard_map/ppermute | solution.py:440
  24.3 0.6 copy-start.9
  24.3 0.6 copy-start.10
  24.3 0.6 copy-start.11
  45.1 13.9 %all-to-all-start.1 = ((bf16[8,128,128]{2,1,0:T(8,128)(2,1)}), bf16[8,128,128]{2,1,0:T(8,128)(2,1)S(1)}, u32[]{:S(2)}, u32[]{:S(2)}) async-start(bf16[8,128,128]{2,1,0:T(8,128)(2,1)} %get-tuple-element.74), calls=%async_computation.1 | async-start | bytes 524288 | tf_op jit(solution)/shard_map/all_to_all | solution.py:490
  50.5 11.2 %collective-permute-start.6 = (bf16[1536,128]{1,0:T(8,128)(2,1)S(1)}, bf16[1536,128]{1,0:T(8,128)(2,1)S(1)}, u32[]{:S(2)}, u32[]{:S(2)}) collective-permute-start(bf16[1536,128]{1,0:T(8,128)(2,1)S(1)} %get-tuple-element.72), channel_id=1, source_target_pairs={{0,16},{8,24},{16,0},{24,8},{1,17},{9,25},{17,1},{25,9},{2,18},{10... | collective-permute-start | bytes 1179656 | tf_op jit(solution)/shard_map/ppermute | solution.py:437
  52.3 15.1 %collective-permute-start.5 = (bf16[4,2,32,1024]{3,2,1,0:T(8,128)(2,1)}, bf16[4,2,32,1024]{3,2,1,0:T(8,128)(2,1)S(1)}, u32[]{:S(2)}, u32[]{:S(2)}) collective-permute-start(bf16[4,2,32,1024]{3,2,1,0:T(8,128)(2,1)} %pad_maximum_fusion), channel_id=1, source_target_pairs={{0,1},{1,0},{2,3},{3,2},{4,5},{5,4},{6,7},{7,6},{8,9},{9,8},{10,11... | collective-permute-start | bytes 1572872 | tf_op jit(solution)/shard_map/ppermute | solution.py:440
  59.0 7.4 %collective-permute-start.10 = (bf16[1024,128]{1,0:T(8,128)(2,1)S(1)}, bf16[1024,128]{1,0:T(8,128)(2,1)S(1)}, u32[]{:S(2)}, u32[]{:S(2)}) collective-permute-start(bf16[1024,128]{1,0:T(8,128)(2,1)S(1)} %bitcast.18), channel_id=1, source_target_pairs={{0,16},{8,24},{16,0},{24,8},{1,17},{9,25},{17,1},{25,9},{2,18},{10... | collective-permute-start | bytes 786440 | tf_op jit(solution)/shard_map/ppermute | solution.py:437
  60.7 6.8 %collective-permute-start.7 = (bf16[1280,128]{1,0:T(8,128)(2,1)S(1)}, bf16[1280,128]{1,0:T(8,128)(2,1)S(1)}, u32[]{:S(2)}, u32[]{:S(2)}) collective-permute-start(bf16[1280,128]{1,0:T(8,128)(2,1)S(1)} %get-tuple-element.73), channel_id=1, source_target_pairs={{0,8},{8,0},{16,24},{24,16},{1,9},{9,1},{17,25},{25,17},{2,10},{10... | collective-permute-start | bytes 983048 | tf_op jit(solution)/shard_map/ppermute | solution.py:437
  61.7 5.8 %collective-permute-start.8 = (bf16[1280,128]{1,0:T(8,128)(2,1)S(1)}, bf16[1280,128]{1,0:T(8,128)(2,1)S(1)}, u32[]{:S(2)}, u32[]{:S(2)}) collective-permute-start(bf16[1280,128]{1,0:T(8,128)(2,1)S(1)} %slice.8), channel_id=1, source_target_pairs={{0,8},{8,0},{16,24},{24,16},{1,9},{9,1},{17,25},{25,17},{2,10},{10... | collective-permute-start | bytes 983048 | tf_op jit(solution)/shard_map/ppermute | solution.py:437
  61.8 5.7 %collective-permute-start.9 = (bf16[1024,128]{1,0:T(8,128)(2,1)S(1)}, bf16[1024,128]{1,0:T(8,128)(2,1)S(1)}, u32[]{:S(2)}, u32[]{:S(2)}) collective-permute-start(bf16[1024,128]{1,0:T(8,128)(2,1)S(1)} %bitcast.19), channel_id=1, source_target_pairs={{0,8},{8,0},{16,24},{24,16},{1,9},{9,1},{17,25},{25,17},{2,10},{10... | collective-permute-start | bytes 786440 | tf_op jit(solution)/shard_map/ppermute | solution.py:437
  66.4 1.5 %collective-permute-start.11 = (bf16[1024,128]{1,0:T(8,128)(2,1)S(1)}, bf16[1024,128]{1,0:T(8,128)(2,1)S(1)}, u32[]{:S(2)}, u32[]{:S(2)}) collective-permute-start(bf16[1024,128]{1,0:T(8,128)(2,1)S(1)} %collective-permute-done.10.refs_10_), channel_id=1, source_target_pairs={{0,8},{8,0},{16,24},{24,16},{1,9},{9,1},{17,25},{25,17},{2,10},{10... | collective-permute-start | bytes 786440 | tf_op jit(solution)/shard_map/ppermute | solution.py:437
  70.6 3.3 %collective-permute-start.12 = (bf16[2,1024,128]{2,1,0:T(8,128)(2,1)S(1)}, bf16[2,1024,128]{2,1,0:T(8,128)(2,1)S(1)}, u32[]{:S(2)}, u32[]{:S(2)}) collective-permute-start(bf16[2,1024,128]{2,1,0:T(8,128)(2,1)S(1)} %get-tuple-element.81), channel_id=1, source_target_pairs={{0,8},{8,0},{16,24},{24,16},{1,9},{9,1},{17,25},{25,17},{2,10},{10... | collective-permute-start | bytes 1572872 | tf_op jit(solution)/shard_map/ppermute | solution.py:437
  73.1 0.8 copy-start.1
  74.0 26.1 %copy-start = (bf16[1024,1024]{1,0:T(8,128)(2,1)S(1)}, bf16[1024,1024]{1,0:T(8,128)(2,1)}, u32[]{:S(2)}) copy-start(bf16[1024,1024]{1,0:T(8,128)(2,1)} %get-tuple-element.97.ext_ref) | copy-start | bytes 6291460
  74.0 15.3 %collective-permute-start.13 = (bf16[2,1280,128]{2,1,0:T(8,128)(2,1)}, bf16[2,1280,128]{2,1,0:T(8,128)(2,1)}, u32[]{:S(2)}, u32[]{:S(2)}) collective-permute-start(bf16[2,1280,128]{2,1,0:T(8,128)(2,1)} %get-tuple-element.84), channel_id=1, source_target_pairs={{0,8},{8,0},{16,24},{24,16},{1,9},{9,1},{17,25},{25,17},{2,10},{10... | collective-permute-start | bytes 1966088 | tf_op jit(solution)/shard_map/ppermute | solution.py:437
  74.5 8.3 %collective-permute-start.14 = (bf16[1024,128]{1,0:T(8,128)(2,1)S(1)}, bf16[1024,128]{1,0:T(8,128)(2,1)S(1)}, u32[]{:S(2)}, u32[]{:S(2)}) collective-permute-start(bf16[1024,128]{1,0:T(8,128)(2,1)S(1)} %get-tuple-element.83), channel_id=1, source_target_pairs={{0,16},{8,24},{16,0},{24,8},{1,17},{9,25},{17,1},{25,9},{2,18},{10... | collective-permute-start | bytes 786440 | tf_op jit(solution)/shard_map/ppermute | solution.py:437
  76.1 16.7 %collective-permute-start.16 = (bf16[4,32,2176]{2,1,0:T(8,128)(2,1)}, bf16[4,32,2176]{2,1,0:T(8,128)(2,1)}, u32[]{:S(2)}, u32[]{:S(2)}) collective-permute-start(bf16[4,32,2176]{2,1,0:T(8,128)(2,1)} %get-tuple-element.90), channel_id=1, source_target_pairs={{0,1},{1,0},{2,3},{3,2},{4,5},{5,4},{6,7},{7,6},{8,9},{9,8},{10,11... | collective-permute-start | bytes 1671176 | tf_op jit(solution)/shard_map/ppermute | solution.py:440
  83.6 16.5 %all-to-all-start.2 = ((bf16[8,128,128]{2,1,0:T(8,128)(2,1)}), bf16[8,128,128]{2,1,0:T(8,128)(2,1)S(1)}, u32[]{:S(2)}, u32[]{:S(2)}) async-start(bf16[8,128,128]{2,1,0:T(8,128)(2,1)} %bitcast.10), calls=%async_computation.2 | async-start | bytes 524288 | tf_op jit(solution)/shard_map/all_to_all | solution.py:563
  91.2 10.4 %collective-permute-start.15 = (bf16[1536,128]{1,0:T(8,128)(2,1)}, bf16[1536,128]{1,0:T(8,128)(2,1)S(1)}, u32[]{:S(2)}, u32[]{:S(2)}) collective-permute-start(bf16[1536,128]{1,0:T(8,128)(2,1)} %get-tuple-element.87), channel_id=1, source_target_pairs={{0,16},{8,24},{16,0},{24,8},{1,17},{9,25},{17,1},{25,9},{2,18},{10... | collective-permute-start | bytes 1179656 | tf_op jit(solution)/shard_map/ppermute | solution.py:437
  92.8 1.1 copy-start.2
  95.7 11.5 %collective-permute-start.17 = (bf16[32,2176]{1,0:T(8,128)(2,1)}, bf16[32,2176]{1,0:T(8,128)(2,1)}, u32[]{:S(2)}, u32[]{:S(2)}) collective-permute-start(bf16[32,2176]{1,0:T(8,128)(2,1)} %get-tuple-element.93), channel_id=1, source_target_pairs={{0,4},{1,5},{2,6},{3,7},{4,0},{5,1},{6,2},{7,3},{8,12},{9,13},{10,... | collective-permute-start | bytes 417800 | tf_op jit(solution)/shard_map/ppermute | solution.py:440
  98.7 8.6 %collective-permute-start.18 = (bf16[32,2176]{1,0:T(8,128)(2,1)}, bf16[32,2176]{1,0:T(8,128)(2,1)}, u32[]{:S(2)}, u32[]{:S(2)}) collective-permute-start(bf16[32,2176]{1,0:T(8,128)(2,1)} %get-tuple-element.94), channel_id=1, source_target_pairs={{0,2},{1,3},{2,0},{3,1},{4,6},{5,7},{6,4},{7,5},{8,10},{9,11},{10,... | collective-permute-start | bytes 417800 | tf_op jit(solution)/shard_map/ppermute | solution.py:440
  100.1 8.6 %collective-permute-start.19 = (bf16[32,2176]{1,0:T(8,128)(2,1)}, bf16[32,2176]{1,0:T(8,128)(2,1)}, u32[]{:S(2)}, u32[]{:S(2)}) collective-permute-start(bf16[32,2176]{1,0:T(8,128)(2,1)} %get-tuple-element.95), channel_id=1, source_target_pairs={{0,6},{1,7},{2,4},{3,5},{4,2},{5,3},{6,0},{7,1},{8,14},{9,15},{10,... | collective-permute-start | bytes 417800 | tf_op jit(solution)/shard_map/ppermute | solution.py:440
  100.6 0.6 copy-start.4
  101.2 8.4 %copy-start.5 = (bf16[128,256]{1,0:T(8,128)(2,1)}, bf16[128,256]{1,0:T(8,128)(2,1)S(1)}, u32[]{:S(2)}) copy-start(bf16[128,256]{1,0:T(8,128)(2,1)S(1)} %get-tuple-element.103) | copy-start | bytes 196612
  101.2 18.0 %copy-start.3 = (bf16[128,1024]{1,0:T(8,128)(2,1)}, bf16[128,1024]{1,0:T(8,128)(2,1)S(1)}, u32[]{:S(2)}) copy-start(bf16[128,1024]{1,0:T(8,128)(2,1)S(1)} %get-tuple-element.109.ga_ref) | copy-start | bytes 786436
  101.6 8.1 %collective-permute-start.20 = (bf16[128,256]{1,0:T(8,128)(2,1)S(1)}, bf16[128,256]{1,0:T(8,128)(2,1)S(1)}, u32[]{:S(2)}, u32[]{:S(2)}) collective-permute-start(bf16[128,256]{1,0:T(8,128)(2,1)S(1)} %get-tuple-element.104), channel_id=1, source_target_pairs={{0,16},{8,24},{16,0},{24,8},{1,17},{9,25},{17,1},{25,9},{2,18},{10... | collective-permute-start | bytes 196616 | tf_op jit(solution)/shard_map/ppermute | solution.py:437
  103.2 6.4 %collective-permute-start.21 = (bf16[128,256]{1,0:T(8,128)(2,1)S(1)}, bf16[128,256]{1,0:T(8,128)(2,1)S(1)}, u32[]{:S(2)}, u32[]{:S(2)}) collective-permute-start(bf16[128,256]{1,0:T(8,128)(2,1)S(1)} %get-tuple-element.105), channel_id=1, source_target_pairs={{0,24},{8,16},{16,8},{24,0},{1,25},{9,17},{17,9},{25,1},{2,26},{10... | collective-permute-start | bytes 196616 | tf_op jit(solution)/shard_map/ppermute | solution.py:437
  109.6 9.6 %copy-start.7 = (bf16[128,256]{1,0:T(8,128)(2,1)}, bf16[128,256]{1,0:T(8,128)(2,1)S(1)}, u32[]{:S(2)}) copy-start(bf16[128,256]{1,0:T(8,128)(2,1)S(1)} %collective-permute-done.20.refs_6_) | copy-start | bytes 196612
  109.6 9.6 %copy-start.8 = (bf16[128,256]{1,0:T(8,128)(2,1)}, bf16[128,256]{1,0:T(8,128)(2,1)S(1)}, u32[]{:S(2)}) copy-start(bf16[128,256]{1,0:T(8,128)(2,1)S(1)} %collective-permute-done.21.refs_7_) | copy-start | bytes 196612
  109.6 22.4 %all-to-all-start.3 = ((bf16[8,8,32,128]{3,2,1,0:T(8,128)(2,1)}), bf16[8,8,32,128]{3,2,1,0:T(8,128)(2,1)S(1)}, u32[]{:S(2)}, u32[]{:S(2)}) async-start(bf16[8,8,32,128]{3,2,1,0:T(8,128)(2,1)} %back_pack.1), calls=%async_computation.3 | async-start | bytes 1048576 | tf_op jit(solution)/shard_map/all_to_all | solution.py:600
  117.2 11.7 %collective-permute-start.24 = (bf16[32,2176]{1,0:T(8,128)(2,1)S(1)}, bf16[32,2176]{1,0:T(8,128)(2,1)S(1)}, u32[]{:S(2)}, u32[]{:S(2)}) collective-permute-start(bf16[32,2176]{1,0:T(8,128)(2,1)S(1)} %w_sum.1.refs_0_), channel_id=1, source_target_pairs={{0,16},{8,24},{16,0},{24,8},{1,17},{9,25},{17,1},{25,9},{2,18},{10... | collective-permute-start | bytes 417800 | tf_op jit(solution)/shard_map/ppermute | solution.py:437
  117.7 1.5 %collective-permute-start.22 = (bf16[128,256]{1,0:T(8,128)(2,1)}, bf16[128,256]{1,0:T(8,128)(2,1)S(1)}, u32[]{:S(2)}, u32[]{:S(2)}) collective-permute-start(bf16[128,256]{1,0:T(8,128)(2,1)} %copy-done.5), channel_id=1, source_target_pairs={{0,8},{8,0},{16,24},{24,16},{1,9},{9,1},{17,25},{25,17},{2,10},{10... | collective-permute-start | bytes 196616 | tf_op jit(solution)/shard_map/ppermute | solution.py:437
  117.7 11.5 %collective-permute-start.23 = (bf16[32,2176]{1,0:T(8,128)(2,1)S(1)}, bf16[32,2176]{1,0:T(8,128)(2,1)S(1)}, u32[]{:S(2)}, u32[]{:S(2)}) collective-permute-start(bf16[32,2176]{1,0:T(8,128)(2,1)S(1)} %w_sum.1.refs_0_), channel_id=1, source_target_pairs={{0,8},{8,0},{16,24},{24,16},{1,9},{9,1},{17,25},{25,17},{2,10},{10... | collective-permute-start | bytes 417800 | tf_op jit(solution)/shard_map/ppermute | solution.py:437
  119.2 0.6 copy-start.12
  128.9 1.4 %collective-permute-start.25 = (bf16[32,2176]{1,0:T(8,128)(2,1)S(1)}, bf16[32,2176]{1,0:T(8,128)(2,1)S(1)}, u32[]{:S(2)}, u32[]{:S(2)}) collective-permute-start(bf16[32,2176]{1,0:T(8,128)(2,1)S(1)} %collective-permute-done.24.refs_2_), channel_id=1, source_target_pairs={{0,8},{8,0},{16,24},{24,16},{1,9},{9,1},{17,25},{25,17},{2,10},{10... | collective-permute-start | bytes 417800 | tf_op jit(solution)/shard_map/ppermute | solution.py:437
  132.1 0.8 copy-start.6
